TPU v7x, 32 devices: a whole 2x2x4 slice. The times are simulated.
32 devices in a mesh: dp: 8 (over z, x), tile: 4 (over y, core).
Axes of the slice: x: 2, y: 2, z: 4, core: 2. Of those that a mesh axis runs over, the one named last changes fastest.
Arguments:
- patch_in: bfloat16 [8, 4, 16, 16, 768], P('dp', 'tile'), may hold values from -6 to 6
- cls_in: bfloat16 [8, 768], P('dp'), may hold values from -6 to 6
- page_side: int32 [8], P('dp'), may hold values from 14 to 32, as said below
- norm_attn: float32 [2, 768], replicated, may hold values from 0.25 to 1.75
- qkv_weight: bfloat16 [2, 768, 2304], replicated, may hold values from -0.21875 to 0.21875
- rel_table: float32 [2, 12, 49], replicated, may hold values from -4 to 4
- out_weight: bfloat16 [2, 768, 768], replicated, may hold values from -0.4375 to 0.4375
- scale_attn: float32 [2, 768], replicated, may hold values from 0.5 to 1.5
- norm_mlp: float32 [2, 768], replicated, may hold values from 0.25 to 1.75
- up_weight: bfloat16 [2, 768, 3072], replicated, may hold values from -0.21875 to 0.21875
- down_weight: bfloat16 [2, 3072, 768], replicated, may hold values from -0.109375 to 0.109375
- scale_mlp: float32 [2, 768], replicated, may hold values from 0.5 to 1.5
- patch_cot: bfloat16 [8, 4, 16, 16, 768], P('dp', 'tile'), may hold values from -6 to 6
- cls_cot: bfloat16 [8, 768], P('dp'), may hold values from -6 to 6
Outputs:
- patch_out: bfloat16 [8, 4, 16, 16, 768], P('dp', 'tile')
- cls_out: bfloat16 [8, 768], P('dp')
- patch_grad: float32 [8, 4, 16, 16, 768], P('dp', 'tile')
- cls_grad: float32 [8, 768], P('dp')
- grad_norm_attn: float32 [2, 768], P(None, ('dp', 'tile'))
- grad_qkv: float32 [2, 768, 2304], P(None, ('dp', 'tile'))
- grad_table: float32 [2, 12, 49], replicated
- grad_out: float32 [2, 768, 768], P(None, ('dp', 'tile'))
- grad_scale_attn: float32 [2, 768], P(None, ('dp', 'tile'))
- grad_norm_mlp: float32 [2, 768], P(None, ('dp', 'tile'))
- grad_up: float32 [2, 768, 3072], P(None, ('dp', 'tile'))
- grad_down: float32 [2, 3072, 768], P(None, ('dp', 'tile'))
- grad_scale_mlp: float32 [2, 768], P(None, ('dp', 'tile'))
Inputs may be any that keep to these rules, and one draw needn't show every extreme that they name: `page_side`: every side is one of 14, 24 and 32; each aligned group of 4 consecutive pages holds a page of side 32.
All inputs are finite; a program needn't handle non-finite values.
Results may differ from a plain program's by a relative error of at most 0.017.
Values may be sent and summed in bfloat16 or wider, within the bound.
No kernel may reach another device: no remote copies, remote signals or barrier semaphores. Data moves between devices by JAX's collectives and lax.ppermute only.
A program may use at most 320 MiB of HBM per device.

v0:
```python
import jax
import jax.numpy as jnp
from jax import lax
from jax.sharding import PartitionSpec as P

RADIUS = 3


epsilon = 1e-06
masked_score = -1e30
highest = lax.Precision.HIGHEST


def from_partner(block, axis, apart):
    count = lax.axis_size(axis)
    route = []
    for low in range(count):
        high = low | 1 << apart
        if high != low and high < count:
            route += [(low, high), (high, low)]
    return lax.ppermute(block, axis, route)


def merged(value, axis, join):
    pieces = jax.tree.map(lambda part: lax.all_gather(part, axis), value)
    head = jax.tree.map(lambda part: part[0], pieces)
    tail = jax.tree.map(lambda part: part[1:], pieces)
    running, _ = lax.scan(lambda running, piece: (join(running, piece), None), head, tail)
    return running


def matmul(left_matrix, right_matrix):
    return jnp.dot(left_matrix, right_matrix, preferred_element_type=jnp.float32)


def matmul_tn(left_matrix, right_matrix):
    return lax.dot_general(
        left_matrix, right_matrix, (((0,), (0,)), ((), ())), preferred_element_type=jnp.float32
    )


def matmul_nt(left_matrix, right_matrix):
    return lax.dot_general(
        left_matrix, right_matrix, (((1,), (1,)), ((), ())), preferred_element_type=jnp.float32
    )


def layer_norm(values, gain_row):
    centre = jnp.mean(values, axis=-1, keepdims=True)
    centred = values - centre
    spread = jnp.mean(centred * centred, axis=-1, keepdims=True)
    return centred * lax.rsqrt(spread + epsilon) * gain_row


def norm_backward(values, gain_row, d_output):
    centre = jnp.mean(values, axis=-1, keepdims=True)
    centred = values - centre
    spread = jnp.mean(centred * centred, axis=-1, keepdims=True)
    inverse = lax.rsqrt(spread + epsilon)
    unit_rows = centred * inverse
    d_unit = d_output * gain_row
    d_values = inverse * (
        d_unit
        - jnp.mean(d_unit, axis=-1, keepdims=True)
        - unit_rows * jnp.mean(d_unit * unit_rows, axis=-1, keepdims=True)
    )
    return (d_values, d_output * unit_rows)


def merge_partial(part_one, part_two):
    top_one, total_one, sum_one = part_one
    top_two, total_two, sum_two = part_two
    top_both = jnp.maximum(top_one, top_two)
    factor_one = jnp.exp(top_one - top_both)
    factor_two = jnp.exp(top_two - top_both)
    return (
        top_both,
        total_one * factor_one + total_two * factor_two,
        sum_one * factor_one[..., None] + sum_two * factor_two[..., None],
    )


def add_block(target, addend, row_start, col_start):
    block_len = addend.shape[1]
    current = target[:, row_start : row_start + block_len, col_start : col_start + block_len]
    return lax.dynamic_update_slice(target, current + addend, (0, row_start, col_start, 0, 0))


def window_tables(side_len, ext_len):
    span = 2 * RADIUS + 1
    cells = jnp.arange(side_len * side_len, dtype=jnp.int32)
    ext_cells = jnp.arange(ext_len * ext_len, dtype=jnp.int32)
    row_gap = (ext_cells // ext_len)[None] - (cells // side_len)[:, None]
    col_gap = (ext_cells % ext_len)[None] - (cells % side_len)[:, None]
    in_window = (row_gap >= 0) & (row_gap < span) & (col_gap >= 0) & (col_gap < span)
    offset_ids = row_gap * span + col_gap
    one_hot = (
        (offset_ids[..., None] == jnp.arange(span * span, dtype=jnp.int32)) & in_window[..., None]
    ).astype(jnp.float32)
    return (in_window, one_hot)


def spread_rims(kv_own, tile_row, tile_col):
    rim_depth = RADIUS
    block_len = kv_own.shape[2]
    send_cols = jnp.where(
        tile_col == 0, kv_own[:, :, :, block_len - rim_depth :], kv_own[:, :, :, :rim_depth]
    )
    got_cols = from_partner(send_cols, "tile", 0)
    zero_cols = jnp.zeros_like(got_cols)
    widened = jnp.concatenate(
        [
            jnp.where(tile_col == 1, got_cols, zero_cols),
            kv_own,
            jnp.where(tile_col == 0, got_cols, zero_cols),
        ],
        axis=3,
    )
    send_rows = jnp.where(
        tile_row == 0, widened[:, :, block_len - rim_depth :], widened[:, :, :rim_depth]
    )
    got_rows = from_partner(send_rows, "tile", 1)
    zero_rows = jnp.zeros_like(got_rows)
    return jnp.concatenate(
        [
            jnp.where(tile_row == 1, got_rows, zero_rows),
            widened,
            jnp.where(tile_row == 0, got_rows, zero_rows),
        ],
        axis=2,
    )


def return_rims(grad_ext, tile_row, tile_col):
    rim_depth = RADIUS
    block_len = grad_ext.shape[2] - 2 * rim_depth
    send_rows = jnp.where(
        tile_row == 0, grad_ext[:, :, block_len + rim_depth :], grad_ext[:, :, :rim_depth]
    )
    got_rows = from_partner(send_rows.astype(jnp.bfloat16), "tile", 1).astype(send_rows.dtype)
    middle = grad_ext[:, :, rim_depth : rim_depth + block_len]
    zero_pad = jnp.zeros(
        got_rows.shape[:2] + (block_len - rim_depth,) + got_rows.shape[3:], jnp.float32
    )
    zero_rows = jnp.zeros_like(got_rows)
    middle = middle + jnp.concatenate(
        [jnp.where(tile_row == 1, got_rows, zero_rows), zero_pad], axis=2
    )
    middle = middle + jnp.concatenate(
        [zero_pad, jnp.where(tile_row == 0, got_rows, zero_rows)], axis=2
    )
    send_cols = jnp.where(
        tile_col == 0, middle[:, :, :, block_len + rim_depth :], middle[:, :, :, :rim_depth]
    )
    got_cols = from_partner(send_cols.astype(jnp.bfloat16), "tile", 0).astype(send_cols.dtype)
    centre = middle[:, :, :, rim_depth : rim_depth + block_len]
    zero_side = jnp.zeros(
        got_cols.shape[:3] + (block_len - rim_depth,) + got_cols.shape[4:], jnp.float32
    )
    zero_cols = jnp.zeros_like(got_cols)
    centre = centre + jnp.concatenate(
        [jnp.where(tile_col == 1, got_cols, zero_cols), zero_side], axis=3
    )
    return centre + jnp.concatenate(
        [zero_side, jnp.where(tile_col == 0, got_cols, zero_cols)], axis=3
    )


def attention_forward(query, kv_ext, cls_query, cls_key, cls_value, bias_table, geometry):
    valid_ext, valid_own, tile_first, tile_row, tile_col, in_window, one_hot = geometry
    page_count, side_len = (query.shape[0], query.shape[1])
    head_count = bias_table.shape[0]
    head_dim = query.shape[-1] // head_count
    score_scale = head_dim ** (-0.5)
    ext_len = kv_ext.shape[2]
    cell_total = side_len * side_len
    ext_total = ext_len * ext_len
    query_low = query.reshape(page_count, cell_total, head_count, head_dim)
    keys_low = kv_ext[:, 0].reshape(page_count, ext_total, head_count, head_dim)
    query_h = query.astype(jnp.float32).reshape(
        page_count, side_len, side_len, head_count, head_dim
    )
    keys_ext = (
        kv_ext[:, 0].astype(jnp.float32).reshape(page_count, ext_len, ext_len, head_count, head_dim)
    )
    values_ext = (
        kv_ext[:, 1].astype(jnp.float32).reshape(page_count, ext_len, ext_len, head_count, head_dim)
    )
    values_flat = values_ext.reshape(page_count, ext_total, head_count, head_dim)
    query_flat = query_h.reshape(page_count, cell_total, head_count, head_dim)
    cls_q = cls_query.astype(jnp.float32).reshape(page_count, head_count, head_dim)
    cls_k = cls_key.astype(jnp.float32).reshape(page_count, head_count, head_dim)
    cls_v = cls_value.astype(jnp.float32).reshape(page_count, head_count, head_dim)
    bias_map = jnp.einsum("qkw,hw->hqk", one_hot, bias_table, precision=highest)
    key_ok = in_window[None, None] & valid_ext.reshape(page_count, 1, 1, ext_total)
    raw_scores = jnp.einsum(
        "pqhd,pkhd->phqk", query_low, keys_low, preferred_element_type=jnp.float32
    )
    window_scores = jnp.where(key_ok, score_scale * raw_scores + bias_map[None], masked_score)
    class_scores = score_scale * jnp.einsum("pqhd,phd->phq", query_flat, cls_k, precision=highest)
    top_score = jnp.maximum(jnp.max(window_scores, axis=-1), class_scores)
    window_exp = jnp.exp(window_scores - top_score[..., None])
    class_exp = jnp.exp(class_scores - top_score)
    row_total = jnp.sum(window_exp, axis=-1) + class_exp
    window_probs = window_exp / row_total[..., None]
    class_probs = class_exp / row_total
    attended = (
        jnp.einsum("phqk,pkhd->pqhd", window_probs, values_flat, precision=highest)
        + class_probs.transpose(0, 2, 1)[..., None] * cls_v[:, None]
    )
    own_keys = keys_ext[:, RADIUS : RADIUS + side_len, RADIUS : RADIUS + side_len]
    own_values = values_ext[:, RADIUS : RADIUS + side_len, RADIUS : RADIUS + side_len]
    cell_scores = jnp.where(
        valid_own[..., None],
        score_scale * jnp.sum(own_keys * cls_q[:, None, None], axis=-1),
        masked_score,
    )
    self_score = jnp.where(tile_first, score_scale * jnp.sum(cls_q * cls_k, axis=-1), masked_score)
    local_top = jnp.maximum(jnp.max(cell_scores, axis=(1, 2)), self_score)
    cell_exp = jnp.where(valid_own[..., None], jnp.exp(cell_scores - local_top[:, None, None]), 0.0)
    self_exp = jnp.where(tile_first, jnp.exp(self_score - local_top), 0.0)
    local_total = jnp.sum(cell_exp, axis=(1, 2)) + self_exp
    local_sum = (
        jnp.einsum("pijh,pijhd->phd", cell_exp, own_values, precision=highest)
        + self_exp[..., None] * cls_v
    )
    cls_top, cls_total, cls_sum = merged((local_top, local_total, local_sum), "tile", merge_partial)
    cls_attended = cls_sum / cls_total[..., None]
    kept_values = (
        query_h,
        keys_ext,
        values_ext,
        cls_q,
        cls_k,
        cls_v,
        window_probs,
        class_probs,
        attended,
        cell_scores,
        self_score,
        cls_top,
        cls_total,
        cls_attended,
    )
    return (attended, cls_attended, kept_values)


def attention_backward(d_patch, d_cls_rows, kept_values, geometry):
    valid_ext, valid_own, tile_first, tile_row, tile_col, in_window, one_hot = geometry
    (
        query_h,
        keys_ext,
        values_ext,
        cls_q,
        cls_k,
        cls_v,
        window_probs,
        class_probs,
        attended,
        cell_scores,
        self_score,
        cls_top,
        cls_total,
        cls_attended,
    ) = kept_values
    page_count, side_len, _, head_count, head_dim = query_h.shape
    ext_len = keys_ext.shape[1]
    cell_total = side_len * side_len
    ext_total = ext_len * ext_len
    score_scale = head_dim ** (-0.5)
    query_flat = query_h.reshape(page_count, cell_total, head_count, head_dim)
    keys_flat = keys_ext.reshape(page_count, ext_total, head_count, head_dim)
    values_flat = values_ext.reshape(page_count, ext_total, head_count, head_dim)
    d_out = d_patch.reshape(page_count, cell_total, head_count, head_dim)
    row_delta = jnp.sum(d_out * attended, axis=-1).transpose(0, 2, 1)
    d_prob = jnp.einsum("pqhd,pkhd->phqk", d_out, values_flat, precision=highest)
    d_score = window_probs * (d_prob - row_delta[..., None])
    d_query = score_scale * jnp.einsum("phqk,pkhd->pqhd", d_score, keys_flat, precision=highest)
    d_keys = score_scale * jnp.einsum("phqk,pqhd->pkhd", d_score, query_flat, precision=highest)
    d_values = jnp.einsum("phqk,pqhd->pkhd", window_probs, d_out, precision=highest)
    g_table = jnp.einsum("phqk,qkw->hw", d_score, one_hot, precision=highest)
    d_class = class_probs * (
        jnp.einsum("pqhd,phd->phq", d_out, cls_v, precision=highest) - row_delta
    )
    d_query = d_query + score_scale * d_class.transpose(0, 2, 1)[..., None] * cls_k[:, None]
    d_cls_k = score_scale * jnp.einsum("phq,pqhd->phd", d_class, query_flat, precision=highest)
    d_cls_v = jnp.einsum("phq,pqhd->phd", class_probs, d_out, precision=highest)
    d_keys = d_keys.reshape(page_count, ext_len, ext_len, head_count, head_dim)
    d_values = d_values.reshape(page_count, ext_len, ext_len, head_count, head_dim)
    d_cls_out = d_cls_rows.reshape(page_count, head_count, head_dim)
    cls_delta = jnp.sum(d_cls_out * cls_attended, axis=-1)
    cell_probs = jnp.where(
        valid_own[..., None],
        jnp.exp(cell_scores - cls_top[:, None, None]) / cls_total[:, None, None],
        0.0,
    )
    self_prob = jnp.where(tile_first, jnp.exp(self_score - cls_top) / cls_total, 0.0)
    own_keys = keys_ext[:, RADIUS : RADIUS + side_len, RADIUS : RADIUS + side_len]
    own_values = values_ext[:, RADIUS : RADIUS + side_len, RADIUS : RADIUS + side_len]
    d_cell = cell_probs * (
        jnp.sum(own_values * d_cls_out[:, None, None], axis=-1) - cls_delta[:, None, None]
    )
    d_cls_q = score_scale * jnp.einsum("pijh,pijhd->phd", d_cell, own_keys, precision=highest)
    d_keys = add_block(
        d_keys, score_scale * d_cell[..., None] * cls_q[:, None, None], RADIUS, RADIUS
    )
    d_values = add_block(d_values, cell_probs[..., None] * d_cls_out[:, None, None], RADIUS, RADIUS)
    d_self = self_prob * (jnp.sum(cls_v * d_cls_out, axis=-1) - cls_delta)
    d_cls_q = d_cls_q + score_scale * d_self[..., None] * cls_k
    d_cls_k = d_cls_k + score_scale * d_self[..., None] * cls_q
    d_cls_v = d_cls_v + self_prob[..., None] * d_cls_out
    d_cls = lax.psum((d_cls_q, d_cls_k, d_cls_v), "tile")
    d_kv_ext = jnp.stack(
        [
            d_keys.reshape(page_count, ext_len, ext_len, -1),
            d_values.reshape(page_count, ext_len, ext_len, -1),
        ],
        axis=1,
    )
    d_kv_own = return_rims(d_kv_ext, tile_row, tile_col)
    model_width = head_count * head_dim
    d_patch_qkv = jnp.concatenate(
        [
            d_query.reshape(page_count, side_len, side_len, model_width),
            d_kv_own[:, 0],
            d_kv_own[:, 1],
        ],
        axis=-1,
    )
    d_cls_qkv = jnp.concatenate(
        [piece.reshape(page_count, model_width) for piece in d_cls], axis=-1
    )
    return (d_patch_qkv, d_cls_qkv, g_table)


def layer_forward(weight_set, residual, geometry):
    norm_a, qkv_w, bias_table, out_w, scale_a, norm_m, up_w, down_w, scale_m = weight_set
    valid_own = geometry[1]
    page_count, side_len = (valid_own.shape[0], valid_own.shape[1])
    cell_count = page_count * side_len * side_len
    model_width = residual.shape[1]
    normed = layer_norm(residual, norm_a).astype(jnp.bfloat16)
    qkv_rows = matmul(normed, qkv_w).astype(jnp.bfloat16)
    patch_qkv = qkv_rows[:cell_count].reshape(page_count, side_len, side_len, 3 * model_width)
    kv_own = jnp.stack(
        [patch_qkv[..., model_width : 2 * model_width], patch_qkv[..., 2 * model_width :]], axis=1
    )
    kv_ext = spread_rims(kv_own, geometry[3], geometry[4])
    cls_qkv = qkv_rows[cell_count:]
    attended, cls_attended, kept_values = attention_forward(
        patch_qkv[..., :model_width],
        kv_ext,
        cls_qkv[:, :model_width],
        cls_qkv[:, model_width : 2 * model_width],
        cls_qkv[:, 2 * model_width :],
        bias_table,
        geometry,
    )
    att_rows = jnp.concatenate(
        [attended.reshape(cell_count, model_width), cls_attended.reshape(page_count, model_width)],
        axis=0,
    ).astype(jnp.bfloat16)
    branch = matmul(att_rows, out_w)
    middle = residual + scale_a * branch
    normed_mlp = layer_norm(middle, norm_m).astype(jnp.bfloat16)
    up_value = matmul(normed_mlp, up_w)
    activation = jax.nn.gelu(up_value).astype(jnp.bfloat16)
    down_value = matmul(activation, down_w)
    result = middle + scale_m * down_value
    layer_cache = (
        residual,
        normed,
        kept_values,
        att_rows,
        branch,
        middle,
        normed_mlp,
        up_value,
        activation,
        down_value,
    )
    return (result, layer_cache)


def layer_backward(weight_set, layer_cache, d_result, keep_rows, geometry):
    norm_a, qkv_w, bias_table, out_w, scale_a, norm_m, up_w, down_w, scale_m = weight_set
    (
        residual,
        normed,
        kept_values,
        att_rows,
        branch,
        middle,
        normed_mlp,
        up_value,
        activation,
        down_value,
    ) = layer_cache
    valid_own = geometry[1]
    page_count, side_len = (valid_own.shape[0], valid_own.shape[1])
    cell_count = page_count * side_len * side_len
    keep_low = keep_rows.astype(jnp.bfloat16)[:, None]
    keep_col = keep_rows[:, None]
    e_down = (scale_m * d_result).astype(jnp.bfloat16)
    g_scale_m = jnp.sum(keep_col * d_result * down_value, axis=0)
    g_down = matmul_tn(activation, e_down * keep_low)
    d_activation = matmul_nt(e_down, down_w)
    _, gelu_back = jax.vjp(jax.nn.gelu, up_value)
    e_up = gelu_back(d_activation)[0].astype(jnp.bfloat16)
    g_up = matmul_tn(normed_mlp, e_up * keep_low)
    d_normed_mlp = matmul_nt(e_up, up_w)
    d_middle_part, gain_rows = norm_backward(middle, norm_m, d_normed_mlp)
    g_norm_m = jnp.sum(keep_col * gain_rows, axis=0)
    d_middle = d_result + d_middle_part
    e_branch = (scale_a * d_middle).astype(jnp.bfloat16)
    g_scale_a = jnp.sum(keep_col * d_middle * branch, axis=0)
    g_out = matmul_tn(att_rows, e_branch * keep_low)
    d_att_rows = matmul_nt(e_branch, out_w)
    d_patch_qkv, d_cls_qkv, g_table = attention_backward(
        d_att_rows[:cell_count], d_att_rows[cell_count:], kept_values, geometry
    )
    e_qkv = jnp.concatenate([d_patch_qkv.reshape(cell_count, -1), d_cls_qkv], axis=0).astype(
        jnp.bfloat16
    )
    g_qkv = matmul_tn(normed, e_qkv * keep_low)
    d_normed = matmul_nt(e_qkv, qkv_w)
    d_residual_part, gain_rows = norm_backward(residual, norm_a, d_normed)
    g_norm_a = jnp.sum(keep_col * gain_rows, axis=0)
    return (
        d_middle + d_residual_part,
        (g_norm_a, g_qkv, g_table, g_out, g_scale_a, g_norm_m, g_up, g_down, g_scale_m),
    )


def local(
    patch_in,
    cls_in,
    page_side,
    norm_attn,
    qkv_weight,
    rel_table,
    out_weight,
    scale_attn,
    norm_mlp,
    up_weight,
    down_weight,
    scale_mlp,
    patch_cot,
    cls_cot,
):
    tile_pos = lax.axis_index("tile")
    tile_row = tile_pos // 2
    tile_col = tile_pos % 2
    tile_first = tile_pos == 0
    page_count, side_len, model_width = (patch_in.shape[0], patch_in.shape[2], patch_in.shape[4])
    cell_count = page_count * side_len * side_len
    layer_total = qkv_weight.shape[0]
    ext_len = side_len + 2 * RADIUS
    offsets = jnp.arange(ext_len, dtype=jnp.int32) - RADIUS
    rows_global = tile_row * side_len + offsets
    cols_global = tile_col * side_len + offsets
    side_rows = page_side[:, None]
    row_ok = (rows_global[None] >= 0) & (rows_global[None] < side_rows)
    col_ok = (cols_global[None] >= 0) & (cols_global[None] < side_rows)
    valid_ext = row_ok[:, :, None] & col_ok[:, None, :]
    valid_own = valid_ext[:, RADIUS : RADIUS + side_len, RADIUS : RADIUS + side_len]
    in_window, one_hot = window_tables(side_len, ext_len)
    geometry = (valid_ext, valid_own, tile_first, tile_row, tile_col, in_window, one_hot)
    all_weights = (
        norm_attn,
        qkv_weight,
        rel_table,
        out_weight,
        scale_attn,
        norm_mlp,
        up_weight,
        down_weight,
        scale_mlp,
    )
    residual = jnp.concatenate(
        [patch_in.reshape(cell_count, model_width).astype(jnp.float32), cls_in.astype(jnp.float32)],
        axis=0,
    )
    caches = []
    for layer_index in range(layer_total):
        weight_set = tuple((stacked[layer_index] for stacked in all_weights))
        residual, layer_cache = layer_forward(weight_set, residual, geometry)
        caches.append(layer_cache)
    own_mask = valid_own.reshape(cell_count, 1)
    patch_out = (
        jnp.where(own_mask, residual[:cell_count], 0.0).astype(jnp.bfloat16).reshape(patch_in.shape)
    )
    cls_out = residual[cell_count:].astype(jnp.bfloat16)
    d_residual = jnp.concatenate(
        [
            jnp.where(
                own_mask, patch_cot.reshape(cell_count, model_width).astype(jnp.float32), 0.0
            ),
            cls_cot.astype(jnp.float32),
        ],
        axis=0,
    )
    keep_rows = jnp.concatenate(
        [
            jnp.ones((cell_count,), jnp.float32),
            jnp.where(tile_first, 1.0, 0.0) * jnp.ones((page_count,), jnp.float32),
        ],
        axis=0,
    )
    grads_per_layer = [None] * layer_total
    for layer_index in reversed(range(layer_total)):
        weight_set = tuple((stacked[layer_index] for stacked in all_weights))
        d_residual, layer_grads = layer_backward(
            weight_set, caches[layer_index], d_residual, keep_rows, geometry
        )
        grads_per_layer[layer_index] = layer_grads
    stacked_grads = tuple(
        (
            jnp.stack([grads_per_layer[layer_index][member] for layer_index in range(layer_total)])
            for member in (0, 1, 3, 4, 5, 6, 7, 8)
        )
    )
    summed = lax.psum_scatter(stacked_grads, ("dp", "tile"), scatter_dimension=1, tiled=True)
    tables = jnp.stack([grads_per_layer[layer_index][2] for layer_index in range(layer_total)])
    table_sum = lax.psum(tables, ("dp", "tile"))
    patch_grad = d_residual[:cell_count].reshape(patch_in.shape)
    cls_grad = d_residual[cell_count:]
    return (
        patch_out,
        cls_out,
        patch_grad,
        cls_grad,
        summed[0],
        summed[1],
        table_sum,
        summed[2],
        summed[3],
        summed[4],
        summed[5],
        summed[6],
        summed[7],
    )


def solution(mesh):
    in_specs = (
        P("dp", "tile", None, None, None),
        P("dp", None),
        P("dp"),
        P(),
        P(),
        P(),
        P(),
        P(),
        P(),
        P(),
        P(),
        P(),
        P("dp", "tile", None, None, None),
        P("dp", None),
    )
    out_specs = (
        P("dp", "tile", None, None, None),
        P("dp", None),
        P("dp", "tile", None, None, None),
        P("dp", None),
        P(None, ("dp", "tile")),
        P(None, ("dp", "tile"), None),
        P(),
        P(None, ("dp", "tile"), None),
        P(None, ("dp", "tile")),
        P(None, ("dp", "tile")),
        P(None, ("dp", "tile"), None),
        P(None, ("dp", "tile"), None),
        P(None, ("dp", "tile")),
    )
    return jax.shard_map(local, mesh=mesh, in_specs=in_specs, out_specs=out_specs, check_vma=False)
```

profile of v0, /device:TPU:1, one launch (start us, length us, event | category | flops | bytes accessed | tf_op | source)
XLA Modules:
  0.0 1140.9 jit_solution(1845421055672235967)
XLA Ops:
  18.8 13.0 %fusion.21 = f32[256,484,12]{0,2,1:T(8,128)} fusion(s32[256,484]{0,1:T(8,128)S(1)} %subtract_add_fusion, pred[256,484]{0,1:T(8,128)(4,1)S(1)} %get-tuple-element.312, f32[1,12,49]{2,0,1:T(1,128)S(1)} %get-tuple-element.309), kind=kOutput, calls=%fused_computation.30 | convolution fusion | flops 886409216 | bytes 6569264 | tf_op jit(solution)/shard_map/qkw,hw->hqk/dot_general | solution.py:194
  31.8 13.0 %fusion.23 = f32[256,484,12]{0,2,1:T(8,128)} fusion(s32[256,484]{0,1:T(8,128)S(1)} %subtract_add_fusion, pred[256,484]{0,1:T(8,128)(4,1)S(1)} %get-tuple-element.312, f32[1,12,49]{2,0,1:T(1,128)S(1)} %get-tuple-element.310), kind=kOutput, calls=%fused_computation.31 | convolution fusion | flops 886409216 | bytes 6569264 | tf_op jit(solution)/shard_map/qkw,hw->hqk/dot_general | solution.py:194
  56.2 5.6 collective-permute-done.1
  75.1 5.4 all_gather.29
  90.5 5.2 all-gather.2
  105.8 7.7 fusion.273
  170.2 6.0 all_gather.33
  201.2 7.6 fusion.275
  227.8 10.0 convolution_bitcast_fusion.9
  244.4 6.4 subtract_multiply_fusion.1
  257.7 8.5 copy.174
  266.2 5.8 copy.177
  278.2 11.2 reduce.51
  300.1 11.2 reduce.50
  327.6 10.3 all-reduce.15
  371.0 10.2 convolution_bitcast_fusion.8
  391.0 5.5 copy.188
  396.4 8.4 copy.191
  411.0 11.2 reduce.58
  437.8 11.2 reduce.57
  471.7 10.7 all-reduce.14
  490.9 11.0 pad_maximum_fusion.2
  503.1 5.4 convolution_bitcast_fusion.2
  511.8 6.7 pad_maximum_fusion.1
  527.0 7.0 pad_maximum_fusion
  534.1 5.6 multiply_add_fusion.3
  541.2 16.9 %fusion.124 = f32[1,12,49]{2,1,0:T(8,128)S(1)} fusion(s32[256,484]{0,1:T(8,128)S(1)} %copy-done.74, pred[256,484]{0,1:T(8,128)(4,1)S(1)} %copy-done.105, f32[12,256,484]{1,2,0:T(8,128)} %copy-done.2), kind=kOutput, calls=%fused_computation.180 | convolution fusion | flops 886409216 | bytes 6569264 | tf_op jit(solution)/shard_map/phqk,qkw->hw/dot_general | solution.py:281
  558.3 15.1 %fusion.119 = f32[1,12,49]{2,1,0:T(8,128)S(1)} fusion(s32[256,484]{0,1:T(8,128)S(1)} %copy-done.74, pred[256,484]{0,1:T(8,128)(4,1)S(1)} %copy-done.105, f32[12,256,484]{1,2,0:T(8,128)S(1)} %bitcast.571), kind=kOutput, calls=%fused_computation.179 | convolution fusion | flops 886409216 | bytes 6569264 | tf_op jit(solution)/shard_map/phqk,qkw->hw/dot_general | solution.py:281
  579.2 42.9 %all-reduce.13 = (f32[2,768]{1,0:T(2,128)S(1)}, f32[2,12,49]{2,1,0:T(8,128)S(1)}, f32[2,768]{1,0:T(2,128)S(1)}, f32[2,768]{1,0:T(2,128)S(1)}, f32[2,768]{1,0:T(2,128)S(1)}) all-reduce(f32[2,768]{1,0:T(2,128)S(1)} %pad_maximum_fusion.23, ...), channel_id=4, replica_groups=mesh['dp'=8,'tile'=4] {'dp','tile'}, use_global_device_ids=true, to_apply=%region_48.49.clone | all-reduce | flops 7320 | bytes 58560
  625.2 84.7 %reduce-scatter.9.cloned.1.call-done = f32[2,24,2304]{2,1,0:T(8,128)} async-done(((f32[2,768,2304]{2,1,0:T(8,128)}), f32[2,24,2304]{2,1,0:T(8,128)}) %reduce-scatter.9.cloned.1.call-update) | async-done | bytes 442384 | tf_op jit(solution)/shard_map/reduce_scatter | solution.py:523
  709.9 212.2 %reduce-scatter.15.cloned.1.call-done = f32[2,96,768]{2,1,0:T(8,128)} async-done(((f32[2,3072,768]{2,1,0:T(8,128)}), f32[2,96,768]{2,1,0:T(8,128)}) %reduce-scatter.15.cloned.1.call-update) | async-done | bytes 589840 | tf_op jit(solution)/shard_map/reduce_scatter | solution.py:523
  922.1 212.0 %reduce-scatter.13.cloned.1.call-done = f32[2,24,3072]{2,1,0:T(8,128)} async-done(((f32[2,768,3072]{2,1,0:T(8,128)}), f32[2,24,3072]{2,1,0:T(8,128)}) %reduce-scatter.13.cloned.1.call-update) | async-done | bytes 589840 | tf_op jit(solution)/shard_map/reduce_scatter | solution.py:523
  (838 shorter events, 321.6 us)
Async XLA Ops:
  7.2 618.0 %reduce-scatter.11.cloned.1.call-start = ((), (), s32[]{:S(2)}) async-start(), calls=%async_computation.5 | async-start | bytes 4866048 | tf_op jit(solution)/shard_map/reduce_scatter | solution.py:523
  15.6 36.5 %collective-permute-start = (bf16[1,2,16,3,768]{4,3,2,1,0:T(4,128)(2,1)}, bf16[1,2,16,3,768]{4,3,2,1,0:T(4,128)(2,1)}, u32[]{:S(2)}, u32[]{:S(2)}) collective-permute-start(bf16[1,2,16,3,768]{4,3,2,1,0:T(4,128)(2,1)} %fusion.178), channel_id=1, source_target_pairs={{0,1},{1,0},{2,3},{3,2},{4,5},{5,4},{6,7},{7,6},{8,9},{9,8},{10,11... | collective-permute-start | bytes 442376 | tf_op jit(solution)/shard_map/ppermute | solution.py:21
  16.9 57.4 %copy-start.108 = (pred[16,16]{1,0:T(8,128)(4,1)}, pred[16,16]{1,0:T(8,128)(4,1)S(1)}, u32[]{:S(2)}) copy-start(pred[16,16]{1,0:T(8,128)(4,1)S(1)} %get-tuple-element.314) | copy-start | bytes 772
  17.0 27.8 %copy-start.191 = (pred[256]{0:T(512)(128)(4,1)}, pred[256]{0:T(512)(128)(4,1)S(1)}, u32[]{:S(2)}) copy-start(pred[256]{0:T(512)(128)(4,1)S(1)} %broadcast_in_dim.89) | copy-start | bytes 772
  17.6 101.7 %copy-start.139 = (f32[768]{0:T(1024)}, f32[768]{0:T(1024)S(1)}, u32[]{:S(2)}) copy-start(f32[768]{0:T(1024)S(1)} %get-tuple-element.196) | copy-start | bytes 9220
  18.2 102.9 %copy-start.90 = (f32[768]{0:T(1024)}, f32[768]{0:T(1024)S(1)}, u32[]{:S(2)}) copy-start(f32[768]{0:T(1024)S(1)} %get-tuple-element.194) | copy-start | bytes 9220
  18.8 87.0 %copy-start.55 = (pred[256,484]{0,1:T(8,128)(4,1)}, pred[256,484]{0,1:T(8,128)(4,1)S(1)}, u32[]{:S(2)}) copy-start(pred[256,484]{0,1:T(8,128)(4,1)S(1)} %get-tuple-element.311) | copy-start | bytes 371716
  47.1 43.4 %copy-start.150 = (f32[12,64]{1,0:T(8,128)}, f32[12,64]{1,0:T(8,128)S(1)}, u32[]{:S(2)}) copy-start(f32[12,64]{1,0:T(8,128)S(1)} %mul.1227) | copy-start | bytes 9220
  49.8 22.5 %copy-start.99 = (f32[12,64]{1,0:T(8,128)}, f32[12,64]{1,0:T(8,128)S(1)}, u32[]{:S(2)}) copy-start(f32[12,64]{1,0:T(8,128)S(1)} %mul.1230) | copy-start | bytes 9220
  50.0 25.1 %copy-start.183 = (f32[12]{0:T(128)}, f32[12]{0:T(128)S(1)}, u32[]{:S(2)}) copy-start(f32[12]{0:T(128)S(1)} %reduce_sum.412) | copy-start | bytes 148
  51.3 54.5 %copy-start.27 = (bf16[256,12,64]{0,2,1:T(8,128)(2,1)}, bf16[256,12,64]{0,2,1:T(8,128)(2,1)S(1)}, u32[]{:S(2)}) copy-start(bf16[256,12,64]{0,2,1:T(8,128)(2,1)S(1)} %copy.155) | copy-start | bytes 1179652
  53.3 8.6 collective-permute-start.1
  128.8 219.4 %copy-start.14 = (f32[257,768]{1,0:T(8,128)}, f32[257,768]{1,0:T(8,128)S(1)}, u32[]{:S(2)}) copy-start(f32[257,768]{1,0:T(8,128)S(1)} %get-tuple-element.260) | copy-start | bytes 2368516
  136.6 30.8 %copy-start.101 = (f32[12,64]{1,0:T(8,128)}, f32[12,64]{1,0:T(8,128)S(1)}, u32[]{:S(2)}) copy-start(f32[12,64]{1,0:T(8,128)S(1)} %mul.1268) | copy-start | bytes 9220
  136.8 33.4 %copy-start.185 = (f32[12]{0:T(128)}, f32[12]{0:T(128)S(1)}, u32[]{:S(2)}) copy-start(f32[12]{0:T(128)S(1)} %reduce_sum.421) | copy-start | bytes 148
  138.0 5.8 collective-permute-start.2
  142.6 58.6 %copy-start.30 = (bf16[256,12,64]{0,2,1:T(8,128)(2,1)}, bf16[256,12,64]{0,2,1:T(8,128)(2,1)S(1)}, u32[]{:S(2)}) copy-start(bf16[256,12,64]{0,2,1:T(8,128)(2,1)S(1)} %copy.162) | copy-start | bytes 1179652
  146.1 6.8 collective-permute-start.3
  157.6 23.7 %copy-start.11 = (bf16[1,22,22,12,64]{4,3,2,1,0:T(8,128)(2,1)}, bf16[1,22,22,12,64]{4,3,2,1,0:T(8,128)(2,1)S(1)}, u32[]{:S(2)}) copy-start(bf16[1,22,22,12,64]{4,3,2,1,0:T(8,128)(2,1)S(1)} %reshape.1539) | copy-start | bytes 2230276
  165.0 20.7 %copy-start.148 = (f32[12,64]{1,0:T(8,128)S(1)}, f32[12,64]{1,0:T(8,128)}, u32[]{:S(2)}) copy-start(f32[12,64]{1,0:T(8,128)} %mul.1265) | copy-start | bytes 9220
  169.3 24.3 %copy-start.43 = (f32[16,16,12]{2,1,0:T(8,128)}, f32[16,16,12]{2,1,0:T(8,128)S(1)}, u32[]{:S(2)}) copy-start(f32[16,16,12]{2,1,0:T(8,128)S(1)} %multiply_reduce_fusion.2) | copy-start | bytes 36868
  226.7 121.5 %copy-start.4 = (f32[257,768]{1,0:T(8,128)}, f32[257,768]{1,0:T(8,128)S(1)}, u32[]{:S(2)}) copy-start(f32[257,768]{1,0:T(8,128)S(1)} %multiply_add_fusion.2) | copy-start | bytes 2368516
  227.4 47.4 %copy-start.97 = (f32[12,64]{1,0:T(8,128)}, f32[12,64]{1,0:T(8,128)S(1)}, u32[]{:S(2)}) copy-start(f32[12,64]{1,0:T(8,128)S(1)} %mul.1324) | copy-start | bytes 9220
  321.8 17.5 %collective-permute-start.4 = (bf16[1,2,3,22,768]{4,3,2,1,0:T(8,128)(2,1)}, bf16[1,2,3,22,768]{4,3,2,1,0:T(8,128)(2,1)}, u32[]{:S(2)}, u32[]{:S(2)}) collective-permute-start(bf16[1,2,3,22,768]{4,3,2,1,0:T(8,128)(2,1)} %fusion.164), channel_id=1, source_target_pairs={{0,2},{2,0},{1,3},{3,1},{4,6},{6,4},{5,7},{7,5},{8,10},{10,8},{9,1... | collective-permute-start | bytes 608264 | tf_op jit(solution)/shard_map/ppermute | solution.py:21
  342.7 2.8 collective-permute-start.5
  433.4 276.4 %reduce-scatter.9.cloned.1.call-start = ((), (), s32[]{:S(2)}) async-start(), calls=%async_computation.4 | async-start | bytes 14598144 | tf_op jit(solution)/shard_map/reduce_scatter | solution.py:523
  457.7 11.7 %collective-permute-start.6 = (bf16[1,2,3,22,768]{4,3,2,1,0:T(8,128)(2,1)S(1)}, bf16[1,2,3,22,768]{4,3,2,1,0:T(8,128)(2,1)S(1)}, u32[]{:S(2)}, u32[]{:S(2)}) collective-permute-start(bf16[1,2,3,22,768]{4,3,2,1,0:T(8,128)(2,1)S(1)} %fusion.163), channel_id=1, source_target_pairs={{0,2},{2,0},{1,3},{3,1},{4,6},{6,4},{5,7},{7,5},{8,10},{10,8},{9,1... | collective-permute-start | bytes 608264 | tf_op jit(solution)/shard_map/ppermute | solution.py:21
  471.2 11.6 %collective-permute-start.7 = (bf16[1,2,16,3,768]{4,3,2,1,0:T(4,128)(2,1)S(1)}, bf16[1,2,16,3,768]{4,3,2,1,0:T(4,128)(2,1)S(1)}, u32[]{:S(2)}, u32[]{:S(2)}) collective-permute-start(bf16[1,2,16,3,768]{4,3,2,1,0:T(4,128)(2,1)S(1)} %fusion.169), channel_id=1, source_target_pairs={{0,1},{1,0},{2,3},{3,2},{4,5},{5,4},{6,7},{7,6},{8,9},{9,8},{10,11... | collective-permute-start | bytes 442376 | tf_op jit(solution)/shard_map/ppermute | solution.py:21
  502.0 420.1 %reduce-scatter.15.cloned.1.call-start = ((), (), s32[]{:S(2)}) async-start(), calls=%async_computation.7 | async-start | bytes 19464192 | tf_op jit(solution)/shard_map/reduce_scatter | solution.py:523
  518.6 615.5 %reduce-scatter.13.cloned.1.call-start = ((), (), s32[]{:S(2)}) async-start(), calls=%async_computation.6 | async-start | bytes 19464192 | tf_op jit(solution)/shard_map/reduce_scatter | solution.py:523
  534.1 24.1 %slice-start.6 = ((s8[5996544]{0:T(1024)(128)(4,1)}), s8[4194304]{0:T(1024)(128)(4,1)S(1)}, s32[]{:S(2)}) async-start(s8[5996544]{0:T(1024)(128)(4,1)} %bitcast.570), calls=%async_computation.14 | async-start | bytes 8388608
  541.2 32.3 %slice-start.30 = ((s8[7077888]{0:T(1024)(128)(4,1)}), s8[4194304]{0:T(1024)(128)(4,1)S(1)}, s32[]{:S(2)}) async-start(s8[7077888]{0:T(1024)(128)(4,1)} %bitcast.639), calls=%async_computation.38 | async-start | bytes 8388608
  (227 other events, 1262.9 us)
Sparse Core Ops, SparseCore 0:
  433.6 106.1 reduce-scatter.10
  547.4 162.4 reduce-scatter.8
  718.0 204.0 reduce-scatter.14
  930.0 204.0 reduce-scatter.12
where the time goes:
time: 1150 us; the launch traced here: 1140 us
  waiting for transfers between devices  520 us (45%)
  matrix products  201 us (17%)
  local copies, waits for them, and re-layouts  180 us (16%)
  other arithmetic  118 us (10%)
  blocking collectives  95.8 us (8%)
  between operations  18.1 us (2%)
    reduce_scatter x4, waiting for transfers between devices, local(): lax.psum_scatter(stacked_grads, ('dp', 'tile'), scatter_dimension=1, tile...  509 us
    dynamic_update_slice x4, other arithmetic, add_block(): lax.dynamic_update_slice(target, current + addend, (0, row_start, col_sta...  44.9 us
    unnamed x1, blocking collectives  42.9 us
    another operation x20, local copies, waits for them, and re-layouts  36.4 us
    dot_general x2, matrix products, attention_backward(): g_table = jnp.einsum('phqk,qkw->hw', d_score, one_hot, precision=highest)  32.1 us
    all_gather x6, blocking collectives, merged(): pieces = jax.tree.map(lambda part: lax.all_gather(part, axis), value)  31.9 us
    unnamed x501, local copies, waits for them, and re-layouts  31.8 us
    dot_general x8, matrix products, matmul_tn(): lax.dot_general(left_matrix, right_matrix, (((0,), (0,)), ((), ())), pref...  30.9 us
  transfers between devices with their start and end apart: 12, of which 5 were waited for; matrix products, arithmetic and copies ran while one was open for 16% of the time, Pallas kernels for 0%

commit v1 on v0

v1 whole, which is shorter than its diff:
```python
import functools

import jax
import jax.numpy as jnp
import numpy as np
from jax import lax
from jax.experimental import pallas as pl
from jax.experimental.pallas import tpu as pltpu
from jax.sharding import PartitionSpec as P

RADIUS = 3
SPAN = 2 * RADIUS + 1
PAD = 8
EPS = 1e-06
MASKED = -1e30
BF = jnp.bfloat16
F32 = jnp.float32
MIB = 1 << 20


def dot(a, b):
    return lax.dot_general(a, b, (((1,), (0,)), ((), ())), preferred_element_type=F32)


def dot_nt(a, b):
    return lax.dot_general(a, b, (((1,), (1,)), ((), ())), preferred_element_type=F32)


def dot_tn(a, b):
    return lax.dot_general(a, b, (((0,), (0,)), ((), ())), preferred_element_type=F32)


def normalized(x):
    centred = x - jnp.mean(x, axis=-1, keepdims=True)
    inverse = lax.rsqrt(jnp.mean(centred * centred, axis=-1, keepdims=True) + EPS)
    return centred * inverse, inverse


def norm_back(x, gain, d_out):
    unit, inverse = normalized(x)
    d_unit = d_out * gain
    d_x = inverse * (
        d_unit
        - jnp.mean(d_unit, axis=-1, keepdims=True)
        - unit * jnp.mean(d_unit * unit, axis=-1, keepdims=True)
    )
    return d_x, d_out * unit


def split3(x):
    high = x.astype(BF).astype(F32)
    rest = x - high
    middle = rest.astype(BF).astype(F32)
    return high, middle, rest - middle


def lane_heads(rows, lanes, width):
    return lax.broadcasted_iota(jnp.int32, (rows, lanes), 1) // width


def head_rows(rows, lanes, width):
    return lane_heads(rows, lanes, width) == lax.broadcasted_iota(jnp.int32, (rows, lanes), 0)


def stacked_heads(block, width):
    rows, lanes = block.shape
    heads = lane_heads(rows, lanes, width)
    zero = jnp.zeros_like(block)
    return jnp.concatenate(
        [jnp.where(heads == h, block, zero) for h in range(lanes // width)], axis=0
    )


def folded_heads(stack, width):
    count = stack.shape[1] // width
    rows = stack.shape[0] // count
    heads = lane_heads(rows, stack.shape[1], width)
    out = stack[:rows]
    for h in range(1, count):
        out = jnp.where(heads == h, stack[h * rows : (h + 1) * rows], out)
    return out


def keep_rows(rows, cells, class_weight):
    row = lax.broadcasted_iota(jnp.int32, (rows, 1), 0)
    return jnp.where(row < cells, 1.0, jnp.where(row == cells, class_weight, 0.0))


class Sizes:
    def __init__(self, side, width, hidden, heads, devices):
        self.side = side
        self.cells = side * side
        self.rows = self.cells + 16
        self.width = width
        self.hidden = hidden
        self.heads = heads
        self.head = width // heads
        self.pitch = side + PAD
        self.ext = side + 2 * RADIUS
        self.ext_rows = self.pitch * self.ext + PAD
        self.brows = 4
        self.blocks = side // self.brows
        self.bq = self.brows * side
        self.bk = 256
        self.class_slot = self.bk - PAD
        self.quad = 4 * self.head
        self.groups = width // self.quad
        self.devices = devices
        self.bits = devices.bit_length() - 1


def stat_rows(values):
    width = values[0].shape[1]
    parts = [split3(v) for v in values]
    flat = [p[k] for k in range(3) for p in parts]
    if len(flat) % 2:
        flat.append(jnp.zeros_like(flat[0]))
    row = lax.broadcasted_iota(jnp.int32, (16, 2 * width), 0)
    out = jnp.zeros((16, 2 * width), F32)
    for i in range(0, len(flat), 2):
        out = jnp.where(row == i // 2, jnp.concatenate(flat[i : i + 2], axis=1), out)
    return out.astype(BF)


def read_stats(block, count, width):
    rows = block.astype(F32)

    def piece(i):
        return rows[i // 2 : i // 2 + 1, (i % 2) * width : (i % 2 + 1) * width]

    return [piece(i) + piece(count + i) + piece(2 * count + i) for i in range(count)]


def in_tile_order(info, pieces):
    me = info[0] * 2 + info[1]
    out = []
    for t in range(4):
        d = me ^ t
        out.append(
            [
                jnp.where(d == 0, a, jnp.where(d == 1, b, jnp.where(d == 2, c, e)))
                for a, b, c, e in zip(*pieces)
            ]
        )
    return out


def class_scores(sz, info, qkv_ref, mask):
    cells, width = sz.cells, sz.width
    own = head_rows(16, width, sz.head)
    class_rows = qkv_ref[cells : cells + 16, :].astype(F32)
    q_c, k_c, v_c = (class_rows[0:1, i * width : (i + 1) * width] for i in range(3))
    q_heads = jnp.where(own, q_c, 0.0)
    scale = sz.head ** (-0.5)
    scores = dot_nt(q_heads.astype(BF), qkv_ref[0:cells, width : 2 * width]) * scale + mask
    self_score = jnp.sum(q_heads * k_c, axis=1, keepdims=True) * scale
    self_score = jnp.where(info[2] == 1, self_score, MASKED)
    return own, q_heads, k_c, v_c, scores, self_score


def write_left(sz, perm_ref, value, mine_ref, send_ref):
    turned = dot_nt(perm_ref[...], value).astype(BF)
    half = turned.shape[0] // 2
    mine_ref[...] = turned[:half]
    send_ref[...] = turned[half:]


def send_rims(sz, info, kv_half, kv_edge_rows, stats, pc_ref, pr_ref, pd_ref):
    side, width = sz.side, sz.width
    cells8 = [kv_half(r) for r in range(side)]
    pc_ref[0 : side * PAD, :] = jnp.concatenate(cells8, axis=0).astype(BF)
    pc_ref[side * PAD : side * PAD + 16, :] = stats
    edge, corner = kv_edge_rows()
    pr_ref[0 : RADIUS * side, :] = jnp.concatenate(edge, axis=0).astype(BF)
    pr_ref[RADIUS * side : RADIUS * side + 16, :] = stats
    zero = jnp.zeros((PAD, 2 * width), F32)
    pd_ref[0 : (RADIUS + 1) * PAD, :] = jnp.concatenate(corner + [zero], axis=0).astype(BF)
    pd_ref[(RADIUS + 1) * PAD : (RADIUS + 1) * PAD + 16, :] = stats


def qkv_kernel(sz, layer, info, x_ref, gain_ref, w_ref, perm_ref, mask_ref,
               h_ref, lm_ref, ls_ref, qkv_ref, pc_ref, pr_ref, pd_ref):
    step = pl.program_id(0)
    width, side, cells = sz.width, sz.side, sz.cells

    @pl.when(step == 0)
    def _():
        unit, _ = normalized(x_ref[...])
        h = (unit * gain_ref[layer : layer + 1, :]).astype(BF)
        h_ref[...] = h
        write_left(sz, perm_ref, h, lm_ref, ls_ref)

    cols = pl.ds(pl.multiple_of(step * width, width), width)
    qkv_ref[:, cols] = dot(h_ref[...], w_ref[...]).astype(BF)

    @pl.when(step == pl.num_programs(0) - 1)
    def _():
        mask = mask_ref[0:1, :]
        own, q_heads, k_c, v_c, scores, self_score = class_scores(sz, info, qkv_ref, mask)
        top = jnp.maximum(jnp.max(scores, axis=1, keepdims=True), self_score)
        probs = jnp.where(mask > -1.0, jnp.exp(scores - top), 0.0)
        self_prob = jnp.where(info[2] == 1, jnp.exp(self_score - top), 0.0)
        total = jnp.sum(probs, axis=1, keepdims=True) + self_prob
        part = dot(probs.astype(BF), qkv_ref[0:cells, 2 * width :]) + self_prob * v_c

        def to_row(v):
            return jnp.sum(jnp.where(own, v, 0.0), axis=0, keepdims=True)

        stats = stat_rows([to_row(part), to_row(top), to_row(total)])
        left_col = info[1] == 0

        def half(r):
            row = qkv_ref[r * side : (r + 1) * side, width:].astype(F32)
            return jnp.where(left_col, row[PAD:], row[:PAD])

        def edges():
            first = pl.multiple_of((1 - info[0]) * (side - RADIUS) * side, 16)
            rows = qkv_ref[pl.ds(first, RADIUS * side), width:].astype(F32)
            edge = [rows[t * side : (t + 1) * side] for t in range(RADIUS)]
            return edge, [jnp.where(left_col, e[PAD:], e[:PAD]) for e in edge]

        send_rims(sz, info, half, edges, stats, pc_ref, pr_ref, pd_ref)


def rim_places(sz, info):
    return sz.pitch * (1 - info[1]), (sz.side + RADIUS) * (1 - info[0])


def attention_kernel(sz, layer, info, qkv_ref, st_ref, rc_ref, rr_ref, rd_ref, bias_ref, mask_ref,
                     x_ref, w_ref, scale_ref, gain_ref, perm_ref,
                     p_ref, kb_ref, vb_ref, stat_ref, br_ref, x1_ref, h2_ref,
                     am_ref, as_ref, bm_ref, bs_ref, kext, vext, att):
    width, side, cells, pitch = sz.width, sz.side, sz.cells, sz.pitch
    beside, above = rim_places(sz, info)
    for ext, lo in ((kext, width), (vext, 2 * width)):
        at = lo - width
        ext[...] = jnp.zeros_like(ext)
        for r in range(side):
            base = pitch * (r + RADIUS)
            ext[base + PAD : base + PAD + side, :] = qkv_ref[r * side : (r + 1) * side, lo : lo + width].astype(F32)
        sides = rc_ref[0 : side * PAD, at : at + width].astype(F32)
        for r in range(side):
            ext[pl.ds(pl.multiple_of(pitch * (r + RADIUS) + beside, 8), PAD), :] = sides[r * PAD : (r + 1) * PAD]
        edge = rr_ref[0 : RADIUS * side, at : at + width].astype(F32)
        corner = rd_ref[0 : (RADIUS + 1) * PAD, at : at + width].astype(F32)
        for t in range(RADIUS):
            base = pitch * (above + t)
            ext[pl.ds(pl.multiple_of(base + PAD, 8), side), :] = edge[t * side : (t + 1) * side]
            ext[pl.ds(pl.multiple_of(base + beside, 8), PAD), :] = corner[t * PAD : (t + 1) * PAD]
    class_rows = qkv_ref[cells : cells + 16, :].astype(F32)[0:PAD]
    scale = sz.head ** (-0.5)
    for b in range(sz.blocks):
        first = b * sz.brows * pitch
        kb = jnp.concatenate([kext[first : first + sz.class_slot, :], class_rows[:, width : 2 * width]], axis=0).astype(BF)
        vb = jnp.concatenate([vext[first : first + sz.class_slot, :], class_rows[:, 2 * width :]], axis=0).astype(BF)
        kb_ref[b] = kb
        vb_ref[b] = vb
        q = qkv_ref[b * sz.bq : (b + 1) * sz.bq, 0:width] * jnp.asarray(scale, BF)
        mask = mask_ref[b]
        mask = jnp.concatenate([mask, mask], axis=1)
        for g in range(sz.groups):
            lanes = slice(g * sz.quad, (g + 1) * sz.quad)
            scores = dot_nt(kb[:, lanes], stacked_heads(q[:, lanes], sz.head)) + bias_ref[g] + mask
            top = jnp.max(scores, axis=0, keepdims=True)
            probs = jnp.exp(scores - top)
            total = jnp.sum(probs, axis=0, keepdims=True)
            probs = (probs * (1.0 / total)).astype(BF)
            p_ref[b * sz.groups + g] = probs
            out = folded_heads(dot_tn(probs, vb[:, lanes]), sz.head)
            att[b * sz.bq : (b + 1) * sz.bq, lanes] = out.astype(BF)
    own_stats = [read_stats(r, 3, width) for r in (
        st_ref[...],
        rc_ref[side * PAD : side * PAD + 16, :],
        rr_ref[RADIUS * side : RADIUS * side + 16, :],
        rd_ref[(RADIUS + 1) * PAD : (RADIUS + 1) * PAD + 16, :],
    )]
    ordered = in_tile_order(info, own_stats)
    top = functools.reduce(jnp.maximum, [s[1] for s in ordered])
    total = jnp.zeros_like(top)
    summed = jnp.zeros_like(top)
    for part, part_top, part_total in ordered:
        factor = jnp.exp(part_top - top)
        total = total + part_total * factor
        summed = summed + part * factor
    class_out = summed / total
    stat_ref[...] = jnp.zeros_like(stat_ref)
    stat_ref[0:1, :] = top
    stat_ref[1:2, :] = total
    stat_ref[2:3, :] = class_out
    row = lax.broadcasted_iota(jnp.int32, (16, width), 0)
    att[cells : cells + 16, :] = jnp.where(row == 0, class_out, 0.0).astype(BF)
    branch = dot(att[...], w_ref[...])
    br_ref[...] = branch
    x1 = x_ref[...] + scale_ref[layer : layer + 1, :] * branch
    x1_ref[...] = x1
    unit, _ = normalized(x1)
    h2 = (unit * gain_ref[layer : layer + 1, :]).astype(BF)
    h2_ref[...] = h2
    write_left(sz, perm_ref, att[...], am_ref, as_ref)
    write_left(sz, perm_ref, h2, bm_ref, bs_ref)


GELU_C = float(np.sqrt(2.0 / np.pi))


def mlp_kernel(sz, layer, info, h2_ref, up_w_ref, down_w_ref, x1_ref, scale_ref, perm_ref,
               up_ref, down_ref, x2_ref, lm_ref, ls_ref):
    step = pl.program_id(0)
    up = dot(h2_ref[...], up_w_ref[...])
    up_ref[...] = up
    act = (0.5 * up * (1.0 + jnp.tanh(GELU_C * (up + 0.044715 * (up * up * up))))).astype(BF)
    part = dot(act, down_w_ref[...])

    @pl.when(step == 0)
    def _():
        down_ref[...] = part

    @pl.when(step > 0)
    def _():
        down_ref[...] += part

    write_left(sz, perm_ref, act, lm_ref, ls_ref)

    @pl.when(step == pl.num_programs(0) - 1)
    def _():
        x2_ref[...] = x1_ref[...] + scale_ref[layer : layer + 1, :] * down_ref[...]


def mlp_back_kernel(sz, layer, info, g_ref, down_ref, scale_m_ref, up_ref, down_w_ref, up_w_ref,
                    x1_ref, gain_ref, scale_a_ref, br_ref,
                    ed_ref, eu_ref, g1_ref, eb_ref, vec_ref, d_h2):
    step = pl.program_id(0)
    keep = keep_rows(sz.rows, sz.cells, jnp.where(info[2] == 1, 1.0, 0.0))

    @pl.when(step == 0)
    def _():
        g = g_ref[...]
        ed_ref[...] = (scale_m_ref[layer : layer + 1, :] * g).astype(BF)
        vec_ref[...] = jnp.zeros_like(vec_ref)
        vec_ref[0:1, :] = jnp.sum(keep * g * down_ref[...], axis=0, keepdims=True)
        d_h2[...] = jnp.zeros_like(d_h2)

    d_act = dot_nt(ed_ref[...], down_w_ref[...])
    u = up_ref[...]
    square = u * u
    th = jnp.tanh(GELU_C * (u + 0.044715 * (square * u)))
    slope = 0.5 * (1.0 + th) + 0.5 * u * (1.0 - th * th) * (GELU_C * (1.0 + (3 * 0.044715) * square))
    e_up = (d_act * slope).astype(BF)
    eu_ref[...] = e_up
    d_h2[...] += dot_nt(e_up, up_w_ref[...])

    @pl.when(step == pl.num_programs(0) - 1)
    def _():
        d_x1, gain_rows = norm_back(x1_ref[...], gain_ref[layer : layer + 1, :], d_h2[...])
        g1 = g_ref[...] + d_x1
        g1_ref[...] = g1
        eb_ref[...] = (scale_a_ref[layer : layer + 1, :] * g1).astype(BF)
        vec_ref[1:2, :] = jnp.sum(keep * gain_rows, axis=0, keepdims=True)
        vec_ref[2:3, :] = jnp.sum(keep * g1 * br_ref[...], axis=0, keepdims=True)


def attention_back_kernel(sz, layer, info, eb_ref, w_ref, qkv_ref, p_ref, kb_ref, vb_ref, stat_ref, own_mask_ref,
                          dq_ref, dkv_ref, pc_ref, pr_ref, pd_ref, tab_ref, kext, vext, d_o, tab):
    width, side, cells, pitch = sz.width, sz.side, sz.cells, sz.pitch
    scale = sz.head ** (-0.5)
    d_o[...] = dot_nt(eb_ref[...], w_ref[...])
    kext[...] = jnp.zeros_like(kext)
    vext[...] = jnp.zeros_like(vext)
    class_k = [jnp.zeros((PAD, sz.quad), F32) for _ in range(sz.groups)]
    class_v = [jnp.zeros((PAD, sz.quad), F32) for _ in range(sz.groups)]
    for b in range(sz.blocks):
        first = b * sz.brows * pitch
        q = qkv_ref[b * sz.bq : (b + 1) * sz.bq, 0:width] * jnp.asarray(scale, BF)
        do = d_o[b * sz.bq : (b + 1) * sz.bq, :].astype(BF)
        for g in range(sz.groups):
            lanes = slice(g * sz.quad, (g + 1) * sz.quad)
            do_stack = stacked_heads(do[:, lanes], sz.head)
            q_stack = stacked_heads(q[:, lanes], sz.head)
            probs = p_ref[b * sz.groups + g]
            wide = probs.astype(F32)
            d_prob = dot_nt(vb_ref[b, :, lanes], do_stack)
            delta = jnp.sum(wide * d_prob, axis=0, keepdims=True)
            d_score = wide * (d_prob - delta)
            if b == 0:
                tab[g] = d_score
            else:
                tab[g] += d_score
            low = d_score.astype(BF)
            d_v = dot(probs, do_stack)
            d_k = dot(low, q_stack)
            vext[first : first + sz.class_slot, lanes] += d_v[: sz.class_slot]
            kext[first : first + sz.class_slot, lanes] += d_k[: sz.class_slot]
            class_v[g] = class_v[g] + d_v[sz.class_slot :]
            class_k[g] = class_k[g] + d_k[sz.class_slot :]
            d_q = folded_heads(dot_tn(low, kb_ref[b, :, lanes]), sz.head) * scale
            dq_ref[b * sz.bq : (b + 1) * sz.bq, lanes] = d_q.astype(BF)
    mask = own_mask_ref[0:1, :]
    own, q_heads, k_c, v_c, scores, self_score = class_scores(sz, info, qkv_ref, mask)
    top = jnp.max(jnp.where(own, stat_ref[0:1, :], MASKED), axis=1, keepdims=True)
    total = jnp.max(jnp.where(own, stat_ref[1:2, :], 0.0), axis=1, keepdims=True)
    real = lax.broadcasted_iota(jnp.int32, (16, 1), 0) < sz.heads
    probs = jnp.where((mask > -1.0) & real, jnp.exp(scores - top) / total, 0.0)
    self_prob = jnp.where((info[2] == 1) & real, jnp.exp(self_score - top) / total, 0.0)
    d_class = jnp.where(own, d_o[cells : cells + 1, :], 0.0)
    delta = jnp.sum(d_class * stat_ref[2:3, :], axis=1, keepdims=True)
    d_low = d_class.astype(BF)
    d_cell = probs * (dot_nt(d_low, qkv_ref[0:cells, 2 * width :]) - delta)
    d_cell_low = d_cell.astype(BF)
    d_self = self_prob * (jnp.sum(d_class * v_c, axis=1, keepdims=True) - delta)

    def to_row(v):
        return jnp.sum(jnp.where(own, v, 0.0), axis=0, keepdims=True)

    g_q = to_row(dot(d_cell_low, qkv_ref[0:cells, width : 2 * width]) + d_self * k_c) * scale
    g_k = to_row(d_self * q_heads) * scale + jnp.concatenate([c[0:1] for c in class_k], axis=1)
    g_v = to_row(self_prob * d_class) + jnp.concatenate([c[0:1] for c in class_v], axis=1)
    add_k = dot_tn(d_cell_low, q_heads.astype(BF)) * scale
    add_v = dot_tn(probs.astype(BF), d_low)
    beside, above = rim_places(sz, info)
    for r in range(side):
        base = pitch * (r + RADIUS) + PAD
        rows = slice(r * side, (r + 1) * side)
        dkv_ref[rows, 0:width] = kext[base : base + side, :] + add_k[rows]
        dkv_ref[rows, width:] = vext[base : base + side, :] + add_v[rows]

    def pair(at, count):
        at = pl.ds(pl.multiple_of(at, 8), count)
        return jnp.concatenate([kext[at, :], vext[at, :]], axis=1)

    def edges():
        return (
            [pair(pitch * (above + t) + PAD, side) for t in range(RADIUS)],
            [pair(pitch * (above + t) + beside, PAD) for t in range(RADIUS)],
        )

    send_rims(sz, info, lambda r: pair(pitch * (r + RADIUS) + beside, PAD), edges,
              stat_rows([g_q, g_k, g_v]), pc_ref, pr_ref, pd_ref)
    per_head = sz.bq
    for g in range(sz.groups):
        turned = tab[g].T
        for h in range(4):
            total_h = jnp.zeros((side, sz.bk), F32)
            for r in range(sz.brows):
                at = h * per_head + r * side
                piece = turned[at : at + side]
                shift = (sz.bk - pitch * r) % sz.bk
                total_h = total_h + (pltpu.roll(piece, shift, 1) if shift else piece)
            tab_row = jnp.zeros((1, sz.bk), F32)
            for c in range(side):
                one = total_h[c : c + 1]
                tab_row = tab_row + (pltpu.roll(one, sz.bk - c, 1) if c else one)
            tab_ref[4 * g + h : 4 * g + h + 1, :] = tab_row
    tab_ref[sz.heads : 16, :] = jnp.zeros((16 - sz.heads, sz.bk), F32)


def qkv_back_kernel(sz, layer, info, dq_ref, dkv_ref, st_ref, rc_ref, rr_ref, rd_ref, w_ref, x_ref, gain_ref, g1_ref,
                    eq_ref, g_ref, vec_ref, dkv, d_h):
    step = pl.program_id(0)
    width, side, cells = sz.width, sz.side, sz.cells

    @pl.when(step == 0)
    def _():
        dkv[...] = dkv_ref[...]
        beside = PAD * (1 - info[1])
        edge = (1 - info[0]) * (side - RADIUS) * side
        sides = rc_ref[0 : side * PAD, :].astype(F32)
        for r in range(side):
            dkv[pl.ds(pl.multiple_of(r * side + beside, 8), PAD), :] += sides[r * PAD : (r + 1) * PAD]
        dkv[pl.ds(pl.multiple_of(edge, 8), RADIUS * side), :] += rr_ref[0 : RADIUS * side, :].astype(F32)
        corner = rd_ref[0 : (RADIUS + 1) * PAD, :].astype(F32)
        for t in range(RADIUS):
            dkv[pl.ds(pl.multiple_of(edge + t * side + beside, 8), PAD), :] += corner[t * PAD : (t + 1) * PAD]
        pieces = [read_stats(r, 3, width) for r in (
            st_ref[...],
            rc_ref[side * PAD : side * PAD + 16, :],
            rr_ref[RADIUS * side : RADIUS * side + 16, :],
            rd_ref[(RADIUS + 1) * PAD : (RADIUS + 1) * PAD + 16, :],
        )]
        ordered = in_tile_order(info, pieces)
        class_row = jnp.concatenate(
            [functools.reduce(lambda a, b: a + b, [o[i] for o in ordered]) for i in range(3)], axis=1
        )
        row = lax.broadcasted_iota(jnp.int32, (16, 3 * width), 0)
        eq_ref[0:cells, 0:width] = dq_ref[...]
        eq_ref[0:cells, width:] = dkv[...].astype(BF)
        eq_ref[cells : cells + 16, :] = jnp.where(row == 0, class_row, 0.0).astype(BF)
        d_h[...] = jnp.zeros_like(d_h)

    cols = pl.ds(pl.multiple_of(step * width, width), width)
    d_h[...] += dot_nt(eq_ref[:, cols], w_ref[...])

    @pl.when(step == pl.num_programs(0) - 1)
    def _():
        keep = keep_rows(sz.rows, sz.cells, jnp.where(info[2] == 1, 1.0, 0.0))
        d_x, gain_rows = norm_back(x_ref[...], gain_ref[layer : layer + 1, :], d_h[...])
        g_ref[...] = g1_ref[...] + d_x
        vec_ref[...] = jnp.zeros_like(vec_ref)
        vec_ref[0:1, :] = jnp.sum(keep * gain_rows, axis=0, keepdims=True)


def product(sz, info, mine_ref, got_ref, own_ref, other_ref):
    row = lax.broadcasted_iota(jnp.int32, own_ref.shape, 0)
    own = own_ref[...]
    own = jnp.where((row < sz.cells) | (info[0] == 0), own, jnp.zeros_like(own))
    return (
        dot(mine_ref[...], own) + dot(got_ref[:, 0 : sz.cells], other_ref[0 : sz.cells, :])
    ).astype(BF)


def store_halves(value, outer, send_ref, keep_ref):
    n = value.shape[0] // 4
    if outer:
        keep_ref[...] = value[: 2 * n]
        send_ref[...] = value[2 * n :]
    else:
        keep_ref[0:n] = value[0:n]
        send_ref[0:n] = value[n : 2 * n]
        keep_ref[n : 2 * n] = value[2 * n : 3 * n]
        send_ref[n : 2 * n] = value[3 * n :]


def grad_kernel(sz, outer, info, mine_ref, got_ref, own_ref, other_ref, send_ref, keep_ref):
    store_halves(product(sz, info, mine_ref, got_ref, own_ref, other_ref), outer, send_ref, keep_ref)


def grad_attn_kernel(sz, info, hm, hg, qo, qg, am, ag, bo, bg, s0, k0, s1, k1):
    step = pl.program_id(0)

    @pl.when(step < 2)
    def _():
        store_halves(product(sz, info, hm, hg, qo, qg), True, s0, k0)

    @pl.when(step == 2)
    def _():
        store_halves(product(sz, info, hm, hg, qo, qg), False, s1, k1)

    @pl.when(step == 3)
    def _():
        store_halves(product(sz, info, am, ag, bo, bg), False, s1, k1)


def bias_kernel(sz, table_ref, out_ref, wide):
    slot = lax.broadcasted_iota(jnp.int32, (sz.side, sz.bk), 1)
    for g in range(sz.groups):
        for h in range(4):
            line = jnp.broadcast_to(table_ref[4 * g + h : 4 * g + h + 1, :], (sz.side, sz.bk))
            line = pltpu.roll(line, 0, 1, stride=1, stride_axis=0)
            for r in range(sz.brows):
                piece = pltpu.roll(line, sz.pitch * r, 1) if r else line
                at = h * sz.bq + r * sz.side
                wide[at : at + sz.side, :] = jnp.where(slot == sz.class_slot, 0.0, piece)
        out_ref[g] = wide[...].T


def shape(dims, dtype):
    return jax.ShapeDtypeStruct(dims, dtype)


def whole(dims):
    return pl.BlockSpec(dims, lambda *_: (0,) * len(dims))


SCALARS = pl.BlockSpec(memory_space=pltpu.SMEM)


def local(patch_in, cls_in, page_side, norm_attn, qkv_weight, rel_table, out_weight, scale_attn,
          norm_mlp, up_weight, down_weight, scale_mlp, patch_cot, cls_cot):
    tiles = lax.axis_size("tile")
    pages = lax.axis_size("dp")
    layers, heads = rel_table.shape[:2]
    sz = Sizes(patch_in.shape[2], patch_in.shape[4], up_weight.shape[2], heads, tiles * pages)
    side, cells, rows, width, hidden = sz.side, sz.cells, sz.rows, sz.width, sz.hidden
    chunks = hidden // width
    tile = lax.axis_index("tile")
    me = lax.axis_index("dp") * tiles + tile
    tile_row, tile_col = tile // 2, tile % 2
    page = page_side[0]

    chunk_bits = chunks.bit_length() - 1
    low_bits = sz.bits - chunk_bits
    info = jnp.stack([tile_row, tile_col, (tile == 0).astype(jnp.int32), me >> low_bits]).astype(jnp.int32)

    def permutation(bits, low):
        per = width >> bits
        order = np.array([int(format(p, f"0{bits}b")[::-1], 2) for p in range(1 << bits)])
        source = (jnp.asarray(np.repeat(order, per)) ^ low) * per + jnp.asarray(np.tile(np.arange(per), 1 << bits))
        return (source[:, None] == jnp.arange(width)[None]).astype(BF)

    perm = permutation(sz.bits, me)
    perm_ff = permutation(low_bits, me & ((1 << low_bits) - 1))

    cell = np.arange(cells)
    own_ok = (tile_row * side + cell // side < page) & (tile_col * side + cell % side < page)
    own_mask = jnp.broadcast_to(jnp.where(own_ok, 0.0, MASKED).astype(F32), (8, cells))
    slot = np.arange(sz.bk)[None] + np.arange(sz.blocks)[:, None] * sz.brows * sz.pitch - PAD + RADIUS
    key_row = tile_row * side + slot // sz.pitch - RADIUS
    key_col = tile_col * side + slot % sz.pitch - RADIUS
    is_class = (np.arange(sz.bk) == sz.class_slot)[None]
    key_ok = (key_row >= 0) & (key_row < page) & (key_col >= 0) & (key_col < page) | is_class
    key_mask = jnp.broadcast_to(
        jnp.where(key_ok, 0.0, MASKED).astype(F32)[:, :, None], (sz.blocks, sz.bk, sz.bk // 2)
    )

    lines = jnp.pad(rel_table.reshape(layers, heads, SPAN, SPAN), ((0, 0), (0, 16 - heads), (0, 0), (0, sz.pitch - SPAN)),
                    constant_values=MASKED).reshape(layers, 16, SPAN * sz.pitch)
    first_slot = PAD - RADIUS
    lines = jnp.pad(lines, ((0, 0), (0, 0), (first_slot, sz.bk - first_slot - SPAN * sz.pitch)), constant_values=MASKED)

    def call(kernel, grid, in_specs, out_specs, out_shape, scratch=(), vmem=40, flops=0, nbytes=0, **kw):
        return pl.pallas_call(
            kernel,
            grid=grid,
            in_specs=in_specs,
            out_specs=out_specs,
            out_shape=out_shape,
            scratch_shapes=list(scratch),
            compiler_params=pltpu.CompilerParams(vmem_limit_bytes=vmem * MIB),
            cost_estimate=pl.CostEstimate(flops=flops, bytes_accessed=nbytes, transcendentals=0),
            **kw,
        )

    bias = call(
        functools.partial(bias_kernel, sz),
        (layers,),
        [pl.BlockSpec((None, 16, sz.bk), lambda l: (l, 0, 0))],
        pl.BlockSpec((None, sz.groups, sz.bk, sz.bk), lambda l: (l, 0, 0, 0)),
        shape((layers, sz.groups, sz.bk, sz.bk), F32),
        [pltpu.VMEM((sz.bk, sz.bk), F32)],
        nbytes=4 << 20,
    )(lines)

    pc_rows, pr_rows, pd_rows = side * PAD + 16, RADIUS * side + 16, (RADIUS + 1) * PAD + 16
    rim_shapes = [shape((n, 2 * width), BF) for n in (pc_rows, pr_rows, pd_rows)]
    rim_specs = [whole(s.shape) for s in rim_shapes]
    half = width // 2
    left_shape = shape((half, rows), BF)
    left_spec = whole((half, rows))
    row_w = whole((rows, width))
    par = whole((layers, width))

    def partner(value, x):
        return lax.ppermute(value, "tile", [(t, t ^ x) for t in range(tiles)])

    def exchange(rims):
        return [partner(v, x + 1) for x, v in enumerate(rims)]

    def layer_forward(l, x):
        third = pl.BlockSpec((None, width, width), lambda i: (l, 0, i))
        h, lm, ls, qkv, *rims = call(
            functools.partial(qkv_kernel, sz, l),
            (3,),
            [SCALARS, row_w, par, third, whole((width, width)), whole((8, cells))],
            [row_w, left_spec, left_spec, whole((rows, 3 * width))] + rim_specs,
            [shape((rows, width), BF), left_shape, left_shape, shape((rows, 3 * width), BF)] + rim_shapes,
            flops=2 * rows * width * width * 4, nbytes=8 << 20,
        )(info, x, norm_attn, qkv_weight, perm, own_mask)
        got = exchange(rims)
        stat_spec = pl.BlockSpec((16, 2 * width), lambda i: (side * PAD // 16, 0))
        nb, ng = sz.blocks, sz.groups
        p, kb, vb, stats, branch, x1, h2, am, as_, bm, bs = call(
            functools.partial(attention_kernel, sz, l),
            (1,),
            [SCALARS, whole((rows, 3 * width)), stat_spec] + rim_specs
            + [pl.BlockSpec((None, ng, sz.bk, sz.bk), lambda i: (l, 0, 0, 0)), whole(key_mask.shape), row_w,
               pl.BlockSpec((None, width, width), lambda i: (l, 0, 0)), par, par, whole((width, width))],
            [whole((nb * ng, sz.bk, sz.bk)), whole((nb, sz.bk, width)), whole((nb, sz.bk, width)), whole((8, width)),
             row_w, row_w, row_w, left_spec, left_spec, left_spec, left_spec],
            [shape((nb * ng, sz.bk, sz.bk), BF), shape((nb, sz.bk, width), BF), shape((nb, sz.bk, width), BF),
             shape((8, width), F32), shape((rows, width), F32), shape((rows, width), F32), shape((rows, width), BF)]
            + [left_shape] * 4,
            [pltpu.VMEM((sz.ext_rows, width), F32), pltpu.VMEM((sz.ext_rows, width), F32), pltpu.VMEM((rows, width), BF)],
            flops=3 << 30, nbytes=20 << 20,
        )(info, qkv, rims[0], *got, bias, key_mask, x, out_weight, scale_attn, norm_mlp, perm)
        up_spec = pl.BlockSpec((None, width, width), lambda i, s: (l, 0, i))
        down_spec = pl.BlockSpec((None, width, width), lambda i, s: (l, i, 0))
        hid_spec = pl.BlockSpec((rows, width), lambda i, s: (0, i))
        act_spec = pl.BlockSpec((None, half, rows), lambda i, s: (i ^ s[3], 0, 0))
        up, down, x2, cm, cs = pl.pallas_call(
            functools.partial(mlp_kernel, sz, l),
            grid_spec=pltpu.PrefetchScalarGridSpec(
                num_scalar_prefetch=1,
                grid=(chunks,),
                in_specs=[row_w, up_spec, down_spec, row_w, par, whole((width, width))],
                out_specs=[hid_spec, row_w, row_w, act_spec, act_spec],
            ),
            out_shape=[shape((rows, hidden), F32), shape((rows, width), F32), shape((rows, width), F32),
                       shape((chunks, half, rows), BF), shape((chunks, half, rows), BF)],
            compiler_params=pltpu.CompilerParams(vmem_limit_bytes=40 * MIB),
            cost_estimate=pl.CostEstimate(flops=2 * rows * width * hidden * 3, bytes_accessed=16 << 20, transcendentals=0),
        )(info, h2, up_weight, down_weight, x1, scale_mlp, perm_ff)
        lefts = [(m, partner(s, 1)) for m, s in ((lm, ls), (am, as_), (bm, bs), (cm, cs))]
        return x2, (x, qkv, p, kb, vb, stats, branch, x1, up, down, lefts)

    def grads(outer, left, right, other):
        mine, got = left
        wide_left = mine.ndim == 3
        lspec = (pl.BlockSpec((None, half, rows), lambda i: (i, 0, 0)) if wide_left else left_spec)
        rspec = row_w if wide_left else pl.BlockSpec((rows, width), lambda i: (0, i))
        out = pl.BlockSpec((None, half // 2, width), lambda i: (i, 0, 0))
        return call(
            functools.partial(grad_kernel, sz, outer),
            (chunks,),
            [SCALARS, lspec, lspec, rspec, rspec],
            [out, out],
            [shape((chunks, half // 2, width), BF)] * 2,
            flops=2 * half * width * hidden * 2, nbytes=10 << 20,
        )(info, mine, got, right, other)

    def grads_attn(h_left, a_left, e_qkv, q_other, e_branch, b_other):
        def block(index):
            return pl.BlockSpec((None, half // 2, width), lambda i: (index(i), 0, 0))

        first, second = block(lambda i: jnp.minimum(i, 1)), block(lambda i: jnp.maximum(i - 2, 0))
        qspec = pl.BlockSpec((rows, width), lambda i: (0, jnp.minimum(i, 2)))
        return call(
            functools.partial(grad_attn_kernel, sz),
            (4,),
            [SCALARS, left_spec, left_spec, qspec, qspec, left_spec, left_spec, row_w, row_w],
            [first, first, second, second],
            [shape((2, half // 2, width), BF)] * 4,
            flops=2 * half * width * width * 8, nbytes=10 << 20,
        )(info, *h_left, e_qkv, q_other, *a_left, e_branch, b_other)

    def swap(value, bit):
        if bit < 2:
            return partner(value, 1 << bit)
        return lax.ppermute(value, "dp", [(d, d ^ (1 << (bit - 2))) for d in range(pages)])

    def scattered(send, keep, dims, first, order):
        bits = [d for d in dims if d[0] is not None]
        send = send.reshape([n for _, n in dims])
        keep = keep.reshape([n for _, n in dims])
        names = [b for b, _ in dims]
        got = swap(send, first)
        for bit in order:
            axis = names.index(bit)
            take = functools.partial(lax.index_in_dim, axis=axis, keepdims=False)
            send = (take(keep, 1).astype(F32) + take(got, 1).astype(F32)).astype(BF)
            keep = (take(keep, 0).astype(F32) + take(got, 0).astype(F32)).astype(BF)
            names.pop(axis)
            got = swap(send, bit)
        return keep.astype(F32) + got.astype(F32)

    rest = list(range(3, sz.bits))
    piece = width // sz.devices
    ff_piece = hidden // sz.devices

    def reduce_cols(halves, outer):
        send, keep = halves
        blocks = send.shape[0]
        kept, first = (2, 1) if outer else (1, 2)
        dims = [(None, blocks), (kept, 2)] + [(b, 2) for b in rest] + [(None, piece), (None, width)]
        out = scattered(send, keep, dims, first, [kept] + rest)
        return jnp.swapaxes(out, 0, 1)

    def reduce_rows(halves):
        send, keep = halves
        top = list(range(sz.bits - 1, low_bits - 1, -1))
        low = [b for b in range(1, low_bits) if b != 2]
        dims = [(b, 2) for b in top] + [(b, 2) for b in low] + [(None, ff_piece), (None, width)]
        return scattered(send, keep, dims, 2, [1] + rest)

    def layer_backward(l, g, kept):
        x, qkv, p, kb, vb, stats, branch, x1, up, down, lefts = kept
        hid_spec = pl.BlockSpec((rows, width), lambda i: (0, i))
        e_down, e_up, g1, e_branch, vec = call(
            functools.partial(mlp_back_kernel, sz, l),
            (chunks,),
            [SCALARS, row_w, row_w, par, hid_spec, pl.BlockSpec((None, width, width), lambda i: (l, i, 0)),
             pl.BlockSpec((None, width, width), lambda i: (l, 0, i)), row_w, par, par, row_w],
            [row_w, hid_spec, row_w, row_w, whole((8, width))],
            [shape((rows, width), BF), shape((rows, hidden), BF), shape((rows, width), F32), shape((rows, width), BF),
             shape((8, width), F32)],
            [pltpu.VMEM((rows, width), F32)],
            flops=2 * rows * width * hidden * 2, nbytes=18 << 20,
        )(info, g, down, scale_mlp, up, down_weight, up_weight, x1, norm_mlp, scale_attn, branch)
        h_left, a_left, b_left, c_left = lefts
        down_halves = grads(False, c_left, e_down, partner(e_down, 1))
        up_halves = grads(True, b_left, e_up, partner(e_up, 1))
        nb, ng = sz.blocks, sz.groups
        d_q, d_kv, *tail = call(
            functools.partial(attention_back_kernel, sz, l),
            (1,),
            [SCALARS, row_w, pl.BlockSpec((None, width, width), lambda i: (l, 0, 0)), whole((rows, 3 * width)),
             whole((nb * ng, sz.bk, sz.bk)), whole((nb, sz.bk, width)), whole((nb, sz.bk, width)), whole((8, width)),
             whole((8, cells))],
            [whole((cells, width)), whole((cells, 2 * width))] + rim_specs + [whole((16, sz.bk))],
            [shape((cells, width), BF), shape((cells, 2 * width), F32)] + rim_shapes + [shape((16, sz.bk), F32)],
            [pltpu.VMEM((sz.ext_rows, width), F32), pltpu.VMEM((sz.ext_rows, width), F32), pltpu.VMEM((rows, width), F32),
             pltpu.VMEM((ng, sz.bk, sz.bk), F32)],
            flops=3 << 30, nbytes=16 << 20,
        )(info, e_branch, out_weight, qkv, p, kb, vb, stats, own_mask)
        rims, table = tail[:3], tail[3]
        got = exchange(rims)
        stat_spec = pl.BlockSpec((16, 2 * width), lambda i: (side * PAD // 16, 0))
        e_qkv, g, vec2 = call(
            functools.partial(qkv_back_kernel, sz, l),
            (3,),
            [SCALARS, whole((cells, width)), whole((cells, 2 * width)), stat_spec] + rim_specs
            + [pl.BlockSpec((None, width, width), lambda i: (l, 0, i)), row_w, par, row_w],
            [whole((rows, 3 * width)), row_w, whole((8, width))],
            [shape((rows, 3 * width), BF), shape((rows, width), F32), shape((8, width), F32)],
            [pltpu.VMEM((cells, 2 * width), F32), pltpu.VMEM((rows, width), F32)],
            flops=2 * rows * width * width * 3, nbytes=12 << 20,
        )(info, d_q, d_kv, rims[0], *got, qkv_weight, x, norm_attn, g1)
        s0, k0, s1, k1 = grads_attn(h_left, a_left, e_qkv, partner(e_qkv, 1), e_branch, partner(e_branch, 1))
        g_down = reduce_rows(down_halves)
        g_up = reduce_cols(up_halves, True)
        first = reduce_cols((s0, k0), True)
        second = reduce_cols((s1, k1), False)
        g_qkv = jnp.concatenate([first, second[:, :1]], axis=1).reshape(piece, 3 * width)
        vectors = jnp.concatenate([vec2[:1], vec[:3]], axis=0)
        return g, (g_qkv, second[:, 1], g_up.reshape(piece, hidden), g_down, vectors, table)

    x = jnp.concatenate([patch_in.reshape(cells, width).astype(F32), cls_in.astype(F32),
                         jnp.zeros((rows - cells - 1, width), F32)], axis=0)
    saved = []
    for l in range(layers):
        x, kept = layer_forward(l, x)
        saved.append(kept)
    valid = own_ok[:, None]
    patch_out = jnp.where(valid, x[:cells], 0.0).astype(BF).reshape(patch_in.shape)
    cls_out = x[cells : cells + 1].astype(BF)
    g = jnp.concatenate([jnp.where(valid, patch_cot.reshape(cells, width).astype(F32), 0.0), cls_cot.astype(F32),
                         jnp.zeros((rows - cells - 1, width), F32)], axis=0)
    results = [None] * layers
    for l in reversed(range(layers)):
        g, results[l] = layer_backward(l, g, saved[l])
    g_qkv, g_out, g_up, g_down, vectors, tables = (jnp.stack([r[i] for r in results]) for i in range(6))
    vectors, tables = lax.psum((vectors, tables), ("dp", "tile"))
    mine = lax.dynamic_slice_in_dim(vectors, me * piece, piece, axis=2)
    tables = tables[:, :heads, first_slot : first_slot + SPAN * sz.pitch].reshape(layers, heads, SPAN, sz.pitch)
    g_table = tables[..., :SPAN].reshape(rel_table.shape)
    return (
        patch_out,
        cls_out,
        g[:cells].reshape(patch_in.shape),
        g[cells : cells + 1],
        mine[:, 0],
        g_qkv,
        g_table,
        g_out,
        mine[:, 3],
        mine[:, 2],
        g_up,
        g_down,
        mine[:, 1],
    )


def solution(mesh):
    tokens = P("dp", "tile", None, None, None)
    split = ("dp", "tile")
    in_specs = (tokens, P("dp", None), P("dp")) + (P(),) * 9 + (tokens, P("dp", None))
    out_specs = (
        tokens,
        P("dp", None),
        tokens,
        P("dp", None),
        P(None, split),
        P(None, split, None),
        P(),
        P(None, split, None),
        P(None, split),
        P(None, split),
        P(None, split, None),
        P(None, split, None),
        P(None, split),
    )
    return jax.shard_map(local, mesh=mesh, in_specs=in_specs, out_specs=out_specs, check_vma=False)
```

time: 1150 us -> 491 us (0.43)
  the two profiles are of different devices: /device:TPU:1 before, /device:TPU:0 now
where the time goes in v1:
time: 491 us; the launch traced here: 481 us
  waiting for transfers between devices  176 us (36%)
  Pallas kernels  108 us (22%)
  local copies, waits for them, and re-layouts  70.9 us (14%)
  starting transfers between devices  53.4 us (11%)
  blocking collectives  40.5 us (8%)
  other arithmetic  29.8 us (6%)
    ppermute x36, waiting for transfers between devices, partner(): return lax.ppermute(value, 'tile', [(t, t ^ x) for t in range(tiles)])  103 us
    ppermute x24, waiting for transfers between devices, swap(): lax.ppermute(value, 'dp', [(d, d ^ 1 << bit - 2) for d in range(pages)])  72.4 us
    unnamed x226, local copies, waits for them, and re-layouts  46 us
    psum x1, blocking collectives, local(): vectors, tables = lax.psum((vectors, tables), ('dp', 'tile'))  40.5 us
    ppermute x24, starting transfers between devices, swap(): lax.ppermute(value, 'dp', [(d, d ^ 1 << bit - 2) for d in range(pages)])  30.5 us
    ppermute x36, starting transfers between devices, partner(): return lax.ppermute(value, 'tile', [(t, t ^ x) for t in range(tiles)])  22.9 us
    pallas_call x2, Pallas kernels, layer_forward(): pl.pallas_call(functools.partial(mlp_kernel, sz, l), grid_spec=pltpu.Pref...  20.5 us
    pallas_call x2, Pallas kernels, layer_backward(): call(functools.partial(mlp_back_kernel, sz, l), (chunks,), [SCALARS, row_...  18.7 us
  transfers between devices with their start and end apart: 60, of which 20 were waited for; matrix products, arithmetic and copies ran while one was open for 10% of the time, Pallas kernels for 17%

profile of v1, /device:TPU:0, one launch (start us, length us, event | category | flops | bytes accessed | tf_op | source)
XLA Modules:
  0.0 481.3 jit_solution(12324722744967629675)
XLA Ops:
  8.6 4.9 %shard_map.318 = (bf16[272,768]{1,0:T(8,128)(2,1)}, bf16[384,272]{1,0:T(8,128)(2,1)S(1)}, bf16[384,272]{1,0:T(8,128)(2,1)S(1)}, bf16[272,2304]{1,0:T(8,128)(2,1)...) custom-call(s32[4]{0:T(128)S(1)} %pad_add_fusion.info, ...), custom_call_target="tpu_custom_call" | custom-call | flops 1283457024 | bytes 8388608 | tf_op jit(solution)/shard_map/pallas_call | solution.py:649
  23.1 4.8 collective-permute-done.2.rd_ref
  28.1 6.0 %shard_map.320 = (bf16[12,256,256]{2,1,0:T(8,128)(2,1)S(1)}, bf16[4,256,768]{2,1,0:T(8,128)(2,1)S(1)}, bf16[4,256,768]{2,1,0:T(8,128)(2,1)S(1)}, f32[8,768]{1,0:...) custom-call(s32[4]{0:T(128)S(1)} %pad_add_fusion.info, ...), custom_call_target="tpu_custom_call" | custom-call | flops 3221225472 | bytes 20971520 | tf_op jit(solution)/shard_map/pallas_call | solution.py:660
  41.4 10.5 %shard_map.321 = (f32[272,3072]{1,0:T(8,128)S(1)}, f32[272,768]{1,0:T(8,128)S(1)}, f32[272,768]{1,0:T(8,128)S(1)}, bf16[4,384,272]{2,1,0:T(8,128)(2,1)S(1)}, bf16[4,384,272]{2,1,0:T(8,128)(2,1)S(1)}) custom-call(s32[4]{0:T(128)S(1)} %pad_add_fusion.info, bf16[272,768]{1,0:T(8,128)(2,1)S(1)} %get-tuple-element.105.h2_ref, bf16[2,768,3072]{2,1,0:T(8,128)(2,1)} %up_w_ref.7, ...), custom_call_target="tpu_custom_call" | custom-call | flops 3850371072 | bytes 16777216 | tf_op jit(solution)/shard_map/pallas_call | solution.py:678
  54.2 5.1 %shard_map.322 = (bf16[272,768]{1,0:T(8,128)(2,1)}, bf16[384,272]{1,0:T(8,128)(2,1)S(1)}, bf16[384,272]{1,0:T(8,128)(2,1)}, bf16[272,2304]{1,0:T(8,128)(2,1)S(1)...) custom-call(s32[4]{0:T(128)S(1)} %pad_add_fusion.info, ...), custom_call_target="tpu_custom_call" | custom-call | flops 1283457024 | bytes 8388608 | tf_op jit(solution)/shard_map/pallas_call | solution.py:649
  65.1 5.6 %collective-permute-done.5.rd_ref = bf16[48,1536]{1,0:T(8,128)(2,1)} collective-permute-done((bf16[48,1536]{1,0:T(8,128)(2,1)}, bf16[48,1536]{1,0:T(8,128)(2,1)}, u32[]{:S(2)}, u32[]{:S(2)}) %collective-permute-start.5) | collective-permute-done | bytes 147488 | tf_op jit(solution)/shard_map/ppermute | solution.py:642
  74.2 6.6 %shard_map.323 = (bf16[12,256,256]{2,1,0:T(8,128)(2,1)S(1)}, bf16[4,256,768]{2,1,0:T(8,128)(2,1)S(1)}, bf16[4,256,768]{2,1,0:T(8,128)(2,1)S(1)}, f32[8,768]{1,0:...) custom-call(s32[4]{0:T(128)S(1)} %pad_add_fusion.info, ...), custom_call_target="tpu_custom_call" | custom-call | flops 3221225472 | bytes 20971520 | tf_op jit(solution)/shard_map/pallas_call | solution.py:660
  81.5 10.1 %shard_map.324 = (f32[272,3072]{1,0:T(8,128)S(1)}, f32[272,768]{1,0:T(8,128)S(1)}, f32[272,768]{1,0:T(8,128)S(1)}, bf16[4,384,272]{2,1,0:T(8,128)(2,1)S(1)}, bf16[4,384,272]{2,1,0:T(8,128)(2,1)S(1)}) custom-call(s32[4]{0:T(128)S(1)} %pad_add_fusion.info, bf16[272,768]{1,0:T(8,128)(2,1)S(1)} %get-tuple-element.112.h2_ref, bf16[2,768,3072]{2,1,0:T(8,128)(2,1)} %up_w_ref.7, ...), custom_call_target="tpu_custom_call" | custom-call | flops 3850371072 | bytes 16777216 | tf_op jit(solution)/shard_map/pallas_call | solution.py:678
  92.7 8.9 %shard_map.325 = (bf16[272,768]{1,0:T(8,128)(2,1)S(1)}, bf16[272,3072]{1,0:T(8,128)(2,1)S(1)}, f32[272,768]{1,0:T(8,128)S(1)}, bf16[272,768]{1,0:T(8,128)(2,1)S(1)}, f32[8,768]{1,0:T(8,128)S(1)}) custom-call(s32[4]{0:T(128)S(1)} %pad_add_fusion.info, f32[272,768]{1,0:T(8,128)S(1)} %copy-done.4, f32[272,768]{1,0:T(8,128)S(1)} %get-tuple-element.115.down_ref, ...), custom_call_target="tpu_custom_call" | custom-call | flops 2566914048 | bytes 18874368 | tf_op jit(solution)/shard_map/pallas_call | solution.py:766
  103.6 5.7 %shard_map.326 = (bf16[256,768]{1,0:T(8,128)(2,1)S(1)}, f32[256,1536]{1,0:T(8,128)S(1)}, bf16[144,1536]{1,0:T(8,128)(2,1)S(1)}, bf16[64,1536]{1,0:T(8,128)(2,1)S...) custom-call(s32[4]{0:T(128)S(1)} %pad_add_fusion.info, bf16[272,768]{1,0:T(8,128)(2,1)S(1)} %get-tuple-element.118.eb_ref.bo, ...), custom_call_target="tpu_custom_call" | custom-call | flops 3221225472 | bytes 16777216 | tf_op jit(solution)/shard_map/pallas_call | solution.py:781
  129.3 4.1 shard_map.327
  133.5 9.8 %shard_map.328 = (bf16[272,768]{1,0:T(8,128)(2,1)}, bf16[272,3072]{1,0:T(8,128)(2,1)}, f32[272,768]{1,0:T(8,128)S(1)}, bf16[272,768]{1,0:T(8,128)(2,1)S(1)}, f32[8,768]{1,0:T(8,128)S(1)}) custom-call(s32[4]{0:T(128)S(1)} %pad_add_fusion.info, f32[272,768]{1,0:T(8,128)S(1)} %get-tuple-element.129.g_ref, f32[272,768]{1,0:T(8,128)S(1)} %copy-done.23, ...), custom_call_target="tpu_custom_call" | custom-call | flops 2566914048 | bytes 18874368 | tf_op jit(solution)/shard_map/pallas_call | solution.py:766
  144.8 6.4 %shard_map.329 = (bf16[256,768]{1,0:T(8,128)(2,1)S(1)}, f32[256,1536]{1,0:T(8,128)S(1)}, bf16[144,1536]{1,0:T(8,128)(2,1)}, bf16[64,1536]{1,0:T(8,128)(2,1)}, bf...) custom-call(s32[4]{0:T(128)S(1)} %pad_add_fusion.info, bf16[272,768]{1,0:T(8,128)(2,1)S(1)} %get-tuple-element.133.eb_ref.bo, ...), custom_call_target="tpu_custom_call" | custom-call | flops 3221225472 | bytes 16777216 | tf_op jit(solution)/shard_map/pallas_call | solution.py:781
  161.2 3.6 shard_map.336
  167.3 3.9 shard_map.335
  173.9 3.9 shard_map.330
  179.8 40.5 %all-reduce.2 = (f32[2,4,768]{2,1,0:T(4,128)S(1)}, f32[2,16,256]{2,1,0:T(8,128)S(1)}) all-reduce(f32[2,4,768]{2,1,0:T(4,128)S(1)} %pad_maximum_fusion.7, f32[2,16,256]{2,1,0:T(8,128)S(1)} %pad_maximum_fusion.6), channel_id=1, replica_groups=mesh['dp'=8,'tile'=4] {'dp','tile'}, use_global_device_ids=true, to_apply=%region_0.1 | all-reduce | flops 14336 | bytes 114688 | tf_op jit(solution)/shard_map/psum | solution.py:830
  229.8 4.3 shard_map.334
  236.0 4.3 shard_map.332
  241.1 8.7 %collective-permute-done.56 = bf16[2,2,2,96,768]{4,3,1,0,2:T(8,128)(2,1)S(1)} collective-permute-done((bf16[2,2,2,96,768]{4,3,1,0,2:T(8,128)(2,1)}, bf16[2,2,2,96,768]{4,3,1,0,2:T(8,128)(2,1)S(1)}, u32[]{:S(2)}, u32[]{:S(2)}) %collective-permute-start.56) | collective-permute-done | bytes 1179680 | tf_op jit(solution)/shard_map/ppermute | solution.py:727
  250.1 24.7 %collective-permute-done.50 = bf16[2,2,2,96,768]{4,3,1,0,2:T(8,128)(2,1)S(1)} collective-permute-done((bf16[2,2,2,96,768]{4,3,1,0,2:T(8,128)(2,1)}, bf16[2,2,2,96,768]{4,3,1,0,2:T(8,128)(2,1)S(1)}, u32[]{:S(2)}, u32[]{:S(2)}) %collective-permute-start.50) | collective-permute-done | bytes 1179680 | tf_op jit(solution)/shard_map/ppermute | solution.py:727
  278.1 4.0 shard_map.333
  287.3 3.6 shard_map.331
  293.5 31.4 %collective-permute-done.28 = bf16[2,2,2,2,24,768]{5,0,4,3,2,1:T(2,128)(2,1)S(1)} collective-permute-done((bf16[2,2,2,2,24,768]{5,0,4,3,2,1:T(2,128)(2,1)S(1)}, bf16[2,2,2,2,24,768]{5,0,4,3,2,1:T(2,128)(2,1)S(1)}, u32[]{:S(2)}, u32[]{:S(2)}) %collective-permute-start.28) | collective-permute-done | bytes 589856 | tf_op jit(solution)/shard_map/ppermute | solution.py:642
  326.8 28.5 %collective-permute-done.33 = bf16[2,2,2,24,768]{4,3,0,2,1:T(8,128)(2,1)S(1)} collective-permute-done((bf16[2,2,2,24,768]{4,3,0,2,1:T(8,128)(2,1)S(1)}, bf16[2,2,2,24,768]{4,3,0,2,1:T(8,128)(2,1)S(1)}, u32[]{:S(2)}, u32[]{:S(2)}) %collective-permute-start.33) | collective-permute-done | bytes 294944 | tf_op jit(solution)/shard_map/ppermute | solution.py:642
  361.7 33.1 %collective-permute-done.16 = bf16[2,2,2,2,24,768]{5,0,4,3,2,1:T(2,128)(2,1)S(1)} collective-permute-done((bf16[2,2,2,2,24,768]{5,0,4,3,2,1:T(2,128)(2,1)S(1)}, bf16[2,2,2,2,24,768]{5,0,4,3,2,1:T(2,128)(2,1)S(1)}, u32[]{:S(2)}, u32[]{:S(2)}) %collective-permute-start.16) | collective-permute-done | bytes 589856 | tf_op jit(solution)/shard_map/ppermute | solution.py:642
  404.0 8.2 %collective-permute-done.35 = bf16[2,24,768]{2,1,0:T(8,128)(2,1)S(1)} collective-permute-done((bf16[2,24,768]{2,1,0:T(8,128)(2,1)S(1)}, bf16[2,24,768]{2,1,0:T(8,128)(2,1)S(1)}, u32[]{:S(2)}, u32[]{:S(2)}) %collective-permute-start.35) | collective-permute-done | bytes 73760 | tf_op jit(solution)/shard_map/ppermute | solution.py:727
  412.1 3.5 collective-permute-start.31
  444.4 3.8 collective-permute-done.23
  457.4 6.0 %collective-permute-done.39 = bf16[4,2,2,24,768]{4,3,2,1,0:T(8,128)(2,1)S(1)} collective-permute-done((bf16[4,2,2,24,768]{4,3,2,1,0:T(8,128)(2,1)S(1)}, bf16[4,2,2,24,768]{4,3,2,1,0:T(8,128)(2,1)S(1)}, u32[]{:S(2)}, u32[]{:S(2)}) %collective-permute-start.39) | collective-permute-done | bytes 589856 | tf_op jit(solution)/shard_map/ppermute | solution.py:727
  467.7 5.8 %collective-permute-done.40 = bf16[4,2,24,768]{3,2,1,0:T(8,128)(2,1)S(1)} collective-permute-done((bf16[4,2,24,768]{3,2,1,0:T(8,128)(2,1)S(1)}, bf16[4,2,24,768]{3,2,1,0:T(8,128)(2,1)S(1)}, u32[]{:S(2)}, u32[]{:S(2)}) %collective-permute-start.40) | collective-permute-done | bytes 294944 | tf_op jit(solution)/shard_map/ppermute | solution.py:727
  473.7 4.0 collective-permute-done.47
  (439 shorter events, 164.0 us)
Async XLA Ops:
  64.6 56.4 %collective-permute-start.48 = (bf16[4,384,272]{1,2,0:T(8,128)(2,1)}, bf16[4,384,272]{1,2,0:T(8,128)(2,1)}, u32[]{:S(2)}, u32[]{:S(2)}) collective-permute-start(bf16[4,384,272]{1,2,0:T(8,128)(2,1)} %copy.157), channel_id=1, source_target_pairs={{0,1},{1,0},{2,3},{3,2},{4,5},{5,4},{6,7},{7,6},{8,9},{9,8},{10,11... | collective-permute-start | bytes 2506760 | tf_op jit(solution)/shard_map/ppermute | solution.py:642
  115.7 38.1 %collective-permute-start.54 = (bf16[4,384,272]{1,2,0:T(8,128)(2,1)}, bf16[4,384,272]{1,2,0:T(8,128)(2,1)}, u32[]{:S(2)}, u32[]{:S(2)}) collective-permute-start(bf16[4,384,272]{1,2,0:T(8,128)(2,1)} %copy.162), channel_id=1, source_target_pairs={{0,1},{1,0},{2,3},{3,2},{4,5},{5,4},{6,7},{7,6},{8,9},{9,8},{10,11... | collective-permute-start | bytes 2506760 | tf_op jit(solution)/shard_map/ppermute | solution.py:642
  121.0 107.0 %collective-permute-start.43 = (bf16[272,3072]{1,0:T(8,128)(2,1)}, bf16[272,3072]{1,0:T(8,128)(2,1)}, u32[]{:S(2)}, u32[]{:S(2)}) collective-permute-start(bf16[272,3072]{1,0:T(8,128)(2,1)} %copy-done.39), channel_id=1, source_target_pairs={{0,1},{1,0},{2,3},{3,2},{4,5},{5,4},{6,7},{7,6},{8,9},{9,8},{10,11... | collective-permute-start | bytes 5013512 | tf_op jit(solution)/shard_map/ppermute | solution.py:642
  123.3 34.3 %collective-permute-start.55 = (bf16[272,768]{1,0:T(8,128)(2,1)}, bf16[272,768]{1,0:T(8,128)(2,1)}, u32[]{:S(2)}, u32[]{:S(2)}) collective-permute-start(bf16[272,768]{1,0:T(8,128)(2,1)} %copy-done.59), channel_id=1, source_target_pairs={{0,1},{1,0},{2,3},{3,2},{4,5},{5,4},{6,7},{7,6},{8,9},{9,8},{10,11... | collective-permute-start | bytes 1253384 | tf_op jit(solution)/shard_map/ppermute | solution.py:642
  152.7 20.7 %collective-permute-start.9 = (bf16[144,1536]{1,0:T(8,128)(2,1)}, bf16[144,1536]{1,0:T(8,128)(2,1)}, u32[]{:S(2)}, u32[]{:S(2)}) collective-permute-start(bf16[144,1536]{1,0:T(8,128)(2,1)} %get-tuple-element.140.st_ref), channel_id=1, source_target_pairs={{0,1},{1,0},{2,3},{3,2},{4,5},{5,4},{6,7},{7,6},{8,9},{9,8},{10,11... | collective-permute-start | bytes 1327112 | tf_op jit(solution)/shard_map/ppermute | solution.py:642
  153.8 19.5 %collective-permute-start.10 = (bf16[64,1536]{1,0:T(8,128)(2,1)}, bf16[64,1536]{1,0:T(8,128)(2,1)S(1)}, u32[]{:S(2)}, u32[]{:S(2)}) collective-permute-start(bf16[64,1536]{1,0:T(8,128)(2,1)} %get-tuple-element.141), channel_id=1, source_target_pairs={{0,2},{1,3},{2,0},{3,1},{4,6},{5,7},{6,4},{7,5},{8,10},{9,11},{10,... | collective-permute-start | bytes 589832 | tf_op jit(solution)/shard_map/ppermute | solution.py:642
  157.6 77.7 %collective-permute-start.25 = (bf16[272,2304]{1,0:T(8,128)(2,1)}, bf16[272,2304]{1,0:T(8,128)(2,1)}, u32[]{:S(2)}, u32[]{:S(2)}) collective-permute-start(bf16[272,2304]{1,0:T(8,128)(2,1)} %copy-done.44), channel_id=1, source_target_pairs={{0,1},{1,0},{2,3},{3,2},{4,5},{5,4},{6,7},{7,6},{8,9},{9,8},{10,11... | collective-permute-start | bytes 3760136 | tf_op jit(solution)/shard_map/ppermute | solution.py:642
  172.7 47.6 %collective-permute-start.24 = (bf16[384,272]{1,0:T(8,128)(2,1)}, bf16[384,272]{1,0:T(8,128)(2,1)}, u32[]{:S(2)}, u32[]{:S(2)}) collective-permute-start(bf16[384,272]{1,0:T(8,128)(2,1)} %get-tuple-element.159), channel_id=1, source_target_pairs={{0,1},{1,0},{2,3},{3,2},{4,5},{5,4},{6,7},{7,6},{8,9},{9,8},{10,11... | collective-permute-start | bytes 626696 | tf_op jit(solution)/shard_map/ppermute | solution.py:642
  173.3 47.1 %collective-permute-start.26 = (bf16[384,272]{1,0:T(8,128)(2,1)}, bf16[384,272]{1,0:T(8,128)(2,1)}, u32[]{:S(2)}, u32[]{:S(2)}) collective-permute-start(bf16[384,272]{1,0:T(8,128)(2,1)} %get-tuple-element.162), channel_id=1, source_target_pairs={{0,1},{1,0},{2,3},{3,2},{4,5},{5,4},{6,7},{7,6},{8,9},{9,8},{10,11... | collective-permute-start | bytes 626696 | tf_op jit(solution)/shard_map/ppermute | solution.py:642
  173.4 54.5 %collective-permute-start.42 = (bf16[384,272]{1,0:T(8,128)(2,1)}, bf16[384,272]{1,0:T(8,128)(2,1)}, u32[]{:S(2)}, u32[]{:S(2)}) collective-permute-start(bf16[384,272]{1,0:T(8,128)(2,1)} %get-tuple-element.175), channel_id=1, source_target_pairs={{0,1},{1,0},{2,3},{3,2},{4,5},{5,4},{6,7},{7,6},{8,9},{9,8},{10,11... | collective-permute-start | bytes 626696 | tf_op jit(solution)/shard_map/ppermute | solution.py:642
  220.4 14.9 %collective-permute-start.27 = (bf16[272,768]{1,0:T(8,128)(2,1)}, bf16[272,768]{1,0:T(8,128)(2,1)S(1)}, u32[]{:S(2)}, u32[]{:S(2)}) collective-permute-start(bf16[272,768]{1,0:T(8,128)(2,1)} %copy-done.57), channel_id=1, source_target_pairs={{0,1},{1,0},{2,3},{3,2},{4,5},{5,4},{6,7},{7,6},{8,9},{9,8},{10,11... | collective-permute-start | bytes 1253384 | tf_op jit(solution)/shard_map/ppermute | solution.py:642
  220.5 29.3 %collective-permute-start.56 = (bf16[2,2,2,96,768]{4,3,1,0,2:T(8,128)(2,1)}, bf16[2,2,2,96,768]{4,3,1,0,2:T(8,128)(2,1)S(1)}, u32[]{:S(2)}, u32[]{:S(2)}) collective-permute-start(bf16[2,2,2,96,768]{4,3,1,0,2:T(8,128)(2,1)} %copy.165), channel_id=1, source_target_pairs={{0,4},{4,0},{8,12},{12,8},{16,20},{20,16},{24,28},{28,24},{1,5},{5... | collective-permute-start | bytes 3538952 | tf_op jit(solution)/shard_map/ppermute | solution.py:727
  227.9 48.4 %collective-permute-start.37 = (bf16[272,3072]{1,0:T(8,128)(2,1)}, bf16[272,3072]{1,0:T(8,128)(2,1)S(1)}, u32[]{:S(2)}, u32[]{:S(2)}) collective-permute-start(bf16[272,3072]{1,0:T(8,128)(2,1)} %get-tuple-element.171.own_ref), channel_id=1, source_target_pairs={{0,1},{1,0},{2,3},{3,2},{4,5},{5,4},{6,7},{7,6},{8,9},{9,8},{10,11... | collective-permute-start | bytes 5013512 | tf_op jit(solution)/shard_map/ppermute | solution.py:642
  228.1 46.8 %collective-permute-start.50 = (bf16[2,2,2,96,768]{4,3,1,0,2:T(8,128)(2,1)}, bf16[2,2,2,96,768]{4,3,1,0,2:T(8,128)(2,1)S(1)}, u32[]{:S(2)}, u32[]{:S(2)}) collective-permute-start(bf16[2,2,2,96,768]{4,3,1,0,2:T(8,128)(2,1)} %copy.160), channel_id=1, source_target_pairs={{0,4},{4,0},{8,12},{12,8},{16,20},{20,16},{24,28},{28,24},{1,5},{5... | collective-permute-start | bytes 3538952 | tf_op jit(solution)/shard_map/ppermute | solution.py:727
  235.2 48.0 %collective-permute-start.12 = (bf16[384,272]{1,0:T(8,128)(2,1)S(1)}, bf16[384,272]{1,0:T(8,128)(2,1)S(1)}, u32[]{:S(2)}, u32[]{:S(2)}) collective-permute-start(bf16[384,272]{1,0:T(8,128)(2,1)S(1)} %copy-done.64), channel_id=1, source_target_pairs={{0,1},{1,0},{2,3},{3,2},{4,5},{5,4},{6,7},{7,6},{8,9},{9,8},{10,11... | collective-permute-start | bytes 626696 | tf_op jit(solution)/shard_map/ppermute | solution.py:642
  235.3 51.4 %collective-permute-start.13 = (bf16[272,2304]{1,0:T(8,128)(2,1)S(1)}, bf16[272,2304]{1,0:T(8,128)(2,1)S(1)}, u32[]{:S(2)}, u32[]{:S(2)}) collective-permute-start(bf16[272,2304]{1,0:T(8,128)(2,1)S(1)} %copy-done.47), channel_id=1, source_target_pairs={{0,1},{1,0},{2,3},{3,2},{4,5},{5,4},{6,7},{7,6},{8,9},{9,8},{10,11... | collective-permute-start | bytes 3760136 | tf_op jit(solution)/shard_map/ppermute | solution.py:642
  249.8 25.4 %collective-permute-start.36 = (bf16[384,272]{1,0:T(8,128)(2,1)S(1)}, bf16[384,272]{1,0:T(8,128)(2,1)S(1)}, u32[]{:S(2)}, u32[]{:S(2)}) collective-permute-start(bf16[384,272]{1,0:T(8,128)(2,1)S(1)} %copy-done.68), channel_id=1, source_target_pairs={{0,1},{1,0},{2,3},{3,2},{4,5},{5,4},{6,7},{7,6},{8,9},{9,8},{10,11... | collective-permute-start | bytes 626696 | tf_op jit(solution)/shard_map/ppermute | solution.py:642
  276.3 15.3 %collective-permute-start.32 = (bf16[2,2,2,2,24,768]{5,4,0,3,2,1:T(8,128)(2,1)S(1)}, bf16[2,2,2,2,24,768]{5,4,0,3,2,1:T(8,128)(2,1)S(1)}, u32[]{:S(2)}, u32[]{:S(2)}) collective-permute-start(bf16[2,2,2,2,24,768]{5,4,0,3,2,1:T(8,128)(2,1)S(1)} %copy.136), channel_id=1, source_target_pairs={{0,4},{4,0},{8,12},{12,8},{16,20},{20,16},{24,28},{28,24},{1,5},{5... | collective-permute-start | bytes 1769480 | tf_op jit(solution)/shard_map/ppermute | solution.py:727
  283.2 137.4 %collective-permute-start.44 = (bf16[4,2,2,2,24,768]{5,4,0,3,2,1:T(8,128)(2,1)}, bf16[4,2,2,2,24,768]{5,4,0,3,2,1:T(8,128)(2,1)}, u32[]{:S(2)}, u32[]{:S(2)}) collective-permute-start(bf16[4,2,2,2,24,768]{5,4,0,3,2,1:T(8,128)(2,1)} %copy.150), channel_id=1, source_target_pairs={{0,2},{1,3},{2,0},{3,1},{4,6},{5,7},{6,4},{7,5},{8,10},{9,11},{10,... | collective-permute-start | bytes 3538952 | tf_op jit(solution)/shard_map/ppermute | solution.py:642
  284.7 40.2 %collective-permute-start.28 = (bf16[2,2,2,2,24,768]{5,0,4,3,2,1:T(2,128)(2,1)S(1)}, bf16[2,2,2,2,24,768]{5,0,4,3,2,1:T(2,128)(2,1)S(1)}, u32[]{:S(2)}, u32[]{:S(2)}) collective-permute-start(bf16[2,2,2,2,24,768]{5,0,4,3,2,1:T(2,128)(2,1)S(1)} %copy.133), channel_id=1, source_target_pairs={{0,2},{1,3},{2,0},{3,1},{4,6},{5,7},{6,4},{7,5},{8,10},{9,11},{10,... | collective-permute-start | bytes 1769480 | tf_op jit(solution)/shard_map/ppermute | solution.py:642
  285.2 72.5 %collective-permute-start.57 = (bf16[2,2,96,768]{3,2,1,0:T(8,128)(2,1)S(1)}, bf16[2,2,96,768]{3,2,1,0:T(8,128)(2,1)S(1)}, u32[]{:S(2)}, u32[]{:S(2)}) collective-permute-start(bf16[2,2,96,768]{3,2,1,0:T(8,128)(2,1)S(1)} %get-tuple-element.222), channel_id=1, source_target_pairs={{0,2},{1,3},{2,0},{3,1},{4,6},{5,7},{6,4},{7,5},{8,10},{9,11},{10,... | collective-permute-start | bytes 1769480 | tf_op jit(solution)/shard_map/ppermute | solution.py:642
  286.8 72.4 %collective-permute-start.51 = (bf16[2,2,96,768]{3,2,1,0:T(8,128)(2,1)S(1)}, bf16[2,2,96,768]{3,2,1,0:T(8,128)(2,1)S(1)}, u32[]{:S(2)}, u32[]{:S(2)}) collective-permute-start(bf16[2,2,96,768]{3,2,1,0:T(8,128)(2,1)S(1)} %get-tuple-element.220), channel_id=1, source_target_pairs={{0,2},{1,3},{2,0},{3,1},{4,6},{5,7},{6,4},{7,5},{8,10},{9,11},{10,... | collective-permute-start | bytes 1769480 | tf_op jit(solution)/shard_map/ppermute | solution.py:642
  291.7 63.6 %collective-permute-start.33 = (bf16[2,2,2,24,768]{4,3,0,2,1:T(8,128)(2,1)S(1)}, bf16[2,2,2,24,768]{4,3,0,2,1:T(8,128)(2,1)S(1)}, u32[]{:S(2)}, u32[]{:S(2)}) collective-permute-start(bf16[2,2,2,24,768]{4,3,0,2,1:T(8,128)(2,1)S(1)} %get-tuple-element.248), channel_id=1, source_target_pairs={{0,2},{1,3},{2,0},{3,1},{4,6},{5,7},{6,4},{7,5},{8,10},{9,11},{10,... | collective-permute-start | bytes 884744 | tf_op jit(solution)/shard_map/ppermute | solution.py:642
  325.7 31.1 %collective-permute-start.29 = (bf16[2,2,2,24,768]{4,0,3,2,1:T(2,128)(2,1)S(1)}, bf16[2,2,2,24,768]{4,0,3,2,1:T(2,128)(2,1)S(1)}, u32[]{:S(2)}, u32[]{:S(2)}) collective-permute-start(bf16[2,2,2,24,768]{4,0,3,2,1:T(2,128)(2,1)S(1)} %get-tuple-element.242), channel_id=1, source_target_pairs={{0,4},{4,0},{8,12},{12,8},{16,20},{20,16},{24,28},{28,24},{1,5},{5... | collective-permute-start | bytes 884744 | tf_op jit(solution)/shard_map/ppermute | solution.py:727
  355.3 97.0 %collective-permute-start.38 = (bf16[4,2,2,2,24,768]{5,4,0,3,2,1:T(8,128)(2,1)}, bf16[4,2,2,2,24,768]{5,4,0,3,2,1:T(8,128)(2,1)}, u32[]{:S(2)}, u32[]{:S(2)}) collective-permute-start(bf16[4,2,2,2,24,768]{5,4,0,3,2,1:T(8,128)(2,1)} %copy.142), channel_id=1, source_target_pairs={{0,2},{1,3},{2,0},{3,1},{4,6},{5,7},{6,4},{7,5},{8,10},{9,11},{10,... | collective-permute-start | bytes 3538952 | tf_op jit(solution)/shard_map/ppermute | solution.py:642
  356.9 38.0 %collective-permute-start.16 = (bf16[2,2,2,2,24,768]{5,0,4,3,2,1:T(2,128)(2,1)S(1)}, bf16[2,2,2,2,24,768]{5,0,4,3,2,1:T(2,128)(2,1)S(1)}, u32[]{:S(2)}, u32[]{:S(2)}) collective-permute-start(bf16[2,2,2,2,24,768]{5,0,4,3,2,1:T(2,128)(2,1)S(1)} %copy.126), channel_id=1, source_target_pairs={{0,2},{1,3},{2,0},{3,1},{4,6},{5,7},{6,4},{7,5},{8,10},{9,11},{10,... | collective-permute-start | bytes 1769480 | tf_op jit(solution)/shard_map/ppermute | solution.py:642
  357.8 40.1 %collective-permute-start.20 = (bf16[2,2,2,2,24,768]{5,4,0,3,2,1:T(8,128)(2,1)S(1)}, bf16[2,2,2,2,24,768]{5,4,0,3,2,1:T(8,128)(2,1)S(1)}, u32[]{:S(2)}, u32[]{:S(2)}) collective-permute-start(bf16[2,2,2,2,24,768]{5,4,0,3,2,1:T(8,128)(2,1)S(1)} %copy.129), channel_id=1, source_target_pairs={{0,4},{4,0},{8,12},{12,8},{16,20},{20,16},{24,28},{28,24},{1,5},{5... | collective-permute-start | bytes 1769480 | tf_op jit(solution)/shard_map/ppermute | solution.py:727
  359.2 40.0 %collective-permute-start.34 = (bf16[2,2,24,768]{3,2,0,1:T(8,128)(2,1)S(1)}, bf16[2,2,24,768]{3,2,0,1:T(8,128)(2,1)S(1)}, u32[]{:S(2)}, u32[]{:S(2)}) collective-permute-start(bf16[2,2,24,768]{3,2,0,1:T(8,128)(2,1)S(1)} %get-tuple-element.246), channel_id=1, source_target_pairs={{0,8},{4,12},{8,0},{12,4},{16,24},{20,28},{24,16},{28,20},{1,9},{5... | collective-permute-start | bytes 442376 | tf_op jit(solution)/shard_map/ppermute | solution.py:727
  397.9 26.5 %collective-permute-start.58 = (bf16[2,96,768]{2,1,0:T(8,128)(2,1)}, bf16[2,96,768]{2,1,0:T(8,128)(2,1)}, u32[]{:S(2)}, u32[]{:S(2)}) collective-permute-start(bf16[2,96,768]{2,1,0:T(8,128)(2,1)} %get-tuple-element.226), channel_id=1, source_target_pairs={{0,8},{4,12},{8,0},{12,4},{16,24},{20,28},{24,16},{28,20},{1,9},{5... | collective-permute-start | bytes 884744 | tf_op jit(solution)/shard_map/ppermute | solution.py:727
  399.2 27.7 %collective-permute-start.52 = (bf16[2,96,768]{2,1,0:T(8,128)(2,1)}, bf16[2,96,768]{2,1,0:T(8,128)(2,1)}, u32[]{:S(2)}, u32[]{:S(2)}) collective-permute-start(bf16[2,96,768]{2,1,0:T(8,128)(2,1)} %get-tuple-element.224), channel_id=1, source_target_pairs={{0,8},{4,12},{8,0},{12,4},{16,24},{20,28},{24,16},{28,20},{1,9},{5... | collective-permute-start | bytes 884744 | tf_op jit(solution)/shard_map/ppermute | solution.py:727
  417.9 12.9 %collective-permute-start.21 = (bf16[2,2,2,24,768]{4,3,0,2,1:T(8,128)(2,1)}, bf16[2,2,2,24,768]{4,3,0,2,1:T(8,128)(2,1)}, u32[]{:S(2)}, u32[]{:S(2)}) collective-permute-start(bf16[2,2,2,24,768]{4,3,0,2,1:T(8,128)(2,1)} %get-tuple-element.236), channel_id=1, source_target_pairs={{0,2},{1,3},{2,0},{3,1},{4,6},{5,7},{6,4},{7,5},{8,10},{9,11},{10,... | collective-permute-start | bytes 884744 | tf_op jit(solution)/shard_map/ppermute | solution.py:642
  424.4 30.8 %collective-permute-start.45 = (bf16[4,2,2,24,768]{4,3,2,1,0:T(8,128)(2,1)}, bf16[4,2,2,24,768]{4,3,2,1,0:T(8,128)(2,1)}, u32[]{:S(2)}, u32[]{:S(2)}) collective-permute-start(bf16[4,2,2,24,768]{4,3,2,1,0:T(8,128)(2,1)} %fusion.11), channel_id=1, source_target_pairs={{0,4},{4,0},{8,12},{12,8},{16,20},{20,16},{24,28},{28,24},{1,5},{5... | collective-permute-start | bytes 1769480 | tf_op jit(solution)/shard_map/ppermute | solution.py:727
  (140 other events, 847.0 us)

commit v2 on v1

v2 whole, which is shorter than its diff:
```python
import functools

import jax
import jax.numpy as jnp
import numpy as np
from jax import lax
from jax.experimental import pallas as pl
from jax.experimental.pallas import tpu as pltpu
from jax.sharding import PartitionSpec as P

RADIUS = 3
SPAN = 2 * RADIUS + 1
PAD = 8
EPS = 1e-06
MASKED = -1e30
BF = jnp.bfloat16
F32 = jnp.float32
MIB = 1 << 20


def dot(a, b):
    return lax.dot_general(a, b, (((1,), (0,)), ((), ())), preferred_element_type=F32)


def dot_nt(a, b):
    return lax.dot_general(a, b, (((1,), (1,)), ((), ())), preferred_element_type=F32)


def dot_tn(a, b):
    return lax.dot_general(a, b, (((0,), (0,)), ((), ())), preferred_element_type=F32)


def normalized(x):
    centred = x - jnp.mean(x, axis=-1, keepdims=True)
    inverse = lax.rsqrt(jnp.mean(centred * centred, axis=-1, keepdims=True) + EPS)
    return centred * inverse, inverse


def norm_back(x, gain, d_out):
    unit, inverse = normalized(x)
    d_unit = d_out * gain
    d_x = inverse * (
        d_unit
        - jnp.mean(d_unit, axis=-1, keepdims=True)
        - unit * jnp.mean(d_unit * unit, axis=-1, keepdims=True)
    )
    return d_x, d_out * unit


def split3(x):
    high = x.astype(BF).astype(F32)
    rest = x - high
    middle = rest.astype(BF).astype(F32)
    return high, middle, rest - middle


def lane_heads(rows, lanes, width):
    return lax.broadcasted_iota(jnp.int32, (rows, lanes), 1) // width


def head_rows(rows, lanes, width):
    return lane_heads(rows, lanes, width) == lax.broadcasted_iota(jnp.int32, (rows, lanes), 0)


def stacked_heads(block, width):
    rows, lanes = block.shape
    heads = lane_heads(rows, lanes, width)
    zero = jnp.zeros_like(block)
    return jnp.concatenate(
        [jnp.where(heads == h, block, zero) for h in range(lanes // width)], axis=0
    )


def folded_heads(stack, width):
    count = stack.shape[1] // width
    rows = stack.shape[0] // count
    heads = lane_heads(rows, stack.shape[1], width)
    out = stack[:rows]
    for h in range(1, count):
        out = jnp.where(heads == h, stack[h * rows : (h + 1) * rows], out)
    return out


def keep_rows(rows, cells, class_weight):
    row = lax.broadcasted_iota(jnp.int32, (rows, 1), 0)
    return jnp.where(row < cells, 1.0, jnp.where(row == cells, class_weight, 0.0))


class Sizes:
    def __init__(self, side, width, hidden, heads, devices):
        self.side = side
        self.cells = side * side
        self.rows = self.cells + 16
        self.width = width
        self.hidden = hidden
        self.heads = heads
        self.head = width // heads
        self.pitch = side + PAD
        self.ext = side + 2 * RADIUS
        self.ext_rows = self.pitch * self.ext + PAD
        self.brows = 4
        self.blocks = side // self.brows
        self.bq = self.brows * side
        self.bk = 256
        self.class_slot = self.bk - PAD
        self.quad = 4 * self.head
        self.groups = width // self.quad
        self.devices = devices
        self.bits = devices.bit_length() - 1


def stat_rows(values):
    width = values[0].shape[1]
    parts = [split3(v) for v in values]
    flat = [p[k] for k in range(3) for p in parts]
    if len(flat) % 2:
        flat.append(jnp.zeros_like(flat[0]))
    row = lax.broadcasted_iota(jnp.int32, (16, 2 * width), 0)
    out = jnp.zeros((16, 2 * width), F32)
    for i in range(0, len(flat), 2):
        out = jnp.where(row == i // 2, jnp.concatenate(flat[i : i + 2], axis=1), out)
    return out.astype(BF)


def read_stats(block, count, width):
    rows = block.astype(F32)

    def piece(i):
        return rows[i // 2 : i // 2 + 1, (i % 2) * width : (i % 2 + 1) * width]

    return [piece(i) + piece(count + i) + piece(2 * count + i) for i in range(count)]


def in_tile_order(info, pieces):
    me = info[0] * 2 + info[1]
    out = []
    for t in range(4):
        d = me ^ t
        out.append(
            [
                jnp.where(d == 0, a, jnp.where(d == 1, b, jnp.where(d == 2, c, e)))
                for a, b, c, e in zip(*pieces)
            ]
        )
    return out


def class_scores(sz, info, qkv_ref, mask):
    cells, width = sz.cells, sz.width
    own = head_rows(16, width, sz.head)
    class_rows = qkv_ref[cells : cells + 16, :].astype(F32)
    q_c, k_c, v_c = (class_rows[0:1, i * width : (i + 1) * width] for i in range(3))
    q_heads = jnp.where(own, q_c, 0.0)
    scale = sz.head ** (-0.5)
    scores = dot_nt(q_heads.astype(BF), qkv_ref[0:cells, width : 2 * width]) * scale + mask
    self_score = jnp.sum(q_heads * k_c, axis=1, keepdims=True) * scale
    self_score = jnp.where(info[2] == 1, self_score, MASKED)
    return own, q_heads, k_c, v_c, scores, self_score


def send_rims(sz, info, kv_half, kv_edge_rows, stats, pc_ref, pr_ref, pd_ref):
    side, width = sz.side, sz.width
    cells8 = [kv_half(r) for r in range(side)]
    pc_ref[0 : side * PAD, :] = jnp.concatenate(cells8, axis=0).astype(BF)
    pc_ref[side * PAD : side * PAD + 16, :] = stats
    edge, corner = kv_edge_rows()
    pr_ref[0 : RADIUS * side, :] = jnp.concatenate(edge, axis=0).astype(BF)
    pr_ref[RADIUS * side : RADIUS * side + 16, :] = stats
    zero = jnp.zeros((PAD, 2 * width), F32)
    pd_ref[0 : (RADIUS + 1) * PAD, :] = jnp.concatenate(corner + [zero], axis=0).astype(BF)
    pd_ref[(RADIUS + 1) * PAD : (RADIUS + 1) * PAD + 16, :] = stats


def rim_places(sz, info):
    return sz.pitch * (1 - info[1]), (sz.side + RADIUS) * (1 - info[0])


GELU_C = float(np.sqrt(2.0 / np.pi))


class Copies:
    def __init__(self, sems):
        self.sems, self.count, self.out = sems, 0, []

    def load(self, src, dst):
        copy = pltpu.make_async_copy(src, dst, self.sems.at[self.count])
        self.count += 1
        copy.start()
        return copy

    def store(self, src, dst):
        self.out.append(self.load(src, dst))

    def finish(self):
        for copy in self.out:
            copy.wait()


def qkv_part(sz, info, x, gain, wq, loads, mask, h_ref, qkv_ref, pc_ref, pr_ref, pd_ref):
    width, side, cells = sz.width, sz.side, sz.cells
    unit, _ = normalized(x)
    h = (unit * gain).astype(BF)
    h_ref[...] = h
    for i in range(3):
        loads[i].wait()
        cols = slice(i * width, (i + 1) * width)
        qkv_ref[:, cols] = dot(h, wq[:, cols]).astype(BF)
    own, q_heads, k_c, v_c, scores, self_score = class_scores(sz, info, qkv_ref, mask)
    top = jnp.maximum(jnp.max(scores, axis=1, keepdims=True), self_score)
    probs = jnp.where(mask > -1.0, jnp.exp(scores - top), 0.0)
    self_prob = jnp.where(info[2] == 1, jnp.exp(self_score - top), 0.0)
    total = jnp.sum(probs, axis=1, keepdims=True) + self_prob
    part = dot(probs.astype(BF), qkv_ref[0:cells, 2 * width :]) + self_prob * v_c

    def to_row(v):
        return jnp.sum(jnp.where(own, v, 0.0), axis=0, keepdims=True)

    stats = stat_rows([to_row(part), to_row(top), to_row(total)])
    left_col = info[1] == 0

    def half(r):
        row = qkv_ref[r * side : (r + 1) * side, width:].astype(F32)
        return jnp.where(left_col, row[PAD:], row[:PAD])

    def edges():
        first = pl.multiple_of((1 - info[0]) * (side - RADIUS) * side, 16)
        rows = qkv_ref[pl.ds(first, RADIUS * side), width:].astype(F32)
        edge = [rows[t * side : (t + 1) * side] for t in range(RADIUS)]
        return edge, [jnp.where(left_col, e[PAD:], e[:PAD]) for e in edge]

    send_rims(sz, info, half, edges, stats, pc_ref, pr_ref, pd_ref)


def first_kernel(sz, info, patch_ref, cls_ref, gain_ref, mask_ref, w_any,
                 x_ref, qkv_ref, pc_ref, pr_ref, pd_ref, h_v, wq, sems):
    copies = Copies(sems)
    width = sz.width
    loads = [copies.load(w_any.at[0, :, pl.ds(i * width, width)], wq.at[:, pl.ds(i * width, width)]) for i in range(3)]
    row = lax.broadcasted_iota(jnp.int32, (16, width), 0)
    x_ref[0 : sz.cells, :] = patch_ref[...].astype(F32)
    x_ref[sz.cells :, :] = jnp.where(row == 0, cls_ref[...].astype(F32), 0.0)
    qkv_part(sz, info, x_ref[...], gain_ref[0:1, :], wq, loads, mask_ref[0:1, :], h_v, qkv_ref, pc_ref, pr_ref, pd_ref)


def extended(sz, info, qkv_ref, rc_ref, rr_ref, rd_ref, kext, vext):
    width, side, pitch = sz.width, sz.side, sz.pitch
    beside, above = rim_places(sz, info)
    for ext, lo in ((kext, width), (vext, 2 * width)):
        at = lo - width
        ext[...] = jnp.zeros_like(ext)
        for r in range(side):
            base = pitch * (r + RADIUS)
            ext[base + PAD : base + PAD + side, :] = qkv_ref[r * side : (r + 1) * side, lo : lo + width].astype(F32)
        sides = rc_ref[0 : side * PAD, at : at + width].astype(F32)
        for r in range(side):
            ext[pl.ds(pl.multiple_of(pitch * (r + RADIUS) + beside, 8), PAD), :] = sides[r * PAD : (r + 1) * PAD]
        edge = rr_ref[0 : RADIUS * side, at : at + width].astype(F32)
        corner = rd_ref[0 : (RADIUS + 1) * PAD, at : at + width].astype(F32)
        for t in range(RADIUS):
            base = pitch * (above + t)
            ext[pl.ds(pl.multiple_of(base + PAD, 8), side), :] = edge[t * side : (t + 1) * side]
            ext[pl.ds(pl.multiple_of(base + beside, 8), PAD), :] = corner[t * PAD : (t + 1) * PAD]


def all_stats(sz, info, st_ref, rc_ref, rr_ref, rd_ref):
    side, width = sz.side, sz.width
    return in_tile_order(info, [read_stats(r, 3, width) for r in (
        st_ref[...],
        rc_ref[side * PAD : side * PAD + 16, :],
        rr_ref[RADIUS * side : RADIUS * side + 16, :],
        rd_ref[(RADIUS + 1) * PAD : (RADIUS + 1) * PAD + 16, :],
    )])


def middle_kernel(sz, layer, last, info, *refs):
    refs = list(refs)

    def take(n):
        out = refs[:n]
        del refs[:n]
        return out

    (qkv_ref, st_ref, rc_ref, rr_ref, rd_ref, bias_ref, mask_ref, x_ref, own_mask_ref,
     scale_a_ref, gain_m_ref, scale_m_ref, gain_a_ref) = take(13)
    out_w, up_w, down_w = take(3)
    if last:
        cot_ref, cls_cot_ref, valid_ref = take(3)
    else:
        (qkv_w,) = take(1)
    p_out, kb_out, vb_out, slope_out, x1_out, br_out, down_out, left_out, stat_ref = take(9)
    if last:
        po_ref, co_ref, right_out, g1_ref, vec_ref = take(5)
    else:
        x2_ref, next_ref, pc_ref, pr_ref, pd_ref = take(5)
    (kext, vext, w_out, w_up, w_down, p_v, kb_v, vb_v, slope_v, x1_v, br_v, down_v, att, h2_v, act_v, acc) = take(16)
    if last:
        ed_v, eu_v, eb_v = take(3)
    else:
        w_qkv, h_v = take(2)
    if layer == 0:
        (first_v,) = take(1)
    (sems,) = take(1)
    width, side, cells, pitch, hidden = sz.width, sz.side, sz.cells, sz.pitch, sz.hidden
    chunks = hidden // width
    copies = Copies(sems)
    out_load = copies.load(out_w.at[layer], w_out)
    up_loads, down_loads = [], []
    for c in range(chunks):
        at = pl.ds(c * width, width)
        up_loads.append(copies.load(up_w.at[layer, :, at], w_up.at[:, at]))
        down_loads.append(copies.load(down_w.at[layer, at, :], w_down.at[at, :]))
    if not last:
        qkv_loads = [
            copies.load(qkv_w.at[layer + 1, :, pl.ds(i * width, width)], w_qkv.at[:, pl.ds(i * width, width)])
            for i in range(3)
        ]
    extended(sz, info, qkv_ref, rc_ref, rr_ref, rd_ref, kext, vext)
    if layer == 0:
        first_v[...] = (normalized(x_ref[...])[0] * gain_a_ref[0:1, :]).astype(BF)
        copies.store(first_v, left_out.at[:, pl.ds(left_out.shape[1] - width, width)])
    class_rows = qkv_ref[cells : cells + 16, :].astype(F32)[0:PAD]
    scale = sz.head ** (-0.5)
    for b in range(sz.blocks):
        first = b * sz.brows * pitch
        kb = jnp.concatenate([kext[first : first + sz.class_slot, :], class_rows[:, width : 2 * width]], axis=0).astype(BF)
        vb = jnp.concatenate([vext[first : first + sz.class_slot, :], class_rows[:, 2 * width :]], axis=0).astype(BF)
        kb_v[b] = kb
        vb_v[b] = vb
        q = qkv_ref[b * sz.bq : (b + 1) * sz.bq, 0:width] * jnp.asarray(scale, BF)
        mask = mask_ref[b]
        mask = jnp.concatenate([mask, mask], axis=1)
        for g in range(sz.groups):
            lanes = slice(g * sz.quad, (g + 1) * sz.quad)
            scores = dot_nt(kb[:, lanes], stacked_heads(q[:, lanes], sz.head)) + bias_ref[g] + mask
            top = jnp.max(scores, axis=0, keepdims=True)
            probs = jnp.exp(scores - top)
            total = jnp.sum(probs, axis=0, keepdims=True)
            probs = (probs * (1.0 / total)).astype(BF)
            p_v[b * sz.groups + g] = probs
            out = folded_heads(dot_tn(probs, vb[:, lanes]), sz.head)
            att[b * sz.bq : (b + 1) * sz.bq, lanes] = out.astype(BF)
    copies.store(kb_v, kb_out)
    copies.store(vb_v, vb_out)
    copies.store(p_v, p_out)
    ordered = all_stats(sz, info, st_ref, rc_ref, rr_ref, rd_ref)
    top = functools.reduce(jnp.maximum, [s[1] for s in ordered])
    total = jnp.zeros_like(top)
    summed = jnp.zeros_like(top)
    for part, part_top, part_total in ordered:
        factor = jnp.exp(part_top - top)
        total = total + part_total * factor
        summed = summed + part * factor
    class_out = summed / total
    stat_ref[...] = jnp.zeros_like(stat_ref)
    stat_ref[0:1, :] = top
    stat_ref[1:2, :] = total
    stat_ref[2:3, :] = class_out
    row = lax.broadcasted_iota(jnp.int32, (16, width), 0)
    att[cells : cells + 16, :] = jnp.where(row == 0, class_out, 0.0).astype(BF)
    copies.store(att, left_out.at[:, pl.ds(0, width)])
    out_load.wait()
    branch = dot(att[...], w_out[...])
    br_v[...] = branch.astype(BF)
    x1_v[...] = x_ref[...] + scale_a_ref[layer : layer + 1, :] * branch
    copies.store(br_v, br_out)
    copies.store(x1_v, x1_out)
    unit, _ = normalized(x1_v[...])
    h2_v[...] = (unit * gain_m_ref[layer : layer + 1, :]).astype(BF)
    copies.store(h2_v, left_out.at[:, pl.ds(width, width)])
    for c in range(chunks):
        at = slice(c * width, (c + 1) * width)
        up_loads[c].wait()
        u = dot(h2_v[...], w_up[:, at])
        square = u * u
        th = jnp.tanh(GELU_C * u * (1.0 + 0.044715 * square))
        half = 0.5 * (1.0 + th)
        act_v[:, at] = (u * half).astype(BF)
        slope = half + (0.5 * u) * (1.0 - th * th) * (GELU_C + (3 * 0.044715 * GELU_C) * square)
        slope_v[:, at] = slope.astype(BF)
        down_loads[c].wait()
        part = dot(act_v[:, at], w_down[at, :])
        if c == 0:
            acc[...] = part
        else:
            acc[...] += part
    copies.store(act_v, left_out.at[:, pl.ds(2 * width, hidden)])
    copies.store(slope_v, slope_out)
    down_v[...] = acc[...].astype(BF)
    copies.store(down_v, down_out)
    x2 = x1_v[...] + scale_m_ref[layer : layer + 1, :] * acc[...]
    if last:
        po_ref[...] = (x2[0:cells] * valid_ref[...]).astype(BF)
        co_ref[...] = x2[cells : cells + 1].astype(BF)
        g_cells = cot_ref[...].astype(F32) * valid_ref[...]
        g_class = jnp.where(row == 0, cls_cot_ref[...].astype(F32), 0.0)
        g = jnp.concatenate([g_cells, g_class], axis=0)
        keep = keep_rows(sz.rows, cells, jnp.where(info[2] == 1, 1.0, 0.0))
        vec_ref[...] = jnp.zeros_like(vec_ref)
        mlp_back_part(sz, layer, g, acc[...], keep, ed_v, eu_v, eb_v, right_out, 0, g1_ref, vec_ref, x1_v, br_v, slope_v,
                      w_up, w_down, None, None, gain_m_ref, scale_a_ref, scale_m_ref, acc, copies)
    else:
        x2_ref[...] = x2
        qkv_part(sz, info, x2, gain_a_ref[layer + 1 : layer + 2, :], w_qkv, qkv_loads, own_mask_ref[0:1, :],
                 h_v, next_ref, pc_ref, pr_ref, pd_ref)
        copies.store(h_v, left_out.at[:, pl.ds(2 * width + hidden, width)])
    copies.finish()


def mlp_back_part(sz, layer, g, down, keep, ed_ref, eu_v, eb_ref, right_out, at0, g1_ref, vec_ref, x1_ref, br_ref, slope_ref,
                  w_up, w_down, up_loads, down_loads, gain_m_ref, scale_a_ref, scale_m_ref, acc, copies):
    width = sz.width
    vec_ref[0:1, :] = jnp.sum(keep * g * down, axis=0, keepdims=True)
    e_down = (scale_m_ref[layer : layer + 1, :] * g).astype(BF)
    ed_ref[...] = e_down
    copies.store(ed_ref, right_out.at[:, pl.ds(at0, width)])
    g1_ref[...] = g
    for c in range(sz.hidden // width):
        at = slice(c * width, (c + 1) * width)
        if down_loads is not None:
            for copy in down_loads[c]:
                copy.wait()
        e_up = (dot_nt(ed_ref[...], w_down[at, :]) * slope_ref[:, at].astype(F32)).astype(BF)
        eu_v[:, at] = e_up
        if up_loads is not None:
            up_loads[c].wait()
        part = dot_nt(eu_v[:, at], w_up[:, at])
        if c == 0:
            acc[...] = part
        else:
            acc[...] += part
    copies.store(eu_v, right_out.at[:, pl.ds(at0 + width, sz.hidden)])
    d_x1, gain_rows = norm_back(x1_ref[...], gain_m_ref[layer : layer + 1, :], acc[...])
    vec_ref[1:2, :] = jnp.sum(keep * gain_rows, axis=0, keepdims=True)
    g1 = g1_ref[...] + d_x1
    g1_ref[...] = g1
    eb_ref[...] = (scale_a_ref[layer : layer + 1, :] * g1).astype(BF)
    copies.store(eb_ref, right_out.at[:, pl.ds(at0 + width + sz.hidden, width)])
    vec_ref[2:3, :] = jnp.sum(keep * g1 * br_ref[...].astype(F32), axis=0, keepdims=True)


def attention_back_kernel(sz, layer, info, eb_ref, qkv_ref, stat_ref, own_mask_ref, w_any, p_any, kb_any, vb_any,
                          dq_ref, dkv_ref, pc_ref, pr_ref, pd_ref, tab_ref,
                          kext, vext, d_o, tab, w, p_v, kb_v, vb_v, sems):
    width, side, cells, pitch = sz.width, sz.side, sz.cells, sz.pitch
    scale = sz.head ** (-0.5)
    copies = Copies(sems)
    w_load = copies.load(w_any.at[layer], w)
    loads = []
    for b in range(sz.blocks):
        at = pl.ds(b * sz.groups, sz.groups)
        loads.append([
            copies.load(vb_any.at[b], vb_v.at[b]),
            copies.load(p_any.at[at], p_v.at[at]),
            copies.load(kb_any.at[b], kb_v.at[b]),
        ])
    kext[...] = jnp.zeros_like(kext)
    vext[...] = jnp.zeros_like(vext)
    w_load.wait()
    d_o[...] = dot_nt(eb_ref[...], w[...])
    class_k = [jnp.zeros((PAD, sz.quad), F32) for _ in range(sz.groups)]
    class_v = [jnp.zeros((PAD, sz.quad), F32) for _ in range(sz.groups)]
    for b in range(sz.blocks):
        for copy in loads[b]:
            copy.wait()
        first = b * sz.brows * pitch
        q = qkv_ref[b * sz.bq : (b + 1) * sz.bq, 0:width] * jnp.asarray(scale, BF)
        do = d_o[b * sz.bq : (b + 1) * sz.bq, :].astype(BF)
        for g in range(sz.groups):
            lanes = slice(g * sz.quad, (g + 1) * sz.quad)
            do_stack = stacked_heads(do[:, lanes], sz.head)
            q_stack = stacked_heads(q[:, lanes], sz.head)
            probs = p_v[b * sz.groups + g]
            wide = probs.astype(F32)
            d_prob = dot_nt(vb_v[b, :, lanes], do_stack)
            delta = jnp.sum(wide * d_prob, axis=0, keepdims=True)
            d_score = wide * (d_prob - delta)
            if b == 0:
                tab[g] = d_score
            else:
                tab[g] += d_score
            low = d_score.astype(BF)
            d_v = dot(probs, do_stack)
            d_k = dot(low, q_stack)
            vext[first : first + sz.class_slot, lanes] += d_v[: sz.class_slot]
            kext[first : first + sz.class_slot, lanes] += d_k[: sz.class_slot]
            class_v[g] = class_v[g] + d_v[sz.class_slot :]
            class_k[g] = class_k[g] + d_k[sz.class_slot :]
            d_q = folded_heads(dot_tn(low, kb_v[b, :, lanes]), sz.head) * scale
            dq_ref[b * sz.bq : (b + 1) * sz.bq, lanes] = d_q.astype(BF)
    mask = own_mask_ref[0:1, :]
    own, q_heads, k_c, v_c, scores, self_score = class_scores(sz, info, qkv_ref, mask)
    top = jnp.max(jnp.where(own, stat_ref[0:1, :], MASKED), axis=1, keepdims=True)
    total = jnp.max(jnp.where(own, stat_ref[1:2, :], 0.0), axis=1, keepdims=True)
    real = lax.broadcasted_iota(jnp.int32, (16, 1), 0) < sz.heads
    probs = jnp.where((mask > -1.0) & real, jnp.exp(scores - top) / total, 0.0)
    self_prob = jnp.where((info[2] == 1) & real, jnp.exp(self_score - top) / total, 0.0)
    d_class = jnp.where(own, d_o[cells : cells + 1, :], 0.0)
    delta = jnp.sum(d_class * stat_ref[2:3, :], axis=1, keepdims=True)
    d_low = d_class.astype(BF)
    d_cell = probs * (dot_nt(d_low, qkv_ref[0:cells, 2 * width :]) - delta)
    d_cell_low = d_cell.astype(BF)
    d_self = self_prob * (jnp.sum(d_class * v_c, axis=1, keepdims=True) - delta)

    def to_row(v):
        return jnp.sum(jnp.where(own, v, 0.0), axis=0, keepdims=True)

    g_q = to_row(dot(d_cell_low, qkv_ref[0:cells, width : 2 * width]) + d_self * k_c) * scale
    g_k = to_row(d_self * q_heads) * scale + jnp.concatenate([c[0:1] for c in class_k], axis=1)
    g_v = to_row(self_prob * d_class) + jnp.concatenate([c[0:1] for c in class_v], axis=1)
    add_k = dot_tn(d_cell_low, q_heads.astype(BF)) * scale
    add_v = dot_tn(probs.astype(BF), d_low)
    beside, above = rim_places(sz, info)
    for r in range(side):
        base = pitch * (r + RADIUS) + PAD
        rows = slice(r * side, (r + 1) * side)
        dkv_ref[rows, 0:width] = kext[base : base + side, :] + add_k[rows]
        dkv_ref[rows, width:] = vext[base : base + side, :] + add_v[rows]

    def pair(at, count):
        at = pl.ds(pl.multiple_of(at, 8), count)
        return jnp.concatenate([kext[at, :], vext[at, :]], axis=1)

    def edges():
        return (
            [pair(pitch * (above + t) + PAD, side) for t in range(RADIUS)],
            [pair(pitch * (above + t) + beside, PAD) for t in range(RADIUS)],
        )

    send_rims(sz, info, lambda r: pair(pitch * (r + RADIUS) + beside, PAD), edges,
              stat_rows([g_q, g_k, g_v]), pc_ref, pr_ref, pd_ref)
    per_head = sz.bq
    for g in range(sz.groups):
        turned = tab[g].T
        for h in range(4):
            total_h = jnp.zeros((side, sz.bk), F32)
            for r in range(sz.brows):
                at = h * per_head + r * side
                piece = turned[at : at + side]
                shift = (sz.bk - pitch * r) % sz.bk
                total_h = total_h + (pltpu.roll(piece, shift, 1) if shift else piece)
            tab_row = jnp.zeros((1, sz.bk), F32)
            for c in range(side):
                one = total_h[c : c + 1]
                tab_row = tab_row + (pltpu.roll(one, sz.bk - c, 1) if c else one)
            tab_ref[4 * g + h : 4 * g + h + 1, :] = tab_row
    tab_ref[sz.heads : 16, :] = jnp.zeros((16 - sz.heads, sz.bk), F32)


def qkv_back_part(sz, info, dq_ref, dkv_ref, st_ref, rc_ref, rr_ref, rd_ref, x_ref, gain, g1_ref, eq_ref, dkv, acc, wq, loads):
    width, side, cells = sz.width, sz.side, sz.cells
    dkv[...] = dkv_ref[...]
    beside = PAD * (1 - info[1])
    edge = (1 - info[0]) * (side - RADIUS) * side
    sides = rc_ref[0 : side * PAD, :].astype(F32)
    for r in range(side):
        dkv[pl.ds(pl.multiple_of(r * side + beside, 8), PAD), :] += sides[r * PAD : (r + 1) * PAD]
    dkv[pl.ds(pl.multiple_of(edge, 8), RADIUS * side), :] += rr_ref[0 : RADIUS * side, :].astype(F32)
    corner = rd_ref[0 : (RADIUS + 1) * PAD, :].astype(F32)
    for t in range(RADIUS):
        dkv[pl.ds(pl.multiple_of(edge + t * side + beside, 8), PAD), :] += corner[t * PAD : (t + 1) * PAD]
    ordered = all_stats(sz, info, st_ref, rc_ref, rr_ref, rd_ref)
    class_row = jnp.concatenate(
        [functools.reduce(lambda a, b: a + b, [o[i] for o in ordered]) for i in range(3)], axis=1
    )
    row = lax.broadcasted_iota(jnp.int32, (16, 3 * width), 0)
    eq_ref[0:cells, 0:width] = dq_ref[...]
    eq_ref[0:cells, width:] = dkv[...].astype(BF)
    eq_ref[cells : cells + 16, :] = jnp.where(row == 0, class_row, 0.0).astype(BF)
    for i in range(3):
        cols = slice(i * width, (i + 1) * width)
        loads[i].wait()
        part = dot_nt(eq_ref[:, cols], wq[:, cols])
        if i == 0:
            acc[...] = part
        else:
            acc[...] += part
    d_x, gain_rows = norm_back(x_ref[...], gain, acc[...])
    return g1_ref[...] + d_x, gain_rows


def small_rows(sz, small_ref, vec_ref, tab_ref, gain_sum):
    small_ref[...] = jnp.zeros_like(small_ref)
    small_ref[0:3, :] = vec_ref[0:3, :]
    small_ref[3:4, :] = gain_sum
    small_ref[8:24, 0 : sz.bk] = tab_ref[...]


def qkv_back_kernel(sz, layer, info, dq_ref, dkv_ref, st_ref, rc_ref, rr_ref, rd_ref, x_ref, g1_ref, vec_ref, tab_ref,
                    gain_a_ref, qkv_w, eq_ref, ek_ref, ev_ref, small_ref, g_ref, dkv, acc, wq, eq_v, sems):
    width = sz.width
    copies = Copies(sems)
    loads = [copies.load(qkv_w.at[layer, :, pl.ds(i * width, width)], wq.at[:, pl.ds(i * width, width)]) for i in range(3)]
    g, gain_rows = qkv_back_part(sz, info, dq_ref, dkv_ref, st_ref, rc_ref, rr_ref, rd_ref, x_ref,
                                 gain_a_ref[layer : layer + 1, :], g1_ref, eq_v, dkv, acc, wq, loads)
    for i, ref in enumerate((eq_ref, ek_ref, ev_ref)):
        ref[...] = eq_v[:, i * width : (i + 1) * width]
    keep = keep_rows(sz.rows, sz.cells, jnp.where(info[2] == 1, 1.0, 0.0))
    small_rows(sz, small_ref, vec_ref, tab_ref, jnp.sum(keep * gain_rows, axis=0, keepdims=True))
    g_ref[...] = g


def mlp_back_kernel(sz, layer, info, g_ref, gain_m_ref, scale_a_ref, scale_m_ref, x1_ref, br_ref, down_ref,
                    up_w, down_w, slope_any, right_out, g1_out, vec_out, acc, w_up, w_down, slope_v, ed_v, eu_v, eb_v, sems):
    width = sz.width
    copies = Copies(sems)
    up_loads, down_loads, slope_loads = [], [], []
    for c in range(sz.hidden // width):
        at = pl.ds(c * width, width)
        down_loads.append(copies.load(down_w.at[layer, at, :], w_down.at[at, :]))
        slope_loads.append(copies.load(slope_any.at[:, at], slope_v.at[:, at]))
        up_loads.append(copies.load(up_w.at[layer, :, at], w_up.at[:, at]))
    keep = keep_rows(sz.rows, sz.cells, jnp.where(info[2] == 1, 1.0, 0.0))
    vec_out[...] = jnp.zeros_like(vec_out)
    mlp_back_part(sz, layer, g_ref[...], down_ref[...].astype(F32), keep, ed_v, eu_v, eb_v, right_out, 0, g1_out, vec_out,
                  x1_ref, br_ref, slope_v, w_up, w_down, up_loads, [(a, b) for a, b in zip(down_loads, slope_loads)],
                  gain_m_ref, scale_a_ref, scale_m_ref, acc, copies)
    copies.finish()


def last_kernel(sz, info, dq_ref, dkv_ref, st_ref, rc_ref, rr_ref, rd_ref, x_ref, g1_ref, vec_ref, tab_ref, gain_a_ref, qkv_w,
                eq_ref, ek_ref, ev_ref, small_ref, pg_ref, cg_ref, dkv, acc, wq, eq_v, sems):
    width = sz.width
    copies = Copies(sems)
    loads = [copies.load(qkv_w.at[0, :, pl.ds(i * width, width)], wq.at[:, pl.ds(i * width, width)]) for i in range(3)]
    g, gain_rows = qkv_back_part(sz, info, dq_ref, dkv_ref, st_ref, rc_ref, rr_ref, rd_ref, x_ref,
                                 gain_a_ref[0:1, :], g1_ref, eq_v, dkv, acc, wq, loads)
    for i, ref in enumerate((eq_ref, ek_ref, ev_ref)):
        ref[...] = eq_v[:, i * width : (i + 1) * width]
    keep = keep_rows(sz.rows, sz.cells, jnp.where(info[2] == 1, 1.0, 0.0))
    small_rows(sz, small_ref, vec_ref, tab_ref, jnp.sum(keep * gain_rows, axis=0, keepdims=True))
    pg_ref[...] = g[0 : sz.cells]
    cg_ref[...] = g[sz.cells : sz.cells + 1]


def product(sz, info, left_ref, left_got, own_ref, other_ref):
    cells = sz.cells
    row = lax.broadcasted_iota(jnp.int32, (16, own_ref.shape[1]), 0)
    tail = own_ref[cells : cells + 16, :]
    tail = jnp.where((row < 0) | (info[0] == 0), tail, jnp.zeros_like(tail))
    left = jnp.concatenate([left_ref[0:cells, :], left_got[0:cells, :], left_ref[cells : cells + 16, :]], axis=0)
    right = jnp.concatenate([own_ref[0:cells, :], other_ref[0:cells, :], tail], axis=0)
    return dot_tn(left, right)


def store_pieces(value, count, pairs, bit, place, send_ref, keep_ref):
    per = value.shape[0] // count
    for a, b in pairs:
        one, two = value[a * per : (a + 1) * per], value[b * per : (b + 1) * per]
        at = place(a)
        keep_ref[at] = jnp.where(bit == 0, one, two).astype(BF)
        send_ref[at] = jnp.where(bit == 0, two, one).astype(BF)


def pairs_of(bits, bit):
    return [(a, a | 1 << bit) for a in range(1 << bits) if not a >> bit & 1]


def place_of(bits, skip, me):
    def place(a):
        names = [b for b in range(bits - 1, -1, -1) if b != skip]
        at = 0
        for b in names:
            mine = (a >> b) & 1
            at = at * 2 + (mine if b == 0 else mine ^ ((me >> b) & 1))
        return at

    return place


def order_of(bits, skip, first):
    def place(a, me):
        names = [first] + [b for b in range(bits - 1, -1, -1) if b not in (skip, first)]
        at = 0
        for b in names:
            mine = (a >> b) & 1
            at = at * 2 + (mine if b == 0 else mine ^ ((me >> b) & 1))
        return at

    return place


def down_kernel(sz, info, act_ref, act_got, own_ref, other_ref, send_ref, keep_ref):
    bits = sz.bits - 2
    me = info[4]
    value = product(sz, info, act_ref, act_got, own_ref, other_ref)
    place = order_of(bits, 2, 1)
    store_pieces(value, 1 << bits, pairs_of(bits, 2), (me >> 2) & 1, lambda a: place(a, me), send_ref, keep_ref)


def columns_step(sz, info, outer, value, send_ref, keep_ref):
    bits = sz.bits - 1
    me = info[4]
    bit, other = (1, 2) if outer else (2, 1)
    place = order_of(bits, bit, other)
    store_pieces(value, 1 << bits, pairs_of(bits, bit), (me >> bit) & 1, lambda a: place(a, me), send_ref, keep_ref)


def up_kernel(sz, info, h_ref, h_got, own_ref, other_ref, send_ref, keep_ref):
    columns_step(sz, info, True, product(sz, info, h_ref, h_got, own_ref, other_ref), send_ref, keep_ref)


def attn_grad_kernel(sz, info, h_ref, h_got, qo, qg, ko, kg, vo, vg, a_ref, a_got, bo, bg, s0, k0, s1, k1):
    step = pl.program_id(0)

    @pl.when(step == 0)
    def _():
        columns_step(sz, info, True, product(sz, info, h_ref, h_got, qo, qg), s0, k0)

    @pl.when(step == 1)
    def _():
        columns_step(sz, info, True, product(sz, info, h_ref, h_got, ko, kg), s0, k0)

    @pl.when(step == 2)
    def _():
        columns_step(sz, info, False, product(sz, info, h_ref, h_got, vo, vg), s1, k1)

    @pl.when(step == 3)
    def _():
        columns_step(sz, info, False, product(sz, info, a_ref, a_got, bo, bg), s1, k1)


def plus(a, b):
    return a.astype(F32) + b.astype(F32)


def second_kernel(info, k0, g0, k1, g1, s0_ref, k0_ref, s1_ref, k1_ref):
    s0_ref[...] = plus(k0[:, 1], g0[:, 1]).astype(BF)
    k0_ref[...] = plus(k0[:, 0], g0[:, 0]).astype(BF)
    s1_ref[...] = plus(k1[:, 1], g1[:, 1]).astype(BF)
    k1_ref[...] = plus(k1[:, 0], g1[:, 0]).astype(BF)


def third_kernel(info, k0, g0, k1, g1, s_ref, k_ref):
    s_ref[0] = plus(k0[1], g0[1]).astype(BF)
    k_ref[0] = plus(k0[0], g0[0]).astype(BF)
    s_ref[1] = plus(k1[1], g1[1]).astype(BF)
    k_ref[1] = plus(k1[0], g1[0]).astype(BF)


def more_kernel(info, k, g, s_ref, k_ref):
    s_ref[...] = plus(k[:, 1], g[:, 1]).astype(BF)
    k_ref[...] = plus(k[:, 0], g[:, 0]).astype(BF)


def fourth_kernel(sz, info, k, g, a_ref, b_ref):
    high = (info[4] >> (sz.bits - 1)) & 1
    one, two = plus(k[:, 0], g[:, 0]), plus(k[:, 1], g[:, 1])
    a_ref[...] = jnp.where(high == 0, one, two).astype(BF)
    b_ref[...] = jnp.where(high == 0, two, one).astype(BF)


def bias_kernel(sz, table_ref, out_ref, wide):
    slot = lax.broadcasted_iota(jnp.int32, (sz.side, sz.bk), 1)
    for g in range(sz.groups):
        for h in range(4):
            line = jnp.broadcast_to(table_ref[4 * g + h : 4 * g + h + 1, :], (sz.side, sz.bk))
            line = pltpu.roll(line, 0, 1, stride=1, stride_axis=0)
            for r in range(sz.brows):
                piece = pltpu.roll(line, sz.pitch * r, 1) if r else line
                at = h * sz.bq + r * sz.side
                wide[at : at + sz.side, :] = jnp.where(slot == sz.class_slot, 0.0, piece)
        out_ref[g] = wide[...].T


def shape(dims, dtype):
    return jax.ShapeDtypeStruct(dims, dtype)


def kept(dims, dtype):
    return pltpu.HBM(dims, dtype)


def whole(dims):
    return pl.BlockSpec(dims, lambda *_: (0,) * len(dims))


ANY = pl.BlockSpec(memory_space=pl.ANY)
LONG = 10**11


def local(patch_in, cls_in, page_side, norm_attn, qkv_weight, rel_table, out_weight, scale_attn,
          norm_mlp, up_weight, down_weight, scale_mlp, patch_cot, cls_cot):
    tiles = lax.axis_size("tile")
    pages = lax.axis_size("dp")
    layers, heads = rel_table.shape[:2]
    sz = Sizes(patch_in.shape[2], patch_in.shape[4], up_weight.shape[2], heads, tiles * pages)
    side, cells, rows, width, hidden = sz.side, sz.cells, sz.rows, sz.width, sz.hidden
    chunks = hidden // width
    tile = lax.axis_index("tile")
    me = lax.axis_index("dp") * tiles + tile
    tile_row, tile_col = tile // 2, tile % 2
    page = page_side[0]
    bits = sz.bits
    top_bit, next_bit = bits - 1, bits - 2
    info = jnp.stack([tile_row, tile_col, (tile == 0).astype(jnp.int32), (me >> next_bit) & 1, me]).astype(jnp.int32)

    cell = np.arange(cells)
    own_ok = (tile_row * side + cell // side < page) & (tile_col * side + cell % side < page)
    own_mask = jnp.broadcast_to(jnp.where(own_ok, 0.0, MASKED).astype(F32), (8, cells))
    valid = own_ok.astype(F32)[:, None]
    slot = np.arange(sz.bk)[None] + np.arange(sz.blocks)[:, None] * sz.brows * sz.pitch - PAD + RADIUS
    key_row = tile_row * side + slot // sz.pitch - RADIUS
    key_col = tile_col * side + slot % sz.pitch - RADIUS
    is_class = (np.arange(sz.bk) == sz.class_slot)[None]
    key_ok = (key_row >= 0) & (key_row < page) & (key_col >= 0) & (key_col < page) | is_class
    key_mask = jnp.broadcast_to(
        jnp.where(key_ok, 0.0, MASKED).astype(F32)[:, :, None], (sz.blocks, sz.bk, sz.bk // 2)
    )
    lines = jnp.pad(rel_table.reshape(layers, heads, SPAN, SPAN), ((0, 0), (0, 16 - heads), (0, 0), (0, sz.pitch - SPAN)),
                    constant_values=MASKED).reshape(layers, 16, SPAN * sz.pitch)
    first_slot = PAD - RADIUS
    lines = jnp.pad(lines, ((0, 0), (0, 0), (first_slot, sz.bk - first_slot - SPAN * sz.pitch)), constant_values=MASKED)

    before = []

    def call(kernel, grid, in_specs, out_specs, out_shape, scratch=(), vmem=56, weight=1, also=()):
        deps = list(before) + list(also)
        count = len(in_specs)

        def body(*refs):
            return kernel(*refs[: 1 + count], *refs[1 + count + len(deps) :])

        run = pl.pallas_call(
            body,
            grid_spec=pltpu.PrefetchScalarGridSpec(
                num_scalar_prefetch=1,
                grid=grid,
                in_specs=list(in_specs) + [ANY] * len(deps),
                out_specs=out_specs,
                scratch_shapes=list(scratch),
            ),
            out_shape=out_shape,
            compiler_params=pltpu.CompilerParams(vmem_limit_bytes=vmem * MIB),
            cost_estimate=pl.CostEstimate(flops=weight, bytes_accessed=1, transcendentals=0),
        )

        def go(*args):
            pinned = [pltpu.with_memory_space_constraint(a, pltpu.HBM) for a in args]
            out = run(info, *pinned, *deps)
            before[:] = [out[-1] if isinstance(out, (list, tuple)) else out]
            return out

        return go

    def partner(value, x):
        return lax.ppermute(value, "tile", [(t, t ^ x) for t in range(tiles)])

    def exchange(rims):
        return [partner(v, x + 1) for x, v in enumerate(rims)]

    def swap(value, bit):
        if bit < 2:
            return partner(value, 1 << bit)
        return lax.ppermute(value, "dp", [(d, d ^ (1 << (bit - 2))) for d in range(pages)])

    def both(value):
        return value, partner(value, 1)

    def vm(dims, dtype):
        return pltpu.VMEM(dims, dtype)

    sems = pltpu.SemaphoreType.DMA((40,))
    row_w, par = whole((rows, width)), whole((layers, width))
    wide = whole((rows, 3 * width))
    pc_rows, pr_rows, pd_rows = side * PAD + 16, RADIUS * side + 16, (RADIUS + 1) * PAD + 16
    rim_shapes = [kept((n, 2 * width), BF) for n in (pc_rows, pr_rows, pd_rows)]
    rim_specs = [whole(s.shape) for s in rim_shapes]
    stat_spec = pl.BlockSpec((16, 2 * width), lambda *_: (side * PAD // 16, 0))
    nb, ng = sz.blocks, sz.groups
    square = (width, width)

    x, qkv, *rims = call(
        functools.partial(first_kernel, sz),
        (1,),
        [whole((cells, width)), whole((1, width)), par, whole((8, cells)), ANY],
        [row_w, wide] + rim_specs,
        [kept((rows, width), F32), kept((rows, 3 * width), BF)] + rim_shapes,
        [vm((rows, width), BF), vm((width, 3 * width), BF), sems],
    )(patch_in.reshape(cells, width), cls_in, norm_attn, own_mask, qkv_weight)
    got = exchange(rims)
    bias = call(
        lambda info, *refs: bias_kernel(sz, *refs),
        (layers,),
        [pl.BlockSpec((None, 16, sz.bk), lambda l, s: (l, 0, 0))],
        pl.BlockSpec((None, ng, sz.bk, sz.bk), lambda l, s: (l, 0, 0, 0)),
        kept((layers, ng, sz.bk, sz.bk), F32),
        [vm((sz.bk, sz.bk), F32)],
    )(lines)
    saved = []
    for l in range(layers):
        last = l == layers - 1
        ins = [wide, stat_spec] + rim_specs + [
            pl.BlockSpec((None, ng, sz.bk, sz.bk), lambda i, s, l=l: (l, 0, 0, 0)), whole(key_mask.shape), row_w,
            whole((8, cells)), par, par, par, par, ANY, ANY, ANY]
        args = [qkv, rims[0], *got, bias, key_mask, x, own_mask, scale_attn, norm_mlp, scale_mlp, norm_attn,
                out_weight, up_weight, down_weight]
        held = [((nb * ng, sz.bk, sz.bk), BF), ((nb, sz.bk, width), BF), ((nb, sz.bk, width), BF), ((rows, hidden), BF),
                ((rows, width), F32), ((rows, width), BF), ((rows, width), BF)]
        left_width = 2 * width + hidden + (0 if last else width) + (0 if l else width)
        scratch = [vm((sz.ext_rows, width), F32)] * 2 + [vm(square, BF), vm((width, hidden), BF), vm((hidden, width), BF)]
        scratch += [vm(d, t) for d, t in held]
        scratch += [vm((rows, width), BF), vm((rows, width), BF), vm((rows, hidden), BF), vm((rows, width), F32)]
        outs = [kept(d, t) for d, t in held] + [kept((rows, left_width), BF), kept((8, width), F32)]
        out_specs = [ANY] * (len(held) + 1) + [whole((8, width))]
        if last:
            ins += [whole((cells, width)), whole((1, width)), whole((cells, 1))]
            args += [patch_cot.reshape(cells, width), cls_cot, valid]
            out_specs += [whole((cells, width)), whole((1, width)), ANY, row_w, whole((8, width))]
            outs += [kept((cells, width), BF), kept((1, width), BF), kept((rows, 2 * width + hidden), BF),
                     kept((rows, width), F32), kept((8, width), F32)]
            scratch += [vm((rows, width), BF), vm((rows, hidden), BF), vm((rows, width), BF)]
        else:
            ins += [ANY]
            args += [qkv_weight]
            out_specs += [row_w, wide] + rim_specs
            outs += [kept((rows, width), F32), kept((rows, 3 * width), BF)] + rim_shapes
            scratch += [vm((width, 3 * width), BF), vm((rows, width), BF)]
        if l == 0:
            scratch += [vm((rows, width), BF)]
        out = call(functools.partial(middle_kernel, sz, l, last), (1,), ins, out_specs, outs, scratch + [sems],
                   )(*args)
        p, kb, vb, slope, x1, branch, down, left, stats = out[:9]
        saved.append(dict(x=x, qkv=qkv, p=p, kb=kb, vb=vb, slope=slope, x1=x1, branch=branch, down=down, stats=stats,
                          left=both(left), h=None))
        if l == 0:
            saved[0]["h"] = (saved[0]["left"], left_width // width - 1)
        else:
            saved[l]["h"] = (saved[l - 1]["left"], 2 + chunks)
        if last:
            patch_out, cls_out, right, g1, vec = out[9:]
        else:
            x, qkv, *rims = out[9:]
            got = exchange(rims)

    def attention_back(l, right, at, also):
        kept_l = saved[l]
        return call(
            functools.partial(attention_back_kernel, sz, l),
            (1,),
            [pl.BlockSpec((rows, width), lambda i, s: (0, at)), wide, whole((8, width)), whole((8, cells)), ANY, ANY, ANY, ANY],
            [whole((cells, width)), whole((cells, 2 * width))] + rim_specs + [whole((16, sz.bk))],
            [kept((cells, width), BF), kept((cells, 2 * width), F32)] + rim_shapes + [kept((16, sz.bk), F32)],
            [vm((sz.ext_rows, width), F32)] * 2 + [vm((rows, width), F32), vm((ng, sz.bk, sz.bk), F32), vm(square, BF),
             vm((nb * ng, sz.bk, sz.bk), BF), vm((nb, sz.bk, width), BF), vm((nb, sz.bk, width), BF), sems],
            also=also,
        )(right, kept_l["qkv"], kept_l["stats"], own_mask, out_weight, kept_l["p"], kept_l["kb"], kept_l["vb"])

    back_ins = [whole((cells, width)), whole((cells, 2 * width)), stat_spec] + rim_specs + [
        row_w, row_w, whole((8, width)), whole((16, sz.bk))]
    back_scratch = [vm((cells, 2 * width), F32), vm((rows, width), F32), vm((width, 3 * width), BF)]

    def qkv_back(l, d_q, d_kv, own, got, g1, vec, table):
        *e_qkv, rows_small, g = call(
            functools.partial(qkv_back_kernel, sz, l),
            (1,),
            back_ins + [par, ANY],
            [row_w, row_w, row_w, whole((24, width)), row_w],
            [kept((rows, width), BF)] * 3 + [kept((24, width), F32), kept((rows, width), F32)],
            back_scratch + [vm((rows, 3 * width), BF), sems],
            weight=LONG,
        )(d_q, d_kv, own, *got, saved[l]["x"], g1, vec, table, norm_attn, qkv_weight)
        return [both(e) for e in e_qkv], rows_small, g

    def mlp_back(l, g):
        low = saved[l]
        return call(
            functools.partial(mlp_back_kernel, sz, l),
            (1,),
            [row_w, par, par, par, row_w, row_w, row_w, ANY, ANY, ANY],
            [ANY, row_w, whole((8, width))],
            [kept((rows, 2 * width + hidden), BF), kept((rows, width), F32), kept((8, width), F32)],
            [vm((rows, width), F32), vm((width, hidden), BF), vm((hidden, width), BF), vm((rows, hidden), BF),
             vm((rows, width), BF), vm((rows, hidden), BF), vm((rows, width), BF), sems],
        )(g, norm_mlp, scale_attn, scale_mlp, low["x1"], low["branch"], low["down"], up_weight, down_weight, low["slope"])

    def finish(d_q, d_kv, own, got, g1, vec, table):
        return call(
            functools.partial(last_kernel, sz),
            (1,),
            back_ins + [par, ANY],
            [row_w, row_w, row_w, whole((24, width)), whole((cells, width)), whole((1, width))],
            [kept((rows, width), BF)] * 3 + [kept((24, width), F32), kept((cells, width), F32), kept((1, width), F32)],
            back_scratch + [vm((rows, 3 * width), BF), sems],
        )(d_q, d_kv, own, *got, saved[0]["x"], g1, vec, table, norm_attn, qkv_weight)

    piece, ff_piece = width // sz.devices, hidden // sz.devices
    half = width // 2
    quarter = sz.devices // 4

    def halves(start):
        return pl.BlockSpec((rows, half), lambda i, s: (0, 2 * start + s[1]))

    def grad_down(act, e_down, weight=1, also=()):
        lspec = pl.BlockSpec((rows, width), lambda i, s: (0, act[1] + s[1] * (chunks // 2) + i))
        rspec = pl.BlockSpec((rows, width), lambda i, s: (0, e_down[1]))
        out = pl.BlockSpec((None, quarter // 2, ff_piece, width), lambda i, s: (i ^ s[3], 0, 0, 0))
        return call(
            functools.partial(down_kernel, sz),
            (2,),
            [lspec, lspec, rspec, rspec],
            [out, out],
            [kept((2, quarter // 2, ff_piece, width), BF)] * 2,
            weight=weight, also=also,
        )(*act[0], *e_down[0])

    def grad_up(h2, e_up):
        lspec = halves(h2[1])
        rspec = pl.BlockSpec((rows, width), lambda i, s: (0, e_up[1] + i))
        out = pl.BlockSpec((quarter, None, piece, width), lambda i, s: (0, i, 0, 0))
        return call(
            functools.partial(up_kernel, sz),
            (chunks,),
            [lspec, lspec, rspec, rspec],
            [out, out],
            [kept((quarter, chunks, piece, width), BF)] * 2,
        )(*h2[0], *e_up[0])

    def grad_attn(h, e_qkv, att, e_branch, weight=1):
        def block(index):
            return pl.BlockSpec((quarter, None, piece, width), lambda i, s: (0, index(i), 0, 0))

        first, second = block(lambda i: jnp.minimum(i, 1)), block(lambda i: jnp.maximum(i - 2, 0))
        hspec, aspec = halves(h[1]), halves(att[1])
        bspec = pl.BlockSpec((rows, width), lambda i, s: (0, e_branch[1]))
        return call(
            functools.partial(attn_grad_kernel, sz),
            (4,),
            [hspec, hspec] + [row_w] * 6 + [aspec, aspec, bspec, bspec],
            [first, first, second, second],
            [kept((quarter, 2, piece, width), BF)] * 4,
            weight=weight,
        )(*h[0], *(v for pair in e_qkv for v in pair), *att[0], *e_branch[0])

    class Sums:
        def __init__(self, y_first, x_first, split):
            (s0, k0), (s1, k1) = y_first, x_first
            self.got = [swap(s0, 1), swap(s1, 2)]
            total = s0.size // width
            self.block = total // (quarter // 2)
            self.outer = split
            self.rows = total
            self.keep = [k0.reshape(1, 2, total // 2, width), k1.reshape(split, 2, total // 2 // split, width)]

        def second(self, weight=1):
            n = self.rows // 4
            got = [g.reshape(k.shape) for g, k in zip(self.got, self.keep)]
            sp = self.outer
            if sp == 1:
                other = pl.BlockSpec((1, 2, n, width), lambda i, s: (0, 0, i, 0))
                other_out = pl.BlockSpec((1, n, width), lambda i, s: (0, i, 0))
            else:
                other = pl.BlockSpec((1, 2, n, width), lambda i, s: (i, 0, 0, 0))
                other_out = pl.BlockSpec((1, n, width), lambda i, s: (i, 0, 0))
            spec = pl.BlockSpec((1, 2, n, width), lambda i, s: (0, 0, i, 0))
            spec_out = pl.BlockSpec((1, n, width), lambda i, s: (0, i, 0))
            s0, k0, s1, k1 = call(
                second_kernel, (2,), [spec, spec, other, other], [spec_out, spec_out, other_out, other_out],
                [kept((1, 2 * n, width), BF)] * 2 + [kept((sp, 2 * n // sp, width), BF)] * 2, weight=weight,
            )(self.keep[0], got[0], self.keep[1], got[1])
            self.got = [swap(s0, 2), swap(s1, 1)]
            self.keep = [k0, k1]
            self.rows //= 2

        def third(self, weight=1):
            n = self.rows // 2
            args = [v.reshape(2, n, width) for pair in zip(self.keep, self.got) for v in pair]
            s, k = call(
                third_kernel, (1,), [whole((2, n, width))] * 4, [whole((2, n, width))] * 2,
                [kept((2, n, width), BF)] * 2, weight=weight,
            )(*args)
            self.rows = n
            self.keep = k
            self.got = swap(s, bits - 2)
            for bit in range(bits - 3, 2, -1):
                n = self.rows // 2
                spec = whole((2, 2, n, width))
                s, k = call(
                    more_kernel, (1,), [spec, spec], [whole((2, n, width))] * 2, [kept((2, n, width), BF)] * 2,
                )(self.keep.reshape(2, 2, n, width), self.got.reshape(2, 2, n, width))
                self.rows = n
                self.keep = k
                self.got = swap(s, bit)

        def fourth(self):
            n = self.rows // 2
            spec = whole((2, 2, n, width))
            a, b = call(
                functools.partial(fourth_kernel, sz), (1,), [spec, spec], [whole((2, n, width))] * 2,
                [kept((2, n, width), BF)] * 2,
            )(self.keep.reshape(2, 2, n, width), self.got.reshape(2, 2, n, width))

            def route(flip):
                out = []
                for d in range(sz.devices):
                    high, core = d >> top_bit, d & 1
                    to = (d & ~(1 << top_bit) & ~1) | core << top_bit | (high ^ flip)
                    out.append((d, to))
                return out

            self.got = [lax.ppermute(a, ("dp", "tile"), route(0)), lax.ppermute(b, ("dp", "tile"), route(1))]

        def result(self):
            return self.got[0].astype(F32) + self.got[1].astype(F32)

    sums = {}
    small = [None] * layers
    early = [v["left"][1] for v in saved[:-1]]
    waiting = None
    for l in reversed(range(layers)):
        left = saved[l]["left"]
        if waiting is not None:
            quads = grad_attn(*waiting)
            sums["attn", l + 1] = Sums(quads[0:2], quads[2:4], 1)
        d_q, d_kv, *rims, table = attention_back(l, right, 1 + chunks, early)
        early = []
        if l + 1 < layers:
            right = both(lax.optimization_barrier((right, table))[0])
            got = exchange(rims)
            sums["mlp", l + 1].second()
            sums["attn", l + 1].second(LONG)
            x_first = grad_down((left, 2), (right, 0), 1, got)
        else:
            right = both(right)
            got = exchange(rims)
            x_first = grad_down((left, 2), (right, 0))
        y_first = grad_up((left, 1), (right, 1))
        sums["mlp", l] = Sums(y_first, x_first, 2)
        if l + 1 < layers:
            sums["mlp", l + 1].third(LONG)
            sums["attn", l + 1].third()
        if l > 0:
            e_qkv, small[l], g = qkv_back(l, d_q, d_kv, rims[0], got, g1, vec, table)
            waiting = (saved[l]["h"], e_qkv, (left, 0), (right, 1 + chunks))
            right, g1, vec = mlp_back(l - 1, g)
        else:
            *e_qkv, small[0], patch_grad, cls_grad = finish(d_q, d_kv, rims[0], got, g1, vec, table)
            waiting = (saved[0]["h"], [both(e) for e in e_qkv], (left, 0), (right, 1 + chunks))
    if layers > 1:
        sums["mlp", 1].fourth()
        sums["attn", 1].fourth()
    sums["mlp", 0].second(LONG)
    quads = grad_attn(*waiting)
    sums["attn", 0] = Sums(quads[0:2], quads[2:4], 1)
    total = jnp.stack(small)
    bit = 0
    for run in (sums["mlp", 0].third, sums["attn", 0].second, sums["mlp", 0].fourth, sums["attn", 0].third, sums["attn", 0].fourth):
        if bit < bits:
            total = lax.optimization_barrier((total, before[0]))[0]
            total = total + swap(total, bit)
            bit += 1
        run()
    for bit in range(bit, bits):
        total = total + swap(total, bit)
    ups, downs, firsts, seconds = [], [], [], []
    for l in range(layers):
        mlp, attn = sums["mlp", l].result(), sums["attn", l].result()
        ups.append(jnp.swapaxes(mlp[0].reshape(chunks, piece, width), 0, 1).reshape(piece, hidden))
        downs.append(mlp[1])
        attn = attn.reshape(4, piece, width)
        firsts.append(jnp.swapaxes(attn[:3], 0, 1).reshape(piece, 3 * width))
        seconds.append(attn[3])
    g_qkv, g_out, g_up, g_down = (jnp.stack(v) for v in (firsts, seconds, ups, downs))
    vectors, tables = total[:, 0:4], total[:, 8 : 8 + heads, 0 : sz.bk]
    mine = lax.dynamic_slice_in_dim(vectors, me * piece, piece, axis=2)
    tables = tables[:, :, first_slot : first_slot + SPAN * sz.pitch].reshape(layers, heads, SPAN, sz.pitch)
    g_table = tables[..., :SPAN].reshape(rel_table.shape)
    return (
        patch_out.reshape(patch_in.shape),
        cls_out,
        patch_grad.reshape(patch_in.shape),
        cls_grad,
        mine[:, 3],
        g_qkv,
        g_table,
        g_out,
        mine[:, 2],
        mine[:, 1],
        g_up,
        g_down,
        mine[:, 0],
    )


def solution(mesh):
    tokens = P("dp", "tile", None, None, None)
    split = ("dp", "tile")
    in_specs = (tokens, P("dp", None), P("dp")) + (P(),) * 9 + (tokens, P("dp", None))
    out_specs = (
        tokens,
        P("dp", None),
        tokens,
        P("dp", None),
        P(None, split),
        P(None, split, None),
        P(),
        P(None, split, None),
        P(None, split),
        P(None, split),
        P(None, split, None),
        P(None, split, None),
        P(None, split),
    )
    return jax.shard_map(local, mesh=mesh, in_specs=in_specs, out_specs=out_specs, check_vma=False)
```

time: 491 us -> 302 us (0.62)
  the two profiles are of different devices: /device:TPU:0 before, /device:TPU:1 now
where the time goes in v2:
time: 302 us; the launch traced here: 298 us
  Pallas kernels  171 us (57%)
  starting transfers between devices  69.3 us (23%)
  waiting for transfers between devices  28.8 us (10%)
  local copies, waits for them, and re-layouts  22.8 us (8%)
  other arithmetic  4.2 us (1%)
    pallas_call x27, Pallas kernels, go(): out = run(info, *pinned, *deps)  171 us
    ppermute x32, starting transfers between devices, partner(): return lax.ppermute(value, 'tile', [(t, t ^ x) for t in range(tiles)])  26.8 us
    ppermute x4, starting transfers between devices, fourth(): lax.ppermute(a, ('dp', 'tile'), route(0))  22.5 us
    ppermute x15, waiting for transfers between devices, swap(): lax.ppermute(value, 'dp', [(d, d ^ 1 << bit - 2) for d in range(pages)])  17.3 us
    unnamed x104, local copies, waits for them, and re-layouts  16.6 us
    ppermute x15, starting transfers between devices, swap(): lax.ppermute(value, 'dp', [(d, d ^ 1 << bit - 2) for d in range(pages)])  12.5 us
    ppermute x32, waiting for transfers between devices, partner(): return lax.ppermute(value, 'tile', [(t, t ^ x) for t in range(tiles)])  11.5 us
    ppermute x4, starting transfers between devices, fourth(): lax.ppermute(b, ('dp', 'tile'), route(1))  7.5 us
  transfers between devices with their start and end apart: 55, of which 7 were waited for; matrix products, arithmetic and copies ran while one was open for 2% of the time, Pallas kernels for 50%

profile of v2, /device:TPU:1, one launch (start us, length us, event | category | flops | bytes accessed | tf_op | source)
XLA Modules:
  0.0 298.0 jit_solution(4684294682064030222)
XLA Ops:
  3.3 6.8 %shard_map.282 = (f32[272,768]{1,0:T(8,128)}, bf16[272,2304]{1,0:T(8,128)(2,1)}, bf16[144,1536]{1,0:T(8,128)(2,1)}, bf16[64,1536]{1,0:T(8,128)(2,1)}, bf16[48,1536]{1,0:T(8,128)(2,1)}) custom-call(s32[5]{0:T(128)} %stack.48.refs_0_, bf16[256,768]{1,0:T(8,128)(2,1)} %bitcast.100, bf16[1,768]{1,0:T(2,128)(2,1)} %refs_2_.2, f32[2,768]{1,0:T(2,128)} %refs_11_.7, ...), custom_call_target="tpu_custom_call" | custom-call | flops 1 | bytes 1 | tf_op jit(solution)/shard_map/pallas_call | solution.py:839
  14.0 4.8 %shard_map.283.refs_6_.refs_18_ = f32[2,3,256,256]{3,2,1,0:T(8,128)} custom-call(s32[5]{0:T(128)} %stack.48.refs_0_, f32[2,16,256]{2,1,0:T(8,128)} %pad.9.refs_1_, bf16[48,1536]{1,0:T(8,128)(2,1)} %get-tuple-element.125.refs_2_), custom_call_target="tpu_custom_call" | custom-call | flops 1 | bytes 1 | tf_op jit(solution)/shard_map/pallas_call | solution.py:839
  22.6 16.1 %shard_map.284 = (bf16[12,256,256]{2,1,0:T(8,128)(2,1)}, bf16[4,256,768]{2,1,0:T(8,128)(2,1)}, bf16[4,256,768]{2,1,0:T(8,128)(2,1)}, bf16[272,3072]{1,0:T(8,128)...) custom-call(s32[5]{0:T(128)} %stack.48.refs_0_, ...), custom_call_target="tpu_custom_call" | custom-call | flops 1 | bytes 1 | tf_op jit(solution)/shard_map/pallas_call | solution.py:839
  42.1 7.3 %collective-permute-done.5.refs_5_ = bf16[48,1536]{1,0:T(8,128)(2,1)} collective-permute-done((bf16[48,1536]{1,0:T(8,128)(2,1)}, bf16[48,1536]{1,0:T(8,128)(2,1)}, u32[]{:S(2)}, u32[]{:S(2)}) %collective-permute-start.5) | collective-permute-done | bytes 147488 | tf_op jit(solution)/shard_map/ppermute | solution.py:846
  50.1 17.2 %shard_map.285 = (bf16[12,256,256]{2,1,0:T(8,128)(2,1)}, bf16[4,256,768]{2,1,0:T(8,128)(2,1)}, bf16[4,256,768]{2,1,0:T(8,128)(2,1)}, bf16[272,3072]{1,0:T(8,128)...) custom-call(s32[5]{0:T(128)} %stack.48.refs_0_, ...), custom_call_target="tpu_custom_call" | custom-call | flops 1 | bytes 1 | tf_op jit(solution)/shard_map/pallas_call | solution.py:839
  69.6 11.5 %shard_map.286 = (bf16[256,768]{1,0:T(8,128)(2,1)}, f32[256,1536]{1,0:T(8,128)}, bf16[144,1536]{1,0:T(8,128)(2,1)}, bf16[64,1536]{1,0:T(8,128)(2,1)}, bf16[48,1536]{1,0:T(8,128)(2,1)}, /*index=5*/f32[16,256]{1,0:T(8,128)}) custom-call(s32[5]{0:T(128)} %stack.48.refs_0_, bf16[272,4608]{1,0:T(8,128)(2,1)} %get-tuple-element.134.refs_1_.refs_3_.refs_11_, ...), custom_call_target="tpu_custom_call" | custom-call | flops 1 | bytes 1 | tf_op jit(solution)/shard_map/pallas_call | solution.py:839
  84.7 5.4 %shard_map.287 = (bf16[2,4,96,768]{3,2,1,0:T(8,128)(2,1)}, bf16[2,4,96,768]{3,2,1,0:T(8,128)(2,1)}) custom-call(s32[5]{0:T(128)} %stack.48.refs_0_, bf16[272,4608]{1,0:T(8,128)(2,1)} %get-tuple-element.148.refs_1_.refs_9_, bf16[272,4608]{1,0:T(8,128)(2,1)} %copy-done.2, bf16[272,4608]{1,0:T(8,128)(2,1)} %get-tuple-element.134.refs_1_.refs_3_.refs_11_, ...), custom_call_target="tpu_custom_call" | custom-call | flops 1 | bytes 1 | tf_op jit(solution)/shard_map/pallas_call | solution.py:839
  90.2 6.4 %shard_map.288 = (bf16[8,4,24,768]{3,2,1,0:T(8,128)(2,1)}, bf16[8,4,24,768]{3,2,1,0:T(8,128)(2,1)}) custom-call(s32[5]{0:T(128)} %stack.48.refs_0_, bf16[272,4608]{1,0:T(8,128)(2,1)} %get-tuple-element.148.refs_1_.refs_9_, bf16[272,4608]{1,0:T(8,128)(2,1)} %copy-done.2, bf16[272,4608]{1,0:T(8,128)(2,1)} %get-tuple-element.134.refs_1_.refs_3_.refs_11_, ...), custom_call_target="tpu_custom_call" | custom-call | flops 1 | bytes 1 | tf_op jit(solution)/shard_map/pallas_call | solution.py:839
  100.1 7.6 %shard_map.289 = (bf16[272,768]{1,0:T(8,128)(2,1)}, bf16[272,768]{1,0:T(8,128)(2,1)}, bf16[272,768]{1,0:T(8,128)(2,1)}, f32[24,768]{1,0:T(8,128)}, f32[272,768]{1,0:T(8,128)}) custom-call(s32[5]{0:T(128)} %stack.48.refs_0_, bf16[256,768]{1,0:T(8,128)(2,1)} %get-tuple-element.141.refs_1_, f32[256,1536]{1,0:T(8,128)} %get-tuple-element.142.refs_2_, ...), custom_call_target="tpu_custom_call" | custom-call | flops 99999997952 | bytes 1 | tf_op jit(solution)/shard_map/pallas_call | solution.py:839
  108.7 11.0 %shard_map.290 = (bf16[272,4608]{1,0:T(8,128)(2,1)}, f32[272,768]{1,0:T(8,128)}, f32[8,768]{1,0:T(8,128)}) custom-call(s32[5]{0:T(128)} %stack.48.refs_0_, f32[272,768]{1,0:T(8,128)} %get-tuple-element.151.refs_1_.refs_11_, f32[2,768]{1,0:T(2,128)} %refs_2_.3, f32[2,768]{1,0:T(2,128)} %refs_3_.3, f32[2,768]{1,0:T(2,128)} %refs_4_.1, ...), custom_call_target="tpu_custom_call" | custom-call | flops 1 | bytes 1 | tf_op jit(solution)/shard_map/pallas_call | solution.py:839
  120.7 7.4 %shard_map.291 = (bf16[8,2,24,768]{3,2,1,0:T(8,128)(2,1)}, bf16[8,2,24,768]{3,2,1,0:T(8,128)(2,1)}, bf16[8,2,24,768]{3,2,1,0:T(8,128)(2,1)}, bf16[8,2,24,768]{3,2,1,0:T(8,128)(2,1)}) custom-call(s32[5]{0:T(128)} %stack.48.refs_0_, bf16[272,6144]{1,0:T(8,128)(2,1)} %get-tuple-element.140.refs_1_.refs_9_, bf16[272,6144]{1,0:T(8,128)(2,1)} %copy-done, ...), custom_call_target="tpu_custom_call" | custom-call | flops 1 | bytes 1 | tf_op jit(solution)/shard_map/pallas_call | solution.py:839
  128.7 11.3 %shard_map.292 = (bf16[256,768]{1,0:T(8,128)(2,1)}, f32[256,1536]{1,0:T(8,128)}, bf16[144,1536]{1,0:T(8,128)(2,1)}, bf16[64,1536]{1,0:T(8,128)(2,1)}, bf16[48,1536]{1,0:T(8,128)(2,1)}, /*index=5*/f32[16,256]{1,0:T(8,128)}) custom-call(s32[5]{0:T(128)} %stack.48.refs_0_, bf16[272,4608]{1,0:T(8,128)(2,1)} %get-tuple-element.186.refs_1_.refs_3_.refs_11_, ...), custom_call_target="tpu_custom_call" | custom-call | flops 1 | bytes 1 | tf_op jit(solution)/shard_map/pallas_call | solution.py:839
  143.3 4.4 %shard_map.293 = (bf16[1,384,768]{2,1,0:T(8,128)(2,1)}, bf16[1,384,768]{2,1,0:T(8,128)(2,1)}, bf16[2,192,768]{2,1,0:T(8,128)(2,1)}, bf16[2,192,768]{2,1,0:T(8,128)(2,1)}) custom-call(s32[5]{0:T(128)} %stack.48.refs_0_, bf16[1,2,384,768]{3,2,1,0:T(8,128)(2,1)} %bitcast.79, bf16[1,2,384,768]{3,2,1,0:T(8,128)(2,1)} %bitcast.80, ...), custom_call_target="tpu_custom_call" | custom-call | flops 1 | bytes 1 | tf_op jit(solution)/shard_map/pallas_call | solution.py:839
  149.9 3.2 %shard_map.294 = (bf16[1,192,768]{2,1,0:T(8,128)(2,1)}, bf16[1,192,768]{2,1,0:T(8,128)(2,1)}, bf16[1,192,768]{2,1,0:T(8,128)(2,1)}, bf16[1,192,768]{2,1,0:T(8,128)(2,1)}) custom-call(s32[5]{0:T(128)} %stack.48.refs_0_, bf16[1,2,192,768]{3,2,1,0:T(8,128)(2,1)} %bitcast.124, bf16[1,2,192,768]{3,2,1,0:T(8,128)(2,1)} %bitcast.126, ...), custom_call_target="tpu_custom_call" | custom-call | flops 99999997952 | bytes 1 | tf_op jit(solution)/shard_map/pallas_call | solution.py:839
  155.6 5.5 %shard_map.295 = (bf16[2,4,96,768]{3,2,1,0:T(8,128)(2,1)}, bf16[2,4,96,768]{3,2,1,0:T(8,128)(2,1)}) custom-call(s32[5]{0:T(128)} %stack.48.refs_0_, bf16[272,6144]{1,0:T(8,128)(2,1)} %get-tuple-element.140.refs_1_.refs_9_, bf16[272,6144]{1,0:T(8,128)(2,1)} %copy-done, bf16[272,4608]{1,0:T(8,128)(2,1)} %get-tuple-element.186.refs_1_.refs_3_.refs_11_, ...), custom_call_target="tpu_custom_call" | custom-call | flops 1 | bytes 1 | tf_op jit(solution)/shard_map/pallas_call | solution.py:839
  161.1 6.4 %shard_map.296 = (bf16[8,4,24,768]{3,2,1,0:T(8,128)(2,1)}, bf16[8,4,24,768]{3,2,1,0:T(8,128)(2,1)}) custom-call(s32[5]{0:T(128)} %stack.48.refs_0_, bf16[272,6144]{1,0:T(8,128)(2,1)} %get-tuple-element.140.refs_1_.refs_9_, bf16[272,6144]{1,0:T(8,128)(2,1)} %copy-done, bf16[272,4608]{1,0:T(8,128)(2,1)} %get-tuple-element.186.refs_1_.refs_3_.refs_11_, ...), custom_call_target="tpu_custom_call" | custom-call | flops 1 | bytes 1 | tf_op jit(solution)/shard_map/pallas_call | solution.py:839
  169.5 3.5 %shard_map.297 = (bf16[2,192,768]{2,1,0:T(8,128)(2,1)}, bf16[2,192,768]{2,1,0:T(8,128)(2,1)}) custom-call(s32[5]{0:T(128)} %stack.48.refs_0_, bf16[2,192,768]{2,1,0:T(8,128)(2,1)} %bitcast.125, bf16[2,192,768]{2,1,0:T(8,128)(2,1)} %bitcast.128, bf16[2,192,768]{2,1,0:T(8,128)(2,1)} %get-tuple-element.178.refs_5_.refs_3_, ...), custom_call_target="tpu_custom_call" | custom-call | flops 99999997952 | bytes 1 | tf_op jit(solution)/shard_map/pallas_call | solution.py:839
  178.1 7.7 %shard_map.299 = (bf16[272,768]{1,0:T(8,128)(2,1)}, bf16[272,768]{1,0:T(8,128)(2,1)}, bf16[272,768]{1,0:T(8,128)(2,1)}, f32[24,768]{1,0:T(8,128)}, f32[256,768]{1,0:T(8,128)}, /*index=5*/f32[1,768]{1,0:T(1,128)}) custom-call(s32[5]{0:T(128)} %stack.48.refs_0_, bf16[256,768]{1,0:T(8,128)(2,1)} %get-tuple-element.166.refs_1_, ...), custom_call_target="tpu_custom_call" | custom-call | flops 1 | bytes 1 | tf_op jit(solution)/shard_map/pallas_call | solution.py:839
  188.2 3.1 %collective-permute-start.28 = (bf16[272,768]{1,0:T(8,128)(2,1)}, bf16[272,768]{1,0:T(8,128)(2,1)S(1)}, u32[]{:S(2)}, u32[]{:S(2)}) collective-permute-start(bf16[272,768]{1,0:T(8,128)(2,1)} %get-tuple-element.196.refs_5_), channel_id=1, source_target_pairs={{0,1},{1,0},{2,3},{3,2},{4,5},{5,4},{6,7},{7,6},{8,9},{9,8},{10,11... | collective-permute-start | bytes 1253384 | tf_op jit(solution)/shard_map/ppermute | solution.py:846
  191.3 2.9 shard_map.300
  199.3 4.3 %shard_map.302 = (bf16[1,384,768]{2,1,0:T(8,128)(2,1)}, bf16[1,384,768]{2,1,0:T(8,128)(2,1)}, bf16[2,192,768]{2,1,0:T(8,128)(2,1)}, bf16[2,192,768]{2,1,0:T(8,128)(2,1)}) custom-call(s32[5]{0:T(128)} %stack.48.refs_0_, bf16[1,2,384,768]{3,2,1,0:T(8,128)(2,1)} %bitcast.120, bf16[1,2,384,768]{3,2,1,0:T(8,128)(2,1)} %bitcast.121, ...), custom_call_target="tpu_custom_call" | custom-call | flops 99999997952 | bytes 1 | tf_op jit(solution)/shard_map/pallas_call | solution.py:839
  206.2 7.2 %shard_map.303 = (bf16[8,2,24,768]{3,2,1,0:T(8,128)(2,1)}, bf16[8,2,24,768]{3,2,1,0:T(8,128)(2,1)}, bf16[8,2,24,768]{3,2,1,0:T(8,128)(2,1)}, bf16[8,2,24,768]{3,2,1,0:T(8,128)(2,1)}) custom-call(s32[5]{0:T(128)} %stack.48.refs_0_, bf16[272,6144]{1,0:T(8,128)(2,1)} %get-tuple-element.140.refs_1_.refs_9_, bf16[272,6144]{1,0:T(8,128)(2,1)} %copy-done, ...), custom_call_target="tpu_custom_call" | custom-call | flops 1 | bytes 1 | tf_op jit(solution)/shard_map/pallas_call | solution.py:839
  219.3 3.5 %shard_map.304 = (bf16[2,192,768]{2,1,0:T(8,128)(2,1)}, bf16[2,192,768]{2,1,0:T(8,128)(2,1)}) custom-call(s32[5]{0:T(128)} %stack.48.refs_0_, bf16[2,192,768]{2,1,0:T(8,128)(2,1)} %bitcast.96, bf16[2,192,768]{2,1,0:T(8,128)(2,1)} %bitcast.97, bf16[2,192,768]{2,1,0:T(8,128)(2,1)} %get-tuple-element.204.refs_13_.refs_3_, bf16[2,192,768]{2,1,0:T(8,128)(2,1)} %copy-done.12, ...), custom_call_target="tpu_custom_call" | custom-call | flops 1 | bytes 1 | tf_op jit(solution)/shard_map/pallas_call | solution.py:839
  225.9 5.8 %collective-permute-start.49 = (bf16[2,48,768]{2,1,0:T(8,128)(2,1)S(1)}, bf16[2,48,768]{2,1,0:T(8,128)(2,1)S(1)}, u32[]{:S(2)}, u32[]{:S(2)}) collective-permute-start(bf16[2,48,768]{2,1,0:T(8,128)(2,1)S(1)} %copy-done.48), channel_id=1, source_target_pairs={{0,0},{1,16},{2,2},{3,18},{4,4},{5,20},{6,6},{7,22},{8,8},{9,24},{... | collective-permute-start | bytes 442376 | tf_op jit(solution)/shard_map/ppermute | solution.py:1100
  232.7 3.3 %shard_map.305 = (bf16[1,192,768]{2,1,0:T(8,128)(2,1)}, bf16[1,192,768]{2,1,0:T(8,128)(2,1)}, bf16[1,192,768]{2,1,0:T(8,128)(2,1)}, bf16[1,192,768]{2,1,0:T(8,128)(2,1)}) custom-call(s32[5]{0:T(128)} %stack.48.refs_0_, bf16[1,2,192,768]{3,2,1,0:T(8,128)(2,1)} %bitcast.95, bf16[1,2,192,768]{3,2,1,0:T(8,128)(2,1)} %bitcast.98, ...), custom_call_target="tpu_custom_call" | custom-call | flops 1 | bytes 1 | tf_op jit(solution)/shard_map/pallas_call | solution.py:839
  239.8 6.1 %collective-permute-start.53 = (bf16[2,96,768]{2,1,0:T(8,128)(2,1)S(1)}, bf16[2,96,768]{2,1,0:T(8,128)(2,1)S(1)}, u32[]{:S(2)}, u32[]{:S(2)}) collective-permute-start(bf16[2,96,768]{2,1,0:T(8,128)(2,1)S(1)} %copy-done.46), channel_id=1, source_target_pairs={{0,0},{1,16},{2,2},{3,18},{4,4},{5,20},{6,6},{7,22},{8,8},{9,24},{... | collective-permute-start | bytes 884744 | tf_op jit(solution)/shard_map/ppermute | solution.py:1100
  247.9 7.2 %collective-permute-done.41 = bf16[2,192,768]{2,1,0:T(8,128)(2,1)S(1)} collective-permute-done((bf16[2,192,768]{2,1,0:T(8,128)(2,1)}, bf16[2,192,768]{2,1,0:T(8,128)(2,1)S(1)}, u32[]{:S(2)}, u32[]{:S(2)}) %collective-permute-start.41) | collective-permute-done | bytes 589856 | tf_op jit(solution)/shard_map/ppermute | solution.py:854
  255.9 2.9 shard_map.306
  258.8 3.4 %collective-permute-start.52 = (bf16[2,96,768]{2,1,0:T(8,128)(2,1)}, bf16[2,96,768]{2,1,0:T(8,128)(2,1)S(1)}, u32[]{:S(2)}, u32[]{:S(2)}) collective-permute-start(bf16[2,96,768]{2,1,0:T(8,128)(2,1)} %get-tuple-element.218.refs_5_), channel_id=1, source_target_pairs={{0,1},{1,17},{2,3},{3,19},{4,5},{5,21},{6,7},{7,23},{8,9},{9,25},{... | collective-permute-start | bytes 884744 | tf_op jit(solution)/shard_map/ppermute | solution.py:1100
  268.0 4.8 %collective-permute-start.51 = (bf16[2,96,768]{2,1,0:T(8,128)(2,1)}, bf16[2,96,768]{2,1,0:T(8,128)(2,1)S(1)}, u32[]{:S(2)}, u32[]{:S(2)}) collective-permute-start(bf16[2,96,768]{2,1,0:T(8,128)(2,1)} %get-tuple-element.229), channel_id=1, source_target_pairs={{0,0},{1,16},{2,2},{3,18},{4,4},{5,20},{6,6},{7,22},{8,8},{9,24},{... | collective-permute-start | bytes 884744 | tf_op jit(solution)/shard_map/ppermute | solution.py:1100
  273.3 9.8 %collective-permute-done.46 = bf16[2,96,768]{2,1,0:T(8,128)(2,1)S(1)} collective-permute-done((bf16[2,96,768]{2,1,0:T(8,128)(2,1)}, bf16[2,96,768]{2,1,0:T(8,128)(2,1)S(1)}, u32[]{:S(2)}, u32[]{:S(2)}) %collective-permute-start.46) | collective-permute-done | bytes 294944 | tf_op jit(solution)/shard_map/ppermute | solution.py:854
  286.4 5.7 %collective-permute-start.47 = (bf16[2,48,768]{2,1,0:T(8,128)(2,1)}, bf16[2,48,768]{2,1,0:T(8,128)(2,1)S(1)}, u32[]{:S(2)}, u32[]{:S(2)}) collective-permute-start(bf16[2,48,768]{2,1,0:T(8,128)(2,1)} %get-tuple-element.226), channel_id=1, source_target_pairs={{0,0},{1,16},{2,2},{3,18},{4,4},{5,20},{6,6},{7,22},{8,8},{9,24},{... | collective-permute-start | bytes 442376 | tf_op jit(solution)/shard_map/ppermute | solution.py:1100
  (253 shorter events, 82.4 us)
Async XLA Ops:
  38.7 29.1 %collective-permute-start.6 = (bf16[272,6144]{1,0:T(8,128)(2,1)}, bf16[272,6144]{1,0:T(8,128)(2,1)S(1)}, u32[]{:S(2)}, u32[]{:S(2)}) collective-permute-start(bf16[272,6144]{1,0:T(8,128)(2,1)} %get-tuple-element.140.refs_1_.refs_9_), channel_id=1, source_target_pairs={{0,1},{1,0},{2,3},{3,2},{4,5},{5,4},{6,7},{7,6},{8,9},{9,8},{10,11... | collective-permute-start | bytes 10027016 | tf_op jit(solution)/shard_map/ppermute | solution.py:846
  67.3 16.0 %collective-permute-start.10 = (bf16[272,4608]{1,0:T(8,128)(2,1)}, bf16[272,4608]{1,0:T(8,128)(2,1)S(1)}, u32[]{:S(2)}, u32[]{:S(2)}) collective-permute-start(bf16[272,4608]{1,0:T(8,128)(2,1)} %get-tuple-element.148.refs_1_.refs_9_), channel_id=1, source_target_pairs={{0,1},{1,0},{2,3},{3,2},{4,5},{5,4},{6,7},{7,6},{8,9},{9,8},{10,11... | collective-permute-start | bytes 7520264 | tf_op jit(solution)/shard_map/ppermute | solution.py:846
  67.3 16.0 %collective-permute-start.11 = (bf16[272,4608]{1,0:T(8,128)(2,1)}, bf16[272,4608]{1,0:T(8,128)(2,1)}, u32[]{:S(2)}, u32[]{:S(2)}) collective-permute-start(bf16[272,4608]{1,0:T(8,128)(2,1)} %get-tuple-element.134.refs_1_.refs_3_.refs_11_), channel_id=1, source_target_pairs={{0,1},{1,0},{2,3},{3,2},{4,5},{5,4},{6,7},{7,6},{8,9},{9,8},{10,11... | collective-permute-start | bytes 7520264 | tf_op jit(solution)/shard_map/ppermute | solution.py:846
  81.1 18.2 %collective-permute-start.7 = (bf16[144,1536]{1,0:T(8,128)(2,1)}, bf16[144,1536]{1,0:T(8,128)(2,1)S(1)}, u32[]{:S(2)}, u32[]{:S(2)}) collective-permute-start(bf16[144,1536]{1,0:T(8,128)(2,1)} %get-tuple-element.143.refs_3_), channel_id=1, source_target_pairs={{0,1},{1,0},{2,3},{3,2},{4,5},{5,4},{6,7},{7,6},{8,9},{9,8},{10,11... | collective-permute-start | bytes 1327112 | tf_op jit(solution)/shard_map/ppermute | solution.py:846
  81.2 18.0 %collective-permute-start.8 = (bf16[64,1536]{1,0:T(8,128)(2,1)}, bf16[64,1536]{1,0:T(8,128)(2,1)S(1)}, u32[]{:S(2)}, u32[]{:S(2)}) collective-permute-start(bf16[64,1536]{1,0:T(8,128)(2,1)} %get-tuple-element.144), channel_id=1, source_target_pairs={{0,2},{1,3},{2,0},{3,1},{4,6},{5,7},{6,4},{7,5},{8,10},{9,11},{10,... | collective-permute-start | bytes 589832 | tf_op jit(solution)/shard_map/ppermute | solution.py:846
  82.7 16.6 %collective-permute-start.9 = (bf16[48,1536]{1,0:T(8,128)(2,1)}, bf16[48,1536]{1,0:T(8,128)(2,1)S(1)}, u32[]{:S(2)}, u32[]{:S(2)}) collective-permute-start(bf16[48,1536]{1,0:T(8,128)(2,1)} %get-tuple-element.145), channel_id=1, source_target_pairs={{0,3},{1,2},{2,1},{3,0},{4,7},{5,6},{6,5},{7,4},{8,11},{9,10},{10,... | collective-permute-start | bytes 442376 | tf_op jit(solution)/shard_map/ppermute | solution.py:846
  96.6 45.2 %collective-permute-start.20 = (bf16[8,4,24,768]{3,2,1,0:T(8,128)(2,1)}, bf16[8,4,24,768]{3,2,1,0:T(8,128)(2,1)S(1)}, u32[]{:S(2)}, u32[]{:S(2)}) collective-permute-start(bf16[8,4,24,768]{3,2,1,0:T(8,128)(2,1)} %get-tuple-element.176), channel_id=1, source_target_pairs={{0,2},{1,3},{2,0},{3,1},{4,6},{5,7},{6,4},{7,5},{8,10},{9,11},{10,... | collective-permute-start | bytes 3538952 | tf_op jit(solution)/shard_map/ppermute | solution.py:846
  98.0 43.8 %collective-permute-start.21 = (bf16[2,4,96,768]{3,2,1,0:T(8,128)(2,1)S(1)}, bf16[2,4,96,768]{3,2,1,0:T(8,128)(2,1)S(1)}, u32[]{:S(2)}, u32[]{:S(2)}) collective-permute-start(bf16[2,4,96,768]{3,2,1,0:T(8,128)(2,1)S(1)} %copy-done.38), channel_id=1, source_target_pairs={{0,4},{4,0},{8,12},{12,8},{16,20},{20,16},{24,28},{28,24},{1,5},{5... | collective-permute-start | bytes 3538952 | tf_op jit(solution)/shard_map/ppermute | solution.py:854
  128.1 19.7 %collective-permute-start.18 = (bf16[8,2,24,768]{3,2,1,0:T(8,128)(2,1)}, bf16[8,2,24,768]{3,2,1,0:T(8,128)(2,1)S(1)}, u32[]{:S(2)}, u32[]{:S(2)}) collective-permute-start(bf16[8,2,24,768]{3,2,1,0:T(8,128)(2,1)} %get-tuple-element.174), channel_id=1, source_target_pairs={{0,2},{1,3},{2,0},{3,1},{4,6},{5,7},{6,4},{7,5},{8,10},{9,11},{10,... | collective-permute-start | bytes 1769480 | tf_op jit(solution)/shard_map/ppermute | solution.py:846
  128.5 20.6 %collective-permute-start.19 = (bf16[8,2,24,768]{3,2,1,0:T(8,128)(2,1)}, bf16[8,2,24,768]{3,2,1,0:T(8,128)(2,1)S(1)}, u32[]{:S(2)}, u32[]{:S(2)}) collective-permute-start(bf16[8,2,24,768]{3,2,1,0:T(8,128)(2,1)} %get-tuple-element.175), channel_id=1, source_target_pairs={{0,4},{4,0},{8,12},{12,8},{16,20},{20,16},{24,28},{28,24},{1,5},{5... | collective-permute-start | bytes 1769480 | tf_op jit(solution)/shard_map/ppermute | solution.py:854
  147.8 20.4 %collective-permute-start.24 = (bf16[1,384,768]{2,1,0:T(8,128)(2,1)}, bf16[1,384,768]{2,1,0:T(8,128)(2,1)S(1)}, u32[]{:S(2)}, u32[]{:S(2)}) collective-permute-start(bf16[1,384,768]{2,1,0:T(8,128)(2,1)} %get-tuple-element.184), channel_id=1, source_target_pairs={{0,4},{4,0},{8,12},{12,8},{16,20},{20,16},{24,28},{28,24},{1,5},{5... | collective-permute-start | bytes 1769480 | tf_op jit(solution)/shard_map/ppermute | solution.py:854
  149.1 20.5 %collective-permute-start.25 = (bf16[2,192,768]{2,1,0:T(8,128)(2,1)}, bf16[2,192,768]{2,1,0:T(8,128)(2,1)}, u32[]{:S(2)}, u32[]{:S(2)}) collective-permute-start(bf16[2,192,768]{2,1,0:T(8,128)(2,1)} %get-tuple-element.185), channel_id=1, source_target_pairs={{0,2},{1,3},{2,0},{3,1},{4,6},{5,7},{6,4},{7,5},{8,10},{9,11},{10,... | collective-permute-start | bytes 1769480 | tf_op jit(solution)/shard_map/ppermute | solution.py:846
  153.1 21.2 %collective-permute-start.22 = (bf16[1,192,768]{2,1,0:T(8,128)(2,1)}, bf16[1,192,768]{2,1,0:T(8,128)(2,1)S(1)}, u32[]{:S(2)}, u32[]{:S(2)}) collective-permute-start(bf16[1,192,768]{2,1,0:T(8,128)(2,1)} %get-tuple-element.180), channel_id=1, source_target_pairs={{0,4},{4,0},{8,12},{12,8},{16,20},{20,16},{24,28},{28,24},{1,5},{5... | collective-permute-start | bytes 884744 | tf_op jit(solution)/shard_map/ppermute | solution.py:854
  153.4 20.9 %collective-permute-start.23 = (bf16[1,192,768]{2,1,0:T(8,128)(2,1)}, bf16[1,192,768]{2,1,0:T(8,128)(2,1)S(1)}, u32[]{:S(2)}, u32[]{:S(2)}) collective-permute-start(bf16[1,192,768]{2,1,0:T(8,128)(2,1)} %get-tuple-element.182), channel_id=1, source_target_pairs={{0,2},{1,3},{2,0},{3,1},{4,6},{5,7},{6,4},{7,5},{8,10},{9,11},{10,... | collective-permute-start | bytes 884744 | tf_op jit(solution)/shard_map/ppermute | solution.py:846
  167.5 30.3 %collective-permute-start.30 = (bf16[8,4,24,768]{3,2,1,0:T(8,128)(2,1)}, bf16[8,4,24,768]{3,2,1,0:T(8,128)(2,1)S(1)}, u32[]{:S(2)}, u32[]{:S(2)}) collective-permute-start(bf16[8,4,24,768]{3,2,1,0:T(8,128)(2,1)} %get-tuple-element.198), channel_id=1, source_target_pairs={{0,2},{1,3},{2,0},{3,1},{4,6},{5,7},{6,4},{7,5},{8,10},{9,11},{10,... | collective-permute-start | bytes 3538952 | tf_op jit(solution)/shard_map/ppermute | solution.py:846
  168.2 29.5 %collective-permute-start.31 = (bf16[2,4,96,768]{3,2,1,0:T(8,128)(2,1)S(1)}, bf16[2,4,96,768]{3,2,1,0:T(8,128)(2,1)S(1)}, u32[]{:S(2)}, u32[]{:S(2)}) collective-permute-start(bf16[2,4,96,768]{3,2,1,0:T(8,128)(2,1)S(1)} %copy-done.40), channel_id=1, source_target_pairs={{0,4},{4,0},{8,12},{12,8},{16,20},{20,16},{24,28},{28,24},{1,5},{5... | collective-permute-start | bytes 3538952 | tf_op jit(solution)/shard_map/ppermute | solution.py:854
  173.0 15.2 %collective-permute-start.33 = (bf16[2,192,768]{2,1,0:T(8,128)(2,1)}, bf16[2,192,768]{2,1,0:T(8,128)(2,1)S(1)}, u32[]{:S(2)}, u32[]{:S(2)}) collective-permute-start(bf16[2,192,768]{2,1,0:T(8,128)(2,1)} %get-tuple-element.201), channel_id=1, source_target_pairs={{0,8},{4,12},{8,0},{12,4},{16,24},{20,28},{24,16},{28,20},{1,9},{5... | collective-permute-start | bytes 1769480 | tf_op jit(solution)/shard_map/ppermute | solution.py:854
  177.9 16.2 %collective-permute-start.32 = (bf16[2,96,768]{2,1,0:T(8,128)(2,1)}, bf16[2,96,768]{2,1,0:T(8,128)(2,1)S(1)}, u32[]{:S(2)}, u32[]{:S(2)}) collective-permute-start(bf16[2,96,768]{2,1,0:T(8,128)(2,1)} %get-tuple-element.200), channel_id=1, source_target_pairs={{0,8},{4,12},{8,0},{12,4},{16,24},{20,28},{24,16},{28,20},{1,9},{5... | collective-permute-start | bytes 884744 | tf_op jit(solution)/shard_map/ppermute | solution.py:854
  185.8 19.4 %collective-permute-start.27 = (bf16[272,768]{1,0:T(8,128)(2,1)}, bf16[272,768]{1,0:T(8,128)(2,1)S(1)}, u32[]{:S(2)}, u32[]{:S(2)}) collective-permute-start(bf16[272,768]{1,0:T(8,128)(2,1)} %get-tuple-element.195.refs_3_), channel_id=1, source_target_pairs={{0,1},{1,0},{2,3},{3,2},{4,5},{5,4},{6,7},{7,6},{8,9},{9,8},{10,11... | collective-permute-start | bytes 1253384 | tf_op jit(solution)/shard_map/ppermute | solution.py:846
  188.2 16.9 %collective-permute-start.28 = (bf16[272,768]{1,0:T(8,128)(2,1)}, bf16[272,768]{1,0:T(8,128)(2,1)S(1)}, u32[]{:S(2)}, u32[]{:S(2)}) collective-permute-start(bf16[272,768]{1,0:T(8,128)(2,1)} %get-tuple-element.196.refs_5_), channel_id=1, source_target_pairs={{0,1},{1,0},{2,3},{3,2},{4,5},{5,4},{6,7},{7,6},{8,9},{9,8},{10,11... | collective-permute-start | bytes 1253384 | tf_op jit(solution)/shard_map/ppermute | solution.py:846
  213.4 18.3 %collective-permute-start.38 = (bf16[8,2,24,768]{3,2,1,0:T(8,128)(2,1)}, bf16[8,2,24,768]{3,2,1,0:T(8,128)(2,1)S(1)}, u32[]{:S(2)}, u32[]{:S(2)}) collective-permute-start(bf16[8,2,24,768]{3,2,1,0:T(8,128)(2,1)} %get-tuple-element.213), channel_id=1, source_target_pairs={{0,2},{1,3},{2,0},{3,1},{4,6},{5,7},{6,4},{7,5},{8,10},{9,11},{10,... | collective-permute-start | bytes 1769480 | tf_op jit(solution)/shard_map/ppermute | solution.py:846
  214.1 17.6 %collective-permute-start.39 = (bf16[8,2,24,768]{3,2,1,0:T(8,128)(2,1)}, bf16[8,2,24,768]{3,2,1,0:T(8,128)(2,1)S(1)}, u32[]{:S(2)}, u32[]{:S(2)}) collective-permute-start(bf16[8,2,24,768]{3,2,1,0:T(8,128)(2,1)} %get-tuple-element.214), channel_id=1, source_target_pairs={{0,4},{4,0},{8,12},{12,8},{16,20},{20,16},{24,28},{28,24},{1,5},{5... | collective-permute-start | bytes 1769480 | tf_op jit(solution)/shard_map/ppermute | solution.py:854
  223.5 16.3 %collective-permute-start.50 = (bf16[2,48,768]{2,1,0:T(8,128)(2,1)S(1)}, bf16[2,48,768]{2,1,0:T(8,128)(2,1)S(1)}, u32[]{:S(2)}, u32[]{:S(2)}) collective-permute-start(bf16[2,48,768]{2,1,0:T(8,128)(2,1)S(1)} %copy-done.49), channel_id=1, source_target_pairs={{0,1},{1,17},{2,3},{3,19},{4,5},{5,21},{6,7},{7,23},{8,9},{9,25},{... | collective-permute-start | bytes 442376 | tf_op jit(solution)/shard_map/ppermute | solution.py:1100
  225.9 20.1 %collective-permute-start.49 = (bf16[2,48,768]{2,1,0:T(8,128)(2,1)S(1)}, bf16[2,48,768]{2,1,0:T(8,128)(2,1)S(1)}, u32[]{:S(2)}, u32[]{:S(2)}) collective-permute-start(bf16[2,48,768]{2,1,0:T(8,128)(2,1)S(1)} %copy-done.48), channel_id=1, source_target_pairs={{0,0},{1,16},{2,2},{3,18},{4,4},{5,20},{6,6},{7,22},{8,8},{9,24},{... | collective-permute-start | bytes 442376 | tf_op jit(solution)/shard_map/ppermute | solution.py:1100
  236.8 18.3 %collective-permute-start.41 = (bf16[2,192,768]{2,1,0:T(8,128)(2,1)}, bf16[2,192,768]{2,1,0:T(8,128)(2,1)S(1)}, u32[]{:S(2)}, u32[]{:S(2)}) collective-permute-start(bf16[2,192,768]{2,1,0:T(8,128)(2,1)} %get-tuple-element.217), channel_id=1, source_target_pairs={{0,8},{4,12},{8,0},{12,4},{16,24},{20,28},{24,16},{28,20},{1,9},{5... | collective-permute-start | bytes 1769480 | tf_op jit(solution)/shard_map/ppermute | solution.py:854
  238.1 29.8 %collective-permute-start.54 = (bf16[2,96,768]{2,1,0:T(8,128)(2,1)S(1)}, bf16[2,96,768]{2,1,0:T(8,128)(2,1)S(1)}, u32[]{:S(2)}, u32[]{:S(2)}) collective-permute-start(bf16[2,96,768]{2,1,0:T(8,128)(2,1)S(1)} %copy-done.22), channel_id=1, source_target_pairs={{0,1},{1,17},{2,3},{3,19},{4,5},{5,21},{6,7},{7,23},{8,9},{9,25},{... | collective-permute-start | bytes 884744 | tf_op jit(solution)/shard_map/ppermute | solution.py:1100
  239.8 33.0 %collective-permute-start.53 = (bf16[2,96,768]{2,1,0:T(8,128)(2,1)S(1)}, bf16[2,96,768]{2,1,0:T(8,128)(2,1)S(1)}, u32[]{:S(2)}, u32[]{:S(2)}) collective-permute-start(bf16[2,96,768]{2,1,0:T(8,128)(2,1)S(1)} %copy-done.46), channel_id=1, source_target_pairs={{0,0},{1,16},{2,2},{3,18},{4,4},{5,20},{6,6},{7,22},{8,8},{9,24},{... | collective-permute-start | bytes 884744 | tf_op jit(solution)/shard_map/ppermute | solution.py:1100
  246.0 16.3 %collective-permute-start.43 = (bf16[1,192,768]{2,1,0:T(8,128)(2,1)}, bf16[1,192,768]{2,1,0:T(8,128)(2,1)S(1)}, u32[]{:S(2)}, u32[]{:S(2)}) collective-permute-start(bf16[1,192,768]{2,1,0:T(8,128)(2,1)} %get-tuple-element.221), channel_id=1, source_target_pairs={{0,4},{4,0},{8,12},{12,8},{16,20},{20,16},{24,28},{28,24},{1,5},{5... | collective-permute-start | bytes 884744 | tf_op jit(solution)/shard_map/ppermute | solution.py:854
  246.8 17.6 %collective-permute-start.44 = (bf16[1,192,768]{2,1,0:T(8,128)(2,1)}, bf16[1,192,768]{2,1,0:T(8,128)(2,1)S(1)}, u32[]{:S(2)}, u32[]{:S(2)}) collective-permute-start(bf16[1,192,768]{2,1,0:T(8,128)(2,1)} %get-tuple-element.222), channel_id=1, source_target_pairs={{0,2},{1,3},{2,0},{3,1},{4,6},{5,7},{6,4},{7,5},{8,10},{9,11},{10,... | collective-permute-start | bytes 884744 | tf_op jit(solution)/shard_map/ppermute | solution.py:846
  258.8 33.4 %collective-permute-start.52 = (bf16[2,96,768]{2,1,0:T(8,128)(2,1)}, bf16[2,96,768]{2,1,0:T(8,128)(2,1)S(1)}, u32[]{:S(2)}, u32[]{:S(2)}) collective-permute-start(bf16[2,96,768]{2,1,0:T(8,128)(2,1)} %get-tuple-element.218.refs_5_), channel_id=1, source_target_pairs={{0,1},{1,17},{2,3},{3,19},{4,5},{5,21},{6,7},{7,23},{8,9},{9,25},{... | collective-permute-start | bytes 884744 | tf_op jit(solution)/shard_map/ppermute | solution.py:1100
  267.9 15.2 %collective-permute-start.46 = (bf16[2,96,768]{2,1,0:T(8,128)(2,1)}, bf16[2,96,768]{2,1,0:T(8,128)(2,1)S(1)}, u32[]{:S(2)}, u32[]{:S(2)}) collective-permute-start(bf16[2,96,768]{2,1,0:T(8,128)(2,1)} %get-tuple-element.225), channel_id=1, source_target_pairs={{0,8},{4,12},{8,0},{12,4},{16,24},{20,28},{24,16},{28,20},{1,9},{5... | collective-permute-start | bytes 884744 | tf_op jit(solution)/shard_map/ppermute | solution.py:854
  268.0 24.2 %collective-permute-start.51 = (bf16[2,96,768]{2,1,0:T(8,128)(2,1)}, bf16[2,96,768]{2,1,0:T(8,128)(2,1)S(1)}, u32[]{:S(2)}, u32[]{:S(2)}) collective-permute-start(bf16[2,96,768]{2,1,0:T(8,128)(2,1)} %get-tuple-element.229), channel_id=1, source_target_pairs={{0,0},{1,16},{2,2},{3,18},{4,4},{5,20},{6,6},{7,22},{8,8},{9,24},{... | collective-permute-start | bytes 884744 | tf_op jit(solution)/shard_map/ppermute | solution.py:1100
  (74 other events, 384.8 us)

commit v3 on v2

--- a/solution.py
+++ b/solution.py
@@ -265,59 +265,42 @@
 def all_stats(sz, info, st_ref, rc_ref, rr_ref, rd_ref):
     side, width = sz.side, sz.width
     return in_tile_order(info, [read_stats(r, 3, width) for r in (
-        st_ref[...],
+        st_ref[side * PAD : side * PAD + 16, :],
         rc_ref[side * PAD : side * PAD + 16, :],
         rr_ref[RADIUS * side : RADIUS * side + 16, :],
         rd_ref[(RADIUS + 1) * PAD : (RADIUS + 1) * PAD + 16, :],
     )])
 
 
-def middle_kernel(sz, layer, last, info, *refs):
-    refs = list(refs)
-
-    def take(n):
-        out = refs[:n]
-        del refs[:n]
-        return out
-
-    (qkv_ref, st_ref, rc_ref, rr_ref, rd_ref, bias_ref, mask_ref, x_ref, own_mask_ref,
-     scale_a_ref, gain_m_ref, scale_m_ref, gain_a_ref) = take(13)
-    out_w, up_w, down_w = take(3)
-    if last:
-        cot_ref, cls_cot_ref, valid_ref = take(3)
-    else:
-        (qkv_w,) = take(1)
-    p_out, kb_out, vb_out, slope_out, x1_out, br_out, down_out, left_out, stat_ref = take(9)
-    if last:
-        po_ref, co_ref, right_out, g1_ref, vec_ref = take(5)
-    else:
-        x2_ref, next_ref, pc_ref, pr_ref, pd_ref = take(5)
-    (kext, vext, w_out, w_up, w_down, p_v, kb_v, vb_v, slope_v, x1_v, br_v, down_v, att, h2_v, act_v, acc) = take(16)
-    if last:
-        ed_v, eu_v, eb_v = take(3)
-    else:
-        w_qkv, h_v = take(2)
-    if layer == 0:
-        (first_v,) = take(1)
-    (sems,) = take(1)
+def middle_kernel(sz, layer, last, names, info, *refs):
+    r = dict(zip(names, refs))
+    qkv_ref, rc_ref, rr_ref, rd_ref = r["qkv"], r["rc"], r["rr"], r["rd"]
+    st_ref, bias_ref, mask_ref, x_ref = r["pc"], r["bias"], r["mask"], r["x"]
+    scale_a_ref, gain_m_ref, scale_m_ref, gain_a_ref = r["scale_a"], r["gain_m"], r["scale_m"], r["gain_a"]
+    w_out, w_up, w_down, stat_ref = r["w_out"], r["w_up"], r["w_down"], r["stats"]
+    p_v, kb_v, vb_v, slope_v, x1_v, br_v, down_v, left = (r[n] for n in ("p", "kb", "vb", "slope", "x1", "br", "down", "left"))
+    kext, vext, acc = r["kext"], r["vext"], r["acc"]
     width, side, cells, pitch, hidden = sz.width, sz.side, sz.cells, sz.pitch, sz.hidden
     chunks = hidden // width
-    copies = Copies(sems)
-    out_load = copies.load(out_w.at[layer], w_out)
-    up_loads, down_loads = [], []
-    for c in range(chunks):
-        at = pl.ds(c * width, width)
-        up_loads.append(copies.load(up_w.at[layer, :, at], w_up.at[:, at]))
-        down_loads.append(copies.load(down_w.at[layer, at, :], w_down.at[at, :]))
+    copies = Copies(r["sems"])
+
+    def hold(name, cols=None):
+        if not last:
+            src, dst = r[name], r[name + "_out"]
+            if cols is not None:
+                at = pl.ds(cols[0], cols[1])
+                src, dst = src.at[:, at], dst.at[:, at]
+            copies.store(src, dst)
+
     if not last:
         qkv_loads = [
-            copies.load(qkv_w.at[layer + 1, :, pl.ds(i * width, width)], w_qkv.at[:, pl.ds(i * width, width)])
+            copies.load(r["qkv_w"].at[layer + 1, :, pl.ds(i * width, width)], r["w_qkv"].at[:, pl.ds(i * width, width)])
             for i in range(3)
         ]
+        hold("qkv")
     extended(sz, info, qkv_ref, rc_ref, rr_ref, rd_ref, kext, vext)
     if layer == 0:
-        first_v[...] = (normalized(x_ref[...])[0] * gain_a_ref[0:1, :]).astype(BF)
-        copies.store(first_v, left_out.at[:, pl.ds(left_out.shape[1] - width, width)])
+        left[:, left.shape[1] - width :] = (normalized(x_ref[...])[0] * gain_a_ref[0:1, :]).astype(BF)
     class_rows = qkv_ref[cells : cells + 16, :].astype(F32)[0:PAD]
     scale = sz.head ** (-0.5)
     for b in range(sz.blocks):
@@ -331,17 +314,16 @@
         mask = jnp.concatenate([mask, mask], axis=1)
         for g in range(sz.groups):
             lanes = slice(g * sz.quad, (g + 1) * sz.quad)
-            scores = dot_nt(kb[:, lanes], stacked_heads(q[:, lanes], sz.head)) + bias_ref[g] + mask
+            scores = dot_nt(kb[:, lanes], stacked_heads(q[:, lanes], sz.head)) + bias_ref[layer, g] + mask
             top = jnp.max(scores, axis=0, keepdims=True)
             probs = jnp.exp(scores - top)
             total = jnp.sum(probs, axis=0, keepdims=True)
             probs = (probs * (1.0 / total)).astype(BF)
             p_v[b * sz.groups + g] = probs
             out = folded_heads(dot_tn(probs, vb[:, lanes]), sz.head)
-            att[b * sz.bq : (b + 1) * sz.bq, lanes] = out.astype(BF)
-    copies.store(kb_v, kb_out)
-    copies.store(vb_v, vb_out)
-    copies.store(p_v, p_out)
+            left[b * sz.bq : (b + 1) * sz.bq, lanes] = out.astype(BF)
+    for name in ("p", "kb", "vb"):
+        hold(name)
     ordered = all_stats(sz, info, st_ref, rc_ref, rr_ref, rd_ref)
     top = functools.reduce(jnp.maximum, [s[1] for s in ordered])
     total = jnp.zeros_like(top)
@@ -356,112 +338,89 @@
     stat_ref[1:2, :] = total
     stat_ref[2:3, :] = class_out
     row = lax.broadcasted_iota(jnp.int32, (16, width), 0)
-    att[cells : cells + 16, :] = jnp.where(row == 0, class_out, 0.0).astype(BF)
-    copies.store(att, left_out.at[:, pl.ds(0, width)])
-    out_load.wait()
-    branch = dot(att[...], w_out[...])
+    left[cells : cells + 16, 0:width] = jnp.where(row == 0, class_out, 0.0).astype(BF)
+    branch = dot(left[:, 0:width], w_out[...])
     br_v[...] = branch.astype(BF)
     x1_v[...] = x_ref[...] + scale_a_ref[layer : layer + 1, :] * branch
-    copies.store(br_v, br_out)
-    copies.store(x1_v, x1_out)
     unit, _ = normalized(x1_v[...])
-    h2_v[...] = (unit * gain_m_ref[layer : layer + 1, :]).astype(BF)
-    copies.store(h2_v, left_out.at[:, pl.ds(width, width)])
+    left[:, width : 2 * width] = (unit * gain_m_ref[layer : layer + 1, :]).astype(BF)
+    hold("br")
+    hold("x1")
+    hold("left", (0, 2 * width))
     for c in range(chunks):
         at = slice(c * width, (c + 1) * width)
-        up_loads[c].wait()
-        u = dot(h2_v[...], w_up[:, at])
+        u = dot(left[:, width : 2 * width], w_up[:, at])
         square = u * u
         th = jnp.tanh(GELU_C * u * (1.0 + 0.044715 * square))
         half = 0.5 * (1.0 + th)
-        act_v[:, at] = (u * half).astype(BF)
+        here = slice((c + 2) * width, (c + 3) * width)
+        left[:, here] = (u * half).astype(BF)
         slope = half + (0.5 * u) * (1.0 - th * th) * (GELU_C + (3 * 0.044715 * GELU_C) * square)
         slope_v[:, at] = slope.astype(BF)
-        down_loads[c].wait()
-        part = dot(act_v[:, at], w_down[at, :])
+        part = dot(left[:, here], w_down[at, :])
         if c == 0:
             acc[...] = part
         else:
             acc[...] += part
-    copies.store(act_v, left_out.at[:, pl.ds(2 * width, hidden)])
-    copies.store(slope_v, slope_out)
     down_v[...] = acc[...].astype(BF)
-    copies.store(down_v, down_out)
+    hold("slope")
+    hold("down")
+    hold("left", (2 * width, hidden))
     x2 = x1_v[...] + scale_m_ref[layer : layer + 1, :] * acc[...]
     if last:
-        po_ref[...] = (x2[0:cells] * valid_ref[...]).astype(BF)
-        co_ref[...] = x2[cells : cells + 1].astype(BF)
-        g_cells = cot_ref[...].astype(F32) * valid_ref[...]
-        g_class = jnp.where(row == 0, cls_cot_ref[...].astype(F32), 0.0)
+        valid_ref, vec_ref = r["valid"], r["vec"]
+        r["patch_out"][...] = (x2[0:cells] * valid_ref[...]).astype(BF)
+        r["cls_out"][...] = x2[cells : cells + 1].astype(BF)
+        g_cells = r["cot"][...].astype(F32) * valid_ref[...]
+        g_class = jnp.where(row == 0, r["cls_cot"][...].astype(F32), 0.0)
         g = jnp.concatenate([g_cells, g_class], axis=0)
         keep = keep_rows(sz.rows, cells, jnp.where(info[2] == 1, 1.0, 0.0))
         vec_ref[...] = jnp.zeros_like(vec_ref)
-        mlp_back_part(sz, layer, g, acc[...], keep, ed_v, eu_v, eb_v, right_out, 0, g1_ref, vec_ref, x1_v, br_v, slope_v,
-                      w_up, w_down, None, None, gain_m_ref, scale_a_ref, scale_m_ref, acc, copies)
+        mlp_back_part(sz, layer, g, acc[...], keep, r["right"], r["g1"], vec_ref, x1_v, br_v, slope_v,
+                      w_up, w_down, gain_m_ref, scale_a_ref, scale_m_ref, acc)
     else:
-        x2_ref[...] = x2
-        qkv_part(sz, info, x2, gain_a_ref[layer + 1 : layer + 2, :], w_qkv, qkv_loads, own_mask_ref[0:1, :],
-                 h_v, next_ref, pc_ref, pr_ref, pd_ref)
-        copies.store(h_v, left_out.at[:, pl.ds(2 * width + hidden, width)])
+        r["x2"][...] = x2
+        qkv_part(sz, info, x2, gain_a_ref[layer + 1 : layer + 2, :], r["w_qkv"], qkv_loads, r["own_mask"][0:1, :],
+                 left.at[:, pl.ds(2 * width + hidden, width)], r["next"], r["pc_out"], r["pr_out"], r["pd_out"])
+        hold("left", (2 * width + hidden, left.shape[1] - 2 * width - hidden))
     copies.finish()
 
 
-def mlp_back_part(sz, layer, g, down, keep, ed_ref, eu_v, eb_ref, right_out, at0, g1_ref, vec_ref, x1_ref, br_ref, slope_ref,
-                  w_up, w_down, up_loads, down_loads, gain_m_ref, scale_a_ref, scale_m_ref, acc, copies):
+def mlp_back_part(sz, layer, g, down, keep, right, g1_ref, vec_ref, x1_ref, br_ref, slope_ref,
+                  w_up, w_down, gain_m_ref, scale_a_ref, scale_m_ref, acc):
     width = sz.width
     vec_ref[0:1, :] = jnp.sum(keep * g * down, axis=0, keepdims=True)
-    e_down = (scale_m_ref[layer : layer + 1, :] * g).astype(BF)
-    ed_ref[...] = e_down
-    copies.store(ed_ref, right_out.at[:, pl.ds(at0, width)])
+    right[:, 0:width] = (scale_m_ref[layer : layer + 1, :] * g).astype(BF)
     g1_ref[...] = g
     for c in range(sz.hidden // width):
         at = slice(c * width, (c + 1) * width)
-        if down_loads is not None:
-            for copy in down_loads[c]:
-                copy.wait()
-        e_up = (dot_nt(ed_ref[...], w_down[at, :]) * slope_ref[:, at].astype(F32)).astype(BF)
-        eu_v[:, at] = e_up
-        if up_loads is not None:
-            up_loads[c].wait()
-        part = dot_nt(eu_v[:, at], w_up[:, at])
+        e_up = (dot_nt(right[:, 0:width], w_down[at, :]) * slope_ref[:, at].astype(F32)).astype(BF)
+        here = slice((c + 1) * width, (c + 2) * width)
+        right[:, here] = e_up
+        part = dot_nt(right[:, here], w_up[:, at])
         if c == 0:
             acc[...] = part
         else:
             acc[...] += part
-    copies.store(eu_v, right_out.at[:, pl.ds(at0 + width, sz.hidden)])
     d_x1, gain_rows = norm_back(x1_ref[...], gain_m_ref[layer : layer + 1, :], acc[...])
     vec_ref[1:2, :] = jnp.sum(keep * gain_rows, axis=0, keepdims=True)
     g1 = g1_ref[...] + d_x1
     g1_ref[...] = g1
-    eb_ref[...] = (scale_a_ref[layer : layer + 1, :] * g1).astype(BF)
-    copies.store(eb_ref, right_out.at[:, pl.ds(at0 + width + sz.hidden, width)])
+    right[:, width + sz.hidden :] = (scale_a_ref[layer : layer + 1, :] * g1).astype(BF)
     vec_ref[2:3, :] = jnp.sum(keep * g1 * br_ref[...].astype(F32), axis=0, keepdims=True)
 
 
-def attention_back_kernel(sz, layer, info, eb_ref, qkv_ref, stat_ref, own_mask_ref, w_any, p_any, kb_any, vb_any,
+def attention_back_kernel(sz, layer, info, right, qkv_ref, stat_ref, own_mask_ref, p_v, kb_v, vb_v, w,
                           dq_ref, dkv_ref, pc_ref, pr_ref, pd_ref, tab_ref,
-                          kext, vext, d_o, tab, w, p_v, kb_v, vb_v, sems):
+                          kext, vext, d_o, tab):
     width, side, cells, pitch = sz.width, sz.side, sz.cells, sz.pitch
     scale = sz.head ** (-0.5)
-    copies = Copies(sems)
-    w_load = copies.load(w_any.at[layer], w)
-    loads = []
-    for b in range(sz.blocks):
-        at = pl.ds(b * sz.groups, sz.groups)
-        loads.append([
-            copies.load(vb_any.at[b], vb_v.at[b]),
-            copies.load(p_any.at[at], p_v.at[at]),
-            copies.load(kb_any.at[b], kb_v.at[b]),
-        ])
     kext[...] = jnp.zeros_like(kext)
     vext[...] = jnp.zeros_like(vext)
-    w_load.wait()
-    d_o[...] = dot_nt(eb_ref[...], w[...])
+    d_o[...] = dot_nt(right[:, right.shape[1] - width :], w[...])
     class_k = [jnp.zeros((PAD, sz.quad), F32) for _ in range(sz.groups)]
     class_v = [jnp.zeros((PAD, sz.quad), F32) for _ in range(sz.groups)]
     for b in range(sz.blocks):
-        for copy in loads[b]:
-            copy.wait()
         first = b * sz.brows * pitch
         q = qkv_ref[b * sz.bq : (b + 1) * sz.bq, 0:width] * jnp.asarray(scale, BF)
         do = d_o[b * sz.bq : (b + 1) * sz.bq, :].astype(BF)
@@ -546,7 +505,7 @@
     tab_ref[sz.heads : 16, :] = jnp.zeros((16 - sz.heads, sz.bk), F32)
 
 
-def qkv_back_part(sz, info, dq_ref, dkv_ref, st_ref, rc_ref, rr_ref, rd_ref, x_ref, gain, g1_ref, eq_ref, dkv, acc, wq, loads):
+def qkv_back_part(sz, info, dq_ref, dkv_ref, st_ref, rc_ref, rr_ref, rd_ref, x_ref, gain, g1_ref, eq_ref, dkv, acc, wq):
     width, side, cells = sz.width, sz.side, sz.cells
     dkv[...] = dkv_ref[...]
     beside = PAD * (1 - info[1])
@@ -568,7 +527,6 @@
     eq_ref[cells : cells + 16, :] = jnp.where(row == 0, class_row, 0.0).astype(BF)
     for i in range(3):
         cols = slice(i * width, (i + 1) * width)
-        loads[i].wait()
         part = dot_nt(eq_ref[:, cols], wq[:, cols])
         if i == 0:
             acc[...] = part
@@ -586,12 +544,10 @@
 
 
 def qkv_back_kernel(sz, layer, info, dq_ref, dkv_ref, st_ref, rc_ref, rr_ref, rd_ref, x_ref, g1_ref, vec_ref, tab_ref,
-                    gain_a_ref, qkv_w, eq_ref, ek_ref, ev_ref, small_ref, g_ref, dkv, acc, wq, eq_v, sems):
+                    gain_a_ref, wq, eq_ref, ek_ref, ev_ref, small_ref, g_ref, dkv, acc, eq_v):
     width = sz.width
-    copies = Copies(sems)
-    loads = [copies.load(qkv_w.at[layer, :, pl.ds(i * width, width)], wq.at[:, pl.ds(i * width, width)]) for i in range(3)]
     g, gain_rows = qkv_back_part(sz, info, dq_ref, dkv_ref, st_ref, rc_ref, rr_ref, rd_ref, x_ref,
-                                 gain_a_ref[layer : layer + 1, :], g1_ref, eq_v, dkv, acc, wq, loads)
+                                 gain_a_ref[layer : layer + 1, :], g1_ref, eq_v, dkv, acc, wq)
     for i, ref in enumerate((eq_ref, ek_ref, ev_ref)):
         ref[...] = eq_v[:, i * width : (i + 1) * width]
     keep = keep_rows(sz.rows, sz.cells, jnp.where(info[2] == 1, 1.0, 0.0))
@@ -600,30 +556,21 @@
 
 
 def mlp_back_kernel(sz, layer, info, g_ref, gain_m_ref, scale_a_ref, scale_m_ref, x1_ref, br_ref, down_ref,
-                    up_w, down_w, slope_any, right_out, g1_out, vec_out, acc, w_up, w_down, slope_v, ed_v, eu_v, eb_v, sems):
-    width = sz.width
-    copies = Copies(sems)
-    up_loads, down_loads, slope_loads = [], [], []
-    for c in range(sz.hidden // width):
-        at = pl.ds(c * width, width)
-        down_loads.append(copies.load(down_w.at[layer, at, :], w_down.at[at, :]))
-        slope_loads.append(copies.load(slope_any.at[:, at], slope_v.at[:, at]))
-        up_loads.append(copies.load(up_w.at[layer, :, at], w_up.at[:, at]))
+                    slope_ref, w_up, w_down, right, g1_out, vec_out, acc):
     keep = keep_rows(sz.rows, sz.cells, jnp.where(info[2] == 1, 1.0, 0.0))
     vec_out[...] = jnp.zeros_like(vec_out)
-    mlp_back_part(sz, layer, g_ref[...], down_ref[...].astype(F32), keep, ed_v, eu_v, eb_v, right_out, 0, g1_out, vec_out,
-                  x1_ref, br_ref, slope_v, w_up, w_down, up_loads, [(a, b) for a, b in zip(down_loads, slope_loads)],
-                  gain_m_ref, scale_a_ref, scale_m_ref, acc, copies)
-    copies.finish()
-
-
-def last_kernel(sz, info, dq_ref, dkv_ref, st_ref, rc_ref, rr_ref, rd_ref, x_ref, g1_ref, vec_ref, tab_ref, gain_a_ref, qkv_w,
-                eq_ref, ek_ref, ev_ref, small_ref, pg_ref, cg_ref, dkv, acc, wq, eq_v, sems):
+    mlp_back_part(sz, layer, g_ref[...], down_ref[...].astype(F32), keep, right, g1_out, vec_out,
+                  x1_ref, br_ref, slope_ref, w_up, w_down, gain_m_ref, scale_a_ref, scale_m_ref, acc)
+
+
+def last_kernel(sz, info, dq_ref, dkv_ref, st_ref, rc_ref, rr_ref, rd_ref, patch_ref, cls_ref, g1_ref, vec_ref, tab_ref,
+                gain_a_ref, wq, eq_ref, ek_ref, ev_ref, small_ref, pg_ref, cg_ref, dkv, acc, x_ref, eq_v):
     width = sz.width
-    copies = Copies(sems)
-    loads = [copies.load(qkv_w.at[0, :, pl.ds(i * width, width)], wq.at[:, pl.ds(i * width, width)]) for i in range(3)]
+    row = lax.broadcasted_iota(jnp.int32, (16, width), 0)
+    x_ref[0 : sz.cells, :] = patch_ref[...].astype(F32)
+    x_ref[sz.cells :, :] = jnp.where(row == 0, cls_ref[...].astype(F32), 0.0)
     g, gain_rows = qkv_back_part(sz, info, dq_ref, dkv_ref, st_ref, rc_ref, rr_ref, rd_ref, x_ref,
-                                 gain_a_ref[0:1, :], g1_ref, eq_v, dkv, acc, wq, loads)
+                                 gain_a_ref[0:1, :], g1_ref, eq_v, dkv, acc, wq)
     for i, ref in enumerate((eq_ref, ek_ref, ev_ref)):
         ref[...] = eq_v[:, i * width : (i + 1) * width]
     keep = keep_rows(sz.rows, sz.cells, jnp.where(info[2] == 1, 1.0, 0.0))
@@ -655,9 +602,9 @@
     return [(a, a | 1 << bit) for a in range(1 << bits) if not a >> bit & 1]
 
 
-def place_of(bits, skip, me):
-    def place(a):
-        names = [b for b in range(bits - 1, -1, -1) if b != skip]
+def order_of(bits, skip, first):
+    def place(a, me):
+        names = list(first) + [b for b in range(bits - 1, -1, -1) if b != skip and b not in first]
         at = 0
         for b in names:
             mine = (a >> b) & 1
@@ -667,56 +614,34 @@
     return place
 
 
-def order_of(bits, skip, first):
-    def place(a, me):
-        names = [first] + [b for b in range(bits - 1, -1, -1) if b not in (skip, first)]
-        at = 0
-        for b in names:
-            mine = (a >> b) & 1
-            at = at * 2 + (mine if b == 0 else mine ^ ((me >> b) & 1))
-        return at
-
-    return place
-
-
 def down_kernel(sz, info, act_ref, act_got, own_ref, other_ref, send_ref, keep_ref):
     bits = sz.bits - 2
     me = info[4]
     value = product(sz, info, act_ref, act_got, own_ref, other_ref)
-    place = order_of(bits, 2, 1)
+    place = order_of(bits, 2, (1,))
     store_pieces(value, 1 << bits, pairs_of(bits, 2), (me >> 2) & 1, lambda a: place(a, me), send_ref, keep_ref)
 
 
-def columns_step(sz, info, outer, value, send_ref, keep_ref):
+def columns_step(sz, info, bit, order, value, send_ref, keep_ref):
     bits = sz.bits - 1
     me = info[4]
-    bit, other = (1, 2) if outer else (2, 1)
-    place = order_of(bits, bit, other)
+    place = order_of(bits, bit, order)
     store_pieces(value, 1 << bits, pairs_of(bits, bit), (me >> bit) & 1, lambda a: place(a, me), send_ref, keep_ref)
 
 
 def up_kernel(sz, info, h_ref, h_got, own_ref, other_ref, send_ref, keep_ref):
-    columns_step(sz, info, True, product(sz, info, h_ref, h_got, own_ref, other_ref), send_ref, keep_ref)
-
-
-def attn_grad_kernel(sz, info, h_ref, h_got, qo, qg, ko, kg, vo, vg, a_ref, a_got, bo, bg, s0, k0, s1, k1):
+    columns_step(sz, info, 1, (2,), product(sz, info, h_ref, h_got, own_ref, other_ref), send_ref, keep_ref)
+
+
+def attn_grad_kernel(sz, info, h_ref, h_got, qo, qg, ko, kg, vo, vg, a_ref, a_got, bo, bg, send_ref, keep_ref):
     step = pl.program_id(0)
-
-    @pl.when(step == 0)
-    def _():
-        columns_step(sz, info, True, product(sz, info, h_ref, h_got, qo, qg), s0, k0)
-
-    @pl.when(step == 1)
-    def _():
-        columns_step(sz, info, True, product(sz, info, h_ref, h_got, ko, kg), s0, k0)
-
-    @pl.when(step == 2)
-    def _():
-        columns_step(sz, info, False, product(sz, info, h_ref, h_got, vo, vg), s1, k1)
-
-    @pl.when(step == 3)
-    def _():
-        columns_step(sz, info, False, product(sz, info, a_ref, a_got, bo, bg), s1, k1)
+    bit = sz.bits - 2
+    cases = [(h_ref, h_got, qo, qg, (1, 2)), (h_ref, h_got, ko, kg, (1, 2)), (h_ref, h_got, vo, vg, (2, 1)),
+             (a_ref, a_got, bo, bg, (2, 1))]
+    for i, (*factors, order) in enumerate(cases):
+        @pl.when(step == i)
+        def _():
+            columns_step(sz, info, bit, order, product(sz, info, *factors), send_ref, keep_ref)
 
 
 def plus(a, b):
@@ -740,6 +665,26 @@
 def more_kernel(info, k, g, s_ref, k_ref):
     s_ref[...] = plus(k[:, 1], g[:, 1]).astype(BF)
     k_ref[...] = plus(k[:, 0], g[:, 0]).astype(BF)
+
+
+def z_second_kernel(info, k, g, s0_ref, s1_ref, k_ref):
+    for i, ref in enumerate((s0_ref, s1_ref)):
+        ref[...] = plus(k[i, 1], g[i, 1]).astype(BF)
+        k_ref[i] = plus(k[i, 0], g[i, 0]).astype(BF)
+
+
+def z_third_kernel(info, k, g0, g1, s0_ref, s1_ref, k_ref):
+    for i, (g, ref) in enumerate(((g0, s0_ref), (g1, s1_ref))):
+        ref[...] = plus(k[i, 1], g[1]).astype(BF)
+        k_ref[i] = plus(k[i, 0], g[0]).astype(BF)
+
+
+def z_fourth_kernel(sz, info, k, g0, g1, a_ref, b_ref):
+    high = (info[4] >> (sz.bits - 1)) & 1
+    for i, g in enumerate((g0, g1)):
+        one, two = plus(k[i, 0], g[0]), plus(k[i, 1], g[1])
+        a_ref[i] = jnp.where(high == 0, one, two).astype(BF)
+        b_ref[i] = jnp.where(high == 0, two, one).astype(BF)
 
 
 def fourth_kernel(sz, info, k, g, a_ref, b_ref):
@@ -770,11 +715,19 @@
     return pltpu.HBM(dims, dtype)
 
 
+def inside(dims, dtype):
+    return pltpu.VMEM(dims, dtype)
+
+
 def whole(dims):
     return pl.BlockSpec(dims, lambda *_: (0,) * len(dims))
 
 
+IN = pl.BlockSpec(memory_space=pltpu.VMEM)
+
+
 ANY = pl.BlockSpec(memory_space=pl.ANY)
+MEDIUM = 4 * 10**9
 LONG = 10**11
 
 
@@ -811,34 +764,76 @@
     first_slot = PAD - RADIUS
     lines = jnp.pad(lines, ((0, 0), (0, 0), (first_slot, sz.bk - first_slot - SPAN * sz.pitch)), constant_values=MASKED)
 
+    resident = {}
     before = []
 
-    def call(kernel, grid, in_specs, out_specs, out_shape, scratch=(), vmem=56, weight=1, also=()):
+    def call(kernel, grid, in_specs, out_specs, out_shape, scratch=(), vmem=12, weight=1, also=(), place=pltpu.HBM, ahead=()):
         deps = list(before) + list(also)
         count = len(in_specs)
 
+        results = list(out_shape) if isinstance(out_shape, (list, tuple)) else [out_shape]
+        result_specs = list(out_specs) if isinstance(out_specs, (list, tuple)) else [out_specs]
+        more, own = len(ahead), len(results)
+
         def body(*refs):
-            return kernel(*refs[: 1 + count], *refs[1 + count + len(deps) :])
+            refs = list(refs)
+            mine, refs = refs[: 1 + count], refs[1 + count + len(deps) :]
+            sources, refs = refs[:more], refs[more:]
+            made, refs = refs[:own], refs[own:]
+            targets, refs = refs[:more], refs[more:]
+            if not more:
+                return kernel(*mine, *made, *refs)
+            sem = refs.pop()
+            copies = [
+                pltpu.make_async_copy(src if index is None else src.at[index], dst, sem.at[n])
+                for n, (src, dst, (_, index)) in enumerate(zip(sources, targets, ahead))
+            ]
+
+            @pl.when(pl.program_id(0) == 0)
+            def _():
+                for copy in copies:
+                    copy.start()
+
+            kernel(*mine, *made, *refs)
+
+            @pl.when(pl.program_id(0) == pl.num_programs(0) - 1)
+            def _():
+                for copy in copies:
+                    copy.wait()
+
+        results += [inside(a.shape if index is None else a.shape[1:], a.dtype) for a, index in ahead]
+        if more:
+            scratch = list(scratch) + [pltpu.SemaphoreType.DMA((more,))]
 
         run = pl.pallas_call(
             body,
             grid_spec=pltpu.PrefetchScalarGridSpec(
                 num_scalar_prefetch=1,
                 grid=grid,
-                in_specs=list(in_specs) + [ANY] * len(deps),
-                out_specs=out_specs,
+                in_specs=list(in_specs) + [ANY] * (len(deps) + more),
+                out_specs=result_specs + [IN] * more,
                 scratch_shapes=list(scratch),
             ),
-            out_shape=out_shape,
+            out_shape=results,
             compiler_params=pltpu.CompilerParams(vmem_limit_bytes=vmem * MIB),
             cost_estimate=pl.CostEstimate(flops=weight, bytes_accessed=1, transcendentals=0),
         )
 
         def go(*args):
-            pinned = [pltpu.with_memory_space_constraint(a, pltpu.HBM) for a in args]
-            out = run(info, *pinned, *deps)
-            before[:] = [out[-1] if isinstance(out, (list, tuple)) else out]
-            return out
+            pinned = []
+            for a, spec in zip(args, in_specs):
+                if id(a) in resident:
+                    a = pltpu.with_memory_space_constraint(a, pltpu.VMEM)
+                elif spec is not IN and place is not None:
+                    a = pltpu.with_memory_space_constraint(a, pltpu.HBM if spec is ANY else place)
+                pinned.append(a)
+            sources = [pltpu.with_memory_space_constraint(a, pltpu.HBM) for a, _ in ahead]
+            out = run(info, *pinned, *deps, *sources)
+            for a, like in zip(out, results):
+                if not isinstance(like, jax.ShapeDtypeStruct) and like.memory_space == pltpu.VMEM:
+                    resident[id(a)] = a
+            before[:] = [out[own - 1]]
+            return out if len(results) > 1 else out[0]
 
         return go
 
@@ -863,7 +858,7 @@
     row_w, par = whole((rows, width)), whole((layers, width))
     wide = whole((rows, 3 * width))
     pc_rows, pr_rows, pd_rows = side * PAD + 16, RADIUS * side + 16, (RADIUS + 1) * PAD + 16
-    rim_shapes = [kept((n, 2 * width), BF) for n in (pc_rows, pr_rows, pd_rows)]
+    rim_shapes = [shape((n, 2 * width), BF) for n in (pc_rows, pr_rows, pd_rows)]
     rim_specs = [whole(s.shape) for s in rim_shapes]
     stat_spec = pl.BlockSpec((16, 2 * width), lambda *_: (side * PAD // 16, 0))
     nb, ng = sz.blocks, sz.groups
@@ -873,119 +868,131 @@
         functools.partial(first_kernel, sz),
         (1,),
         [whole((cells, width)), whole((1, width)), par, whole((8, cells)), ANY],
-        [row_w, wide] + rim_specs,
-        [kept((rows, width), F32), kept((rows, 3 * width), BF)] + rim_shapes,
+        [IN] * 5,
+        [inside((rows, width), F32), inside((rows, 3 * width), BF)] + rim_shapes,
         [vm((rows, width), BF), vm((width, 3 * width), BF), sems],
     )(patch_in.reshape(cells, width), cls_in, norm_attn, own_mask, qkv_weight)
     got = exchange(rims)
-    bias = call(
+    bias, w_out, w_up, w_down, gain_a, scale_a, gain_m, scale_m = call(
         lambda info, *refs: bias_kernel(sz, *refs),
         (layers,),
         [pl.BlockSpec((None, 16, sz.bk), lambda l, s: (l, 0, 0))],
         pl.BlockSpec((None, ng, sz.bk, sz.bk), lambda l, s: (l, 0, 0, 0)),
-        kept((layers, ng, sz.bk, sz.bk), F32),
+        inside((layers, ng, sz.bk, sz.bk), F32),
         [vm((sz.bk, sz.bk), F32)],
+        ahead=[(out_weight, 0), (up_weight, 0), (down_weight, 0)]
+        + [(v, None) for v in (norm_attn, scale_attn, norm_mlp, scale_mlp)],
     )(lines)
     saved = []
     for l in range(layers):
         last = l == layers - 1
-        ins = [wide, stat_spec] + rim_specs + [
-            pl.BlockSpec((None, ng, sz.bk, sz.bk), lambda i, s, l=l: (l, 0, 0, 0)), whole(key_mask.shape), row_w,
-            whole((8, cells)), par, par, par, par, ANY, ANY, ANY]
-        args = [qkv, rims[0], *got, bias, key_mask, x, own_mask, scale_attn, norm_mlp, scale_mlp, norm_attn,
-                out_weight, up_weight, down_weight]
-        held = [((nb * ng, sz.bk, sz.bk), BF), ((nb, sz.bk, width), BF), ((nb, sz.bk, width), BF), ((rows, hidden), BF),
-                ((rows, width), F32), ((rows, width), BF), ((rows, width), BF)]
+        given = dict(qkv=qkv, pc=rims[0], rc=got[0], rr=got[1], rd=got[2], bias=bias, mask=key_mask, x=x, own_mask=own_mask,
+                     scale_a=scale_a, gain_m=gain_m, scale_m=scale_m, gain_a=gain_a,
+                     w_out=w_out, w_up=w_up, w_down=w_down)
         left_width = 2 * width + hidden + (0 if last else width) + (0 if l else width)
-        scratch = [vm((sz.ext_rows, width), F32)] * 2 + [vm(square, BF), vm((width, hidden), BF), vm((hidden, width), BF)]
-        scratch += [vm(d, t) for d, t in held]
-        scratch += [vm((rows, width), BF), vm((rows, width), BF), vm((rows, hidden), BF), vm((rows, width), F32)]
-        outs = [kept(d, t) for d, t in held] + [kept((rows, left_width), BF), kept((8, width), F32)]
-        out_specs = [ANY] * (len(held) + 1) + [whole((8, width))]
+        held = dict(p=((nb * ng, sz.bk, sz.bk), BF), kb=((nb, sz.bk, width), BF), vb=((nb, sz.bk, width), BF),
+                    left=((rows, left_width), BF))
+        local_only = dict(slope=((rows, hidden), BF), x1=((rows, width), F32), br=((rows, width), BF), down=((rows, width), BF))
+        made = dict(stats=inside((8, width), F32))
+        spots = dict(kext=vm((sz.ext_rows, width), F32), vext=vm((sz.ext_rows, width), F32), acc=vm((rows, width), F32))
+        spots.update({n: vm(*d) for n, d in local_only.items()})
         if last:
-            ins += [whole((cells, width)), whole((1, width)), whole((cells, 1))]
-            args += [patch_cot.reshape(cells, width), cls_cot, valid]
-            out_specs += [whole((cells, width)), whole((1, width)), ANY, row_w, whole((8, width))]
-            outs += [kept((cells, width), BF), kept((1, width), BF), kept((rows, 2 * width + hidden), BF),
-                     kept((rows, width), F32), kept((8, width), F32)]
-            scratch += [vm((rows, width), BF), vm((rows, hidden), BF), vm((rows, width), BF)]
+            given.update(cot=cot, cls_cot=cls_cot, valid=valid)
+            made.update({n: inside(*d) for n, d in held.items()})
+            made.update(right=inside((rows, 2 * width + hidden), BF), g1=inside((rows, width), F32), vec=inside((8, width), F32),
+                        patch_out=shape((cells, width), BF), cls_out=shape((1, width), BF))
+            specs = [IN] * len(made)
         else:
-            ins += [ANY]
-            args += [qkv_weight]
-            out_specs += [row_w, wide] + rim_specs
-            outs += [kept((rows, width), F32), kept((rows, 3 * width), BF)] + rim_shapes
-            scratch += [vm((width, 3 * width), BF), vm((rows, width), BF)]
-        if l == 0:
-            scratch += [vm((rows, width), BF)]
-        out = call(functools.partial(middle_kernel, sz, l, last), (1,), ins, out_specs, outs, scratch + [sems],
-                   )(*args)
-        p, kb, vb, slope, x1, branch, down, left, stats = out[:9]
-        saved.append(dict(x=x, qkv=qkv, p=p, kb=kb, vb=vb, slope=slope, x1=x1, branch=branch, down=down, stats=stats,
-                          left=both(left), h=None))
-        if l == 0:
-            saved[0]["h"] = (saved[0]["left"], left_width // width - 1)
+            given.update(qkv_w=qkv_weight)
+            made.update(x2=inside((rows, width), F32), next=inside((rows, 3 * width), BF),
+                        pc_out=rim_shapes[0], pr_out=rim_shapes[1], pd_out=rim_shapes[2])
+            specs = [IN] * len(made)
+            spots.update({n: vm(*d) for n, d in held.items()})
+            spots.update(w_qkv=vm((width, 3 * width), BF))
+            stored = dict(held, **local_only, qkv=((rows, 3 * width), BF))
+            made = dict({n + "_out": kept(*d) for n, d in stored.items()}, **made)
+            specs = [ANY] * len(stored) + specs
+        spots.update(sems=sems)
+        names = list(given) + list(made) + list(spots)
+        out = call(functools.partial(middle_kernel, sz, l, last, names), (1,),
+                   [ANY if n == "qkv_w" else IN for n in given], specs, list(made.values()), list(spots.values()), vmem=18 if last else 28,
+                   )(*given.values())
+        res = dict(zip(made, out))
+        keep_names = list(held) if last else list(stored)
+        entry = {n: res[n if last else n + "_out"] for n in keep_names}
+        entry.setdefault("qkv", qkv)
+        entry.update(x=x, stats=res["stats"])
+        entry["left"] = both(entry["left"])
+        entry["h"] = (entry["left"], left_width // width - 1) if l == 0 else (saved[l - 1]["left"], 2 + chunks)
+        saved.append(entry)
+        if last:
+            patch_out, cls_out, right, g1, vec = (res[n] for n in ("patch_out", "cls_out", "right", "g1", "vec"))
         else:
-            saved[l]["h"] = (saved[l - 1]["left"], 2 + chunks)
-        if last:
-            patch_out, cls_out, right, g1, vec = out[9:]
-        else:
-            x, qkv, *rims = out[9:]
+            x, qkv = res["x2"], res["next"]
+            rims = [res[n] for n in ("pc_out", "pr_out", "pd_out")]
             got = exchange(rims)
-
-    def attention_back(l, right, at, also):
-        kept_l = saved[l]
+            _, w_out, w_up, w_down, cot = call(
+                lambda info, a, b: None, (1,), [ANY], [ANY], [kept((8, width), F32)],
+                ahead=[(out_weight, l + 1), (up_weight, l + 1), (down_weight, l + 1), (patch_cot.reshape(cells, width), None)],
+                vmem=2,
+            )(x)
+
+    def attention_back(l, right, v, also):
         return call(
             functools.partial(attention_back_kernel, sz, l),
             (1,),
-            [pl.BlockSpec((rows, width), lambda i, s: (0, at)), wide, whole((8, width)), whole((8, cells)), ANY, ANY, ANY, ANY],
-            [whole((cells, width)), whole((cells, 2 * width))] + rim_specs + [whole((16, sz.bk))],
-            [kept((cells, width), BF), kept((cells, 2 * width), F32)] + rim_shapes + [kept((16, sz.bk), F32)],
-            [vm((sz.ext_rows, width), F32)] * 2 + [vm((rows, width), F32), vm((ng, sz.bk, sz.bk), F32), vm(square, BF),
-             vm((nb * ng, sz.bk, sz.bk), BF), vm((nb, sz.bk, width), BF), vm((nb, sz.bk, width), BF), sems],
-            also=also,
-        )(right, kept_l["qkv"], kept_l["stats"], own_mask, out_weight, kept_l["p"], kept_l["kb"], kept_l["vb"])
-
-    back_ins = [whole((cells, width)), whole((cells, 2 * width)), stat_spec] + rim_specs + [
-        row_w, row_w, whole((8, width)), whole((16, sz.bk))]
-    back_scratch = [vm((cells, 2 * width), F32), vm((rows, width), F32), vm((width, 3 * width), BF)]
-
-    def qkv_back(l, d_q, d_kv, own, got, g1, vec, table):
-        *e_qkv, rows_small, g = call(
+            [IN] * 8,
+            [IN] * 6,
+            [inside((cells, width), BF), inside((cells, 2 * width), F32)] + rim_shapes + [inside((16, sz.bk), F32)],
+            [vm((sz.ext_rows, width), F32)] * 2 + [vm((rows, width), F32), vm((ng, sz.bk, sz.bk), F32)],
+            also=also, ahead=[(qkv_weight, l)] + ([] if l else [(patch_in.reshape(cells, width), None)]),
+        )(right, v["qkv"], v["stats"], own_mask, v["p"], v["kb"], v["vb"], v["w_out"])
+
+    back_scratch = [vm((cells, 2 * width), F32), vm((rows, width), F32)]
+
+    def qkv_back(l, d_q, d_kv, own, got, g1, vec, table, wq):
+        *e_qkv, rows_small, g, down_w, up_w = call(
             functools.partial(qkv_back_kernel, sz, l),
             (1,),
-            back_ins + [par, ANY],
-            [row_w, row_w, row_w, whole((24, width)), row_w],
-            [kept((rows, width), BF)] * 3 + [kept((24, width), F32), kept((rows, width), F32)],
-            back_scratch + [vm((rows, 3 * width), BF), sems],
-            weight=LONG,
-        )(d_q, d_kv, own, *got, saved[l]["x"], g1, vec, table, norm_attn, qkv_weight)
-        return [both(e) for e in e_qkv], rows_small, g
-
-    def mlp_back(l, g):
-        low = saved[l]
-        return call(
+            [IN] * 12,
+            [IN] * 5,
+            [inside((rows, width), BF)] * 3 + [inside((24, width), F32), inside((rows, width), F32)],
+            back_scratch + [vm((rows, 3 * width), BF)],
+            weight=LONG, ahead=[(down_weight, l - 1), (up_weight, l - 1)],
+        )(d_q, d_kv, own, *got, saved[l]["x"], g1, vec, table, gain_a, wq)
+        return [both(e) for e in e_qkv], rows_small, g, up_w, down_w
+
+    def mlp_back(l, g, up_w, down_w):
+        v = saved[l]
+        names = ["qkv", "p", "kb", "vb"]
+        out = call(
             functools.partial(mlp_back_kernel, sz, l),
             (1,),
-            [row_w, par, par, par, row_w, row_w, row_w, ANY, ANY, ANY],
-            [ANY, row_w, whole((8, width))],
-            [kept((rows, 2 * width + hidden), BF), kept((rows, width), F32), kept((8, width), F32)],
-            [vm((rows, width), F32), vm((width, hidden), BF), vm((hidden, width), BF), vm((rows, hidden), BF),
-             vm((rows, width), BF), vm((rows, hidden), BF), vm((rows, width), BF), sems],
-        )(g, norm_mlp, scale_attn, scale_mlp, low["x1"], low["branch"], low["down"], up_weight, down_weight, low["slope"])
-
-    def finish(d_q, d_kv, own, got, g1, vec, table):
+            [IN] * 10,
+            [IN] * 3,
+            [inside((rows, 2 * width + hidden), BF), inside((rows, width), F32), inside((8, width), F32)],
+            [vm((rows, width), F32)],
+            ahead=[(v[n], None) for n in names] + [(out_weight, l)],
+        )(g, gain_m, scale_a, scale_m, v["x1"], v["br"], v["down"], v["slope"], up_w, down_w)
+        near = dict(zip(names + ["w_out"], out[3:]), stats=v["stats"])
+        return out[0], out[1], out[2], near
+
+    def finish(d_q, d_kv, own, got, g1, vec, table, wq, first):
         return call(
             functools.partial(last_kernel, sz),
             (1,),
-            back_ins + [par, ANY],
-            [row_w, row_w, row_w, whole((24, width)), whole((cells, width)), whole((1, width))],
-            [kept((rows, width), BF)] * 3 + [kept((24, width), F32), kept((cells, width), F32), kept((1, width), F32)],
-            back_scratch + [vm((rows, 3 * width), BF), sems],
-        )(d_q, d_kv, own, *got, saved[0]["x"], g1, vec, table, norm_attn, qkv_weight)
+            [IN] * 13,
+            [IN] * 6,
+            [inside((rows, width), BF)] * 3 + [inside((24, width), F32), shape((cells, width), F32), shape((1, width), F32)],
+            back_scratch + [vm((rows, width), F32), vm((rows, 3 * width), BF)],
+        )(d_q, d_kv, own, *got, first, cls_in, g1, vec, table, gain_a, wq)
 
     piece, ff_piece = width // sz.devices, hidden // sz.devices
     half = width // 2
     quarter = sz.devices // 4
+
+    def pair(dims):
+        return [shape(dims, BF), inside(dims, BF)]
 
     def halves(start):
         return pl.BlockSpec((rows, half), lambda i, s: (0, 2 * start + s[1]))
@@ -999,11 +1006,12 @@
             (2,),
             [lspec, lspec, rspec, rspec],
             [out, out],
-            [kept((2, quarter // 2, ff_piece, width), BF)] * 2,
+            pair((2, quarter // 2, ff_piece, width)),
             weight=weight, also=also,
+            vmem=20, place=None,
         )(*act[0], *e_down[0])
 
-    def grad_up(h2, e_up):
+    def grad_up(h2, e_up, also=()):
         lspec = halves(h2[1])
         rspec = pl.BlockSpec((rows, width), lambda i, s: (0, e_up[1] + i))
         out = pl.BlockSpec((quarter, None, piece, width), lambda i, s: (0, i, 0, 0))
@@ -1012,24 +1020,74 @@
             (chunks,),
             [lspec, lspec, rspec, rspec],
             [out, out],
-            [kept((quarter, chunks, piece, width), BF)] * 2,
+            pair((quarter, chunks, piece, width)),
+            also=also, vmem=20, place=None,
         )(*h2[0], *e_up[0])
 
-    def grad_attn(h, e_qkv, att, e_branch, weight=1):
-        def block(index):
-            return pl.BlockSpec((quarter, None, piece, width), lambda i, s: (0, index(i), 0, 0))
-
-        first, second = block(lambda i: jnp.minimum(i, 1)), block(lambda i: jnp.maximum(i - 2, 0))
+    def grad_attn(h, e_qkv, att, e_branch):
+        out = pl.BlockSpec((None, quarter, None, piece, width), lambda i, s: (i // 2, 0, i % 2, 0, 0))
         hspec, aspec = halves(h[1]), halves(att[1])
         bspec = pl.BlockSpec((rows, width), lambda i, s: (0, e_branch[1]))
         return call(
             functools.partial(attn_grad_kernel, sz),
             (4,),
             [hspec, hspec] + [row_w] * 6 + [aspec, aspec, bspec, bspec],
-            [first, first, second, second],
-            [kept((quarter, 2, piece, width), BF)] * 4,
-            weight=weight,
-        )(*h[0], *(v for pair in e_qkv for v in pair), *att[0], *e_branch[0])
+            [out, out],
+            pair((2, quarter, 2, piece, width)),
+            vmem=20, place=None,
+        )(*h[0], *(v for both_e in e_qkv for v in both_e), *att[0], *e_branch[0])
+
+    def last_route(flip):
+        out = []
+        for d in range(sz.devices):
+            high, core = d >> top_bit, d & 1
+            out.append((d, (d & ~(1 << top_bit) & ~1) | core << top_bit | (high ^ flip)))
+        return out
+
+    class ZSums:
+        def __init__(self, halves_made):
+            send, keep = halves_made
+            self.n = quarter * 2 * piece // 2
+            self.got = swap(send, next_bit).reshape(2, 2, self.n, width)
+            self.keep = keep.reshape(2, 2, self.n, width)
+
+        def second(self, weight=1):
+            n = self.n
+            s0, s1, k = call(
+                z_second_kernel, (1,), [whole((2, 2, n, width))] * 2, [whole((n, width))] * 2 + [whole((2, n, width))],
+                [shape((n, width), BF)] * 2 + [inside((2, n, width), BF)], place=None, weight=weight,
+            )(self.keep, self.got)
+            self.got = [swap(s0, 1), swap(s1, 2)]
+            self.keep = k
+
+        def third(self):
+            n = self.n = self.n // 2
+            s0, s1, k = call(
+                z_third_kernel, (1,), [whole((2, 2, n, width))] + [whole((2, n, width))] * 2,
+                [whole((n, width))] * 2 + [whole((2, n, width))],
+                [shape((n, width), BF)] * 2 + [inside((2, n, width), BF)], place=None,
+            )(self.keep.reshape(2, 2, n, width), *(g.reshape(2, n, width) for g in self.got))
+            self.got = [swap(s0, 2), swap(s1, 1)]
+            self.keep = k
+            for bit in range(bits - 3, 2, -1):
+                n = self.n = self.n // 2
+                spec = whole((2, 2, n, width))
+                s, k = call(
+                    more_kernel, (1,), [spec, spec], [whole((2, n, width))] * 2, pair((2, n, width)), place=None,
+                )(self.keep.reshape(2, 2, n, width), jnp.stack(self.got).reshape(2, 2, n, width))
+                self.keep = k
+                self.got = list(swap(s, bit))
+
+        def fourth(self):
+            n = self.n = self.n // 2
+            a, b = call(
+                functools.partial(z_fourth_kernel, sz), (1,), [whole((2, 2, n, width))] + [whole((2, n, width))] * 2,
+                [whole((2, n, width))] * 2, [shape((2, n, width), BF)] * 2, place=None,
+            )(self.keep.reshape(2, 2, n, width), *(g.reshape(2, n, width) for g in self.got))
+            self.got = [lax.ppermute(a, ("dp", "tile"), last_route(0)), lax.ppermute(b, ("dp", "tile"), last_route(1))]
+
+        def result(self):
+            return self.got[0].astype(F32) + self.got[1].astype(F32)
 
     class Sums:
         def __init__(self, y_first, x_first, split):
@@ -1041,7 +1099,7 @@
             self.rows = total
             self.keep = [k0.reshape(1, 2, total // 2, width), k1.reshape(split, 2, total // 2 // split, width)]
 
-        def second(self, weight=1):
+        def second(self, weight=1, also=()):
             n = self.rows // 4
             got = [g.reshape(k.shape) for g, k in zip(self.got, self.keep)]
             sp = self.outer
@@ -1055,7 +1113,7 @@
             spec_out = pl.BlockSpec((1, n, width), lambda i, s: (0, i, 0))
             s0, k0, s1, k1 = call(
                 second_kernel, (2,), [spec, spec, other, other], [spec_out, spec_out, other_out, other_out],
-                [kept((1, 2 * n, width), BF)] * 2 + [kept((sp, 2 * n // sp, width), BF)] * 2, weight=weight,
+                pair((1, 2 * n, width)) + pair((sp, 2 * n // sp, width)), weight=weight, place=None, also=also,
             )(self.keep[0], got[0], self.keep[1], got[1])
             self.got = [swap(s0, 2), swap(s1, 1)]
             self.keep = [k0, k1]
@@ -1066,7 +1124,7 @@
             args = [v.reshape(2, n, width) for pair in zip(self.keep, self.got) for v in pair]
             s, k = call(
                 third_kernel, (1,), [whole((2, n, width))] * 4, [whole((2, n, width))] * 2,
-                [kept((2, n, width), BF)] * 2, weight=weight,
+                pair((2, n, width)), weight=weight, place=None,
             )(*args)
             self.rows = n
             self.keep = k
@@ -1075,7 +1133,7 @@
                 n = self.rows // 2
                 spec = whole((2, 2, n, width))
                 s, k = call(
-                    more_kernel, (1,), [spec, spec], [whole((2, n, width))] * 2, [kept((2, n, width), BF)] * 2,
+                    more_kernel, (1,), [spec, spec], [whole((2, n, width))] * 2, pair((2, n, width)), place=None,
                 )(self.keep.reshape(2, 2, n, width), self.got.reshape(2, 2, n, width))
                 self.rows = n
                 self.keep = k
@@ -1086,18 +1144,10 @@
             spec = whole((2, 2, n, width))
             a, b = call(
                 functools.partial(fourth_kernel, sz), (1,), [spec, spec], [whole((2, n, width))] * 2,
-                [kept((2, n, width), BF)] * 2,
+                [shape((2, n, width), BF)] * 2, place=None,
             )(self.keep.reshape(2, 2, n, width), self.got.reshape(2, 2, n, width))
 
-            def route(flip):
-                out = []
-                for d in range(sz.devices):
-                    high, core = d >> top_bit, d & 1
-                    to = (d & ~(1 << top_bit) & ~1) | core << top_bit | (high ^ flip)
-                    out.append((d, to))
-                return out
-
-            self.got = [lax.ppermute(a, ("dp", "tile"), route(0)), lax.ppermute(b, ("dp", "tile"), route(1))]
+            self.got = [lax.ppermute(a, ("dp", "tile"), last_route(0)), lax.ppermute(b, ("dp", "tile"), last_route(1))]
 
         def result(self):
             return self.got[0].astype(F32) + self.got[1].astype(F32)
@@ -1106,51 +1156,64 @@
     small = [None] * layers
     early = [v["left"][1] for v in saved[:-1]]
     waiting = None
+    near = dict(saved[-1], w_out=w_out)
     for l in reversed(range(layers)):
         left = saved[l]["left"]
+        result = attention_back(l, right, near, early)
+        d_q, d_kv, *rims, table, wq = result[:7]
+        if l == 0:
+            first = result[7]
+        early = []
         if waiting is not None:
-            quads = grad_attn(*waiting)
-            sums["attn", l + 1] = Sums(quads[0:2], quads[2:4], 1)
-        d_q, d_kv, *rims, table = attention_back(l, right, 1 + chunks, early)
-        early = []
-        if l + 1 < layers:
             right = both(lax.optimization_barrier((right, table))[0])
             got = exchange(rims)
-            sums["mlp", l + 1].second()
-            sums["attn", l + 1].second(LONG)
-            x_first = grad_down((left, 2), (right, 0), 1, got)
+            sums["attn", l + 1] = ZSums(grad_attn(*waiting))
+            sums["mlp", l + 1].second(LONG)
         else:
             right = both(right)
             got = exchange(rims)
-            x_first = grad_down((left, 2), (right, 0))
-        y_first = grad_up((left, 1), (right, 1))
+        x_first = grad_down((left, 2), (right, 0))
+        y_first = grad_up((left, 1), (right, 1), got if waiting is not None else ())
         sums["mlp", l] = Sums(y_first, x_first, 2)
-        if l + 1 < layers:
-            sums["mlp", l + 1].third(LONG)
-            sums["attn", l + 1].third()
         if l > 0:
-            e_qkv, small[l], g = qkv_back(l, d_q, d_kv, rims[0], got, g1, vec, table)
+            e_qkv, small[l], g, up_w, down_w = qkv_back(l, d_q, d_kv, rims[0], got, g1, vec, table, wq)
             waiting = (saved[l]["h"], e_qkv, (left, 0), (right, 1 + chunks))
-            right, g1, vec = mlp_back(l - 1, g)
+            right, g1, vec, near = mlp_back(l - 1, g, up_w, down_w)
         else:
-            *e_qkv, small[0], patch_grad, cls_grad = finish(d_q, d_kv, rims[0], got, g1, vec, table)
+            *e_qkv, small[0], patch_grad, cls_grad = finish(d_q, d_kv, rims[0], got, g1, vec, table, wq, first)
             waiting = (saved[0]["h"], [both(e) for e in e_qkv], (left, 0), (right, 1 + chunks))
+    total = [jnp.stack(small), None, 0]
+
+    def step():
+        value, got_value, bit = total
+        if got_value is not None:
+            value = value + lax.optimization_barrier((got_value, before[0]))[0]
+        total[:] = [value, swap(value, bit) if bit < bits else None, bit + 1]
+
+    step()
     if layers > 1:
+        sums["mlp", 1].third()
+    sums["attn", 0] = ZSums(grad_attn(*waiting))
+    step()
+    if layers > 1:
+        sums["attn", 1].second(MEDIUM)
+    sums["mlp", 0].second()
+    step()
+    if layers > 1:
+        sums["attn", 1].third()
         sums["mlp", 1].fourth()
+    sums["mlp", 0].third()
+    step()
+    sums["attn", 0].second()
+    if layers > 1:
         sums["attn", 1].fourth()
-    sums["mlp", 0].second(LONG)
-    quads = grad_attn(*waiting)
-    sums["attn", 0] = Sums(quads[0:2], quads[2:4], 1)
-    total = jnp.stack(small)
-    bit = 0
-    for run in (sums["mlp", 0].third, sums["attn", 0].second, sums["mlp", 0].fourth, sums["attn", 0].third, sums["attn", 0].fourth):
-        if bit < bits:
-            total = lax.optimization_barrier((total, before[0]))[0]
-            total = total + swap(total, bit)
-            bit += 1
-        run()
-    for bit in range(bit, bits):
-        total = total + swap(total, bit)
+    step()
+    sums["attn", 0].third()
+    sums["mlp", 0].fourth()
+    while total[1] is not None:
+        step()
+    sums["attn", 0].fourth()
+    total = total[0]
     ups, downs, firsts, seconds = [], [], [], []
     for l in range(layers):
         mlp, attn = sums["mlp", l].result(), sums["attn", l].result()

time: 302 us -> 255 us (0.84)
  Pallas kernels: 171 us -> 109 us
  waiting for transfers between devices: 28.8 us -> 53.4 us
  starting transfers between devices: 69.3 us -> 59.2 us
  other arithmetic: 4.2 us -> 8.88 us
  local copies, waits for them, and re-layouts: 22.8 us -> 18.5 us
    pallas_call x27 -> x28, Pallas kernels: 171 us -> 109 us  [go(): out = run(info, *pinned, *deps, *sources)]
    ppermute x8, waiting for transfers between devices: 0.02 us -> 16.9 us  [the longest x4 13.4 us: fourth(): lax.ppermute(a, ('dp', 'tile'), last_route(0))]
    ppermute x8, starting transfers between devices: 30 us -> 19.2 us  [the longest x4 13.9 us: fourth(): lax.ppermute(a, ('dp', 'tile'), last_route(0))]
    ppermute x32, waiting for transfers between devices: 11.5 us -> 21.1 us  [partner(): return lax.ppermute(value, 'tile', [(t, t ^ x) for t in range(tiles)])]
    unnamed x104 -> x86, local copies, waits for them, and re-layouts: 16.6 us -> 12.8 us
  transfers between devices with their start and end apart: 55 -> 55, of which waited for: 7 -> 12; matrix products, arithmetic and copies ran while one was open for 2% -> 5% of each run, Pallas kernels for 50% -> 36%
where the time goes in v3:
time: 255 us; the launch traced here: 251 us
  Pallas kernels  109 us (43%)
  starting transfers between devices  59.2 us (23%)
  waiting for transfers between devices  53.4 us (21%)
  local copies, waits for them, and re-layouts  18.5 us (7%)
  other arithmetic  8.88 us (3%)
    pallas_call x28, Pallas kernels, go(): out = run(info, *pinned, *deps, *sources)  109 us
    ppermute x32, starting transfers between devices, partner(): return lax.ppermute(value, 'tile', [(t, t ^ x) for t in range(tiles)])  27 us
    ppermute x32, waiting for transfers between devices, partner(): return lax.ppermute(value, 'tile', [(t, t ^ x) for t in range(tiles)])  21.1 us
    ppermute x15, waiting for transfers between devices, swap(): lax.ppermute(value, 'dp', [(d, d ^ 1 << bit - 2) for d in range(pages)])  15.4 us
    ppermute x4, starting transfers between devices, fourth(): lax.ppermute(a, ('dp', 'tile'), last_route(0))  13.9 us
    ppermute x4, waiting for transfers between devices, fourth(): lax.ppermute(a, ('dp', 'tile'), last_route(0))  13.4 us
    ppermute x15, starting transfers between devices, swap(): lax.ppermute(value, 'dp', [(d, d ^ 1 << bit - 2) for d in range(pages)])  13 us
    unnamed x86, local copies, waits for them, and re-layouts  12.8 us
  transfers between devices with their start and end apart: 55, of which 12 were waited for; matrix products, arithmetic and copies ran while one was open for 5% of the time, Pallas kernels for 36%

profile of v3, /device:TPU:1, one launch (start us, length us, event | category | flops | bytes accessed | tf_op | source)
XLA Modules:
  0.0 251.1 jit_solution(6785972375345183597)
XLA Ops:
  2.7 6.1 %shard_map.282 = (f32[272,768]{1,0:T(8,128)S(1)}, bf16[272,2304]{1,0:T(8,128)(2,1)S(1)}, bf16[144,1536]{1,0:T(8,128)(2,1)S(1)}, bf16[64,1536]{1,0:T(8,128)(2,1)}, bf16[48,1536]{1,0:T(8,128)(2,1)S(1)}) custom-call(s32[5]{0:T(128)S(1)} %stack.48.refs_0_, bf16[256,768]{1,0:T(8,128)(2,1)} %bitcast.104, bf16[1,768]{1,0:T(2,128)(2,1)} %refs_8_.3, ...), custom_call_target="tpu_custom_call" | custom-call | flops 1 | bytes 1 | tf_op jit(solution)/shard_map/pallas_call | solution.py:831
  8.9 2.7 %collective-permute-start.1 = (bf16[64,1536]{1,0:T(8,128)(2,1)}, bf16[64,1536]{1,0:T(8,128)(2,1)S(1)}, u32[]{:S(2)}, u32[]{:S(2)}) collective-permute-start(bf16[64,1536]{1,0:T(8,128)(2,1)} %get-tuple-element.144), channel_id=1, source_target_pairs={{0,2},{1,3},{2,0},{3,1},{4,6},{5,7},{6,4},{7,5},{8,10},{9,11},{10,... | collective-permute-start | bytes 589832 | tf_op jit(solution)/shard_map/ppermute | solution.py:841
  14.2 6.1 %shard_map.283 = (f32[2,3,256,256]{3,2,1,0:T(8,128)S(1)}, bf16[768,768]{1,0:T(8,128)(2,1)S(1)}, bf16[768,3072]{1,0:T(8,128)(2,1)S(1)}, bf16[3072,768]{1,0:T(8,12...) custom-call(s32[5]{0:T(128)S(1)} %stack.48.refs_0_, ...), custom_call_target="tpu_custom_call" | custom-call | flops 1 | bytes 1 | tf_op jit(solution)/shard_map/pallas_call | solution.py:831
  20.6 11.3 %shard_map.284 = (bf16[12,256,256]{2,1,0:T(8,128)(2,1)}, bf16[4,256,768]{2,1,0:T(8,128)(2,1)}, bf16[4,256,768]{2,1,0:T(8,128)(2,1)}, bf16[272,6144]{1,0:T(8,128)...) custom-call(s32[5]{0:T(128)S(1)} %stack.48.refs_0_, ...), custom_call_target="tpu_custom_call" | custom-call | flops 1 | bytes 1 | tf_op jit(solution)/shard_map/pallas_call | solution.py:831
  37.8 4.9 %shard_map.285 = (f32[8,768]{1,0:T(8,128)}, bf16[768,768]{1,0:T(8,128)(2,1)S(1)}, bf16[768,3072]{1,0:T(8,128)(2,1)S(1)}, bf16[3072,768]{1,0:T(8,128)(2,1)S(1)}, bf16[256,768]{1,0:T(8,128)(2,1)S(1)}) custom-call(s32[5]{0:T(128)S(1)} %stack.48.refs_0_, f32[272,768]{1,0:T(8,128)S(1)} %copy-done.8, bf16[48,1536]{1,0:T(8,128)(2,1)} %get-tuple-element.158.refs_2_, ...), custom_call_target="tpu_custom_call" | custom-call | flops 1 | bytes 1 | tf_op jit(solution)/shard_map/pallas_call | solution.py:831
  42.7 2.0 collective-permute-done.5.refs_5_
  45.5 13.1 %shard_map.286 = (f32[8,768]{1,0:T(8,128)S(1)}, bf16[12,256,256]{2,1,0:T(8,128)(2,1)S(1)}, bf16[4,256,768]{2,1,0:T(8,128)(2,1)S(1)}, bf16[4,256,768]{2,1,0:T(8,1...) custom-call(s32[5]{0:T(128)S(1)} %stack.48.refs_0_, ...), custom_call_target="tpu_custom_call" | custom-call | flops 1 | bytes 1 | tf_op jit(solution)/shard_map/pallas_call | solution.py:831
  59.9 7.6 %shard_map.287 = (bf16[256,768]{1,0:T(8,128)(2,1)S(1)}, f32[256,1536]{1,0:T(8,128)S(1)}, bf16[144,1536]{1,0:T(8,128)(2,1)S(1)}, bf16[64,1536]{1,0:T(8,128)(2,1)S...) custom-call(s32[5]{0:T(128)S(1)} %stack.48.refs_0_, ...), custom_call_target="tpu_custom_call" | custom-call | flops 1 | bytes 1 | tf_op jit(solution)/shard_map/pallas_call | solution.py:831
  71.5 3.9 %shard_map.288 = (bf16[2,4,96,768]{3,2,1,0:T(8,128)(2,1)}, bf16[2,4,96,768]{3,2,1,0:T(8,128)(2,1)S(1)}) custom-call(s32[5]{0:T(128)S(1)} %stack.48.refs_0_, bf16[272,4608]{1,0:T(8,128)(2,1)S(1)} %get-tuple-element.182.refs_1_.refs_9_, bf16[272,4608]{1,0:T(8,128)(2,1)S(1)} %collective-permute-done.10.refs_2_.refs_10_, ...), custom_call_target="tpu_custom_call" | custom-call | flops 1 | bytes 1 | tf_op jit(solution)/shard_map/pallas_call | solution.py:831
  75.4 4.7 %shard_map.289 = (bf16[8,4,24,768]{3,2,1,0:T(8,128)(2,1)}, bf16[8,4,24,768]{3,2,1,0:T(8,128)(2,1)S(1)}) custom-call(s32[5]{0:T(128)S(1)} %stack.48.refs_0_, bf16[272,4608]{1,0:T(8,128)(2,1)S(1)} %get-tuple-element.182.refs_1_.refs_9_, bf16[272,4608]{1,0:T(8,128)(2,1)S(1)} %collective-permute-done.10.refs_2_.refs_10_, ...), custom_call_target="tpu_custom_call" | custom-call | flops 1 | bytes 1 | tf_op jit(solution)/shard_map/pallas_call | solution.py:831
  82.9 5.0 %shard_map.290 = (bf16[272,768]{1,0:T(8,128)(2,1)S(1)}, bf16[272,768]{1,0:T(8,128)(2,1)S(1)}, bf16[272,768]{1,0:T(8,128)(2,1)S(1)}, f32[24,768]{1,0:T(8,128)S(1)...) custom-call(s32[5]{0:T(128)S(1)} %stack.48.refs_0_, ...), custom_call_target="tpu_custom_call" | custom-call | flops 99999997952 | bytes 1 | tf_op jit(solution)/shard_map/pallas_call | solution.py:831
  88.8 4.7 %shard_map.291 = (bf16[272,4608]{1,0:T(8,128)(2,1)S(1)}, f32[272,768]{1,0:T(8,128)S(1)}, f32[8,768]{1,0:T(8,128)S(1)}, bf16[272,2304]{1,0:T(8,128)(2,1)S(1)}, bf...) custom-call(s32[5]{0:T(128)S(1)} %stack.48.refs_0_, ...), custom_call_target="tpu_custom_call" | custom-call | flops 1 | bytes 1 | tf_op jit(solution)/shard_map/pallas_call | solution.py:831
  93.5 7.6 %shard_map.292 = (bf16[256,768]{1,0:T(8,128)(2,1)S(1)}, f32[256,1536]{1,0:T(8,128)S(1)}, bf16[144,1536]{1,0:T(8,128)(2,1)S(1)}, bf16[64,1536]{1,0:T(8,128)(2,1)S...) custom-call(s32[5]{0:T(128)S(1)} %stack.48.refs_0_, ...), custom_call_target="tpu_custom_call" | custom-call | flops 1 | bytes 1 | tf_op jit(solution)/shard_map/pallas_call | solution.py:831
  102.0 4.4 %shard_map.293 = (bf16[2,8,2,24,768]{4,3,2,1,0:T(8,128)(2,1)S(1)}, bf16[2,8,2,24,768]{4,3,2,1,0:T(8,128)(2,1)S(1)}) custom-call(s32[5]{0:T(128)S(1)} %stack.48.refs_0_, bf16[272,6144]{1,0:T(8,128)(2,1)S(1)} %copy-done, bf16[272,6144]{1,0:T(8,128)(2,1)S(1)} %collective-permute-done.6.refs_10_.refs_2_, bf16[272,768]{1,0:T(8,128)(2,1)S(1)} %get-tuple-element.216.refs_3_, ...), custom_call_target="tpu_custom_call" | custom-call | flops 1 | bytes 1 | tf_op jit(solution)/shard_map/pallas_call | solution.py:831
  109.7 2.5 shard_map.294
  114.9 3.1 %shard_map.295 = (bf16[2,4,96,768]{3,2,1,0:T(8,128)(2,1)S(1)}, bf16[2,4,96,768]{3,2,1,0:T(8,128)(2,1)S(1)}) custom-call(s32[5]{0:T(128)S(1)} %stack.48.refs_0_, bf16[272,6144]{1,0:T(8,128)(2,1)S(1)} %copy-done, bf16[272,6144]{1,0:T(8,128)(2,1)S(1)} %collective-permute-done.6.refs_10_.refs_2_, ...), custom_call_target="tpu_custom_call" | custom-call | flops 1 | bytes 1 | tf_op jit(solution)/shard_map/pallas_call | solution.py:831
  118.4 3.8 %shard_map.296 = (bf16[8,4,24,768]{3,2,1,0:T(8,128)(2,1)S(1)}, bf16[8,4,24,768]{3,2,1,0:T(8,128)(2,1)S(1)}) custom-call(s32[5]{0:T(128)S(1)} %stack.48.refs_0_, bf16[272,6144]{1,0:T(8,128)(2,1)S(1)} %copy-done, bf16[272,6144]{1,0:T(8,128)(2,1)S(1)} %collective-permute-done.6.refs_10_.refs_2_, ...), custom_call_target="tpu_custom_call" | custom-call | flops 1 | bytes 1 | tf_op jit(solution)/shard_map/pallas_call | solution.py:831
  122.2 3.1 %shard_map.297 = (bf16[272,768]{1,0:T(8,128)(2,1)S(1)}, bf16[272,768]{1,0:T(8,128)(2,1)S(1)}, bf16[272,768]{1,0:T(8,128)(2,1)S(1)}, f32[24,768]{1,0:T(8,128)S(1)}, f32[256,768]{1,0:T(8,128)}, /*index=5*/f32[1,768]{1,0:T(1,128)}) custom-call(s32[5]{0:T(128)S(1)} %stack.48.refs_0_, bf16[256,768]{1,0:T(8,128)(2,1)S(1)} %get-tuple-element.204.refs_1_, ...), custom_call_target="tpu_custom_call" | custom-call | flops 1 | bytes 1 | tf_op jit(solution)/shard_map/pallas_call | solution.py:831
  125.4 4.4 %collective-permute-start.22 = (bf16[272,768]{1,0:T(8,128)(2,1)S(1)}, bf16[272,768]{1,0:T(8,128)(2,1)S(1)}, u32[]{:S(2)}, u32[]{:S(2)}) collective-permute-start(bf16[272,768]{1,0:T(8,128)(2,1)S(1)} %get-tuple-element.227.refs_3_), channel_id=1, source_target_pairs={{0,1},{1,0},{2,3},{3,2},{4,5},{5,4},{6,7},{7,6},{8,9},{9,8},{10,11... | collective-permute-start | bytes 1253384 | tf_op jit(solution)/shard_map/ppermute | solution.py:841
  131.3 2.7 %collective-permute-start.23 = (bf16[272,768]{1,0:T(8,128)(2,1)S(1)}, bf16[272,768]{1,0:T(8,128)(2,1)S(1)}, u32[]{:S(2)}, u32[]{:S(2)}) collective-permute-start(bf16[272,768]{1,0:T(8,128)(2,1)S(1)} %get-tuple-element.228.refs_5_), channel_id=1, source_target_pairs={{0,1},{1,0},{2,3},{3,2},{4,5},{5,4},{6,7},{7,6},{8,9},{9,8},{10,11... | collective-permute-start | bytes 1253384 | tf_op jit(solution)/shard_map/ppermute | solution.py:841
  136.0 4.6 %shard_map.299 = (bf16[2,8,2,24,768]{4,3,2,1,0:T(8,128)(2,1)}, bf16[2,8,2,24,768]{4,3,2,1,0:T(8,128)(2,1)S(1)}) custom-call(s32[5]{0:T(128)S(1)} %stack.48.refs_0_, bf16[272,6144]{1,0:T(8,128)(2,1)S(1)} %copy-done, bf16[272,6144]{1,0:T(8,128)(2,1)S(1)} %collective-permute-done.6.refs_10_.refs_2_, bf16[272,768]{1,0:T(8,128)(2,1)S(1)} %get-tuple-element.227.refs_3_, ...), custom_call_target="tpu_custom_call" | custom-call | flops 1 | bytes 1 | tf_op jit(solution)/shard_map/pallas_call | solution.py:831
  144.1 13.7 %collective-permute-done.28 = bf16[8,4,24,768]{3,2,1,0:T(8,128)(2,1)S(1)} collective-permute-done((bf16[8,4,24,768]{3,2,1,0:T(8,128)(2,1)S(1)}, bf16[8,4,24,768]{3,2,1,0:T(8,128)(2,1)S(1)}, u32[]{:S(2)}, u32[]{:S(2)}) %collective-permute-start.28) | collective-permute-done | bytes 1179680 | tf_op jit(solution)/shard_map/ppermute | solution.py:841
  160.6 3.5 %collective-permute-done.35 = bf16[192,768]{1,0:T(8,128)(2,1)S(1)} collective-permute-done((bf16[192,768]{1,0:T(8,128)(2,1)S(1)}, bf16[192,768]{1,0:T(8,128)(2,1)S(1)}, u32[]{:S(2)}, u32[]{:S(2)}) %collective-permute-start.35) | collective-permute-done | bytes 294944 | tf_op jit(solution)/shard_map/ppermute | solution.py:841
  167.6 13.2 %collective-permute-done.34 = bf16[2,192,768]{2,1,0:T(8,128)(2,1)S(1)} collective-permute-done((bf16[2,192,768]{2,1,0:T(8,128)(2,1)S(1)}, bf16[2,192,768]{2,1,0:T(8,128)(2,1)S(1)}, u32[]{:S(2)}, u32[]{:S(2)}) %collective-permute-start.34) | collective-permute-done | bytes 589856 | tf_op jit(solution)/shard_map/ppermute | solution.py:849
  182.3 2.3 collective-permute-start.54
  184.6 3.4 %collective-permute-start.53 = (bf16[2,96,768]{2,1,0:T(8,128)(2,1)}, bf16[2,96,768]{2,1,0:T(8,128)(2,1)}, u32[]{:S(2)}, u32[]{:S(2)}) collective-permute-start(bf16[2,96,768]{2,1,0:T(8,128)(2,1)} %get-tuple-element.270), channel_id=1, source_target_pairs={{0,0},{1,16},{2,2},{3,18},{4,4},{5,20},{6,6},{7,22},{8,8},{9,24},{... | collective-permute-start | bytes 884744 | tf_op jit(solution)/shard_map/ppermute | solution.py:1150
  206.8 4.1 %collective-permute-start.49 = (bf16[2,48,768]{2,1,0:T(8,128)(2,1)S(1)}, bf16[2,48,768]{2,1,0:T(8,128)(2,1)}, u32[]{:S(2)}, u32[]{:S(2)}) collective-permute-start(bf16[2,48,768]{2,1,0:T(8,128)(2,1)S(1)} %get-tuple-element.268), channel_id=1, source_target_pairs={{0,0},{1,16},{2,2},{3,18},{4,4},{5,20},{6,6},{7,22},{8,8},{9,24},{... | collective-permute-start | bytes 442376 | tf_op jit(solution)/shard_map/ppermute | solution.py:1087
  214.3 3.5 %collective-permute-done.50 = bf16[2,48,768]{2,1,0:T(8,128)(2,1)} collective-permute-done((bf16[2,48,768]{2,1,0:T(8,128)(2,1)S(1)}, bf16[2,48,768]{2,1,0:T(8,128)(2,1)}, u32[]{:S(2)}, u32[]{:S(2)}) %collective-permute-start.50) | collective-permute-done | bytes 147488 | tf_op jit(solution)/shard_map/ppermute | solution.py:1087
  225.7 4.2 %collective-permute-start.47 = (bf16[2,48,768]{2,1,0:T(8,128)(2,1)S(1)}, bf16[2,48,768]{2,1,0:T(8,128)(2,1)S(1)}, u32[]{:S(2)}, u32[]{:S(2)}) collective-permute-start(bf16[2,48,768]{2,1,0:T(8,128)(2,1)S(1)} %get-tuple-element.266), channel_id=1, source_target_pairs={{0,0},{1,16},{2,2},{3,18},{4,4},{5,20},{6,6},{7,22},{8,8},{9,24},{... | collective-permute-start | bytes 442376 | tf_op jit(solution)/shard_map/ppermute | solution.py:1087
  231.4 2.3 collective-permute-start.51
  234.3 5.1 %collective-permute-done.47 = bf16[2,48,768]{2,1,0:T(8,128)(2,1)S(1)} collective-permute-done((bf16[2,48,768]{2,1,0:T(8,128)(2,1)S(1)}, bf16[2,48,768]{2,1,0:T(8,128)(2,1)S(1)}, u32[]{:S(2)}, u32[]{:S(2)}) %collective-permute-start.47) | collective-permute-done | bytes 147488 | tf_op jit(solution)/shard_map/ppermute | solution.py:1087
  241.2 7.6 %collective-permute-done.51 = bf16[2,96,768]{2,1,0:T(8,128)(2,1)S(1)} collective-permute-done((bf16[2,96,768]{2,1,0:T(8,128)(2,1)S(1)}, bf16[2,96,768]{2,1,0:T(8,128)(2,1)S(1)}, u32[]{:S(2)}, u32[]{:S(2)}) %collective-permute-start.51) | collective-permute-done | bytes 294944 | tf_op jit(solution)/shard_map/ppermute | solution.py:1150
  (236 shorter events, 77.9 us)
Async XLA Ops:
  33.9 25.3 %collective-permute-start.6 = (bf16[272,6144]{1,0:T(8,128)(2,1)}, bf16[272,6144]{1,0:T(8,128)(2,1)S(1)}, u32[]{:S(2)}, u32[]{:S(2)}) collective-permute-start(bf16[272,6144]{1,0:T(8,128)(2,1)} %get-tuple-element.172.refs_1_.refs_9_), channel_id=1, source_target_pairs={{0,1},{1,0},{2,3},{3,2},{4,5},{5,4},{6,7},{7,6},{8,9},{9,8},{10,11... | collective-permute-start | bytes 10027016 | tf_op jit(solution)/shard_map/ppermute | solution.py:841
  58.6 12.9 %collective-permute-start.10 = (bf16[272,4608]{1,0:T(8,128)(2,1)S(1)}, bf16[272,4608]{1,0:T(8,128)(2,1)S(1)}, u32[]{:S(2)}, u32[]{:S(2)}) collective-permute-start(bf16[272,4608]{1,0:T(8,128)(2,1)S(1)} %get-tuple-element.182.refs_1_.refs_9_), channel_id=1, source_target_pairs={{0,1},{1,0},{2,3},{3,2},{4,5},{5,4},{6,7},{7,6},{8,9},{9,8},{10,11... | collective-permute-start | bytes 7520264 | tf_op jit(solution)/shard_map/ppermute | solution.py:841
  58.8 12.7 %collective-permute-start.11 = (bf16[272,4608]{1,0:T(8,128)(2,1)S(1)}, bf16[272,4608]{1,0:T(8,128)(2,1)S(1)}, u32[]{:S(2)}, u32[]{:S(2)}) collective-permute-start(bf16[272,4608]{1,0:T(8,128)(2,1)S(1)} %get-tuple-element.167.refs_1_.refs_3_.refs_11_), channel_id=1, source_target_pairs={{0,1},{1,0},{2,3},{3,2},{4,5},{5,4},{6,7},{7,6},{8,9},{9,8},{10,11... | collective-permute-start | bytes 7520264 | tf_op jit(solution)/shard_map/ppermute | solution.py:841
  69.4 13.4 %collective-permute-start.7 = (bf16[144,1536]{1,0:T(8,128)(2,1)S(1)}, bf16[144,1536]{1,0:T(8,128)(2,1)S(1)}, u32[]{:S(2)}, u32[]{:S(2)}) collective-permute-start(bf16[144,1536]{1,0:T(8,128)(2,1)S(1)} %get-tuple-element.175.refs_3_), channel_id=1, source_target_pairs={{0,1},{1,0},{2,3},{3,2},{4,5},{5,4},{6,7},{7,6},{8,9},{9,8},{10,11... | collective-permute-start | bytes 1327112 | tf_op jit(solution)/shard_map/ppermute | solution.py:841
  69.5 13.3 %collective-permute-start.8 = (bf16[64,1536]{1,0:T(8,128)(2,1)S(1)}, bf16[64,1536]{1,0:T(8,128)(2,1)S(1)}, u32[]{:S(2)}, u32[]{:S(2)}) collective-permute-start(bf16[64,1536]{1,0:T(8,128)(2,1)S(1)} %get-tuple-element.176), channel_id=1, source_target_pairs={{0,2},{1,3},{2,0},{3,1},{4,6},{5,7},{6,4},{7,5},{8,10},{9,11},{10,... | collective-permute-start | bytes 589832 | tf_op jit(solution)/shard_map/ppermute | solution.py:841
  80.1 27.8 %collective-permute-start.16 = (bf16[8,4,24,768]{3,2,1,0:T(8,128)(2,1)}, bf16[8,4,24,768]{3,2,1,0:T(8,128)(2,1)}, u32[]{:S(2)}, u32[]{:S(2)}) collective-permute-start(bf16[8,4,24,768]{3,2,1,0:T(8,128)(2,1)} %get-tuple-element.214), channel_id=1, source_target_pairs={{0,2},{1,3},{2,0},{3,1},{4,6},{5,7},{6,4},{7,5},{8,10},{9,11},{10,... | collective-permute-start | bytes 3538952 | tf_op jit(solution)/shard_map/ppermute | solution.py:841
  81.5 28.1 %collective-permute-start.17 = (bf16[2,4,96,768]{3,2,1,0:T(8,128)(2,1)}, bf16[2,4,96,768]{3,2,1,0:T(8,128)(2,1)}, u32[]{:S(2)}, u32[]{:S(2)}) collective-permute-start(bf16[2,4,96,768]{3,2,1,0:T(8,128)(2,1)} %get-tuple-element.215), channel_id=1, source_target_pairs={{0,4},{4,0},{8,12},{12,8},{16,20},{20,16},{24,28},{28,24},{1,5},{5... | collective-permute-start | bytes 3538952 | tf_op jit(solution)/shard_map/ppermute | solution.py:849
  87.8 13.3 %collective-permute-start.18 = (bf16[272,768]{1,0:T(8,128)(2,1)S(1)}, bf16[272,768]{1,0:T(8,128)(2,1)S(1)}, u32[]{:S(2)}, u32[]{:S(2)}) collective-permute-start(bf16[272,768]{1,0:T(8,128)(2,1)S(1)} %get-tuple-element.216.refs_3_), channel_id=1, source_target_pairs={{0,1},{1,0},{2,3},{3,2},{4,5},{5,4},{6,7},{7,6},{8,9},{9,8},{10,11... | collective-permute-start | bytes 1253384 | tf_op jit(solution)/shard_map/ppermute | solution.py:841
  88.3 13.1 %collective-permute-start.19 = (bf16[272,768]{1,0:T(8,128)(2,1)S(1)}, bf16[272,768]{1,0:T(8,128)(2,1)S(1)}, u32[]{:S(2)}, u32[]{:S(2)}) collective-permute-start(bf16[272,768]{1,0:T(8,128)(2,1)S(1)} %get-tuple-element.217.refs_5_), channel_id=1, source_target_pairs={{0,1},{1,0},{2,3},{3,2},{4,5},{5,4},{6,7},{7,6},{8,9},{9,8},{10,11... | collective-permute-start | bytes 1253384 | tf_op jit(solution)/shard_map/ppermute | solution.py:841
  88.4 13.5 %collective-permute-start.20 = (bf16[272,768]{1,0:T(8,128)(2,1)S(1)}, bf16[272,768]{1,0:T(8,128)(2,1)S(1)}, u32[]{:S(2)}, u32[]{:S(2)}) collective-permute-start(bf16[272,768]{1,0:T(8,128)(2,1)S(1)} %get-tuple-element.218.refs_7_), channel_id=1, source_target_pairs={{0,1},{1,0},{2,3},{3,2},{4,5},{5,4},{6,7},{7,6},{8,9},{9,8},{10,11... | collective-permute-start | bytes 1253384 | tf_op jit(solution)/shard_map/ppermute | solution.py:841
  101.1 17.3 %collective-permute-start.12 = (bf16[144,1536]{1,0:T(8,128)(2,1)S(1)}, bf16[144,1536]{1,0:T(8,128)(2,1)S(1)}, u32[]{:S(2)}, u32[]{:S(2)}) collective-permute-start(bf16[144,1536]{1,0:T(8,128)(2,1)S(1)} %get-tuple-element.206.refs_3_), channel_id=1, source_target_pairs={{0,1},{1,0},{2,3},{3,2},{4,5},{5,4},{6,7},{7,6},{8,9},{9,8},{10,11... | collective-permute-start | bytes 1327112 | tf_op jit(solution)/shard_map/ppermute | solution.py:841
  101.4 12.1 %collective-permute-start.14 = (bf16[48,1536]{1,0:T(8,128)(2,1)S(1)}, bf16[48,1536]{1,0:T(8,128)(2,1)S(1)}, u32[]{:S(2)}, u32[]{:S(2)}) collective-permute-start(bf16[48,1536]{1,0:T(8,128)(2,1)S(1)} %get-tuple-element.208), channel_id=1, source_target_pairs={{0,3},{1,2},{2,1},{3,0},{4,7},{5,6},{6,5},{7,4},{8,11},{9,10},{10,... | collective-permute-start | bytes 442376 | tf_op jit(solution)/shard_map/ppermute | solution.py:841
  101.9 12.8 %collective-permute-start.15 = (bf16[272,4608]{1,0:T(8,128)(2,1)S(1)}, bf16[272,4608]{1,0:T(8,128)(2,1)S(1)}, u32[]{:S(2)}, u32[]{:S(2)}) collective-permute-start(bf16[272,4608]{1,0:T(8,128)(2,1)S(1)} %get-tuple-element.213.refs_1_.refs_3_.refs_11_), channel_id=1, source_target_pairs={{0,1},{1,0},{2,3},{3,2},{4,5},{5,4},{6,7},{7,6},{8,9},{9,8},{10,11... | collective-permute-start | bytes 7520264 | tf_op jit(solution)/shard_map/ppermute | solution.py:841
  107.8 34.1 %collective-permute-start.30 = (bf16[2,8,2,24,768]{4,3,2,1,0:T(8,128)(2,1)S(1)}, bf16[2,8,2,24,768]{4,3,2,1,0:T(8,128)(2,1)S(1)}, u32[]{:S(2)}, u32[]{:S(2)}) collective-permute-start(bf16[2,8,2,24,768]{4,3,2,1,0:T(8,128)(2,1)S(1)} %get-tuple-element.238), channel_id=1, source_target_pairs={{0,8},{4,12},{8,0},{12,4},{16,24},{20,28},{24,16},{28,20},{1,9},{5... | collective-permute-start | bytes 3538952 | tf_op jit(solution)/shard_map/ppermute | solution.py:849
  112.2 18.9 %collective-permute-start.25 = (bf16[1,384,768]{2,1,0:T(8,128)(2,1)S(1)}, bf16[1,384,768]{2,1,0:T(8,128)(2,1)S(1)}, u32[]{:S(2)}, u32[]{:S(2)}) collective-permute-start(bf16[1,384,768]{2,1,0:T(8,128)(2,1)S(1)} %get-tuple-element.231), channel_id=1, source_target_pairs={{0,4},{4,0},{8,12},{12,8},{16,20},{20,16},{24,28},{28,24},{1,5},{5... | collective-permute-start | bytes 1769480 | tf_op jit(solution)/shard_map/ppermute | solution.py:849
  114.7 16.6 %collective-permute-start.26 = (bf16[2,192,768]{2,1,0:T(8,128)(2,1)S(1)}, bf16[2,192,768]{2,1,0:T(8,128)(2,1)S(1)}, u32[]{:S(2)}, u32[]{:S(2)}) collective-permute-start(bf16[2,192,768]{2,1,0:T(8,128)(2,1)S(1)} %get-tuple-element.232), channel_id=1, source_target_pairs={{0,2},{1,3},{2,0},{3,1},{4,6},{5,7},{6,4},{7,5},{8,10},{9,11},{10,... | collective-permute-start | bytes 1769480 | tf_op jit(solution)/shard_map/ppermute | solution.py:841
  129.7 28.1 %collective-permute-start.28 = (bf16[8,4,24,768]{3,2,1,0:T(8,128)(2,1)S(1)}, bf16[8,4,24,768]{3,2,1,0:T(8,128)(2,1)S(1)}, u32[]{:S(2)}, u32[]{:S(2)}) collective-permute-start(bf16[8,4,24,768]{3,2,1,0:T(8,128)(2,1)S(1)} %get-tuple-element.236), channel_id=1, source_target_pairs={{0,2},{1,3},{2,0},{3,1},{4,6},{5,7},{6,4},{7,5},{8,10},{9,11},{10,... | collective-permute-start | bytes 3538952 | tf_op jit(solution)/shard_map/ppermute | solution.py:841
  131.0 27.3 %collective-permute-start.29 = (bf16[2,4,96,768]{3,2,1,0:T(8,128)(2,1)S(1)}, bf16[2,4,96,768]{3,2,1,0:T(8,128)(2,1)S(1)}, u32[]{:S(2)}, u32[]{:S(2)}) collective-permute-start(bf16[2,4,96,768]{3,2,1,0:T(8,128)(2,1)S(1)} %get-tuple-element.237), channel_id=1, source_target_pairs={{0,4},{4,0},{8,12},{12,8},{16,20},{20,16},{24,28},{28,24},{1,5},{5... | collective-permute-start | bytes 3538952 | tf_op jit(solution)/shard_map/ppermute | solution.py:849
  140.6 58.1 %collective-permute-start.40 = (bf16[2,8,2,24,768]{4,3,2,1,0:T(8,128)(2,1)}, bf16[2,8,2,24,768]{4,3,2,1,0:T(8,128)(2,1)S(1)}, u32[]{:S(2)}, u32[]{:S(2)}) collective-permute-start(bf16[2,8,2,24,768]{4,3,2,1,0:T(8,128)(2,1)} %get-tuple-element.254), channel_id=1, source_target_pairs={{0,8},{4,12},{8,0},{12,4},{16,24},{20,28},{24,16},{28,20},{1,9},{5... | collective-permute-start | bytes 3538952 | tf_op jit(solution)/shard_map/ppermute | solution.py:849
  142.8 21.3 %collective-permute-start.35 = (bf16[192,768]{1,0:T(8,128)(2,1)S(1)}, bf16[192,768]{1,0:T(8,128)(2,1)S(1)}, u32[]{:S(2)}, u32[]{:S(2)}) collective-permute-start(bf16[192,768]{1,0:T(8,128)(2,1)S(1)} %get-tuple-element.246), channel_id=1, source_target_pairs={{0,2},{1,3},{2,0},{3,1},{4,6},{5,7},{6,4},{7,5},{8,10},{9,11},{10,... | collective-permute-start | bytes 884744 | tf_op jit(solution)/shard_map/ppermute | solution.py:841
  142.9 37.9 %collective-permute-start.34 = (bf16[2,192,768]{2,1,0:T(8,128)(2,1)S(1)}, bf16[2,192,768]{2,1,0:T(8,128)(2,1)S(1)}, u32[]{:S(2)}, u32[]{:S(2)}) collective-permute-start(bf16[2,192,768]{2,1,0:T(8,128)(2,1)S(1)} %get-tuple-element.245), channel_id=1, source_target_pairs={{0,8},{4,12},{8,0},{12,4},{16,24},{20,28},{24,16},{28,20},{1,9},{5... | collective-permute-start | bytes 1769480 | tf_op jit(solution)/shard_map/ppermute | solution.py:849
  159.6 29.1 %collective-permute-start.32 = (bf16[1,384,768]{2,1,0:T(8,128)(2,1)S(1)}, bf16[1,384,768]{2,1,0:T(8,128)(2,1)S(1)}, u32[]{:S(2)}, u32[]{:S(2)}) collective-permute-start(bf16[1,384,768]{2,1,0:T(8,128)(2,1)S(1)} %get-tuple-element.243), channel_id=1, source_target_pairs={{0,4},{4,0},{8,12},{12,8},{16,20},{20,16},{24,28},{28,24},{1,5},{5... | collective-permute-start | bytes 1769480 | tf_op jit(solution)/shard_map/ppermute | solution.py:849
  164.1 25.6 %collective-permute-start.33 = (bf16[2,192,768]{2,1,0:T(8,128)(2,1)S(1)}, bf16[2,192,768]{2,1,0:T(8,128)(2,1)S(1)}, u32[]{:S(2)}, u32[]{:S(2)}) collective-permute-start(bf16[2,192,768]{2,1,0:T(8,128)(2,1)S(1)} %get-tuple-element.244), channel_id=1, source_target_pairs={{0,2},{1,3},{2,0},{3,1},{4,6},{5,7},{6,4},{7,5},{8,10},{9,11},{10,... | collective-permute-start | bytes 1769480 | tf_op jit(solution)/shard_map/ppermute | solution.py:841
  165.4 16.9 %collective-permute-start.27 = (f32[2,24,768]{2,1,0:T(8,128)S(1)}, f32[2,24,768]{2,1,0:T(8,128)S(1)}, u32[]{:S(2)}, u32[]{:S(2)}) collective-permute-start(f32[2,24,768]{2,1,0:T(8,128)S(1)} %fusion.9), channel_id=1, source_target_pairs={{0,2},{1,3},{2,0},{3,1},{4,6},{5,7},{6,4},{7,5},{8,10},{9,11},{10,... | collective-permute-start | bytes 442376 | tf_op jit(solution)/shard_map/ppermute | solution.py:841
  182.3 19.5 %collective-permute-start.54 = (bf16[2,96,768]{2,1,0:T(8,128)(2,1)}, bf16[2,96,768]{2,1,0:T(8,128)(2,1)}, u32[]{:S(2)}, u32[]{:S(2)}) collective-permute-start(bf16[2,96,768]{2,1,0:T(8,128)(2,1)} %get-tuple-element.249.refs_5_), channel_id=1, source_target_pairs={{0,1},{1,17},{2,3},{3,19},{4,5},{5,21},{6,7},{7,23},{8,9},{9,25},{... | collective-permute-start | bytes 884744 | tf_op jit(solution)/shard_map/ppermute | solution.py:1150
  184.6 17.6 %collective-permute-start.53 = (bf16[2,96,768]{2,1,0:T(8,128)(2,1)}, bf16[2,96,768]{2,1,0:T(8,128)(2,1)}, u32[]{:S(2)}, u32[]{:S(2)}) collective-permute-start(bf16[2,96,768]{2,1,0:T(8,128)(2,1)} %get-tuple-element.270), channel_id=1, source_target_pairs={{0,0},{1,16},{2,2},{3,18},{4,4},{5,20},{6,6},{7,22},{8,8},{9,24},{... | collective-permute-start | bytes 884744 | tf_op jit(solution)/shard_map/ppermute | solution.py:1150
  200.6 22.4 %collective-permute-start.42 = (bf16[2,192,768]{2,1,0:T(8,128)(2,1)}, bf16[2,192,768]{2,1,0:T(8,128)(2,1)S(1)}, u32[]{:S(2)}, u32[]{:S(2)}) collective-permute-start(bf16[2,192,768]{2,1,0:T(8,128)(2,1)} %get-tuple-element.258), channel_id=1, source_target_pairs={{0,8},{4,12},{8,0},{12,4},{16,24},{20,28},{24,16},{28,20},{1,9},{5... | collective-permute-start | bytes 1769480 | tf_op jit(solution)/shard_map/ppermute | solution.py:849
  205.1 12.7 %collective-permute-start.50 = (bf16[2,48,768]{2,1,0:T(8,128)(2,1)S(1)}, bf16[2,48,768]{2,1,0:T(8,128)(2,1)}, u32[]{:S(2)}, u32[]{:S(2)}) collective-permute-start(bf16[2,48,768]{2,1,0:T(8,128)(2,1)S(1)} %get-tuple-element.256.refs_4_), channel_id=1, source_target_pairs={{0,1},{1,17},{2,3},{3,19},{4,5},{5,21},{6,7},{7,23},{8,9},{9,25},{... | collective-permute-start | bytes 442376 | tf_op jit(solution)/shard_map/ppermute | solution.py:1087
  206.8 13.4 %collective-permute-start.49 = (bf16[2,48,768]{2,1,0:T(8,128)(2,1)S(1)}, bf16[2,48,768]{2,1,0:T(8,128)(2,1)}, u32[]{:S(2)}, u32[]{:S(2)}) collective-permute-start(bf16[2,48,768]{2,1,0:T(8,128)(2,1)S(1)} %get-tuple-element.268), channel_id=1, source_target_pairs={{0,0},{1,16},{2,2},{3,18},{4,4},{5,20},{6,6},{7,22},{8,8},{9,24},{... | collective-permute-start | bytes 442376 | tf_op jit(solution)/shard_map/ppermute | solution.py:1087
  212.2 18.0 %collective-permute-start.41 = (f32[2,24,768]{2,1,0:T(8,128)S(1)}, f32[2,24,768]{2,1,0:T(8,128)S(1)}, u32[]{:S(2)}, u32[]{:S(2)}) collective-permute-start(f32[2,24,768]{2,1,0:T(8,128)S(1)} %add.81), channel_id=1, source_target_pairs={{0,16},{4,20},{8,24},{12,28},{16,0},{20,4},{24,8},{28,12},{1,17},{... | collective-permute-start | bytes 442376 | tf_op jit(solution)/shard_map/ppermute | solution.py:849
  225.7 13.7 %collective-permute-start.47 = (bf16[2,48,768]{2,1,0:T(8,128)(2,1)S(1)}, bf16[2,48,768]{2,1,0:T(8,128)(2,1)S(1)}, u32[]{:S(2)}, u32[]{:S(2)}) collective-permute-start(bf16[2,48,768]{2,1,0:T(8,128)(2,1)S(1)} %get-tuple-element.266), channel_id=1, source_target_pairs={{0,0},{1,16},{2,2},{3,18},{4,4},{5,20},{6,6},{7,22},{8,8},{9,24},{... | collective-permute-start | bytes 442376 | tf_op jit(solution)/shard_map/ppermute | solution.py:1087
  231.4 17.5 %collective-permute-start.51 = (bf16[2,96,768]{2,1,0:T(8,128)(2,1)S(1)}, bf16[2,96,768]{2,1,0:T(8,128)(2,1)S(1)}, u32[]{:S(2)}, u32[]{:S(2)}) collective-permute-start(bf16[2,96,768]{2,1,0:T(8,128)(2,1)S(1)} %get-tuple-element.269), channel_id=1, source_target_pairs={{0,0},{1,16},{2,2},{3,18},{4,4},{5,20},{6,6},{7,22},{8,8},{9,24},{... | collective-permute-start | bytes 884744 | tf_op jit(solution)/shard_map/ppermute | solution.py:1150
  (65 other events, 459.0 us)

commit v4 on v3

--- a/solution.py
+++ b/solution.py
@@ -768,11 +768,13 @@
     before = []
 
     def call(kernel, grid, in_specs, out_specs, out_shape, scratch=(), vmem=12, weight=1, also=(), place=pltpu.HBM, ahead=()):
-        deps = list(before) + list(also)
+        deps = [pltpu.with_memory_space_constraint(a, pltpu.HBM) for a in before] + list(also)
         count = len(in_specs)
 
         results = list(out_shape) if isinstance(out_shape, (list, tuple)) else [out_shape]
         result_specs = list(out_specs) if isinstance(out_specs, (list, tuple)) else [out_specs]
+        results.append(kept((8, 128), F32))
+        result_specs.append(ANY)
         more, own = len(ahead), len(results)
 
         def body(*refs):
@@ -781,6 +783,7 @@
             sources, refs = refs[:more], refs[more:]
             made, refs = refs[:own], refs[own:]
             targets, refs = refs[:more], refs[more:]
+            made.pop()
             if not more:
                 return kernel(*mine, *made, *refs)
             sem = refs.pop()
@@ -832,8 +835,9 @@
             for a, like in zip(out, results):
                 if not isinstance(like, jax.ShapeDtypeStruct) and like.memory_space == pltpu.VMEM:
                     resident[id(a)] = a
-            before[:] = [out[own - 1]]
-            return out if len(results) > 1 else out[0]
+            out = list(out)
+            before[:] = [out.pop(own - 1)]
+            return out if len(out) > 1 else out[0]
 
         return go
 
@@ -931,11 +935,11 @@
             x, qkv = res["x2"], res["next"]
             rims = [res[n] for n in ("pc_out", "pr_out", "pd_out")]
             got = exchange(rims)
-            _, w_out, w_up, w_down, cot = call(
-                lambda info, a, b: None, (1,), [ANY], [ANY], [kept((8, width), F32)],
+            w_out, w_up, w_down, cot = call(
+                lambda info, a: None, (1,), [IN], [], [],
                 ahead=[(out_weight, l + 1), (up_weight, l + 1), (down_weight, l + 1), (patch_cot.reshape(cells, width), None)],
                 vmem=2,
-            )(x)
+            )(own_mask)
 
     def attention_back(l, right, v, also):
         return call(
@@ -945,7 +949,7 @@
             [IN] * 6,
             [inside((cells, width), BF), inside((cells, 2 * width), F32)] + rim_shapes + [inside((16, sz.bk), F32)],
             [vm((sz.ext_rows, width), F32)] * 2 + [vm((rows, width), F32), vm((ng, sz.bk, sz.bk), F32)],
-            also=also, ahead=[(qkv_weight, l)] + ([] if l else [(patch_in.reshape(cells, width), None)]),
+            also=also,
         )(right, v["qkv"], v["stats"], own_mask, v["p"], v["kb"], v["vb"], v["w_out"])
 
     back_scratch = [vm((cells, 2 * width), F32), vm((rows, width), F32)]
@@ -1011,7 +1015,7 @@
             vmem=20, place=None,
         )(*act[0], *e_down[0])
 
-    def grad_up(h2, e_up, also=()):
+    def grad_up(h2, e_up, also, ahead):
         lspec = halves(h2[1])
         rspec = pl.BlockSpec((rows, width), lambda i, s: (0, e_up[1] + i))
         out = pl.BlockSpec((quarter, None, piece, width), lambda i, s: (0, i, 0, 0))
@@ -1021,7 +1025,7 @@
             [lspec, lspec, rspec, rspec],
             [out, out],
             pair((quarter, chunks, piece, width)),
-            also=also, vmem=20, place=None,
+            also=also, vmem=20, place=None, ahead=ahead,
         )(*h2[0], *e_up[0])
 
     def grad_attn(h, e_qkv, att, e_branch):
@@ -1160,9 +1164,7 @@
     for l in reversed(range(layers)):
         left = saved[l]["left"]
         result = attention_back(l, right, near, early)
-        d_q, d_kv, *rims, table, wq = result[:7]
-        if l == 0:
-            first = result[7]
+        d_q, d_kv, *rims, table = result
         early = []
         if waiting is not None:
             right = both(lax.optimization_barrier((right, table))[0])
@@ -1173,14 +1175,14 @@
             right = both(right)
             got = exchange(rims)
         x_first = grad_down((left, 2), (right, 0))
-        y_first = grad_up((left, 1), (right, 1), got if waiting is not None else ())
+        *y_first, wq = grad_up((left, 1), (right, 1), got if waiting is not None else (), [(qkv_weight, l)])
         sums["mlp", l] = Sums(y_first, x_first, 2)
         if l > 0:
             e_qkv, small[l], g, up_w, down_w = qkv_back(l, d_q, d_kv, rims[0], got, g1, vec, table, wq)
             waiting = (saved[l]["h"], e_qkv, (left, 0), (right, 1 + chunks))
             right, g1, vec, near = mlp_back(l - 1, g, up_w, down_w)
         else:
-            *e_qkv, small[0], patch_grad, cls_grad = finish(d_q, d_kv, rims[0], got, g1, vec, table, wq, first)
+            *e_qkv, small[0], patch_grad, cls_grad = finish(d_q, d_kv, rims[0], got, g1, vec, table, wq, patch_in.reshape(cells, width))
             waiting = (saved[0]["h"], [both(e) for e in e_qkv], (left, 0), (right, 1 + chunks))
     total = [jnp.stack(small), None, 0]
 

time: 255 us -> 251 us (0.984)
  Pallas kernels: 109 us -> 105 us
  starting transfers between devices: 59.2 us -> 56 us
  local copies, waits for them, and re-layouts: 18.5 us -> 21.1 us
    pallas_call x28, Pallas kernels: 109 us -> 105 us  [go(): out = run(info, *pinned, *deps, *sources)]
    unnamed x86 -> x94, local copies, waits for them, and re-layouts: 12.8 us -> 15.4 us
  transfers between devices with their start and end apart: 55 -> 55, of which waited for: 12 -> 12; matrix products, arithmetic and copies ran while one was open for 5% -> 5% of each run, Pallas kernels for 36% -> 35%
where the time goes in v4:
time: 251 us; the launch traced here: 248 us
  Pallas kernels  105 us (42%)
  starting transfers between devices  56 us (22%)
  waiting for transfers between devices  54.1 us (22%)
  local copies, waits for them, and re-layouts  21.1 us (8%)
  other arithmetic  8.88 us (4%)
    pallas_call x28, Pallas kernels, go(): out = run(info, *pinned, *deps, *sources)  105 us
    ppermute x32, starting transfers between devices, partner(): return lax.ppermute(value, 'tile', [(t, t ^ x) for t in range(tiles)])  25.5 us
    ppermute x32, waiting for transfers between devices, partner(): return lax.ppermute(value, 'tile', [(t, t ^ x) for t in range(tiles)])  21.6 us
    unnamed x94, local copies, waits for them, and re-layouts  15.4 us
    ppermute x4, waiting for transfers between devices, fourth(): lax.ppermute(a, ('dp', 'tile'), last_route(0))  14.8 us
    ppermute x4, starting transfers between devices, fourth(): lax.ppermute(a, ('dp', 'tile'), last_route(0))  14 us
    ppermute x15, waiting for transfers between devices, swap(): lax.ppermute(value, 'dp', [(d, d ^ 1 << bit - 2) for d in range(pages)])  14 us
    ppermute x15, starting transfers between devices, swap(): lax.ppermute(value, 'dp', [(d, d ^ 1 << bit - 2) for d in range(pages)])  11.4 us
  transfers between devices with their start and end apart: 55, of which 12 were waited for; matrix products, arithmetic and copies ran while one was open for 5% of the time, Pallas kernels for 35%

profile of v4, /device:TPU:1, one launch (start us, length us, event | category | flops | bytes accessed | tf_op | source)
XLA Modules:
  0.0 247.6 jit_solution(10560265736727751006)
XLA Ops:
  2.7 6.1 %shard_map.282 = (f32[272,768]{1,0:T(8,128)S(1)}, bf16[272,2304]{1,0:T(8,128)(2,1)S(1)}, bf16[144,1536]{1,0:T(8,128)(2,1)S(1)}, bf16[64,1536]{1,0:T(8,128)(2,1)}...) custom-call(s32[5]{0:T(128)S(1)} %stack.48.refs_0_, bf16[256,768]{1,0:T(8,128)(2,1)} %bitcast.69, ...), custom_call_target="tpu_custom_call" | custom-call | flops 1 | bytes 1 | tf_op jit(solution)/shard_map/pallas_call | solution.py:834
  8.9 2.7 %collective-permute-start.1 = (bf16[64,1536]{1,0:T(8,128)(2,1)}, bf16[64,1536]{1,0:T(8,128)(2,1)S(1)}, u32[]{:S(2)}, u32[]{:S(2)}) collective-permute-start(bf16[64,1536]{1,0:T(8,128)(2,1)} %get-tuple-element.169), channel_id=1, source_target_pairs={{0,2},{1,3},{2,0},{3,1},{4,6},{5,7},{6,4},{7,5},{8,10},{9,11},{10,... | collective-permute-start | bytes 589832 | tf_op jit(solution)/shard_map/ppermute | solution.py:845
  14.2 6.1 %shard_map.283 = (f32[2,3,256,256]{3,2,1,0:T(8,128)S(1)}, f32[8,128]{1,0:T(8,128)}, bf16[768,768]{1,0:T(8,128)(2,1)S(1)}, bf16[768,3072]{1,0:T(8,128)(2,1)S(1)},...) custom-call(s32[5]{0:T(128)S(1)} %stack.48.refs_0_, ...), custom_call_target="tpu_custom_call" | custom-call | flops 1 | bytes 1 | tf_op jit(solution)/shard_map/pallas_call | solution.py:834
  20.6 11.5 %shard_map.284 = (bf16[12,256,256]{2,1,0:T(8,128)(2,1)}, bf16[4,256,768]{2,1,0:T(8,128)(2,1)}, bf16[4,256,768]{2,1,0:T(8,128)(2,1)}, bf16[272,6144]{1,0:T(8,128)...) custom-call(s32[5]{0:T(128)S(1)} %stack.48.refs_0_, ...), custom_call_target="tpu_custom_call" | custom-call | flops 1 | bytes 1 | tf_op jit(solution)/shard_map/pallas_call | solution.py:834
  36.8 4.9 %shard_map.285 = (f32[8,128]{1,0:T(8,128)}, bf16[768,768]{1,0:T(8,128)(2,1)S(1)}, bf16[768,3072]{1,0:T(8,128)(2,1)S(1)}, bf16[3072,768]{1,0:T(8,128)(2,1)S(1)}, bf16[256,768]{1,0:T(8,128)(2,1)S(1)}) custom-call(s32[5]{0:T(128)S(1)} %stack.48.refs_0_, f32[8,256]{1,0:T(8,128)S(1)} %copy-done.30, f32[8,128]{1,0:T(8,128)} %get-tuple-element.187.refs_2_, ...), custom_call_target="tpu_custom_call" | custom-call | flops 1 | bytes 1 | tf_op jit(solution)/shard_map/pallas_call | solution.py:834
  41.8 3.2 %collective-permute-done.5.refs_5_ = bf16[48,1536]{1,0:T(8,128)(2,1)} collective-permute-done((bf16[48,1536]{1,0:T(8,128)(2,1)}, bf16[48,1536]{1,0:T(8,128)(2,1)}, u32[]{:S(2)}, u32[]{:S(2)}) %collective-permute-start.5) | collective-permute-done | bytes 147488 | tf_op jit(solution)/shard_map/ppermute | solution.py:845
  45.0 13.1 %shard_map.286 = (f32[8,768]{1,0:T(8,128)S(1)}, bf16[12,256,256]{2,1,0:T(8,128)(2,1)S(1)}, bf16[4,256,768]{2,1,0:T(8,128)(2,1)S(1)}, bf16[4,256,768]{2,1,0:T(8,1...) custom-call(s32[5]{0:T(128)S(1)} %stack.48.refs_0_, ...), custom_call_target="tpu_custom_call" | custom-call | flops 1 | bytes 1 | tf_op jit(solution)/shard_map/pallas_call | solution.py:834
  58.7 5.7 %shard_map.287 = (bf16[256,768]{1,0:T(8,128)(2,1)S(1)}, f32[256,1536]{1,0:T(8,128)S(1)}, bf16[144,1536]{1,0:T(8,128)(2,1)S(1)}, bf16[64,1536]{1,0:T(8,128)(2,1)S...) custom-call(s32[5]{0:T(128)S(1)} %stack.48.refs_0_, ...), custom_call_target="tpu_custom_call" | custom-call | flops 1 | bytes 1 | tf_op jit(solution)/shard_map/pallas_call | solution.py:834
  66.6 3.9 %shard_map.288 = (bf16[2,4,96,768]{3,2,1,0:T(8,128)(2,1)}, bf16[2,4,96,768]{3,2,1,0:T(8,128)(2,1)S(1)}, f32[8,128]{1,0:T(8,128)}) custom-call(s32[5]{0:T(128)S(1)} %stack.48.refs_0_, bf16[272,4608]{1,0:T(8,128)(2,1)S(1)} %get-tuple-element.210.refs_1_.refs_9_, bf16[272,4608]{1,0:T(8,128)(2,1)S(1)} %collective-permute-done.10.refs_2_.refs_10_, ...), custom_call_target="tpu_custom_call" | custom-call | flops 1 | bytes 1 | tf_op jit(solution)/shard_map/pallas_call | solution.py:834
  70.6 4.7 %shard_map.289 = (bf16[8,4,24,768]{3,2,1,0:T(8,128)(2,1)}, bf16[8,4,24,768]{3,2,1,0:T(8,128)(2,1)S(1)}, f32[8,128]{1,0:T(8,128)}, bf16[768,2304]{1,0:T(8,128)(2,1)S(1)}) custom-call(s32[5]{0:T(128)S(1)} %stack.48.refs_0_, bf16[272,4608]{1,0:T(8,128)(2,1)S(1)} %get-tuple-element.210.refs_1_.refs_9_, ...), custom_call_target="tpu_custom_call" | custom-call | flops 1 | bytes 1 | tf_op jit(solution)/shard_map/pallas_call | solution.py:834
  79.0 4.8 %shard_map.290 = (bf16[272,768]{1,0:T(8,128)(2,1)S(1)}, bf16[272,768]{1,0:T(8,128)(2,1)S(1)}, bf16[272,768]{1,0:T(8,128)(2,1)S(1)}, f32[24,768]{1,0:T(8,128)S(1)...) custom-call(s32[5]{0:T(128)S(1)} %stack.48.refs_0_, ...), custom_call_target="tpu_custom_call" | custom-call | flops 99999997952 | bytes 1 | tf_op jit(solution)/shard_map/pallas_call | solution.py:834
  85.0 4.7 %shard_map.291 = (bf16[272,4608]{1,0:T(8,128)(2,1)S(1)}, f32[272,768]{1,0:T(8,128)S(1)}, f32[8,768]{1,0:T(8,128)S(1)}, f32[8,128]{1,0:T(8,128)}, bf16[272,2304]{...) custom-call(s32[5]{0:T(128)S(1)} %stack.48.refs_0_, ...), custom_call_target="tpu_custom_call" | custom-call | flops 1 | bytes 1 | tf_op jit(solution)/shard_map/pallas_call | solution.py:834
  89.8 5.7 %shard_map.292 = (bf16[256,768]{1,0:T(8,128)(2,1)S(1)}, f32[256,1536]{1,0:T(8,128)S(1)}, bf16[144,1536]{1,0:T(8,128)(2,1)S(1)}, bf16[64,1536]{1,0:T(8,128)(2,1)S...) custom-call(s32[5]{0:T(128)S(1)} %stack.48.refs_0_, ...), custom_call_target="tpu_custom_call" | custom-call | flops 1 | bytes 1 | tf_op jit(solution)/shard_map/pallas_call | solution.py:834
  101.5 4.3 %shard_map.293 = (bf16[2,8,2,24,768]{4,3,2,1,0:T(8,128)(2,1)S(1)}, bf16[2,8,2,24,768]{4,3,2,1,0:T(8,128)(2,1)S(1)}, f32[8,128]{1,0:T(8,128)}) custom-call(s32[5]{0:T(128)S(1)} %stack.48.refs_0_, bf16[272,6144]{1,0:T(8,128)(2,1)S(1)} %copy-done, bf16[272,6144]{1,0:T(8,128)(2,1)S(1)} %collective-permute-done.6.refs_10_.refs_2_, ...), custom_call_target="tpu_custom_call" | custom-call | flops 1 | bytes 1 | tf_op jit(solution)/shard_map/pallas_call | solution.py:834
  107.2 2.6 %shard_map.294 = (bf16[1,384,768]{2,1,0:T(8,128)(2,1)S(1)}, bf16[1,384,768]{2,1,0:T(8,128)(2,1)S(1)}, bf16[2,192,768]{2,1,0:T(8,128)(2,1)S(1)}, bf16[2,192,768]{2,1,0:T(8,128)(2,1)S(1)}, f32[8,128]{1,0:T(8,128)}) custom-call(s32[5]{0:T(128)S(1)} %stack.48.refs_0_, bf16[1,2,384,768]{3,2,1,0:T(8,128)(2,1)S(1)} %bitcast.105, ...), custom_call_target="tpu_custom_call" | custom-call | flops 99999997952 | bytes 1 | tf_op jit(solution)/shard_map/pallas_call | solution.py:834
  111.6 3.1 %shard_map.295 = (bf16[2,4,96,768]{3,2,1,0:T(8,128)(2,1)S(1)}, bf16[2,4,96,768]{3,2,1,0:T(8,128)(2,1)S(1)}, f32[8,128]{1,0:T(8,128)}) custom-call(s32[5]{0:T(128)S(1)} %stack.48.refs_0_, bf16[272,6144]{1,0:T(8,128)(2,1)S(1)} %copy-done, bf16[272,6144]{1,0:T(8,128)(2,1)S(1)} %collective-permute-done.6.refs_10_.refs_2_, ...), custom_call_target="tpu_custom_call" | custom-call | flops 1 | bytes 1 | tf_op jit(solution)/shard_map/pallas_call | solution.py:834
  115.3 3.8 %shard_map.296 = (bf16[8,4,24,768]{3,2,1,0:T(8,128)(2,1)S(1)}, bf16[8,4,24,768]{3,2,1,0:T(8,128)(2,1)S(1)}, f32[8,128]{1,0:T(8,128)}, bf16[768,2304]{1,0:T(8,128)(2,1)S(1)}) custom-call(s32[5]{0:T(128)S(1)} %stack.48.refs_0_, bf16[272,6144]{1,0:T(8,128)(2,1)S(1)} %copy-done, bf16[272,6144]{1,0:T(8,128)(2,1)S(1)} %collective-permute-done.6.refs_10_.refs_2_, ...), custom_call_target="tpu_custom_call" | custom-call | flops 1 | bytes 1 | tf_op jit(solution)/shard_map/pallas_call | solution.py:834
  119.1 3.2 %shard_map.297 = (bf16[272,768]{1,0:T(8,128)(2,1)S(1)}, bf16[272,768]{1,0:T(8,128)(2,1)S(1)}, bf16[272,768]{1,0:T(8,128)(2,1)S(1)}, f32[24,768]{1,0:T(8,128)S(1)...) custom-call(s32[5]{0:T(128)S(1)} %stack.48.refs_0_, bf16[256,768]{1,0:T(8,128)(2,1)S(1)} %get-tuple-element.235.refs_1_, ...), custom_call_target="tpu_custom_call" | custom-call | flops 1 | bytes 1 | tf_op jit(solution)/shard_map/pallas_call | solution.py:834
  122.4 3.9 %collective-permute-start.22 = (bf16[272,768]{1,0:T(8,128)(2,1)S(1)}, bf16[272,768]{1,0:T(8,128)(2,1)S(1)}, u32[]{:S(2)}, u32[]{:S(2)}) collective-permute-start(bf16[272,768]{1,0:T(8,128)(2,1)S(1)} %get-tuple-element.261.refs_3_), channel_id=1, source_target_pairs={{0,1},{1,0},{2,3},{3,2},{4,5},{5,4},{6,7},{7,6},{8,9},{9,8},{10,11... | collective-permute-start | bytes 1253384 | tf_op jit(solution)/shard_map/ppermute | solution.py:845
  128.5 2.1 collective-permute-start.23
  132.6 4.5 %shard_map.299 = (bf16[2,8,2,24,768]{4,3,2,1,0:T(8,128)(2,1)}, bf16[2,8,2,24,768]{4,3,2,1,0:T(8,128)(2,1)S(1)}, f32[8,128]{1,0:T(8,128)}) custom-call(s32[5]{0:T(128)S(1)} %stack.48.refs_0_, bf16[272,6144]{1,0:T(8,128)(2,1)S(1)} %copy-done, bf16[272,6144]{1,0:T(8,128)(2,1)S(1)} %collective-permute-done.6.refs_10_.refs_2_, ...), custom_call_target="tpu_custom_call" | custom-call | flops 1 | bytes 1 | tf_op jit(solution)/shard_map/pallas_call | solution.py:834
  140.8 13.6 %collective-permute-done.28 = bf16[8,4,24,768]{3,2,1,0:T(8,128)(2,1)S(1)} collective-permute-done((bf16[8,4,24,768]{3,2,1,0:T(8,128)(2,1)S(1)}, bf16[8,4,24,768]{3,2,1,0:T(8,128)(2,1)S(1)}, u32[]{:S(2)}, u32[]{:S(2)}) %collective-permute-start.28) | collective-permute-done | bytes 1179680 | tf_op jit(solution)/shard_map/ppermute | solution.py:845
  157.2 3.5 %collective-permute-done.35 = bf16[192,768]{1,0:T(8,128)(2,1)S(1)} collective-permute-done((bf16[192,768]{1,0:T(8,128)(2,1)S(1)}, bf16[192,768]{1,0:T(8,128)(2,1)S(1)}, u32[]{:S(2)}, u32[]{:S(2)}) %collective-permute-start.35) | collective-permute-done | bytes 294944 | tf_op jit(solution)/shard_map/ppermute | solution.py:845
  165.2 12.0 %collective-permute-done.34 = bf16[2,192,768]{2,1,0:T(8,128)(2,1)S(1)} collective-permute-done((bf16[2,192,768]{2,1,0:T(8,128)(2,1)S(1)}, bf16[2,192,768]{2,1,0:T(8,128)(2,1)S(1)}, u32[]{:S(2)}, u32[]{:S(2)}) %collective-permute-start.34) | collective-permute-done | bytes 589856 | tf_op jit(solution)/shard_map/ppermute | solution.py:853
  178.7 2.3 collective-permute-start.54
  181.0 3.5 %collective-permute-start.53 = (bf16[2,96,768]{2,1,0:T(8,128)(2,1)}, bf16[2,96,768]{2,1,0:T(8,128)(2,1)}, u32[]{:S(2)}, u32[]{:S(2)}) collective-permute-start(bf16[2,96,768]{2,1,0:T(8,128)(2,1)} %get-tuple-element.319), channel_id=1, source_target_pairs={{0,0},{1,16},{2,2},{3,18},{4,4},{5,20},{6,6},{7,22},{8,8},{9,24},{... | collective-permute-start | bytes 884744 | tf_op jit(solution)/shard_map/ppermute | solution.py:1154
  204.5 4.1 %collective-permute-start.49 = (bf16[2,48,768]{2,1,0:T(8,128)(2,1)S(1)}, bf16[2,48,768]{2,1,0:T(8,128)(2,1)}, u32[]{:S(2)}, u32[]{:S(2)}) collective-permute-start(bf16[2,48,768]{2,1,0:T(8,128)(2,1)S(1)} %get-tuple-element.315), channel_id=1, source_target_pairs={{0,0},{1,16},{2,2},{3,18},{4,4},{5,20},{6,6},{7,22},{8,8},{9,24},{... | collective-permute-start | bytes 442376 | tf_op jit(solution)/shard_map/ppermute | solution.py:1091
  210.8 3.6 %collective-permute-done.50 = bf16[2,48,768]{2,1,0:T(8,128)(2,1)} collective-permute-done((bf16[2,48,768]{2,1,0:T(8,128)(2,1)S(1)}, bf16[2,48,768]{2,1,0:T(8,128)(2,1)}, u32[]{:S(2)}, u32[]{:S(2)}) %collective-permute-start.50) | collective-permute-done | bytes 147488 | tf_op jit(solution)/shard_map/ppermute | solution.py:1091
  222.2 4.3 %collective-permute-start.47 = (bf16[2,48,768]{2,1,0:T(8,128)(2,1)S(1)}, bf16[2,48,768]{2,1,0:T(8,128)(2,1)S(1)}, u32[]{:S(2)}, u32[]{:S(2)}) collective-permute-start(bf16[2,48,768]{2,1,0:T(8,128)(2,1)S(1)} %get-tuple-element.313), channel_id=1, source_target_pairs={{0,0},{1,16},{2,2},{3,18},{4,4},{5,20},{6,6},{7,22},{8,8},{9,24},{... | collective-permute-start | bytes 442376 | tf_op jit(solution)/shard_map/ppermute | solution.py:1091
  228.0 2.1 collective-permute-start.51
  230.7 5.1 %collective-permute-done.47 = bf16[2,48,768]{2,1,0:T(8,128)(2,1)S(1)} collective-permute-done((bf16[2,48,768]{2,1,0:T(8,128)(2,1)S(1)}, bf16[2,48,768]{2,1,0:T(8,128)(2,1)S(1)}, u32[]{:S(2)}, u32[]{:S(2)}) %collective-permute-start.47) | collective-permute-done | bytes 147488 | tf_op jit(solution)/shard_map/ppermute | solution.py:1091
  237.7 7.6 %collective-permute-done.51 = bf16[2,96,768]{2,1,0:T(8,128)(2,1)S(1)} collective-permute-done((bf16[2,96,768]{2,1,0:T(8,128)(2,1)S(1)}, bf16[2,96,768]{2,1,0:T(8,128)(2,1)S(1)}, u32[]{:S(2)}, u32[]{:S(2)}) %collective-permute-start.51) | collective-permute-done | bytes 294944 | tf_op jit(solution)/shard_map/ppermute | solution.py:1154
  (244 shorter events, 78.7 us)
Async XLA Ops:
  8.8 11.6 %collective-permute-start = (bf16[144,1536]{1,0:T(8,128)(2,1)S(1)}, bf16[144,1536]{1,0:T(8,128)(2,1)S(1)}, u32[]{:S(2)}, u32[]{:S(2)}) collective-permute-start(bf16[144,1536]{1,0:T(8,128)(2,1)S(1)} %get-tuple-element.168.refs_2_), channel_id=1, source_target_pairs={{0,1},{1,0},{2,3},{3,2},{4,5},{5,4},{6,7},{7,6},{8,9},{9,8},{10,11... | collective-permute-start | bytes 1327112 | tf_op jit(solution)/shard_map/ppermute | solution.py:845
  34.1 24.6 %collective-permute-start.6 = (bf16[272,6144]{1,0:T(8,128)(2,1)}, bf16[272,6144]{1,0:T(8,128)(2,1)S(1)}, u32[]{:S(2)}, u32[]{:S(2)}) collective-permute-start(bf16[272,6144]{1,0:T(8,128)(2,1)} %get-tuple-element.201.refs_1_.refs_9_), channel_id=1, source_target_pairs={{0,1},{1,0},{2,3},{3,2},{4,5},{5,4},{6,7},{7,6},{8,9},{9,8},{10,11... | collective-permute-start | bytes 10027016 | tf_op jit(solution)/shard_map/ppermute | solution.py:845
  64.4 14.6 %collective-permute-start.7 = (bf16[144,1536]{1,0:T(8,128)(2,1)S(1)}, bf16[144,1536]{1,0:T(8,128)(2,1)S(1)}, u32[]{:S(2)}, u32[]{:S(2)}) collective-permute-start(bf16[144,1536]{1,0:T(8,128)(2,1)S(1)} %get-tuple-element.204.refs_3_), channel_id=1, source_target_pairs={{0,1},{1,0},{2,3},{3,2},{4,5},{5,4},{6,7},{7,6},{8,9},{9,8},{10,11... | collective-permute-start | bytes 1327112 | tf_op jit(solution)/shard_map/ppermute | solution.py:845
  64.6 14.4 %collective-permute-start.8 = (bf16[64,1536]{1,0:T(8,128)(2,1)S(1)}, bf16[64,1536]{1,0:T(8,128)(2,1)S(1)}, u32[]{:S(2)}, u32[]{:S(2)}) collective-permute-start(bf16[64,1536]{1,0:T(8,128)(2,1)S(1)} %get-tuple-element.205), channel_id=1, source_target_pairs={{0,2},{1,3},{2,0},{3,1},{4,6},{5,7},{6,4},{7,5},{8,10},{9,11},{10,... | collective-permute-start | bytes 589832 | tf_op jit(solution)/shard_map/ppermute | solution.py:845
  66.0 13.0 %collective-permute-start.9 = (bf16[48,1536]{1,0:T(8,128)(2,1)S(1)}, bf16[48,1536]{1,0:T(8,128)(2,1)S(1)}, u32[]{:S(2)}, u32[]{:S(2)}) collective-permute-start(bf16[48,1536]{1,0:T(8,128)(2,1)S(1)} %get-tuple-element.206), channel_id=1, source_target_pairs={{0,3},{1,2},{2,1},{3,0},{4,7},{5,6},{6,5},{7,4},{8,11},{9,10},{10,... | collective-permute-start | bytes 442376 | tf_op jit(solution)/shard_map/ppermute | solution.py:845
  76.3 29.5 %collective-permute-start.16 = (bf16[8,4,24,768]{3,2,1,0:T(8,128)(2,1)}, bf16[8,4,24,768]{3,2,1,0:T(8,128)(2,1)}, u32[]{:S(2)}, u32[]{:S(2)}) collective-permute-start(bf16[8,4,24,768]{3,2,1,0:T(8,128)(2,1)} %get-tuple-element.245), channel_id=1, source_target_pairs={{0,2},{1,3},{2,0},{3,1},{4,6},{5,7},{6,4},{7,5},{8,10},{9,11},{10,... | collective-permute-start | bytes 3538952 | tf_op jit(solution)/shard_map/ppermute | solution.py:845
  77.8 29.4 %collective-permute-start.17 = (bf16[2,4,96,768]{3,2,1,0:T(8,128)(2,1)}, bf16[2,4,96,768]{3,2,1,0:T(8,128)(2,1)}, u32[]{:S(2)}, u32[]{:S(2)}) collective-permute-start(bf16[2,4,96,768]{3,2,1,0:T(8,128)(2,1)} %get-tuple-element.247), channel_id=1, source_target_pairs={{0,4},{4,0},{8,12},{12,8},{16,20},{20,16},{24,28},{28,24},{1,5},{5... | collective-permute-start | bytes 3538952 | tf_op jit(solution)/shard_map/ppermute | solution.py:853
  83.9 11.6 %collective-permute-start.18 = (bf16[272,768]{1,0:T(8,128)(2,1)S(1)}, bf16[272,768]{1,0:T(8,128)(2,1)S(1)}, u32[]{:S(2)}, u32[]{:S(2)}) collective-permute-start(bf16[272,768]{1,0:T(8,128)(2,1)S(1)} %get-tuple-element.248.refs_3_), channel_id=1, source_target_pairs={{0,1},{1,0},{2,3},{3,2},{4,5},{5,4},{6,7},{7,6},{8,9},{9,8},{10,11... | collective-permute-start | bytes 1253384 | tf_op jit(solution)/shard_map/ppermute | solution.py:845
  84.5 11.8 %collective-permute-start.19 = (bf16[272,768]{1,0:T(8,128)(2,1)S(1)}, bf16[272,768]{1,0:T(8,128)(2,1)S(1)}, u32[]{:S(2)}, u32[]{:S(2)}) collective-permute-start(bf16[272,768]{1,0:T(8,128)(2,1)S(1)} %get-tuple-element.249.refs_5_), channel_id=1, source_target_pairs={{0,1},{1,0},{2,3},{3,2},{4,5},{5,4},{6,7},{7,6},{8,9},{9,8},{10,11... | collective-permute-start | bytes 1253384 | tf_op jit(solution)/shard_map/ppermute | solution.py:845
  84.6 13.0 %collective-permute-start.20 = (bf16[272,768]{1,0:T(8,128)(2,1)S(1)}, bf16[272,768]{1,0:T(8,128)(2,1)S(1)}, u32[]{:S(2)}, u32[]{:S(2)}) collective-permute-start(bf16[272,768]{1,0:T(8,128)(2,1)S(1)} %get-tuple-element.250.refs_7_), channel_id=1, source_target_pairs={{0,1},{1,0},{2,3},{3,2},{4,5},{5,4},{6,7},{7,6},{8,9},{9,8},{10,11... | collective-permute-start | bytes 1253384 | tf_op jit(solution)/shard_map/ppermute | solution.py:845
  96.3 19.0 %collective-permute-start.12 = (bf16[144,1536]{1,0:T(8,128)(2,1)S(1)}, bf16[144,1536]{1,0:T(8,128)(2,1)S(1)}, u32[]{:S(2)}, u32[]{:S(2)}) collective-permute-start(bf16[144,1536]{1,0:T(8,128)(2,1)S(1)} %get-tuple-element.237.refs_3_), channel_id=1, source_target_pairs={{0,1},{1,0},{2,3},{3,2},{4,5},{5,4},{6,7},{7,6},{8,9},{9,8},{10,11... | collective-permute-start | bytes 1327112 | tf_op jit(solution)/shard_map/ppermute | solution.py:845
  97.1 13.0 %collective-permute-start.14 = (bf16[48,1536]{1,0:T(8,128)(2,1)S(1)}, bf16[48,1536]{1,0:T(8,128)(2,1)S(1)}, u32[]{:S(2)}, u32[]{:S(2)}) collective-permute-start(bf16[48,1536]{1,0:T(8,128)(2,1)S(1)} %get-tuple-element.239), channel_id=1, source_target_pairs={{0,3},{1,2},{2,1},{3,0},{4,7},{5,6},{6,5},{7,4},{8,11},{9,10},{10,... | collective-permute-start | bytes 442376 | tf_op jit(solution)/shard_map/ppermute | solution.py:845
  98.4 12.9 %collective-permute-start.15 = (bf16[272,4608]{1,0:T(8,128)(2,1)S(1)}, bf16[272,4608]{1,0:T(8,128)(2,1)S(1)}, u32[]{:S(2)}, u32[]{:S(2)}) collective-permute-start(bf16[272,4608]{1,0:T(8,128)(2,1)S(1)} %get-tuple-element.243.refs_1_.refs_3_.refs_11_), channel_id=1, source_target_pairs={{0,1},{1,0},{2,3},{3,2},{4,5},{5,4},{6,7},{7,6},{8,9},{9,8},{10,11... | collective-permute-start | bytes 7520264 | tf_op jit(solution)/shard_map/ppermute | solution.py:845
  105.9 31.5 %collective-permute-start.30 = (bf16[2,8,2,24,768]{4,3,2,1,0:T(8,128)(2,1)S(1)}, bf16[2,8,2,24,768]{4,3,2,1,0:T(8,128)(2,1)S(1)}, u32[]{:S(2)}, u32[]{:S(2)}) collective-permute-start(bf16[2,8,2,24,768]{4,3,2,1,0:T(8,128)(2,1)S(1)} %get-tuple-element.277), channel_id=1, source_target_pairs={{0,8},{4,12},{8,0},{12,4},{16,24},{20,28},{24,16},{28,20},{1,9},{5... | collective-permute-start | bytes 3538952 | tf_op jit(solution)/shard_map/ppermute | solution.py:853
  109.8 17.8 %collective-permute-start.25 = (bf16[1,384,768]{2,1,0:T(8,128)(2,1)S(1)}, bf16[1,384,768]{2,1,0:T(8,128)(2,1)S(1)}, u32[]{:S(2)}, u32[]{:S(2)}) collective-permute-start(bf16[1,384,768]{2,1,0:T(8,128)(2,1)S(1)} %get-tuple-element.265), channel_id=1, source_target_pairs={{0,4},{4,0},{8,12},{12,8},{16,20},{20,16},{24,28},{28,24},{1,5},{5... | collective-permute-start | bytes 1769480 | tf_op jit(solution)/shard_map/ppermute | solution.py:853
  111.3 17.2 %collective-permute-start.26 = (bf16[2,192,768]{2,1,0:T(8,128)(2,1)S(1)}, bf16[2,192,768]{2,1,0:T(8,128)(2,1)S(1)}, u32[]{:S(2)}, u32[]{:S(2)}) collective-permute-start(bf16[2,192,768]{2,1,0:T(8,128)(2,1)S(1)} %get-tuple-element.267), channel_id=1, source_target_pairs={{0,2},{1,3},{2,0},{3,1},{4,6},{5,7},{6,4},{7,5},{8,10},{9,11},{10,... | collective-permute-start | bytes 1769480 | tf_op jit(solution)/shard_map/ppermute | solution.py:845
  126.3 28.1 %collective-permute-start.28 = (bf16[8,4,24,768]{3,2,1,0:T(8,128)(2,1)S(1)}, bf16[8,4,24,768]{3,2,1,0:T(8,128)(2,1)S(1)}, u32[]{:S(2)}, u32[]{:S(2)}) collective-permute-start(bf16[8,4,24,768]{3,2,1,0:T(8,128)(2,1)S(1)} %get-tuple-element.273), channel_id=1, source_target_pairs={{0,2},{1,3},{2,0},{3,1},{4,6},{5,7},{6,4},{7,5},{8,10},{9,11},{10,... | collective-permute-start | bytes 3538952 | tf_op jit(solution)/shard_map/ppermute | solution.py:845
  127.5 27.8 %collective-permute-start.29 = (bf16[2,4,96,768]{3,2,1,0:T(8,128)(2,1)S(1)}, bf16[2,4,96,768]{3,2,1,0:T(8,128)(2,1)S(1)}, u32[]{:S(2)}, u32[]{:S(2)}) collective-permute-start(bf16[2,4,96,768]{3,2,1,0:T(8,128)(2,1)S(1)} %get-tuple-element.275), channel_id=1, source_target_pairs={{0,4},{4,0},{8,12},{12,8},{16,20},{20,16},{24,28},{28,24},{1,5},{5... | collective-permute-start | bytes 3538952 | tf_op jit(solution)/shard_map/ppermute | solution.py:853
  137.2 58.2 %collective-permute-start.40 = (bf16[2,8,2,24,768]{4,3,2,1,0:T(8,128)(2,1)}, bf16[2,8,2,24,768]{4,3,2,1,0:T(8,128)(2,1)S(1)}, u32[]{:S(2)}, u32[]{:S(2)}) collective-permute-start(bf16[2,8,2,24,768]{4,3,2,1,0:T(8,128)(2,1)} %get-tuple-element.298), channel_id=1, source_target_pairs={{0,8},{4,12},{8,0},{12,4},{16,24},{20,28},{24,16},{28,20},{1,9},{5... | collective-permute-start | bytes 3538952 | tf_op jit(solution)/shard_map/ppermute | solution.py:853
  138.2 22.5 %collective-permute-start.35 = (bf16[192,768]{1,0:T(8,128)(2,1)S(1)}, bf16[192,768]{1,0:T(8,128)(2,1)S(1)}, u32[]{:S(2)}, u32[]{:S(2)}) collective-permute-start(bf16[192,768]{1,0:T(8,128)(2,1)S(1)} %get-tuple-element.288), channel_id=1, source_target_pairs={{0,2},{1,3},{2,0},{3,1},{4,6},{5,7},{6,4},{7,5},{8,10},{9,11},{10,... | collective-permute-start | bytes 884744 | tf_op jit(solution)/shard_map/ppermute | solution.py:845
  139.5 37.7 %collective-permute-start.34 = (bf16[2,192,768]{2,1,0:T(8,128)(2,1)S(1)}, bf16[2,192,768]{2,1,0:T(8,128)(2,1)S(1)}, u32[]{:S(2)}, u32[]{:S(2)}) collective-permute-start(bf16[2,192,768]{2,1,0:T(8,128)(2,1)S(1)} %get-tuple-element.286), channel_id=1, source_target_pairs={{0,8},{4,12},{8,0},{12,4},{16,24},{20,28},{24,16},{28,20},{1,9},{5... | collective-permute-start | bytes 1769480 | tf_op jit(solution)/shard_map/ppermute | solution.py:853
  156.6 28.6 %collective-permute-start.32 = (bf16[1,384,768]{2,1,0:T(8,128)(2,1)S(1)}, bf16[1,384,768]{2,1,0:T(8,128)(2,1)S(1)}, u32[]{:S(2)}, u32[]{:S(2)}) collective-permute-start(bf16[1,384,768]{2,1,0:T(8,128)(2,1)S(1)} %get-tuple-element.282), channel_id=1, source_target_pairs={{0,4},{4,0},{8,12},{12,8},{16,20},{20,16},{24,28},{28,24},{1,5},{5... | collective-permute-start | bytes 1769480 | tf_op jit(solution)/shard_map/ppermute | solution.py:853
  160.7 26.8 %collective-permute-start.33 = (bf16[2,192,768]{2,1,0:T(8,128)(2,1)S(1)}, bf16[2,192,768]{2,1,0:T(8,128)(2,1)S(1)}, u32[]{:S(2)}, u32[]{:S(2)}) collective-permute-start(bf16[2,192,768]{2,1,0:T(8,128)(2,1)S(1)} %get-tuple-element.284), channel_id=1, source_target_pairs={{0,2},{1,3},{2,0},{3,1},{4,6},{5,7},{6,4},{7,5},{8,10},{9,11},{10,... | collective-permute-start | bytes 1769480 | tf_op jit(solution)/shard_map/ppermute | solution.py:845
  161.9 16.7 %collective-permute-start.27 = (f32[2,24,768]{2,1,0:T(8,128)S(1)}, f32[2,24,768]{2,1,0:T(8,128)S(1)}, u32[]{:S(2)}, u32[]{:S(2)}) collective-permute-start(f32[2,24,768]{2,1,0:T(8,128)S(1)} %fusion.9), channel_id=1, source_target_pairs={{0,2},{1,3},{2,0},{3,1},{4,6},{5,7},{6,4},{7,5},{8,10},{9,11},{10,... | collective-permute-start | bytes 442376 | tf_op jit(solution)/shard_map/ppermute | solution.py:845
  178.7 19.7 %collective-permute-start.54 = (bf16[2,96,768]{2,1,0:T(8,128)(2,1)}, bf16[2,96,768]{2,1,0:T(8,128)(2,1)}, u32[]{:S(2)}, u32[]{:S(2)}) collective-permute-start(bf16[2,96,768]{2,1,0:T(8,128)(2,1)} %get-tuple-element.320), channel_id=1, source_target_pairs={{0,1},{1,17},{2,3},{3,19},{4,5},{5,21},{6,7},{7,23},{8,9},{9,25},{... | collective-permute-start | bytes 884744 | tf_op jit(solution)/shard_map/ppermute | solution.py:1154
  181.0 17.7 %collective-permute-start.53 = (bf16[2,96,768]{2,1,0:T(8,128)(2,1)}, bf16[2,96,768]{2,1,0:T(8,128)(2,1)}, u32[]{:S(2)}, u32[]{:S(2)}) collective-permute-start(bf16[2,96,768]{2,1,0:T(8,128)(2,1)} %get-tuple-element.319), channel_id=1, source_target_pairs={{0,0},{1,16},{2,2},{3,18},{4,4},{5,20},{6,6},{7,22},{8,8},{9,24},{... | collective-permute-start | bytes 884744 | tf_op jit(solution)/shard_map/ppermute | solution.py:1154
  197.1 22.5 %collective-permute-start.42 = (bf16[2,192,768]{2,1,0:T(8,128)(2,1)}, bf16[2,192,768]{2,1,0:T(8,128)(2,1)S(1)}, u32[]{:S(2)}, u32[]{:S(2)}) collective-permute-start(bf16[2,192,768]{2,1,0:T(8,128)(2,1)} %get-tuple-element.303), channel_id=1, source_target_pairs={{0,8},{4,12},{8,0},{12,4},{16,24},{20,28},{24,16},{28,20},{1,9},{5... | collective-permute-start | bytes 1769480 | tf_op jit(solution)/shard_map/ppermute | solution.py:853
  202.8 11.6 %collective-permute-start.50 = (bf16[2,48,768]{2,1,0:T(8,128)(2,1)S(1)}, bf16[2,48,768]{2,1,0:T(8,128)(2,1)}, u32[]{:S(2)}, u32[]{:S(2)}) collective-permute-start(bf16[2,48,768]{2,1,0:T(8,128)(2,1)S(1)} %get-tuple-element.316), channel_id=1, source_target_pairs={{0,1},{1,17},{2,3},{3,19},{4,5},{5,21},{6,7},{7,23},{8,9},{9,25},{... | collective-permute-start | bytes 442376 | tf_op jit(solution)/shard_map/ppermute | solution.py:1091
  204.5 12.2 %collective-permute-start.49 = (bf16[2,48,768]{2,1,0:T(8,128)(2,1)S(1)}, bf16[2,48,768]{2,1,0:T(8,128)(2,1)}, u32[]{:S(2)}, u32[]{:S(2)}) collective-permute-start(bf16[2,48,768]{2,1,0:T(8,128)(2,1)S(1)} %get-tuple-element.315), channel_id=1, source_target_pairs={{0,0},{1,16},{2,2},{3,18},{4,4},{5,20},{6,6},{7,22},{8,8},{9,24},{... | collective-permute-start | bytes 442376 | tf_op jit(solution)/shard_map/ppermute | solution.py:1091
  209.9 16.9 %collective-permute-start.41 = (f32[2,24,768]{2,1,0:T(8,128)S(1)}, f32[2,24,768]{2,1,0:T(8,128)S(1)}, u32[]{:S(2)}, u32[]{:S(2)}) collective-permute-start(f32[2,24,768]{2,1,0:T(8,128)S(1)} %add.81), channel_id=1, source_target_pairs={{0,16},{4,20},{8,24},{12,28},{16,0},{20,4},{24,8},{28,12},{1,17},{... | collective-permute-start | bytes 442376 | tf_op jit(solution)/shard_map/ppermute | solution.py:853
  222.2 13.7 %collective-permute-start.47 = (bf16[2,48,768]{2,1,0:T(8,128)(2,1)S(1)}, bf16[2,48,768]{2,1,0:T(8,128)(2,1)S(1)}, u32[]{:S(2)}, u32[]{:S(2)}) collective-permute-start(bf16[2,48,768]{2,1,0:T(8,128)(2,1)S(1)} %get-tuple-element.313), channel_id=1, source_target_pairs={{0,0},{1,16},{2,2},{3,18},{4,4},{5,20},{6,6},{7,22},{8,8},{9,24},{... | collective-permute-start | bytes 442376 | tf_op jit(solution)/shard_map/ppermute | solution.py:1091
  228.0 17.3 %collective-permute-start.51 = (bf16[2,96,768]{2,1,0:T(8,128)(2,1)S(1)}, bf16[2,96,768]{2,1,0:T(8,128)(2,1)S(1)}, u32[]{:S(2)}, u32[]{:S(2)}) collective-permute-start(bf16[2,96,768]{2,1,0:T(8,128)(2,1)S(1)} %get-tuple-element.317), channel_id=1, source_target_pairs={{0,0},{1,16},{2,2},{3,18},{4,4},{5,20},{6,6},{7,22},{8,8},{9,24},{... | collective-permute-start | bytes 884744 | tf_op jit(solution)/shard_map/ppermute | solution.py:1154
  (69 other events, 438.3 us)

commit v5 on v4

--- a/solution.py
+++ b/solution.py
@@ -827,7 +827,9 @@
             for a, spec in zip(args, in_specs):
                 if id(a) in resident:
                     a = pltpu.with_memory_space_constraint(a, pltpu.VMEM)
-                elif spec is not IN and place is not None:
+                elif place is pltpu.VMEM and a.size <= 2 * sz.ext_rows * width:
+                    a = pltpu.with_memory_space_constraint(a, pltpu.VMEM)
+                elif spec is not IN and place is pltpu.HBM:
                     a = pltpu.with_memory_space_constraint(a, pltpu.HBM if spec is ANY else place)
                 pinned.append(a)
             sources = [pltpu.with_memory_space_constraint(a, pltpu.HBM) for a, _ in ahead]
@@ -1059,7 +1061,7 @@
             n = self.n
             s0, s1, k = call(
                 z_second_kernel, (1,), [whole((2, 2, n, width))] * 2, [whole((n, width))] * 2 + [whole((2, n, width))],
-                [shape((n, width), BF)] * 2 + [inside((2, n, width), BF)], place=None, weight=weight,
+                [shape((n, width), BF)] * 2 + [inside((2, n, width), BF)], place=pltpu.VMEM, weight=weight,
             )(self.keep, self.got)
             self.got = [swap(s0, 1), swap(s1, 2)]
             self.keep = k
@@ -1069,7 +1071,7 @@
             s0, s1, k = call(
                 z_third_kernel, (1,), [whole((2, 2, n, width))] + [whole((2, n, width))] * 2,
                 [whole((n, width))] * 2 + [whole((2, n, width))],
-                [shape((n, width), BF)] * 2 + [inside((2, n, width), BF)], place=None,
+                [shape((n, width), BF)] * 2 + [inside((2, n, width), BF)], place=pltpu.VMEM,
             )(self.keep.reshape(2, 2, n, width), *(g.reshape(2, n, width) for g in self.got))
             self.got = [swap(s0, 2), swap(s1, 1)]
             self.keep = k
@@ -1077,7 +1079,7 @@
                 n = self.n = self.n // 2
                 spec = whole((2, 2, n, width))
                 s, k = call(
-                    more_kernel, (1,), [spec, spec], [whole((2, n, width))] * 2, pair((2, n, width)), place=None,
+                    more_kernel, (1,), [spec, spec], [whole((2, n, width))] * 2, pair((2, n, width)), place=pltpu.VMEM,
                 )(self.keep.reshape(2, 2, n, width), jnp.stack(self.got).reshape(2, 2, n, width))
                 self.keep = k
                 self.got = list(swap(s, bit))
@@ -1086,7 +1088,7 @@
             n = self.n = self.n // 2
             a, b = call(
                 functools.partial(z_fourth_kernel, sz), (1,), [whole((2, 2, n, width))] + [whole((2, n, width))] * 2,
-                [whole((2, n, width))] * 2, [shape((2, n, width), BF)] * 2, place=None,
+                [whole((2, n, width))] * 2, [shape((2, n, width), BF)] * 2, place=pltpu.VMEM,
             )(self.keep.reshape(2, 2, n, width), *(g.reshape(2, n, width) for g in self.got))
             self.got = [lax.ppermute(a, ("dp", "tile"), last_route(0)), lax.ppermute(b, ("dp", "tile"), last_route(1))]
 
@@ -1117,7 +1119,7 @@
             spec_out = pl.BlockSpec((1, n, width), lambda i, s: (0, i, 0))
             s0, k0, s1, k1 = call(
                 second_kernel, (2,), [spec, spec, other, other], [spec_out, spec_out, other_out, other_out],
-                pair((1, 2 * n, width)) + pair((sp, 2 * n // sp, width)), weight=weight, place=None, also=also,
+                pair((1, 2 * n, width)) + pair((sp, 2 * n // sp, width)), weight=weight, place=pltpu.VMEM, also=also,
             )(self.keep[0], got[0], self.keep[1], got[1])
             self.got = [swap(s0, 2), swap(s1, 1)]
             self.keep = [k0, k1]
@@ -1128,7 +1130,7 @@
             args = [v.reshape(2, n, width) for pair in zip(self.keep, self.got) for v in pair]
             s, k = call(
                 third_kernel, (1,), [whole((2, n, width))] * 4, [whole((2, n, width))] * 2,
-                pair((2, n, width)), weight=weight, place=None,
+                pair((2, n, width)), weight=weight, place=pltpu.VMEM,
             )(*args)
             self.rows = n
             self.keep = k
@@ -1137,7 +1139,7 @@
                 n = self.rows // 2
                 spec = whole((2, 2, n, width))
                 s, k = call(
-                    more_kernel, (1,), [spec, spec], [whole((2, n, width))] * 2, pair((2, n, width)), place=None,
+                    more_kernel, (1,), [spec, spec], [whole((2, n, width))] * 2, pair((2, n, width)), place=pltpu.VMEM,
                 )(self.keep.reshape(2, 2, n, width), self.got.reshape(2, 2, n, width))
                 self.rows = n
                 self.keep = k
@@ -1148,7 +1150,7 @@
             spec = whole((2, 2, n, width))
             a, b = call(
                 functools.partial(fourth_kernel, sz), (1,), [spec, spec], [whole((2, n, width))] * 2,
-                [shape((2, n, width), BF)] * 2, place=None,
+                [shape((2, n, width), BF)] * 2, place=pltpu.VMEM,
             )(self.keep.reshape(2, 2, n, width), self.got.reshape(2, 2, n, width))
 
             self.got = [lax.ppermute(a, ("dp", "tile"), last_route(0)), lax.ppermute(b, ("dp", "tile"), last_route(1))]

time: 251 us -> 251 us (level)
  no operation moved by 1% of the time
where the time goes in v5:
time: 251 us; the launch traced here: 248 us
  Pallas kernels  105 us (42%)
  starting transfers between devices  56 us (22%)
  waiting for transfers between devices  54.1 us (22%)
  local copies, waits for them, and re-layouts  21.1 us (8%)
  other arithmetic  8.88 us (4%)
    pallas_call x28, Pallas kernels, go(): out = run(info, *pinned, *deps, *sources)  105 us
    ppermute x32, starting transfers between devices, partner(): return lax.ppermute(value, 'tile', [(t, t ^ x) for t in range(tiles)])  25.5 us
    ppermute x32, waiting for transfers between devices, partner(): return lax.ppermute(value, 'tile', [(t, t ^ x) for t in range(tiles)])  21.6 us
    unnamed x94, local copies, waits for them, and re-layouts  15.4 us
    ppermute x4, waiting for transfers between devices, fourth(): lax.ppermute(a, ('dp', 'tile'), last_route(0))  14.8 us
    ppermute x4, starting transfers between devices, fourth(): lax.ppermute(a, ('dp', 'tile'), last_route(0))  14 us
    ppermute x15, waiting for transfers between devices, swap(): lax.ppermute(value, 'dp', [(d, d ^ 1 << bit - 2) for d in range(pages)])  14 us
    ppermute x15, starting transfers between devices, swap(): lax.ppermute(value, 'dp', [(d, d ^ 1 << bit - 2) for d in range(pages)])  11.4 us
  transfers between devices with their start and end apart: 55, of which 12 were waited for; matrix products, arithmetic and copies ran while one was open for 5% of the time, Pallas kernels for 35%

profile of v5, /device:TPU:1, one launch (start us, length us, event | category | flops | bytes accessed | tf_op | source)
XLA Modules:
  0.0 247.6 jit_solution(10560265736727751006)
XLA Ops:
  2.7 6.1 %shard_map.282 = (f32[272,768]{1,0:T(8,128)S(1)}, bf16[272,2304]{1,0:T(8,128)(2,1)S(1)}, bf16[144,1536]{1,0:T(8,128)(2,1)S(1)}, bf16[64,1536]{1,0:T(8,128)(2,1)}...) custom-call(s32[5]{0:T(128)S(1)} %stack.48.refs_0_, bf16[256,768]{1,0:T(8,128)(2,1)} %bitcast.69, ...), custom_call_target="tpu_custom_call" | custom-call | flops 1 | bytes 1 | tf_op jit(solution)/shard_map/pallas_call | solution.py:836
  8.9 2.7 %collective-permute-start.1 = (bf16[64,1536]{1,0:T(8,128)(2,1)}, bf16[64,1536]{1,0:T(8,128)(2,1)S(1)}, u32[]{:S(2)}, u32[]{:S(2)}) collective-permute-start(bf16[64,1536]{1,0:T(8,128)(2,1)} %get-tuple-element.169), channel_id=1, source_target_pairs={{0,2},{1,3},{2,0},{3,1},{4,6},{5,7},{6,4},{7,5},{8,10},{9,11},{10,... | collective-permute-start | bytes 589832 | tf_op jit(solution)/shard_map/ppermute | solution.py:847
  14.2 6.1 %shard_map.283 = (f32[2,3,256,256]{3,2,1,0:T(8,128)S(1)}, f32[8,128]{1,0:T(8,128)}, bf16[768,768]{1,0:T(8,128)(2,1)S(1)}, bf16[768,3072]{1,0:T(8,128)(2,1)S(1)},...) custom-call(s32[5]{0:T(128)S(1)} %stack.48.refs_0_, ...), custom_call_target="tpu_custom_call" | custom-call | flops 1 | bytes 1 | tf_op jit(solution)/shard_map/pallas_call | solution.py:836
  20.6 11.5 %shard_map.284 = (bf16[12,256,256]{2,1,0:T(8,128)(2,1)}, bf16[4,256,768]{2,1,0:T(8,128)(2,1)}, bf16[4,256,768]{2,1,0:T(8,128)(2,1)}, bf16[272,6144]{1,0:T(8,128)...) custom-call(s32[5]{0:T(128)S(1)} %stack.48.refs_0_, ...), custom_call_target="tpu_custom_call" | custom-call | flops 1 | bytes 1 | tf_op jit(solution)/shard_map/pallas_call | solution.py:836
  36.8 4.9 %shard_map.285 = (f32[8,128]{1,0:T(8,128)}, bf16[768,768]{1,0:T(8,128)(2,1)S(1)}, bf16[768,3072]{1,0:T(8,128)(2,1)S(1)}, bf16[3072,768]{1,0:T(8,128)(2,1)S(1)}, bf16[256,768]{1,0:T(8,128)(2,1)S(1)}) custom-call(s32[5]{0:T(128)S(1)} %stack.48.refs_0_, f32[8,256]{1,0:T(8,128)S(1)} %copy-done.30, f32[8,128]{1,0:T(8,128)} %get-tuple-element.187.refs_2_, ...), custom_call_target="tpu_custom_call" | custom-call | flops 1 | bytes 1 | tf_op jit(solution)/shard_map/pallas_call | solution.py:836
  41.8 3.2 %collective-permute-done.5.refs_5_ = bf16[48,1536]{1,0:T(8,128)(2,1)} collective-permute-done((bf16[48,1536]{1,0:T(8,128)(2,1)}, bf16[48,1536]{1,0:T(8,128)(2,1)}, u32[]{:S(2)}, u32[]{:S(2)}) %collective-permute-start.5) | collective-permute-done | bytes 147488 | tf_op jit(solution)/shard_map/ppermute | solution.py:847
  45.0 13.1 %shard_map.286 = (f32[8,768]{1,0:T(8,128)S(1)}, bf16[12,256,256]{2,1,0:T(8,128)(2,1)S(1)}, bf16[4,256,768]{2,1,0:T(8,128)(2,1)S(1)}, bf16[4,256,768]{2,1,0:T(8,1...) custom-call(s32[5]{0:T(128)S(1)} %stack.48.refs_0_, ...), custom_call_target="tpu_custom_call" | custom-call | flops 1 | bytes 1 | tf_op jit(solution)/shard_map/pallas_call | solution.py:836
  58.7 5.7 %shard_map.287 = (bf16[256,768]{1,0:T(8,128)(2,1)S(1)}, f32[256,1536]{1,0:T(8,128)S(1)}, bf16[144,1536]{1,0:T(8,128)(2,1)S(1)}, bf16[64,1536]{1,0:T(8,128)(2,1)S...) custom-call(s32[5]{0:T(128)S(1)} %stack.48.refs_0_, ...), custom_call_target="tpu_custom_call" | custom-call | flops 1 | bytes 1 | tf_op jit(solution)/shard_map/pallas_call | solution.py:836
  66.6 3.9 %shard_map.288 = (bf16[2,4,96,768]{3,2,1,0:T(8,128)(2,1)}, bf16[2,4,96,768]{3,2,1,0:T(8,128)(2,1)S(1)}, f32[8,128]{1,0:T(8,128)}) custom-call(s32[5]{0:T(128)S(1)} %stack.48.refs_0_, bf16[272,4608]{1,0:T(8,128)(2,1)S(1)} %get-tuple-element.210.refs_1_.refs_9_, bf16[272,4608]{1,0:T(8,128)(2,1)S(1)} %collective-permute-done.10.refs_2_.refs_10_, ...), custom_call_target="tpu_custom_call" | custom-call | flops 1 | bytes 1 | tf_op jit(solution)/shard_map/pallas_call | solution.py:836
  70.6 4.7 %shard_map.289 = (bf16[8,4,24,768]{3,2,1,0:T(8,128)(2,1)}, bf16[8,4,24,768]{3,2,1,0:T(8,128)(2,1)S(1)}, f32[8,128]{1,0:T(8,128)}, bf16[768,2304]{1,0:T(8,128)(2,1)S(1)}) custom-call(s32[5]{0:T(128)S(1)} %stack.48.refs_0_, bf16[272,4608]{1,0:T(8,128)(2,1)S(1)} %get-tuple-element.210.refs_1_.refs_9_, ...), custom_call_target="tpu_custom_call" | custom-call | flops 1 | bytes 1 | tf_op jit(solution)/shard_map/pallas_call | solution.py:836
  79.0 4.8 %shard_map.290 = (bf16[272,768]{1,0:T(8,128)(2,1)S(1)}, bf16[272,768]{1,0:T(8,128)(2,1)S(1)}, bf16[272,768]{1,0:T(8,128)(2,1)S(1)}, f32[24,768]{1,0:T(8,128)S(1)...) custom-call(s32[5]{0:T(128)S(1)} %stack.48.refs_0_, ...), custom_call_target="tpu_custom_call" | custom-call | flops 99999997952 | bytes 1 | tf_op jit(solution)/shard_map/pallas_call | solution.py:836
  85.0 4.7 %shard_map.291 = (bf16[272,4608]{1,0:T(8,128)(2,1)S(1)}, f32[272,768]{1,0:T(8,128)S(1)}, f32[8,768]{1,0:T(8,128)S(1)}, f32[8,128]{1,0:T(8,128)}, bf16[272,2304]{...) custom-call(s32[5]{0:T(128)S(1)} %stack.48.refs_0_, ...), custom_call_target="tpu_custom_call" | custom-call | flops 1 | bytes 1 | tf_op jit(solution)/shard_map/pallas_call | solution.py:836
  89.8 5.7 %shard_map.292 = (bf16[256,768]{1,0:T(8,128)(2,1)S(1)}, f32[256,1536]{1,0:T(8,128)S(1)}, bf16[144,1536]{1,0:T(8,128)(2,1)S(1)}, bf16[64,1536]{1,0:T(8,128)(2,1)S...) custom-call(s32[5]{0:T(128)S(1)} %stack.48.refs_0_, ...), custom_call_target="tpu_custom_call" | custom-call | flops 1 | bytes 1 | tf_op jit(solution)/shard_map/pallas_call | solution.py:836
  101.5 4.3 %shard_map.293 = (bf16[2,8,2,24,768]{4,3,2,1,0:T(8,128)(2,1)S(1)}, bf16[2,8,2,24,768]{4,3,2,1,0:T(8,128)(2,1)S(1)}, f32[8,128]{1,0:T(8,128)}) custom-call(s32[5]{0:T(128)S(1)} %stack.48.refs_0_, bf16[272,6144]{1,0:T(8,128)(2,1)S(1)} %copy-done, bf16[272,6144]{1,0:T(8,128)(2,1)S(1)} %collective-permute-done.6.refs_10_.refs_2_, ...), custom_call_target="tpu_custom_call" | custom-call | flops 1 | bytes 1 | tf_op jit(solution)/shard_map/pallas_call | solution.py:836
  107.2 2.6 %shard_map.294 = (bf16[1,384,768]{2,1,0:T(8,128)(2,1)S(1)}, bf16[1,384,768]{2,1,0:T(8,128)(2,1)S(1)}, bf16[2,192,768]{2,1,0:T(8,128)(2,1)S(1)}, bf16[2,192,768]{2,1,0:T(8,128)(2,1)S(1)}, f32[8,128]{1,0:T(8,128)}) custom-call(s32[5]{0:T(128)S(1)} %stack.48.refs_0_, bf16[1,2,384,768]{3,2,1,0:T(8,128)(2,1)S(1)} %bitcast.105, ...), custom_call_target="tpu_custom_call" | custom-call | flops 99999997952 | bytes 1 | tf_op jit(solution)/shard_map/pallas_call | solution.py:836
  111.6 3.1 %shard_map.295 = (bf16[2,4,96,768]{3,2,1,0:T(8,128)(2,1)S(1)}, bf16[2,4,96,768]{3,2,1,0:T(8,128)(2,1)S(1)}, f32[8,128]{1,0:T(8,128)}) custom-call(s32[5]{0:T(128)S(1)} %stack.48.refs_0_, bf16[272,6144]{1,0:T(8,128)(2,1)S(1)} %copy-done, bf16[272,6144]{1,0:T(8,128)(2,1)S(1)} %collective-permute-done.6.refs_10_.refs_2_, ...), custom_call_target="tpu_custom_call" | custom-call | flops 1 | bytes 1 | tf_op jit(solution)/shard_map/pallas_call | solution.py:836
  115.3 3.8 %shard_map.296 = (bf16[8,4,24,768]{3,2,1,0:T(8,128)(2,1)S(1)}, bf16[8,4,24,768]{3,2,1,0:T(8,128)(2,1)S(1)}, f32[8,128]{1,0:T(8,128)}, bf16[768,2304]{1,0:T(8,128)(2,1)S(1)}) custom-call(s32[5]{0:T(128)S(1)} %stack.48.refs_0_, bf16[272,6144]{1,0:T(8,128)(2,1)S(1)} %copy-done, bf16[272,6144]{1,0:T(8,128)(2,1)S(1)} %collective-permute-done.6.refs_10_.refs_2_, ...), custom_call_target="tpu_custom_call" | custom-call | flops 1 | bytes 1 | tf_op jit(solution)/shard_map/pallas_call | solution.py:836
  119.1 3.2 %shard_map.297 = (bf16[272,768]{1,0:T(8,128)(2,1)S(1)}, bf16[272,768]{1,0:T(8,128)(2,1)S(1)}, bf16[272,768]{1,0:T(8,128)(2,1)S(1)}, f32[24,768]{1,0:T(8,128)S(1)...) custom-call(s32[5]{0:T(128)S(1)} %stack.48.refs_0_, bf16[256,768]{1,0:T(8,128)(2,1)S(1)} %get-tuple-element.235.refs_1_, ...), custom_call_target="tpu_custom_call" | custom-call | flops 1 | bytes 1 | tf_op jit(solution)/shard_map/pallas_call | solution.py:836
  122.4 3.9 %collective-permute-start.22 = (bf16[272,768]{1,0:T(8,128)(2,1)S(1)}, bf16[272,768]{1,0:T(8,128)(2,1)S(1)}, u32[]{:S(2)}, u32[]{:S(2)}) collective-permute-start(bf16[272,768]{1,0:T(8,128)(2,1)S(1)} %get-tuple-element.261.refs_3_), channel_id=1, source_target_pairs={{0,1},{1,0},{2,3},{3,2},{4,5},{5,4},{6,7},{7,6},{8,9},{9,8},{10,11... | collective-permute-start | bytes 1253384 | tf_op jit(solution)/shard_map/ppermute | solution.py:847
  128.5 2.1 collective-permute-start.23
  132.6 4.5 %shard_map.299 = (bf16[2,8,2,24,768]{4,3,2,1,0:T(8,128)(2,1)}, bf16[2,8,2,24,768]{4,3,2,1,0:T(8,128)(2,1)S(1)}, f32[8,128]{1,0:T(8,128)}) custom-call(s32[5]{0:T(128)S(1)} %stack.48.refs_0_, bf16[272,6144]{1,0:T(8,128)(2,1)S(1)} %copy-done, bf16[272,6144]{1,0:T(8,128)(2,1)S(1)} %collective-permute-done.6.refs_10_.refs_2_, ...), custom_call_target="tpu_custom_call" | custom-call | flops 1 | bytes 1 | tf_op jit(solution)/shard_map/pallas_call | solution.py:836
  140.8 13.6 %collective-permute-done.28 = bf16[8,4,24,768]{3,2,1,0:T(8,128)(2,1)S(1)} collective-permute-done((bf16[8,4,24,768]{3,2,1,0:T(8,128)(2,1)S(1)}, bf16[8,4,24,768]{3,2,1,0:T(8,128)(2,1)S(1)}, u32[]{:S(2)}, u32[]{:S(2)}) %collective-permute-start.28) | collective-permute-done | bytes 1179680 | tf_op jit(solution)/shard_map/ppermute | solution.py:847
  157.2 3.5 %collective-permute-done.35 = bf16[192,768]{1,0:T(8,128)(2,1)S(1)} collective-permute-done((bf16[192,768]{1,0:T(8,128)(2,1)S(1)}, bf16[192,768]{1,0:T(8,128)(2,1)S(1)}, u32[]{:S(2)}, u32[]{:S(2)}) %collective-permute-start.35) | collective-permute-done | bytes 294944 | tf_op jit(solution)/shard_map/ppermute | solution.py:847
  165.2 12.0 %collective-permute-done.34 = bf16[2,192,768]{2,1,0:T(8,128)(2,1)S(1)} collective-permute-done((bf16[2,192,768]{2,1,0:T(8,128)(2,1)S(1)}, bf16[2,192,768]{2,1,0:T(8,128)(2,1)S(1)}, u32[]{:S(2)}, u32[]{:S(2)}) %collective-permute-start.34) | collective-permute-done | bytes 589856 | tf_op jit(solution)/shard_map/ppermute | solution.py:855
  178.7 2.3 collective-permute-start.54
  181.0 3.5 %collective-permute-start.53 = (bf16[2,96,768]{2,1,0:T(8,128)(2,1)}, bf16[2,96,768]{2,1,0:T(8,128)(2,1)}, u32[]{:S(2)}, u32[]{:S(2)}) collective-permute-start(bf16[2,96,768]{2,1,0:T(8,128)(2,1)} %get-tuple-element.319), channel_id=1, source_target_pairs={{0,0},{1,16},{2,2},{3,18},{4,4},{5,20},{6,6},{7,22},{8,8},{9,24},{... | collective-permute-start | bytes 884744 | tf_op jit(solution)/shard_map/ppermute | solution.py:1156
  204.5 4.1 %collective-permute-start.49 = (bf16[2,48,768]{2,1,0:T(8,128)(2,1)S(1)}, bf16[2,48,768]{2,1,0:T(8,128)(2,1)}, u32[]{:S(2)}, u32[]{:S(2)}) collective-permute-start(bf16[2,48,768]{2,1,0:T(8,128)(2,1)S(1)} %get-tuple-element.315), channel_id=1, source_target_pairs={{0,0},{1,16},{2,2},{3,18},{4,4},{5,20},{6,6},{7,22},{8,8},{9,24},{... | collective-permute-start | bytes 442376 | tf_op jit(solution)/shard_map/ppermute | solution.py:1093
  210.8 3.6 %collective-permute-done.50 = bf16[2,48,768]{2,1,0:T(8,128)(2,1)} collective-permute-done((bf16[2,48,768]{2,1,0:T(8,128)(2,1)S(1)}, bf16[2,48,768]{2,1,0:T(8,128)(2,1)}, u32[]{:S(2)}, u32[]{:S(2)}) %collective-permute-start.50) | collective-permute-done | bytes 147488 | tf_op jit(solution)/shard_map/ppermute | solution.py:1093
  222.2 4.3 %collective-permute-start.47 = (bf16[2,48,768]{2,1,0:T(8,128)(2,1)S(1)}, bf16[2,48,768]{2,1,0:T(8,128)(2,1)S(1)}, u32[]{:S(2)}, u32[]{:S(2)}) collective-permute-start(bf16[2,48,768]{2,1,0:T(8,128)(2,1)S(1)} %get-tuple-element.313), channel_id=1, source_target_pairs={{0,0},{1,16},{2,2},{3,18},{4,4},{5,20},{6,6},{7,22},{8,8},{9,24},{... | collective-permute-start | bytes 442376 | tf_op jit(solution)/shard_map/ppermute | solution.py:1093
  228.0 2.1 collective-permute-start.51
  230.7 5.1 %collective-permute-done.47 = bf16[2,48,768]{2,1,0:T(8,128)(2,1)S(1)} collective-permute-done((bf16[2,48,768]{2,1,0:T(8,128)(2,1)S(1)}, bf16[2,48,768]{2,1,0:T(8,128)(2,1)S(1)}, u32[]{:S(2)}, u32[]{:S(2)}) %collective-permute-start.47) | collective-permute-done | bytes 147488 | tf_op jit(solution)/shard_map/ppermute | solution.py:1093
  237.7 7.6 %collective-permute-done.51 = bf16[2,96,768]{2,1,0:T(8,128)(2,1)S(1)} collective-permute-done((bf16[2,96,768]{2,1,0:T(8,128)(2,1)S(1)}, bf16[2,96,768]{2,1,0:T(8,128)(2,1)S(1)}, u32[]{:S(2)}, u32[]{:S(2)}) %collective-permute-start.51) | collective-permute-done | bytes 294944 | tf_op jit(solution)/shard_map/ppermute | solution.py:1156
  (244 shorter events, 78.7 us)
Async XLA Ops:
  8.8 11.6 %collective-permute-start = (bf16[144,1536]{1,0:T(8,128)(2,1)S(1)}, bf16[144,1536]{1,0:T(8,128)(2,1)S(1)}, u32[]{:S(2)}, u32[]{:S(2)}) collective-permute-start(bf16[144,1536]{1,0:T(8,128)(2,1)S(1)} %get-tuple-element.168.refs_2_), channel_id=1, source_target_pairs={{0,1},{1,0},{2,3},{3,2},{4,5},{5,4},{6,7},{7,6},{8,9},{9,8},{10,11... | collective-permute-start | bytes 1327112 | tf_op jit(solution)/shard_map/ppermute | solution.py:847
  34.1 24.6 %collective-permute-start.6 = (bf16[272,6144]{1,0:T(8,128)(2,1)}, bf16[272,6144]{1,0:T(8,128)(2,1)S(1)}, u32[]{:S(2)}, u32[]{:S(2)}) collective-permute-start(bf16[272,6144]{1,0:T(8,128)(2,1)} %get-tuple-element.201.refs_1_.refs_9_), channel_id=1, source_target_pairs={{0,1},{1,0},{2,3},{3,2},{4,5},{5,4},{6,7},{7,6},{8,9},{9,8},{10,11... | collective-permute-start | bytes 10027016 | tf_op jit(solution)/shard_map/ppermute | solution.py:847
  64.4 14.6 %collective-permute-start.7 = (bf16[144,1536]{1,0:T(8,128)(2,1)S(1)}, bf16[144,1536]{1,0:T(8,128)(2,1)S(1)}, u32[]{:S(2)}, u32[]{:S(2)}) collective-permute-start(bf16[144,1536]{1,0:T(8,128)(2,1)S(1)} %get-tuple-element.204.refs_3_), channel_id=1, source_target_pairs={{0,1},{1,0},{2,3},{3,2},{4,5},{5,4},{6,7},{7,6},{8,9},{9,8},{10,11... | collective-permute-start | bytes 1327112 | tf_op jit(solution)/shard_map/ppermute | solution.py:847
  64.6 14.4 %collective-permute-start.8 = (bf16[64,1536]{1,0:T(8,128)(2,1)S(1)}, bf16[64,1536]{1,0:T(8,128)(2,1)S(1)}, u32[]{:S(2)}, u32[]{:S(2)}) collective-permute-start(bf16[64,1536]{1,0:T(8,128)(2,1)S(1)} %get-tuple-element.205), channel_id=1, source_target_pairs={{0,2},{1,3},{2,0},{3,1},{4,6},{5,7},{6,4},{7,5},{8,10},{9,11},{10,... | collective-permute-start | bytes 589832 | tf_op jit(solution)/shard_map/ppermute | solution.py:847
  66.0 13.0 %collective-permute-start.9 = (bf16[48,1536]{1,0:T(8,128)(2,1)S(1)}, bf16[48,1536]{1,0:T(8,128)(2,1)S(1)}, u32[]{:S(2)}, u32[]{:S(2)}) collective-permute-start(bf16[48,1536]{1,0:T(8,128)(2,1)S(1)} %get-tuple-element.206), channel_id=1, source_target_pairs={{0,3},{1,2},{2,1},{3,0},{4,7},{5,6},{6,5},{7,4},{8,11},{9,10},{10,... | collective-permute-start | bytes 442376 | tf_op jit(solution)/shard_map/ppermute | solution.py:847
  76.3 29.5 %collective-permute-start.16 = (bf16[8,4,24,768]{3,2,1,0:T(8,128)(2,1)}, bf16[8,4,24,768]{3,2,1,0:T(8,128)(2,1)}, u32[]{:S(2)}, u32[]{:S(2)}) collective-permute-start(bf16[8,4,24,768]{3,2,1,0:T(8,128)(2,1)} %get-tuple-element.245), channel_id=1, source_target_pairs={{0,2},{1,3},{2,0},{3,1},{4,6},{5,7},{6,4},{7,5},{8,10},{9,11},{10,... | collective-permute-start | bytes 3538952 | tf_op jit(solution)/shard_map/ppermute | solution.py:847
  77.8 29.4 %collective-permute-start.17 = (bf16[2,4,96,768]{3,2,1,0:T(8,128)(2,1)}, bf16[2,4,96,768]{3,2,1,0:T(8,128)(2,1)}, u32[]{:S(2)}, u32[]{:S(2)}) collective-permute-start(bf16[2,4,96,768]{3,2,1,0:T(8,128)(2,1)} %get-tuple-element.247), channel_id=1, source_target_pairs={{0,4},{4,0},{8,12},{12,8},{16,20},{20,16},{24,28},{28,24},{1,5},{5... | collective-permute-start | bytes 3538952 | tf_op jit(solution)/shard_map/ppermute | solution.py:855
  83.9 11.6 %collective-permute-start.18 = (bf16[272,768]{1,0:T(8,128)(2,1)S(1)}, bf16[272,768]{1,0:T(8,128)(2,1)S(1)}, u32[]{:S(2)}, u32[]{:S(2)}) collective-permute-start(bf16[272,768]{1,0:T(8,128)(2,1)S(1)} %get-tuple-element.248.refs_3_), channel_id=1, source_target_pairs={{0,1},{1,0},{2,3},{3,2},{4,5},{5,4},{6,7},{7,6},{8,9},{9,8},{10,11... | collective-permute-start | bytes 1253384 | tf_op jit(solution)/shard_map/ppermute | solution.py:847
  84.5 11.8 %collective-permute-start.19 = (bf16[272,768]{1,0:T(8,128)(2,1)S(1)}, bf16[272,768]{1,0:T(8,128)(2,1)S(1)}, u32[]{:S(2)}, u32[]{:S(2)}) collective-permute-start(bf16[272,768]{1,0:T(8,128)(2,1)S(1)} %get-tuple-element.249.refs_5_), channel_id=1, source_target_pairs={{0,1},{1,0},{2,3},{3,2},{4,5},{5,4},{6,7},{7,6},{8,9},{9,8},{10,11... | collective-permute-start | bytes 1253384 | tf_op jit(solution)/shard_map/ppermute | solution.py:847
  84.6 13.0 %collective-permute-start.20 = (bf16[272,768]{1,0:T(8,128)(2,1)S(1)}, bf16[272,768]{1,0:T(8,128)(2,1)S(1)}, u32[]{:S(2)}, u32[]{:S(2)}) collective-permute-start(bf16[272,768]{1,0:T(8,128)(2,1)S(1)} %get-tuple-element.250.refs_7_), channel_id=1, source_target_pairs={{0,1},{1,0},{2,3},{3,2},{4,5},{5,4},{6,7},{7,6},{8,9},{9,8},{10,11... | collective-permute-start | bytes 1253384 | tf_op jit(solution)/shard_map/ppermute | solution.py:847
  96.3 19.0 %collective-permute-start.12 = (bf16[144,1536]{1,0:T(8,128)(2,1)S(1)}, bf16[144,1536]{1,0:T(8,128)(2,1)S(1)}, u32[]{:S(2)}, u32[]{:S(2)}) collective-permute-start(bf16[144,1536]{1,0:T(8,128)(2,1)S(1)} %get-tuple-element.237.refs_3_), channel_id=1, source_target_pairs={{0,1},{1,0},{2,3},{3,2},{4,5},{5,4},{6,7},{7,6},{8,9},{9,8},{10,11... | collective-permute-start | bytes 1327112 | tf_op jit(solution)/shard_map/ppermute | solution.py:847
  97.1 13.0 %collective-permute-start.14 = (bf16[48,1536]{1,0:T(8,128)(2,1)S(1)}, bf16[48,1536]{1,0:T(8,128)(2,1)S(1)}, u32[]{:S(2)}, u32[]{:S(2)}) collective-permute-start(bf16[48,1536]{1,0:T(8,128)(2,1)S(1)} %get-tuple-element.239), channel_id=1, source_target_pairs={{0,3},{1,2},{2,1},{3,0},{4,7},{5,6},{6,5},{7,4},{8,11},{9,10},{10,... | collective-permute-start | bytes 442376 | tf_op jit(solution)/shard_map/ppermute | solution.py:847
  98.4 12.9 %collective-permute-start.15 = (bf16[272,4608]{1,0:T(8,128)(2,1)S(1)}, bf16[272,4608]{1,0:T(8,128)(2,1)S(1)}, u32[]{:S(2)}, u32[]{:S(2)}) collective-permute-start(bf16[272,4608]{1,0:T(8,128)(2,1)S(1)} %get-tuple-element.243.refs_1_.refs_3_.refs_11_), channel_id=1, source_target_pairs={{0,1},{1,0},{2,3},{3,2},{4,5},{5,4},{6,7},{7,6},{8,9},{9,8},{10,11... | collective-permute-start | bytes 7520264 | tf_op jit(solution)/shard_map/ppermute | solution.py:847
  105.9 31.5 %collective-permute-start.30 = (bf16[2,8,2,24,768]{4,3,2,1,0:T(8,128)(2,1)S(1)}, bf16[2,8,2,24,768]{4,3,2,1,0:T(8,128)(2,1)S(1)}, u32[]{:S(2)}, u32[]{:S(2)}) collective-permute-start(bf16[2,8,2,24,768]{4,3,2,1,0:T(8,128)(2,1)S(1)} %get-tuple-element.277), channel_id=1, source_target_pairs={{0,8},{4,12},{8,0},{12,4},{16,24},{20,28},{24,16},{28,20},{1,9},{5... | collective-permute-start | bytes 3538952 | tf_op jit(solution)/shard_map/ppermute | solution.py:855
  109.8 17.8 %collective-permute-start.25 = (bf16[1,384,768]{2,1,0:T(8,128)(2,1)S(1)}, bf16[1,384,768]{2,1,0:T(8,128)(2,1)S(1)}, u32[]{:S(2)}, u32[]{:S(2)}) collective-permute-start(bf16[1,384,768]{2,1,0:T(8,128)(2,1)S(1)} %get-tuple-element.265), channel_id=1, source_target_pairs={{0,4},{4,0},{8,12},{12,8},{16,20},{20,16},{24,28},{28,24},{1,5},{5... | collective-permute-start | bytes 1769480 | tf_op jit(solution)/shard_map/ppermute | solution.py:855
  111.3 17.2 %collective-permute-start.26 = (bf16[2,192,768]{2,1,0:T(8,128)(2,1)S(1)}, bf16[2,192,768]{2,1,0:T(8,128)(2,1)S(1)}, u32[]{:S(2)}, u32[]{:S(2)}) collective-permute-start(bf16[2,192,768]{2,1,0:T(8,128)(2,1)S(1)} %get-tuple-element.267), channel_id=1, source_target_pairs={{0,2},{1,3},{2,0},{3,1},{4,6},{5,7},{6,4},{7,5},{8,10},{9,11},{10,... | collective-permute-start | bytes 1769480 | tf_op jit(solution)/shard_map/ppermute | solution.py:847
  126.3 28.1 %collective-permute-start.28 = (bf16[8,4,24,768]{3,2,1,0:T(8,128)(2,1)S(1)}, bf16[8,4,24,768]{3,2,1,0:T(8,128)(2,1)S(1)}, u32[]{:S(2)}, u32[]{:S(2)}) collective-permute-start(bf16[8,4,24,768]{3,2,1,0:T(8,128)(2,1)S(1)} %get-tuple-element.273), channel_id=1, source_target_pairs={{0,2},{1,3},{2,0},{3,1},{4,6},{5,7},{6,4},{7,5},{8,10},{9,11},{10,... | collective-permute-start | bytes 3538952 | tf_op jit(solution)/shard_map/ppermute | solution.py:847
  127.5 27.8 %collective-permute-start.29 = (bf16[2,4,96,768]{3,2,1,0:T(8,128)(2,1)S(1)}, bf16[2,4,96,768]{3,2,1,0:T(8,128)(2,1)S(1)}, u32[]{:S(2)}, u32[]{:S(2)}) collective-permute-start(bf16[2,4,96,768]{3,2,1,0:T(8,128)(2,1)S(1)} %get-tuple-element.275), channel_id=1, source_target_pairs={{0,4},{4,0},{8,12},{12,8},{16,20},{20,16},{24,28},{28,24},{1,5},{5... | collective-permute-start | bytes 3538952 | tf_op jit(solution)/shard_map/ppermute | solution.py:855
  137.2 58.2 %collective-permute-start.40 = (bf16[2,8,2,24,768]{4,3,2,1,0:T(8,128)(2,1)}, bf16[2,8,2,24,768]{4,3,2,1,0:T(8,128)(2,1)S(1)}, u32[]{:S(2)}, u32[]{:S(2)}) collective-permute-start(bf16[2,8,2,24,768]{4,3,2,1,0:T(8,128)(2,1)} %get-tuple-element.298), channel_id=1, source_target_pairs={{0,8},{4,12},{8,0},{12,4},{16,24},{20,28},{24,16},{28,20},{1,9},{5... | collective-permute-start | bytes 3538952 | tf_op jit(solution)/shard_map/ppermute | solution.py:855
  138.2 22.5 %collective-permute-start.35 = (bf16[192,768]{1,0:T(8,128)(2,1)S(1)}, bf16[192,768]{1,0:T(8,128)(2,1)S(1)}, u32[]{:S(2)}, u32[]{:S(2)}) collective-permute-start(bf16[192,768]{1,0:T(8,128)(2,1)S(1)} %get-tuple-element.288), channel_id=1, source_target_pairs={{0,2},{1,3},{2,0},{3,1},{4,6},{5,7},{6,4},{7,5},{8,10},{9,11},{10,... | collective-permute-start | bytes 884744 | tf_op jit(solution)/shard_map/ppermute | solution.py:847
  139.5 37.7 %collective-permute-start.34 = (bf16[2,192,768]{2,1,0:T(8,128)(2,1)S(1)}, bf16[2,192,768]{2,1,0:T(8,128)(2,1)S(1)}, u32[]{:S(2)}, u32[]{:S(2)}) collective-permute-start(bf16[2,192,768]{2,1,0:T(8,128)(2,1)S(1)} %get-tuple-element.286), channel_id=1, source_target_pairs={{0,8},{4,12},{8,0},{12,4},{16,24},{20,28},{24,16},{28,20},{1,9},{5... | collective-permute-start | bytes 1769480 | tf_op jit(solution)/shard_map/ppermute | solution.py:855
  156.6 28.6 %collective-permute-start.32 = (bf16[1,384,768]{2,1,0:T(8,128)(2,1)S(1)}, bf16[1,384,768]{2,1,0:T(8,128)(2,1)S(1)}, u32[]{:S(2)}, u32[]{:S(2)}) collective-permute-start(bf16[1,384,768]{2,1,0:T(8,128)(2,1)S(1)} %get-tuple-element.282), channel_id=1, source_target_pairs={{0,4},{4,0},{8,12},{12,8},{16,20},{20,16},{24,28},{28,24},{1,5},{5... | collective-permute-start | bytes 1769480 | tf_op jit(solution)/shard_map/ppermute | solution.py:855
  160.7 26.8 %collective-permute-start.33 = (bf16[2,192,768]{2,1,0:T(8,128)(2,1)S(1)}, bf16[2,192,768]{2,1,0:T(8,128)(2,1)S(1)}, u32[]{:S(2)}, u32[]{:S(2)}) collective-permute-start(bf16[2,192,768]{2,1,0:T(8,128)(2,1)S(1)} %get-tuple-element.284), channel_id=1, source_target_pairs={{0,2},{1,3},{2,0},{3,1},{4,6},{5,7},{6,4},{7,5},{8,10},{9,11},{10,... | collective-permute-start | bytes 1769480 | tf_op jit(solution)/shard_map/ppermute | solution.py:847
  161.9 16.7 %collective-permute-start.27 = (f32[2,24,768]{2,1,0:T(8,128)S(1)}, f32[2,24,768]{2,1,0:T(8,128)S(1)}, u32[]{:S(2)}, u32[]{:S(2)}) collective-permute-start(f32[2,24,768]{2,1,0:T(8,128)S(1)} %fusion.9), channel_id=1, source_target_pairs={{0,2},{1,3},{2,0},{3,1},{4,6},{5,7},{6,4},{7,5},{8,10},{9,11},{10,... | collective-permute-start | bytes 442376 | tf_op jit(solution)/shard_map/ppermute | solution.py:847
  178.7 19.7 %collective-permute-start.54 = (bf16[2,96,768]{2,1,0:T(8,128)(2,1)}, bf16[2,96,768]{2,1,0:T(8,128)(2,1)}, u32[]{:S(2)}, u32[]{:S(2)}) collective-permute-start(bf16[2,96,768]{2,1,0:T(8,128)(2,1)} %get-tuple-element.320), channel_id=1, source_target_pairs={{0,1},{1,17},{2,3},{3,19},{4,5},{5,21},{6,7},{7,23},{8,9},{9,25},{... | collective-permute-start | bytes 884744 | tf_op jit(solution)/shard_map/ppermute | solution.py:1156
  181.0 17.7 %collective-permute-start.53 = (bf16[2,96,768]{2,1,0:T(8,128)(2,1)}, bf16[2,96,768]{2,1,0:T(8,128)(2,1)}, u32[]{:S(2)}, u32[]{:S(2)}) collective-permute-start(bf16[2,96,768]{2,1,0:T(8,128)(2,1)} %get-tuple-element.319), channel_id=1, source_target_pairs={{0,0},{1,16},{2,2},{3,18},{4,4},{5,20},{6,6},{7,22},{8,8},{9,24},{... | collective-permute-start | bytes 884744 | tf_op jit(solution)/shard_map/ppermute | solution.py:1156
  197.1 22.5 %collective-permute-start.42 = (bf16[2,192,768]{2,1,0:T(8,128)(2,1)}, bf16[2,192,768]{2,1,0:T(8,128)(2,1)S(1)}, u32[]{:S(2)}, u32[]{:S(2)}) collective-permute-start(bf16[2,192,768]{2,1,0:T(8,128)(2,1)} %get-tuple-element.303), channel_id=1, source_target_pairs={{0,8},{4,12},{8,0},{12,4},{16,24},{20,28},{24,16},{28,20},{1,9},{5... | collective-permute-start | bytes 1769480 | tf_op jit(solution)/shard_map/ppermute | solution.py:855
  202.8 11.6 %collective-permute-start.50 = (bf16[2,48,768]{2,1,0:T(8,128)(2,1)S(1)}, bf16[2,48,768]{2,1,0:T(8,128)(2,1)}, u32[]{:S(2)}, u32[]{:S(2)}) collective-permute-start(bf16[2,48,768]{2,1,0:T(8,128)(2,1)S(1)} %get-tuple-element.316), channel_id=1, source_target_pairs={{0,1},{1,17},{2,3},{3,19},{4,5},{5,21},{6,7},{7,23},{8,9},{9,25},{... | collective-permute-start | bytes 442376 | tf_op jit(solution)/shard_map/ppermute | solution.py:1093
  204.5 12.2 %collective-permute-start.49 = (bf16[2,48,768]{2,1,0:T(8,128)(2,1)S(1)}, bf16[2,48,768]{2,1,0:T(8,128)(2,1)}, u32[]{:S(2)}, u32[]{:S(2)}) collective-permute-start(bf16[2,48,768]{2,1,0:T(8,128)(2,1)S(1)} %get-tuple-element.315), channel_id=1, source_target_pairs={{0,0},{1,16},{2,2},{3,18},{4,4},{5,20},{6,6},{7,22},{8,8},{9,24},{... | collective-permute-start | bytes 442376 | tf_op jit(solution)/shard_map/ppermute | solution.py:1093
  209.9 16.9 %collective-permute-start.41 = (f32[2,24,768]{2,1,0:T(8,128)S(1)}, f32[2,24,768]{2,1,0:T(8,128)S(1)}, u32[]{:S(2)}, u32[]{:S(2)}) collective-permute-start(f32[2,24,768]{2,1,0:T(8,128)S(1)} %add.81), channel_id=1, source_target_pairs={{0,16},{4,20},{8,24},{12,28},{16,0},{20,4},{24,8},{28,12},{1,17},{... | collective-permute-start | bytes 442376 | tf_op jit(solution)/shard_map/ppermute | solution.py:855
  222.2 13.7 %collective-permute-start.47 = (bf16[2,48,768]{2,1,0:T(8,128)(2,1)S(1)}, bf16[2,48,768]{2,1,0:T(8,128)(2,1)S(1)}, u32[]{:S(2)}, u32[]{:S(2)}) collective-permute-start(bf16[2,48,768]{2,1,0:T(8,128)(2,1)S(1)} %get-tuple-element.313), channel_id=1, source_target_pairs={{0,0},{1,16},{2,2},{3,18},{4,4},{5,20},{6,6},{7,22},{8,8},{9,24},{... | collective-permute-start | bytes 442376 | tf_op jit(solution)/shard_map/ppermute | solution.py:1093
  228.0 17.3 %collective-permute-start.51 = (bf16[2,96,768]{2,1,0:T(8,128)(2,1)S(1)}, bf16[2,96,768]{2,1,0:T(8,128)(2,1)S(1)}, u32[]{:S(2)}, u32[]{:S(2)}) collective-permute-start(bf16[2,96,768]{2,1,0:T(8,128)(2,1)S(1)} %get-tuple-element.317), channel_id=1, source_target_pairs={{0,0},{1,16},{2,2},{3,18},{4,4},{5,20},{6,6},{7,22},{8,8},{9,24},{... | collective-permute-start | bytes 884744 | tf_op jit(solution)/shard_map/ppermute | solution.py:1156
  (69 other events, 438.3 us)
